TPU v7x, 32 devices: a whole 2x2x4 slice. The times are simulated.
32 devices in a mesh: groups: 2 (over y), row: 8 (over z, x), col: 2 (over core).
Axes of the slice: x: 2, y: 2, z: 4, core: 2. Of those that a mesh axis runs over, the one named last changes fastest.
Arguments:
- activations: bfloat16 [384, 14336], P(('groups', 'row', 'col')), parts along dimension 0, may hold values from -6 to 6
- pseudo_grads: bfloat16 [384, 4096], P(('groups', 'row', 'col')), parts along dimension 0, may hold values from -6 to 6
- row_counts: int32 [32], P(('groups', 'row', 'col')), parts along dimension 0, may hold values from 1 to 12, 144 in all
Outputs:
- act_cov: float32 [28672, 14336], P(('groups', 'row'), 'col'), parts along dimension 0
- grad_cov: float32 [8192, 4096], P(('groups', 'row'), 'col'), parts along dimension 0
There are 2 independent parts, one for each index of `groups`. A program takes and returns all parts, laid end to end along the dimension named above; each array names one. Nothing has to cross between parts.
Inputs may be any that keep to these rules, and one draw needn't show every extreme that they name: `row_counts`: the counts sum to 144; some device holds exactly 12.
All inputs are finite; a program needn't handle non-finite values.
Results may differ from a plain program's by a relative error of at most 0.0003.
Values may be sent and summed in bfloat16 or wider, within the bound.
No kernel may reach another device: no remote copies, remote signals or barrier semaphores. Data moves between devices by JAX's collectives and lax.ppermute only.
A program may use at most 384 MiB of HBM per device.

v0:
```python
import jax
import jax.numpy as jnp
from jax import lax
from jax.sharding import PartitionSpec as P


def gram_part(left_rows, right_rows):
    return lax.dot_general(
        left_rows, right_rows, (((0,), (0,)), ((), ())), preferred_element_type=jnp.float32
    )


def local(activations, pseudo_grads, row_counts):
    position = jnp.arange(activations.shape[0], dtype=jnp.int32)
    live_mask = (position < row_counts[0]).astype(jnp.bfloat16)[:, None]
    masked_act = activations * live_mask
    masked_grad = pseudo_grads * live_mask
    live = lax.psum(row_counts.astype(jnp.float32), ("row", "col"))
    col_size = lax.axis_size("col")
    pair_act, pair_grad = (
        lax.all_gather(masked_act, "col", axis=0, tiled=True),
        lax.all_gather(masked_grad, "col", axis=0, tiled=True),
    )
    left_act, left_grad = (
        lax.all_to_all(pair_act, "row", split_axis=1, concat_axis=0, tiled=True),
        lax.all_to_all(pair_grad, "row", split_axis=1, concat_axis=0, tiled=True),
    )
    col_index = lax.axis_index("col")
    act_half = activations.shape[1] // col_size
    grad_half = pseudo_grads.shape[1] // col_size
    right_act = lax.dynamic_slice_in_dim(pair_act, col_index * act_half, act_half, 1)
    right_grad = lax.dynamic_slice_in_dim(pair_grad, col_index * grad_half, grad_half, 1)
    act_tile = gram_part(left_act, lax.all_gather(right_act, "row", axis=0, tiled=True))
    grad_tile = gram_part(left_grad, lax.all_gather(right_grad, "row", axis=0, tiled=True))
    return (act_tile / live[0], grad_tile / live[0])


def solution(mesh):
    return jax.shard_map(
        local,
        mesh=mesh,
        in_specs=(
            P(("groups", "row", "col"), None),
            P(("groups", "row", "col"), None),
            P(("groups", "row", "col")),
        ),
        out_specs=(P(("groups", "row"), "col"), P(("groups", "row"), "col")),
        check_vma=False,
    )
```

profile of v0, /device:TPU:0, one launch (start us, length us, event | category | flops | bytes accessed | tf_op | source)
XLA Modules:
  0.0 152.0 jit_solution(13132086824213208329)
XLA Ops:
  7.2 0.0 copy-start
  7.2 0.0 all-gather.4.cloned.1.call-start
  7.9 1.1 multiply_bitcast_fusion
  9.0 2.5 %all-gather = bf16[2,12,14336]{2,1,0:T(8,128)(2,1)S(1)} all-gather(bf16[1,12,14336]{2,1,0:T(8,128)(2,1)S(1)} %multiply_bitcast_fusion), channel_id=1, replica_groups=mesh['groups'=2,'row'=8,'col'=2] {'col'}, dimensions={0}, use_global_device_ids=true | all-gather | bytes 1032192 | tf_op jit(solution)/shard_map/all_gather | solution.py:21
  11.6 0.2 reshape.16
  11.8 0.8 constant_dynamic-slice_fusion.1
  12.5 0.0 all-gather.4.cloned.1.call-update
  12.6 0.0 copy-done
  12.6 0.1 multiply_bitcast_fusion.1
  12.7 2.0 %all-gather.1 = bf16[2,12,4096]{2,1,0:T(8,128)(2,1)S(1)} all-gather(bf16[1,12,4096]{2,1,0:T(8,128)(2,1)S(1)} %multiply_bitcast_fusion.1), channel_id=1, replica_groups=mesh['groups'=2,'row'=8,'col'=2] {'col'}, dimensions={0}, use_global_device_ids=true | all-gather | bytes 294912 | tf_op jit(solution)/shard_map/all_gather | solution.py:22
  14.7 0.1 all_to_all.32
  14.8 0.7 copy.8
  15.6 7.2 %all-to-all-start.1 = ((bf16[24,8,512]{2,0,1:T(8,128)(2,1)}), bf16[24,8,512]{2,0,1:T(8,128)(2,1)S(1)}, u32[]{:S(2)}, u32[]{:S(2)}) async-start(bf16[24,8,512]{2,0,1:T(8,128)(2,1)} %copy.8), calls=%async_computation.1 | async-start | bytes 393216 | tf_op jit(solution)/shard_map/all_to_all | solution.py:26
  22.7 0.6 all_to_all.28
  23.3 1.0 copy.7
  24.3 10.7 %all-to-all-done.1 = bf16[24,8,512]{2,0,1:T(8,128)(2,1)S(1)} async-done(((bf16[24,8,512]{2,0,1:T(8,128)(2,1)}), bf16[24,8,512]{2,0,1:T(8,128)(2,1)S(1)}, u32[]{:S(2)}, u32[]{:S(2)}) %all-to-all-start.1) | async-done | bytes 196640 | tf_op jit(solution)/shard_map/all_to_all | solution.py:26
  34.9 4.3 %all-to-all-start = ((bf16[24,8,1792]{2,0,1:T(8,128)(2,1)}), bf16[24,8,1792]{2,0,1:T(8,128)(2,1)S(1)}, u32[]{:S(2)}, u32[]{:S(2)}) async-start(bf16[24,8,1792]{2,0,1:T(8,128)(2,1)} %copy.7), calls=%async_computation | async-start | bytes 1376256 | tf_op jit(solution)/shard_map/all_to_all | solution.py:25
  39.2 44.7 %psum.7 = f32[]{:T(128)} all-reduce(f32[]{:T(128)} %bitcast.4), channel_id=1, replica_groups=mesh['groups'=2,'row'=8,'col'=2] {'row','col'}, use_global_device_ids=true, to_apply=%region_0.0 | all-reduce | flops 1 | bytes 8 | tf_op jit(solution)/shard_map/psum | solution.py:18
  83.9 0.1 reshape.18
  84.0 34.3 %all_gather.15 = bf16[192,2048]{1,0:T(8,128)(2,1)S(1)} all-gather(bf16[24,2048]{1,0:T(8,128)(2,1)S(1)} %constant_dynamic-slice_fusion), channel_id=1, replica_groups=mesh['groups'=2,'row'=8,'col'=2] {'row'}, dimensions={0}, use_global_device_ids=true | all-gather | bytes 884736 | tf_op jit(solution)/shard_map/all_gather | solution.py:34
  118.3 3.3 %convolution_divide_fusion = f32[512,2048]{1,0:T(8,128)} fusion(bf16[192,512]{1,0:T(8,128)(2,1)S(1)} %bitcast.18, bf16[192,2048]{1,0:T(8,128)(2,1)S(1)} %all_gather.15, f32[]{:T(128)} %psum.7), kind=kOutput, calls=%fused_computation.1 | convolution fusion | flops 403701760 | bytes 5177348 | tf_op jit(solution)/shard_map/dot_general | solution.py:8
  121.6 0.0 all-to-all-done
  121.6 0.0 all-gather.4.cloned.1.call-done
  121.6 23.5 %broadcast_divide_fusion = f32[1792,7168]{1,0:T(8,128)} fusion(f32[]{:T(128)} %psum.7, bf16[192,1792]{1,0:T(8,128)(2,1)S(1)} %bitcast.17, bf16[192,7168]{1,0:T(8,128)(2,1)} %all-gather.4.cloned.1.call-done), kind=kOutput, calls=%fused_computation | convolution fusion | flops 4945346560 | bytes 54820868 | tf_op jit(solution)/shard_map/dot_general | solution.py:8
  (2 shorter events, 0.0 us)
Async XLA Ops:
  7.2 5.4 %copy-start = (bf16[12,4096]{1,0:T(8,128)(2,1)S(1)}, bf16[12,4096]{1,0:T(8,128)(2,1)}, u32[]{:S(2)}) copy-start(bf16[12,4096]{1,0:T(8,128)(2,1)} %param.4) | copy-start | bytes 294916
  7.2 114.5 %all-gather.4.cloned.1.call-start = ((), (), s32[]{:S(2)}) async-start(), calls=%async_computation.2 | async-start | bytes 3096576 | tf_op jit(solution)/shard_map/all_gather | solution.py:33
  15.6 19.4 %all-to-all-start.1 = ((bf16[24,8,512]{2,0,1:T(8,128)(2,1)}), bf16[24,8,512]{2,0,1:T(8,128)(2,1)S(1)}, u32[]{:S(2)}, u32[]{:S(2)}) async-start(bf16[24,8,512]{2,0,1:T(8,128)(2,1)} %copy.8), calls=%async_computation.1 | async-start | bytes 393216 | tf_op jit(solution)/shard_map/all_to_all | solution.py:26
  34.9 86.7 %all-to-all-start = ((bf16[24,8,1792]{2,0,1:T(8,128)(2,1)}), bf16[24,8,1792]{2,0,1:T(8,128)(2,1)S(1)}, u32[]{:S(2)}, u32[]{:S(2)}) async-start(bf16[24,8,1792]{2,0,1:T(8,128)(2,1)} %copy.7), calls=%async_computation | async-start | bytes 1376256 | tf_op jit(solution)/shard_map/all_to_all | solution.py:25
Sparse Core Ops, SparseCore 0:
  12.7 66.6 all-gather.3
where the time goes:
time: 152 us
  blocking collectives  83.5 us (55%)
  matrix products  26.8 us (18%)
  between operations  14.8 us (10%)
  starting transfers between devices  11.5 us (8%)
  waiting for transfers between devices  10.7 us (7%)
  local copies, waits for them, and re-layouts  3.46 us (2%)
    psum x1, blocking collectives, local(): live = lax.psum(row_counts.astype(jnp.float32), ('row', 'col'))  44.7 us
    all_gather x1, blocking collectives, local(): lax.all_gather(right_grad, 'row', axis=0, tiled=True)  34.3 us
    dot_general x2, matrix products, gram_part(): lax.dot_general(left_rows, right_rows, (((0,), (0,)), ((), ())), preferre...  26.8 us
    all_to_all x1, waiting for transfers between devices, local(): lax.all_to_all(pair_grad, 'row', split_axis=1, concat_axis=0, tiled=True)  10.7 us
    all_to_all x1, starting transfers between devices, local(): lax.all_to_all(pair_grad, 'row', split_axis=1, concat_axis=0, tiled=True)  7.16 us
    all_to_all x1, starting transfers between devices, local(): lax.all_to_all(pair_act, 'row', split_axis=1, concat_axis=0, tiled=True)  4.31 us
  transfers between devices with their start and end apart: 3, of which 1 were waited for; matrix products, arithmetic and copies ran while one was open for 3% of the time, Pallas kernels for 0%

commit v1 on v0

v1 whole, which is shorter than its diff:
```python
import functools

import jax
import jax.numpy as jnp
from jax import lax
from jax.experimental import pallas as pl
from jax.experimental.pallas import tpu as pltpu
from jax.sharding import PartitionSpec as P


def chip_ring(rows):
    width = 2 if rows <= 8 else 4
    depth = rows // width
    order = [z * width for z in range(depth)]
    for step, z in enumerate(reversed(range(depth))):
        columns = range(1, width) if step % 2 == 0 else range(width - 1, 0, -1)
        order += [z * width + x for x in columns]
    return order


def gram_kernel(live, left_ref, *refs):
    right_refs, out_ref, turned = refs[:-2], refs[-2], refs[-1]

    @pl.when(pl.program_id(0) == 0)
    def _():
        turned[...] = left_ref[...].T

    right = jnp.concatenate([ref[...] for ref in right_refs], axis=0)
    out_ref[...] = jnp.dot(turned[...], right, preferred_element_type=jnp.float32) / live


def gram(left, rights, live, tile):
    tokens, height = left.shape
    width = rights[0].shape[1]
    return pl.pallas_call(
        functools.partial(gram_kernel, live),
        grid=(width // tile,),
        in_specs=[pl.BlockSpec((tokens, height), lambda j: (0, 0))]
        + [pl.BlockSpec((part.shape[0], tile), lambda j: (0, j)) for part in rights],
        out_specs=pl.BlockSpec((height, tile), lambda j: (0, j)),
        out_shape=jax.ShapeDtypeStruct((height, width), jnp.float32),
        scratch_shapes=[pltpu.VMEM((height, tokens), jnp.bfloat16)],
        compiler_params=pltpu.CompilerParams(vmem_limit_bytes=40 * 1024 * 1024),
        cost_estimate=pl.CostEstimate(
            flops=2 * tokens * height * width, bytes_accessed=4 * height * width, transcendentals=0
        ),
    )(left, *rights)


def solution(mesh):
    rows, cols = mesh.shape["row"], mesh.shape["col"]
    order = chip_ring(rows)
    ahead = [(order[p], order[(p + 1) % rows]) for p in range(rows)]
    behind = [(target, source) for source, target in ahead]
    swap = [(0, 1), (1, 0)]
    live = 9.0 * rows * cols

    def local(activations, pseudo_grads, row_counts):
        row, col = lax.axis_index("row"), lax.axis_index("col")
        slots, act_width = activations.shape
        grad_width = pseudo_grads.shape[1]
        act_half, grad_half = act_width // cols, grad_width // cols
        act_block, grad_block = act_width // rows, grad_width // rows
        position = jnp.arange(slots, dtype=jnp.int32)
        live_mask = (position < row_counts[0]).astype(jnp.bfloat16)[:, None]

        def pair_half(values, half):
            masked = values * live_mask
            mine = lax.dynamic_slice_in_dim(masked, col * half, half, 1)
            other = lax.ppermute(lax.dynamic_slice_in_dim(masked, (1 - col) * half, half, 1), "col", swap)
            first = jnp.where(col == 0, mine, other)
            second = jnp.where(col == 0, other, mine)
            return jnp.concatenate([first, second], axis=0)

        shards = [[pair_half(activations, act_half)], [pair_half(pseudo_grads, grad_half)]]
        forward = [shards[0][0], shards[1][0]]
        backward = list(forward)
        for _ in range(rows // 2 - 1):
            for k in (0, 1):
                forward[k] = lax.ppermute(forward[k], "row", ahead)
                backward[k] = lax.ppermute(backward[k], "row", behind)
                shards[k] += [forward[k], backward[k]]
        for k in (0, 1):
            middle = forward[k].shape[1] // 2
            shards[k].append(
                jnp.concatenate(
                    [
                        lax.ppermute(forward[k][:, :middle], "row", ahead),
                        lax.ppermute(backward[k][:, middle:], "row", behind),
                    ],
                    axis=1,
                )
            )
        half_rows = rows // cols
        outs = []
        for parts, block, tile in ((shards[0], act_block, 512), (shards[1], grad_block, 512)):
            here = (row % half_rows) * block
            own = [lax.dynamic_slice_in_dim(part, here, block, 1) for part in parts]
            early = len(parts) - 3
            groups = [jnp.concatenate(own[:early], axis=0), jnp.concatenate(own[early:], axis=0)]
            left = jnp.concatenate(
                [jnp.where(col == row // half_rows, g, lax.ppermute(g, "col", swap)) for g in groups], axis=0
            )
            outs.append(gram(left, parts, live, tile))
        return tuple(outs)

    return jax.shard_map(
        local,
        mesh=mesh,
        in_specs=(
            P(("groups", "row", "col"), None),
            P(("groups", "row", "col"), None),
            P(("groups", "row", "col")),
        ),
        out_specs=(P(("groups", "row"), "col"), P(("groups", "row"), "col")),
        check_vma=False,
    )
```

time: 152 us -> 82.4 us (0.54)
  blocking collectives: 83.5 us -> 0 us
  matrix products: 26.8 us -> 0 us
  waiting for transfers between devices: 10.7 us -> 36.9 us
  Pallas kernels: 0 us -> 22.3 us
  between operations: 14.8 us -> 1.5 us
  starting transfers between devices: 11.5 us -> 18.6 us
  local copies, waits for them, and re-layouts: 3.46 us -> 0.18 us
  other arithmetic: 1.21 us -> 2.78 us
    psum x1 -> x0, blocking collectives: 44.7 us -> none  [local(): live = lax.psum(row_counts.astype(jnp.float32), ('row', 'col'))]
    all_gather x3 -> x0, blocking collectives: 38.8 us -> none  [the longest x1 34.3 us: local(): lax.all_gather(right_grad, 'row', axis=0, tiled=True)]
    ppermute x0 -> x22, waiting for transfers between devices: none -> 36.9 us  [the longest x6 25.5 us: local(): forward[k] = lax.ppermute(forward[k], 'row', ahead)]
    dot_general x2 -> x0, matrix products: 26.8 us -> none  [gram_part(): lax.dot_general(left_rows, right_rows, (((0,), (0,)), ((), ())), preferre...]
    pallas_call x0 -> x2, Pallas kernels: none -> 22.3 us  [gram(): pl.pallas_call(functools.partial(gram_kernel, live), grid=(width // tile,...]
    ppermute x0 -> x22, starting transfers between devices: none -> 18.6 us  [the longest x6 12 us: local(): forward[k] = lax.ppermute(forward[k], 'row', ahead)]
    all_to_all x2 -> x0, starting transfers between devices: 11.5 us -> none  [the longest x1 7.16 us: local(): lax.all_to_all(pair_grad, 'row', split_axis=1, concat_axis=0, tiled=True)]
    all_to_all x2 -> x0, waiting for transfers between devices: 10.7 us -> none  [the longest x1 10.7 us: local(): lax.all_to_all(pair_grad, 'row', split_axis=1, concat_axis=0, tiled=True)]
  transfers between devices with their start and end apart: 3 -> 22, of which waited for: 1 -> 11; matrix products, arithmetic and copies ran while one was open for 3% -> 2% of each run, Pallas kernels for 0% -> 4%
where the time goes in v1:
time: 82.4 us; the launch traced here: 82.2 us
  waiting for transfers between devices  36.9 us (45%)
  Pallas kernels  22.3 us (27%)
  starting transfers between devices  18.6 us (23%)
  other arithmetic  2.78 us (3%)
  between operations  1.5 us (2%)
    ppermute x6, waiting for transfers between devices, local(): forward[k] = lax.ppermute(forward[k], 'row', ahead)  25.5 us
    pallas_call x2, Pallas kernels, gram(): pl.pallas_call(functools.partial(gram_kernel, live), grid=(width // tile,...  22.3 us
    ppermute x6, starting transfers between devices, local(): forward[k] = lax.ppermute(forward[k], 'row', ahead)  12 us
    ppermute x2, waiting for transfers between devices, local(): lax.ppermute(forward[k][:, :middle], 'row', ahead)  5.29 us
    ppermute x2, waiting for transfers between devices, local(): lax.ppermute(backward[k][:, middle:], 'row', behind)  3.49 us
    ppermute x2, starting transfers between devices, local(): lax.ppermute(forward[k][:, :middle], 'row', ahead)  3.44 us
    ppermute x4, waiting for transfers between devices, local(): lax.ppermute(g, 'col', swap)  2.67 us
    mul x2, other arithmetic, pair_half(): masked = values * live_mask  2.11 us
  transfers between devices with their start and end apart: 22, of which 11 were waited for; matrix products, arithmetic and copies ran while one was open for 2% of the time, Pallas kernels for 4%

profile of v1, /device:TPU:0, one launch (start us, length us, event | category | flops | bytes accessed | tf_op | source)
XLA Modules:
  0.0 82.2 jit_solution(14166732330534052713)
XLA Ops:
  1.3 1.0 %broadcast_multiply_fusion.1 = bf16[12,4096]{1,0:T(8,128)(2,1)S(1)} fusion(bf16[12,4096]{1,0:T(8,128)(2,1)} %param.4, bf16[12]{0:T(256)(128)(2,1)S(1)} %compare_convert_fusion), kind=kLoop, calls=%fused_computation.23 | loop fusion | flops 49152 | bytes 196632 | tf_op jit(solution)/shard_map/mul | solution.py:68
  2.3 0.5 collective-permute-start.11
  2.8 1.1 %broadcast_multiply_fusion = bf16[12,14336]{1,0:T(8,128)(2,1)S(1)} fusion(bf16[12,14336]{1,0:T(8,128)(2,1)} %param.3, bf16[12]{0:T(256)(128)(2,1)S(1)} %compare_convert_fusion), kind=kLoop, calls=%fused_computation.7 | loop fusion | flops 172032 | bytes 688152 | tf_op jit(solution)/shard_map/mul | solution.py:68
  4.0 0.1 collective-permute-start
  4.1 0.0 collective-permute-done.11
  4.2 3.1 %collective-permute-start.12 = (bf16[24,2048]{1,0:T(8,128)(2,1)S(1)}, bf16[24,2048]{1,0:T(8,128)(2,1)S(1)}, u32[]{:S(2)}, u32[]{:S(2)}) collective-permute-start(bf16[24,2048]{1,0:T(8,128)(2,1)S(1)} %pad_maximum_fusion.4.refs_0_), channel_id=1, source_target_pairs={{0,4},{4,8},{8,12},{12,14},{14,10},{10,6},{6,2},{2,0},{1,5},{5,9},... | collective-permute-start | bytes 294920 | tf_op jit(solution)/shard_map/ppermute | solution.py:80
  7.2 0.0 collective-permute-start.13
  7.3 0.1 constant_dynamic-update-slice_fusion.6
  7.3 2.9 %collective-permute-done.12.refs_1_ = bf16[24,2048]{1,0:T(8,128)(2,1)S(1)} collective-permute-done((bf16[24,2048]{1,0:T(8,128)(2,1)S(1)}, bf16[24,2048]{1,0:T(8,128)(2,1)S(1)}, u32[]{:S(2)}, u32[]{:S(2)}) %collective-permute-start.12) | collective-permute-done | bytes 98336 | tf_op jit(solution)/shard_map/ppermute | solution.py:80
  10.2 1.8 %collective-permute-start.14 = (bf16[24,2048]{1,0:T(8,128)(2,1)S(1)}, bf16[24,2048]{1,0:T(8,128)(2,1)S(1)}, u32[]{:S(2)}, u32[]{:S(2)}) collective-permute-start(bf16[24,2048]{1,0:T(8,128)(2,1)S(1)} %collective-permute-done.12.refs_1_), channel_id=1, source_target_pairs={{0,4},{4,8},{8,12},{12,14},{14,10},{10,6},{6,2},{2,0},{1,5},{5,9},... | collective-permute-start | bytes 294920 | tf_op jit(solution)/shard_map/ppermute | solution.py:80
  12.0 0.0 collective-permute-done.13.refs_2_
  12.0 0.2 collective-permute-start.15
  12.2 0.0 collective-permute-done
  12.2 0.1 broadcast_select_fusion.3
  12.3 0.1 pad_maximum_fusion.1.refs_0_
  12.4 1.9 %collective-permute-start.1 = (bf16[24,7168]{1,0:T(8,128)(2,1)S(1)}, bf16[24,7168]{1,0:T(8,128)(2,1)S(1)}, u32[]{:S(2)}, u32[]{:S(2)}) collective-permute-start(bf16[24,7168]{1,0:T(8,128)(2,1)S(1)} %pad_maximum_fusion.1.refs_0_), channel_id=1, source_target_pairs={{0,4},{4,8},{8,12},{12,14},{14,10},{10,6},{6,2},{2,0},{1,5},{5,9},... | collective-permute-start | bytes 1032200 | tf_op jit(solution)/shard_map/ppermute | solution.py:80
  14.3 0.2 collective-permute-start.2
  14.5 0.1 fusion.1
  14.6 1.0 %collective-permute-done.14.refs_3_ = bf16[24,2048]{1,0:T(8,128)(2,1)S(1)} collective-permute-done((bf16[24,2048]{1,0:T(8,128)(2,1)S(1)}, bf16[24,2048]{1,0:T(8,128)(2,1)S(1)}, u32[]{:S(2)}, u32[]{:S(2)}) %collective-permute-start.14) | collective-permute-done | bytes 98336 | tf_op jit(solution)/shard_map/ppermute | solution.py:80
  15.6 2.1 %collective-permute-start.17 = (bf16[24,2048]{1,0:T(8,128)(2,1)S(1)}, bf16[24,2048]{1,0:T(8,128)(2,1)S(1)}, u32[]{:S(2)}, u32[]{:S(2)}) collective-permute-start(bf16[24,2048]{1,0:T(8,128)(2,1)S(1)} %collective-permute-done.14.refs_3_), channel_id=1, source_target_pairs={{0,4},{4,8},{8,12},{12,14},{14,10},{10,6},{6,2},{2,0},{1,5},{5,9},... | collective-permute-start | bytes 294920 | tf_op jit(solution)/shard_map/ppermute | solution.py:80
  17.7 0.0 collective-permute-done.15.refs_4_
  17.7 0.2 collective-permute-start.18
  17.9 0.0 collective-permute-start.16
  17.9 6.4 %collective-permute-done.17.refs_5_ = bf16[24,2048]{1,0:T(8,128)(2,1)S(1)} collective-permute-done((bf16[24,2048]{1,0:T(8,128)(2,1)S(1)}, bf16[24,2048]{1,0:T(8,128)(2,1)S(1)}, u32[]{:S(2)}, u32[]{:S(2)}) %collective-permute-start.17) | collective-permute-done | bytes 98336 | tf_op jit(solution)/shard_map/ppermute | solution.py:80
  24.3 1.8 %collective-permute-start.19 = (bf16[24,1024]{1,0:T(8,128)(2,1)S(1)}, bf16[24,1024]{1,0:T(8,128)(2,1)S(1)}, u32[]{:S(2)}, u32[]{:S(2)}) collective-permute-start(bf16[24,1024]{1,0:T(8,128)(2,1)S(1)} %slice.18), channel_id=1, source_target_pairs={{0,4},{4,8},{8,12},{12,14},{14,10},{10,6},{6,2},{2,0},{1,5},{5,9},... | collective-permute-start | bytes 147464 | tf_op jit(solution)/shard_map/ppermute | solution.py:88
  26.1 0.0 collective-permute-done.18.refs_6_
  26.1 0.3 collective-permute-start.20
  26.4 2.0 %collective-permute-done.19 = bf16[24,1024]{1,0:T(8,128)(2,1)S(1)} collective-permute-done((bf16[24,1024]{1,0:T(8,128)(2,1)S(1)}, bf16[24,1024]{1,0:T(8,128)(2,1)S(1)}, u32[]{:S(2)}, u32[]{:S(2)}) %collective-permute-start.19) | collective-permute-done | bytes 49184 | tf_op jit(solution)/shard_map/ppermute | solution.py:88
  28.4 1.9 %collective-permute-done.20 = bf16[24,1024]{1,0:T(8,128)(2,1)S(1)} collective-permute-done((bf16[24,1024]{1,0:T(8,128)(2,1)S(1)}, bf16[24,1024]{1,0:T(8,128)(2,1)S(1)}, u32[]{:S(2)}, u32[]{:S(2)}) %collective-permute-start.20) | collective-permute-done | bytes 49184 | tf_op jit(solution)/shard_map/ppermute | solution.py:89
  30.3 0.1 collective-permute-start.21
  30.4 0.0 collective-permute-done.16
  30.4 1.2 %collective-permute-done.21 = bf16[72,512]{1,0:T(8,128)(2,1)S(1)} collective-permute-done((bf16[72,512]{1,0:T(8,128)(2,1)S(1)}, bf16[72,512]{1,0:T(8,128)(2,1)S(1)}, u32[]{:S(2)}, u32[]{:S(2)}) %collective-permute-start.21) | collective-permute-done | bytes 73760 | tf_op jit(solution)/shard_map/ppermute | solution.py:102
  31.7 3.2 %shard_map.51 = f32[512,2048]{1,0:T(8,128)} custom-call(bf16[192,512]{1,0:T(8,128)(2,1)S(1)} %pad_maximum_fusion.3.left_ref, bf16[24,2048]{1,0:T(8,128)(2,1)S(1)} %pad_maximum_fusion.4.refs_0_, bf16[24,2048]{1,0:T(8,128)(2,1)S(1)} %collective-permute-done.12.refs_1_, bf16[24,2048]{1,0:T(8,128)(2,1)S(1)} %collective-permute-done.13.refs_2_, ...), custom_call_target="tpu_custom_call" | custom-call | flops 402653184 | bytes 4194304 | tf_op jit(solution)/shard_map/pallas_call | solution.py:35
  34.8 0.0 collective-permute-done.1.refs_1_
  34.8 1.6 %collective-permute-start.3 = (bf16[24,7168]{1,0:T(8,128)(2,1)S(1)}, bf16[24,7168]{1,0:T(8,128)(2,1)S(1)}, u32[]{:S(2)}, u32[]{:S(2)}) collective-permute-start(bf16[24,7168]{1,0:T(8,128)(2,1)S(1)} %collective-permute-done.1.refs_1_), channel_id=1, source_target_pairs={{0,4},{4,8},{8,12},{12,14},{14,10},{10,6},{6,2},{2,0},{1,5},{5,9},... | collective-permute-start | bytes 1032200 | tf_op jit(solution)/shard_map/ppermute | solution.py:80
  36.4 0.0 collective-permute-done.2.refs_2_
  36.4 0.4 collective-permute-start.4
  36.9 8.1 %collective-permute-done.3.refs_3_ = bf16[24,7168]{1,0:T(8,128)(2,1)S(1)} collective-permute-done((bf16[24,7168]{1,0:T(8,128)(2,1)S(1)}, bf16[24,7168]{1,0:T(8,128)(2,1)S(1)}, u32[]{:S(2)}, u32[]{:S(2)}) %collective-permute-start.3) | collective-permute-done | bytes 344096 | tf_op jit(solution)/shard_map/ppermute | solution.py:80
  45.0 1.6 %collective-permute-start.6 = (bf16[24,7168]{1,0:T(8,128)(2,1)S(1)}, bf16[24,7168]{1,0:T(8,128)(2,1)S(1)}, u32[]{:S(2)}, u32[]{:S(2)}) collective-permute-start(bf16[24,7168]{1,0:T(8,128)(2,1)S(1)} %collective-permute-done.3.refs_3_), channel_id=1, source_target_pairs={{0,4},{4,8},{8,12},{12,14},{14,10},{10,6},{6,2},{2,0},{1,5},{5,9},... | collective-permute-start | bytes 1032200 | tf_op jit(solution)/shard_map/ppermute | solution.py:80
  46.5 0.0 collective-permute-done.4.refs_4_
  46.5 0.4 collective-permute-start.7
  47.0 0.1 collective-permute-start.5
  47.1 7.2 %collective-permute-done.6.refs_5_ = bf16[24,7168]{1,0:T(8,128)(2,1)S(1)} collective-permute-done((bf16[24,7168]{1,0:T(8,128)(2,1)S(1)}, bf16[24,7168]{1,0:T(8,128)(2,1)S(1)}, u32[]{:S(2)}, u32[]{:S(2)}) %collective-permute-start.6) | collective-permute-done | bytes 344096 | tf_op jit(solution)/shard_map/ppermute | solution.py:80
  54.3 1.6 %collective-permute-start.8 = (bf16[24,3584]{1,0:T(8,128)(2,1)S(1)}, bf16[24,3584]{1,0:T(8,128)(2,1)S(1)}, u32[]{:S(2)}, u32[]{:S(2)}) collective-permute-start(bf16[24,3584]{1,0:T(8,128)(2,1)S(1)} %slice.16), channel_id=1, source_target_pairs={{0,4},{4,8},{8,12},{12,14},{14,10},{10,6},{6,2},{2,0},{1,5},{5,9},... | collective-permute-start | bytes 516104 | tf_op jit(solution)/shard_map/ppermute | solution.py:88
  55.9 0.0 collective-permute-done.7.refs_6_
  55.9 0.5 collective-permute-start.9
  56.4 3.3 %collective-permute-done.8 = bf16[24,3584]{1,0:T(8,128)(2,1)S(1)} collective-permute-done((bf16[24,3584]{1,0:T(8,128)(2,1)S(1)}, bf16[24,3584]{1,0:T(8,128)(2,1)S(1)}, u32[]{:S(2)}, u32[]{:S(2)}) %collective-permute-start.8) | collective-permute-done | bytes 172064 | tf_op jit(solution)/shard_map/ppermute | solution.py:88
  59.7 1.6 %collective-permute-done.9 = bf16[24,3584]{1,0:T(8,128)(2,1)S(1)} collective-permute-done((bf16[24,3584]{1,0:T(8,128)(2,1)S(1)}, bf16[24,3584]{1,0:T(8,128)(2,1)S(1)}, u32[]{:S(2)}, u32[]{:S(2)}) %collective-permute-start.9) | collective-permute-done | bytes 172064 | tf_op jit(solution)/shard_map/ppermute | solution.py:89
  61.4 0.1 collective-permute-start.10
  61.5 0.0 collective-permute-done.5
  61.5 0.1 broadcast_select_fusion
  61.6 1.4 %collective-permute-done.10 = bf16[72,1792]{1,0:T(8,128)(2,1)S(1)} collective-permute-done((bf16[72,1792]{1,0:T(8,128)(2,1)S(1)}, bf16[72,1792]{1,0:T(8,128)(2,1)S(1)}, u32[]{:S(2)}, u32[]{:S(2)}) %collective-permute-start.10) | collective-permute-done | bytes 258080 | tf_op jit(solution)/shard_map/ppermute | solution.py:102
  63.0 0.1 broadcast_select_fusion.1
  63.2 19.1 %shard_map.50 = f32[1792,7168]{1,0:T(8,128)} custom-call(bf16[192,1792]{1,0:T(8,128)(2,1)S(1)} %pad_maximum_fusion.left_ref, bf16[24,7168]{1,0:T(8,128)(2,1)S(1)} %pad_maximum_fusion.1.refs_0_, bf16[24,7168]{1,0:T(8,128)(2,1)S(1)} %collective-permute-done.1.refs_1_, bf16[24,7168]{1,0:T(8,128)(2,1)S(1)} %collective-permute-done.2.refs_2_, ...), custom_call_target="tpu_custom_call" | custom-call | flops 4932501504 | bytes 51380224 | tf_op jit(solution)/shard_map/pallas_call | solution.py:35
  (33 shorter events, 0.4 us)
Async XLA Ops:
  2.3 1.8 %collective-permute-start.11 = (bf16[12,2048]{1,0:T(8,128)(2,1)S(1)}, bf16[12,2048]{1,0:T(8,128)(2,1)S(1)}, u32[]{:S(2)}, u32[]{:S(2)}) collective-permute-start(bf16[12,2048]{1,0:T(8,128)(2,1)S(1)} %constant_dynamic-slice_fusion.3), channel_id=1, source_target_pairs={{0,1},{1,0},{2,3},{3,2},{4,5},{5,4},{6,7},{7,6},{8,9},{9,8},{10,11... | collective-permute-start | bytes 147464 | tf_op jit(solution)/shard_map/ppermute | solution.py:70
  4.0 8.2 %collective-permute-start = (bf16[12,7168]{1,0:T(8,128)(2,1)S(1)}, bf16[12,7168]{1,0:T(8,128)(2,1)S(1)}, u32[]{:S(2)}, u32[]{:S(2)}) collective-permute-start(bf16[12,7168]{1,0:T(8,128)(2,1)S(1)} %constant_dynamic-slice_fusion.7), channel_id=1, source_target_pairs={{0,1},{1,0},{2,3},{3,2},{4,5},{5,4},{6,7},{7,6},{8,9},{9,8},{10,11... | collective-permute-start | bytes 516104 | tf_op jit(solution)/shard_map/ppermute | solution.py:70
  4.2 6.0 %collective-permute-start.12 = (bf16[24,2048]{1,0:T(8,128)(2,1)S(1)}, bf16[24,2048]{1,0:T(8,128)(2,1)S(1)}, u32[]{:S(2)}, u32[]{:S(2)}) collective-permute-start(bf16[24,2048]{1,0:T(8,128)(2,1)S(1)} %pad_maximum_fusion.4.refs_0_), channel_id=1, source_target_pairs={{0,4},{4,8},{8,12},{12,14},{14,10},{10,6},{6,2},{2,0},{1,5},{5,9},... | collective-permute-start | bytes 294920 | tf_op jit(solution)/shard_map/ppermute | solution.py:80
  7.2 4.8 %collective-permute-start.13 = (bf16[24,2048]{1,0:T(8,128)(2,1)S(1)}, bf16[24,2048]{1,0:T(8,128)(2,1)S(1)}, u32[]{:S(2)}, u32[]{:S(2)}) collective-permute-start(bf16[24,2048]{1,0:T(8,128)(2,1)S(1)} %pad_maximum_fusion.4.refs_0_), channel_id=1, source_target_pairs={{4,0},{8,4},{12,8},{14,12},{10,14},{6,10},{2,6},{0,2},{5,1},{9,5},... | collective-permute-start | bytes 294920 | tf_op jit(solution)/shard_map/ppermute | solution.py:81
  10.2 5.4 %collective-permute-start.14 = (bf16[24,2048]{1,0:T(8,128)(2,1)S(1)}, bf16[24,2048]{1,0:T(8,128)(2,1)S(1)}, u32[]{:S(2)}, u32[]{:S(2)}) collective-permute-start(bf16[24,2048]{1,0:T(8,128)(2,1)S(1)} %collective-permute-done.12.refs_1_), channel_id=1, source_target_pairs={{0,4},{4,8},{8,12},{12,14},{14,10},{10,6},{6,2},{2,0},{1,5},{5,9},... | collective-permute-start | bytes 294920 | tf_op jit(solution)/shard_map/ppermute | solution.py:80
  12.0 5.7 %collective-permute-start.15 = (bf16[24,2048]{1,0:T(8,128)(2,1)S(1)}, bf16[24,2048]{1,0:T(8,128)(2,1)S(1)}, u32[]{:S(2)}, u32[]{:S(2)}) collective-permute-start(bf16[24,2048]{1,0:T(8,128)(2,1)S(1)} %collective-permute-done.13.refs_2_), channel_id=1, source_target_pairs={{4,0},{8,4},{12,8},{14,12},{10,14},{6,10},{2,6},{0,2},{5,1},{9,5},... | collective-permute-start | bytes 294920 | tf_op jit(solution)/shard_map/ppermute | solution.py:81
  12.4 22.4 %collective-permute-start.1 = (bf16[24,7168]{1,0:T(8,128)(2,1)S(1)}, bf16[24,7168]{1,0:T(8,128)(2,1)S(1)}, u32[]{:S(2)}, u32[]{:S(2)}) collective-permute-start(bf16[24,7168]{1,0:T(8,128)(2,1)S(1)} %pad_maximum_fusion.1.refs_0_), channel_id=1, source_target_pairs={{0,4},{4,8},{8,12},{12,14},{14,10},{10,6},{6,2},{2,0},{1,5},{5,9},... | collective-permute-start | bytes 1032200 | tf_op jit(solution)/shard_map/ppermute | solution.py:80
  14.3 22.1 %collective-permute-start.2 = (bf16[24,7168]{1,0:T(8,128)(2,1)S(1)}, bf16[24,7168]{1,0:T(8,128)(2,1)S(1)}, u32[]{:S(2)}, u32[]{:S(2)}) collective-permute-start(bf16[24,7168]{1,0:T(8,128)(2,1)S(1)} %pad_maximum_fusion.1.refs_0_), channel_id=1, source_target_pairs={{4,0},{8,4},{12,8},{14,12},{10,14},{6,10},{2,6},{0,2},{5,1},{9,5},... | collective-permute-start | bytes 1032200 | tf_op jit(solution)/shard_map/ppermute | solution.py:81
  15.6 8.7 %collective-permute-start.17 = (bf16[24,2048]{1,0:T(8,128)(2,1)S(1)}, bf16[24,2048]{1,0:T(8,128)(2,1)S(1)}, u32[]{:S(2)}, u32[]{:S(2)}) collective-permute-start(bf16[24,2048]{1,0:T(8,128)(2,1)S(1)} %collective-permute-done.14.refs_3_), channel_id=1, source_target_pairs={{0,4},{4,8},{8,12},{12,14},{14,10},{10,6},{6,2},{2,0},{1,5},{5,9},... | collective-permute-start | bytes 294920 | tf_op jit(solution)/shard_map/ppermute | solution.py:80
  17.7 8.4 %collective-permute-start.18 = (bf16[24,2048]{1,0:T(8,128)(2,1)S(1)}, bf16[24,2048]{1,0:T(8,128)(2,1)S(1)}, u32[]{:S(2)}, u32[]{:S(2)}) collective-permute-start(bf16[24,2048]{1,0:T(8,128)(2,1)S(1)} %collective-permute-done.15.refs_4_), channel_id=1, source_target_pairs={{4,0},{8,4},{12,8},{14,12},{10,14},{6,10},{2,6},{0,2},{5,1},{9,5},... | collective-permute-start | bytes 294920 | tf_op jit(solution)/shard_map/ppermute | solution.py:81
  17.9 12.5 %collective-permute-start.16 = (bf16[120,512]{1,0:T(8,128)(2,1)S(1)}, bf16[120,512]{1,0:T(8,128)(2,1)S(1)}, u32[]{:S(2)}, u32[]{:S(2)}) collective-permute-start(bf16[120,512]{1,0:T(8,128)(2,1)S(1)} %constant_dynamic-update-slice_fusion.2), channel_id=1, source_target_pairs={{0,1},{1,0},{2,3},{3,2},{4,5},{5,4},{6,7},{7,6},{8,9},{9,8},{10,11... | collective-permute-start | bytes 368648 | tf_op jit(solution)/shard_map/ppermute | solution.py:102
  24.3 4.1 %collective-permute-start.19 = (bf16[24,1024]{1,0:T(8,128)(2,1)S(1)}, bf16[24,1024]{1,0:T(8,128)(2,1)S(1)}, u32[]{:S(2)}, u32[]{:S(2)}) collective-permute-start(bf16[24,1024]{1,0:T(8,128)(2,1)S(1)} %slice.18), channel_id=1, source_target_pairs={{0,4},{4,8},{8,12},{12,14},{14,10},{10,6},{6,2},{2,0},{1,5},{5,9},... | collective-permute-start | bytes 147464 | tf_op jit(solution)/shard_map/ppermute | solution.py:88
  26.1 4.1 %collective-permute-start.20 = (bf16[24,1024]{1,0:T(8,128)(2,1)S(1)}, bf16[24,1024]{1,0:T(8,128)(2,1)S(1)}, u32[]{:S(2)}, u32[]{:S(2)}) collective-permute-start(bf16[24,1024]{1,0:T(8,128)(2,1)S(1)} %slice.19), channel_id=1, source_target_pairs={{4,0},{8,4},{12,8},{14,12},{10,14},{6,10},{2,6},{0,2},{5,1},{9,5},... | collective-permute-start | bytes 147464 | tf_op jit(solution)/shard_map/ppermute | solution.py:89
  30.3 1.3 %collective-permute-start.21 = (bf16[72,512]{1,0:T(8,128)(2,1)S(1)}, bf16[72,512]{1,0:T(8,128)(2,1)S(1)}, u32[]{:S(2)}, u32[]{:S(2)}) collective-permute-start(bf16[72,512]{1,0:T(8,128)(2,1)S(1)} %pad_maximum_fusion.5), channel_id=1, source_target_pairs={{0,1},{1,0},{2,3},{3,2},{4,5},{5,4},{6,7},{7,6},{8,9},{9,8},{10,11... | collective-permute-start | bytes 221192 | tf_op jit(solution)/shard_map/ppermute | solution.py:102
  34.8 10.1 %collective-permute-start.3 = (bf16[24,7168]{1,0:T(8,128)(2,1)S(1)}, bf16[24,7168]{1,0:T(8,128)(2,1)S(1)}, u32[]{:S(2)}, u32[]{:S(2)}) collective-permute-start(bf16[24,7168]{1,0:T(8,128)(2,1)S(1)} %collective-permute-done.1.refs_1_), channel_id=1, source_target_pairs={{0,4},{4,8},{8,12},{12,14},{14,10},{10,6},{6,2},{2,0},{1,5},{5,9},... | collective-permute-start | bytes 1032200 | tf_op jit(solution)/shard_map/ppermute | solution.py:80
  36.4 10.1 %collective-permute-start.4 = (bf16[24,7168]{1,0:T(8,128)(2,1)S(1)}, bf16[24,7168]{1,0:T(8,128)(2,1)S(1)}, u32[]{:S(2)}, u32[]{:S(2)}) collective-permute-start(bf16[24,7168]{1,0:T(8,128)(2,1)S(1)} %collective-permute-done.2.refs_2_), channel_id=1, source_target_pairs={{4,0},{8,4},{12,8},{14,12},{10,14},{6,10},{2,6},{0,2},{5,1},{9,5},... | collective-permute-start | bytes 1032200 | tf_op jit(solution)/shard_map/ppermute | solution.py:81
  45.0 9.3 %collective-permute-start.6 = (bf16[24,7168]{1,0:T(8,128)(2,1)S(1)}, bf16[24,7168]{1,0:T(8,128)(2,1)S(1)}, u32[]{:S(2)}, u32[]{:S(2)}) collective-permute-start(bf16[24,7168]{1,0:T(8,128)(2,1)S(1)} %collective-permute-done.3.refs_3_), channel_id=1, source_target_pairs={{0,4},{4,8},{8,12},{12,14},{14,10},{10,6},{6,2},{2,0},{1,5},{5,9},... | collective-permute-start | bytes 1032200 | tf_op jit(solution)/shard_map/ppermute | solution.py:80
  46.5 9.4 %collective-permute-start.7 = (bf16[24,7168]{1,0:T(8,128)(2,1)S(1)}, bf16[24,7168]{1,0:T(8,128)(2,1)S(1)}, u32[]{:S(2)}, u32[]{:S(2)}) collective-permute-start(bf16[24,7168]{1,0:T(8,128)(2,1)S(1)} %collective-permute-done.4.refs_4_), channel_id=1, source_target_pairs={{4,0},{8,4},{12,8},{14,12},{10,14},{6,10},{2,6},{0,2},{5,1},{9,5},... | collective-permute-start | bytes 1032200 | tf_op jit(solution)/shard_map/ppermute | solution.py:81
  47.0 14.5 %collective-permute-start.5 = (bf16[120,1792]{1,0:T(8,128)(2,1)S(1)}, bf16[120,1792]{1,0:T(8,128)(2,1)S(1)}, u32[]{:S(2)}, u32[]{:S(2)}) collective-permute-start(bf16[120,1792]{1,0:T(8,128)(2,1)S(1)} %dynamic-slice_dynamic-update-slice_fusion), channel_id=1, source_target_pairs={{0,1},{1,0},{2,3},{3,2},{4,5},{5,4},{6,7},{7,6},{8,9},{9,8},{10,11... | collective-permute-start | bytes 1290248 | tf_op jit(solution)/shard_map/ppermute | solution.py:102
  54.3 5.5 %collective-permute-start.8 = (bf16[24,3584]{1,0:T(8,128)(2,1)S(1)}, bf16[24,3584]{1,0:T(8,128)(2,1)S(1)}, u32[]{:S(2)}, u32[]{:S(2)}) collective-permute-start(bf16[24,3584]{1,0:T(8,128)(2,1)S(1)} %slice.16), channel_id=1, source_target_pairs={{0,4},{4,8},{8,12},{12,14},{14,10},{10,6},{6,2},{2,0},{1,5},{5,9},... | collective-permute-start | bytes 516104 | tf_op jit(solution)/shard_map/ppermute | solution.py:88
  55.9 5.5 %collective-permute-start.9 = (bf16[24,3584]{1,0:T(8,128)(2,1)S(1)}, bf16[24,3584]{1,0:T(8,128)(2,1)S(1)}, u32[]{:S(2)}, u32[]{:S(2)}) collective-permute-start(bf16[24,3584]{1,0:T(8,128)(2,1)S(1)} %slice.17), channel_id=1, source_target_pairs={{4,0},{8,4},{12,8},{14,12},{10,14},{6,10},{2,6},{0,2},{5,1},{9,5},... | collective-permute-start | bytes 516104 | tf_op jit(solution)/shard_map/ppermute | solution.py:89
  61.4 1.6 %collective-permute-start.10 = (bf16[72,1792]{1,0:T(8,128)(2,1)S(1)}, bf16[72,1792]{1,0:T(8,128)(2,1)S(1)}, u32[]{:S(2)}, u32[]{:S(2)}) collective-permute-start(bf16[72,1792]{1,0:T(8,128)(2,1)S(1)} %pad_maximum_fusion.2), channel_id=1, source_target_pairs={{0,1},{1,0},{2,3},{3,2},{4,5},{5,4},{6,7},{7,6},{8,9},{9,8},{10,11... | collective-permute-start | bytes 774152 | tf_op jit(solution)/shard_map/ppermute | solution.py:102

commit v2 on v1

v2 whole, which is shorter than its diff:
```python
import functools

import jax
import jax.numpy as jnp
from jax import lax
from jax.experimental import pallas as pl
from jax.experimental.pallas import tpu as pltpu
from jax.sharding import PartitionSpec as P


def chip_ring(rows):
    width = 2 if rows <= 8 else 4
    depth = rows // width
    order = [z * width for z in range(depth)]
    for step, z in enumerate(reversed(range(depth))):
        columns = range(1, width) if step % 2 == 0 else range(width - 1, 0, -1)
        order += [z * width + x for x in columns]
    return order


def gram_kernel(scale, shards, lists, pieces, left_ref, *refs):
    out_ref, turned, joined = refs[-3:]
    column, which, piece = pl.program_id(0), pl.program_id(1), pl.program_id(2)

    @pl.when((column == 0) & (which == 0) & (piece == 0))
    def _():
        turned[...] = left_ref[...].T

    for index in range(lists):

        @pl.when((which == index) & (piece == 0))
        def _(index=index):
            parts = refs[index * shards : (index + 1) * shards]
            joined[...] = jnp.concatenate([ref[...] for ref in parts], axis=0)

    height = out_ref.shape[0]
    if pieces == 1:
        rows = turned[...]
    else:
        rows = turned[pl.ds(pl.multiple_of(piece * height, height), height), :]
    out_ref[...] = jnp.dot(rows, joined[...], preferred_element_type=jnp.float32) * scale


def gram(left, right_lists, scale, out_shape, blocks, tile, pieces, out_index, out=None):
    tokens, height = left.shape
    shards, lists = len(right_lists[0]), len(right_lists)
    flat = [part for parts in right_lists for part in parts]
    in_specs = [pl.BlockSpec((tokens, height), lambda j, w, h: (0, 0))]
    in_specs += [pl.BlockSpec((part.shape[0], tile), lambda j, w, h: (0, j)) for part in flat]
    operands, aliases = [left, *flat], {}
    if out is not None:
        aliases = {len(operands): 0}
        in_specs.append(pl.BlockSpec(memory_space=pl.ANY))
        operands.append(out)
    work = tokens * height * blocks * lists * tile
    return pl.pallas_call(
        functools.partial(gram_kernel, scale, shards, lists, pieces),
        grid=(blocks, lists, pieces),
        in_specs=in_specs,
        out_specs=pl.BlockSpec((height // pieces, tile), out_index),
        out_shape=jax.ShapeDtypeStruct(out_shape, jnp.float32),
        scratch_shapes=[pltpu.VMEM((height, tokens), jnp.bfloat16), pltpu.VMEM((tokens, tile), jnp.bfloat16)],
        input_output_aliases=aliases,
        compiler_params=pltpu.CompilerParams(vmem_limit_bytes=40 * 1024 * 1024),
        cost_estimate=pl.CostEstimate(
            flops=2 * work, bytes_accessed=4 * work // tokens, transcendentals=0
        ),
    )(*operands)


def split_kernel(halves, order, half_ref, count_ref, act_ref, grad_ref, keep_ref, send_ref):
    live = lax.broadcasted_iota(jnp.int32, (act_ref.shape[0], 128), 0) < count_ref[0]
    for half in range(halves):
        for flip, out_ref in ((0, keep_ref), (1, send_ref)):

            @pl.when((half_ref[0] + flip) % halves == half)
            def _(half=half, out_ref=out_ref):
                for source, start, width, target in order:
                    ref = (grad_ref, act_ref)[source]
                    first = half * (ref.shape[1] // halves) + start
                    values = ref[:, first : first + width]
                    mask = jnp.concatenate([live] * (width // 128), axis=1)
                    out_ref[:, target : target + width] = jnp.where(mask, values, jnp.zeros_like(values))


def solution(mesh):
    rows, cols = mesh.shape["row"], mesh.shape["col"]
    order = chip_ring(rows)
    ahead = [(order[p], order[(p + 1) % rows]) for p in range(rows)]
    behind = [(target, source) for source, target in ahead]
    swap = [(0, 1), (1, 0)]
    half_rows = rows // cols
    scale = 1.0 / (9.0 * rows * cols)

    def local(activations, pseudo_grads, row_counts):
        row, col = lax.axis_index("row"), lax.axis_index("col")
        slots, act_width = activations.shape
        grad_width = pseudo_grads.shape[1]
        act_half, grad_half = act_width // cols, grad_width // cols
        act_block, grad_block = act_width // rows, grad_width // rows
        lists = 2 if act_block % 256 == 0 else 1
        sub = act_block // lists
        widths = [grad_half] + [act_half // lists] * lists
        offsets = [sum(widths[:k]) for k in range(len(widths))]

        layout = [(0, 0, grad_half, 0)]
        if lists == 1:
            layout.append((1, 0, act_half, offsets[1]))
        else:
            for k in range(lists):
                for j in range(half_rows):
                    layout.append((1, j * act_block + k * sub, sub, offsets[1 + k] + j * sub))
        half_shape = jax.ShapeDtypeStruct((slots, grad_half + act_half), jnp.bfloat16)
        keep, send = pl.pallas_call(
            functools.partial(split_kernel, cols, layout),
            in_specs=[pl.BlockSpec(memory_space=pltpu.SMEM)] * 2 + [pl.BlockSpec(memory_space=pltpu.VMEM)] * 2,
            out_specs=[pl.BlockSpec(memory_space=pltpu.VMEM)] * 2,
            out_shape=[half_shape, half_shape],
        )(col[None], row_counts, activations, pseudo_grads)
        other = lax.ppermute(send, "col", swap)
        first, second = jnp.where(col == 0, keep, other), jnp.where(col == 0, other, keep)

        chains = []
        for start, width in zip(offsets, widths):
            own = jnp.concatenate([first[:, start : start + width], second[:, start : start + width]], axis=0)
            chains.append([own])
        forward = [chain[0] for chain in chains]
        backward = list(forward)
        steps, halfway = [0] * len(chains), rows // 2
        sequence = [0, 1, 2, 0, 1, 0, 2, 1, 0, 2, 1, 2] if lists == 2 and halfway == 4 else list(range(len(chains))) * halfway
        previous = ()
        for k in sequence:
            chain, latest = chains[k], (forward[k], backward[k])
            (ahead_of, behind_of), _ = lax.optimization_barrier((latest, previous))
            previous = latest
            steps[k] += 1
            if steps[k] < halfway:
                forward[k] = lax.ppermute(ahead_of, "row", ahead)
                backward[k] = lax.ppermute(behind_of, "row", behind)
                chain += [forward[k], backward[k]]
            else:
                middle = widths[k] // 2
                upper = lax.ppermute(ahead_of[:, :middle], "row", ahead)
                lower = lax.ppermute(behind_of[:, middle:], "row", behind)
                chain.append(jnp.concatenate([upper, lower], axis=1))

        lefts = []
        for chain, block in zip(chains, [grad_block] + [sub] * lists):
            here = (row % half_rows) * block
            own = [lax.dynamic_slice_in_dim(part, here, block, 1) for part in chain]
            early = len(chain) - 3
            groups = [jnp.concatenate(own[:early], axis=0), jnp.concatenate(own[early:], axis=0)]
            lefts.append(
                jnp.concatenate(
                    [jnp.where(col == row // half_rows, g, lax.ppermute(g, "col", swap)) for g in groups], axis=0
                )
            )

        grad_tile = min(512, grad_half)
        grad_cov = gram(
            lefts[0], [chains[0]], scale, (grad_block, grad_half), grad_half // grad_tile, grad_tile, 1,
            lambda j, w, h: (0, j),
        )
        shape = (act_block, act_half)
        if lists == 1:
            act_cov = gram(lefts[1], [chains[1]], scale, shape, act_half // 256, 256, 1, lambda j, w, h: (0, j))
        else:
            act_cov = gram(
                lefts[1], [chains[1]], scale, shape, half_rows, sub, 2, lambda j, w, h: (h, 2 * j)
            )
            act_cov = gram(
                lefts[1], [chains[2]], scale, shape, half_rows, sub, 2, lambda j, w, h: (h, 2 * j + 1), act_cov
            )
            act_cov = gram(
                lefts[2], chains[1:], scale, shape, half_rows, sub, 2, lambda j, w, h: (2 + h, 2 * j + w), act_cov
            )
        return act_cov, grad_cov

    return jax.shard_map(
        local,
        mesh=mesh,
        in_specs=(
            P(("groups", "row", "col"), None),
            P(("groups", "row", "col"), None),
            P(("groups", "row", "col")),
        ),
        out_specs=(P(("groups", "row"), "col"), P(("groups", "row"), "col")),
        check_vma=False,
    )
```

time: 82.4 us -> 88.6 us (1.075)
  waiting for transfers between devices: 36.9 us -> 19.8 us
  starting transfers between devices: 18.6 us -> 31.7 us
  Pallas kernels: 22.3 us -> 33.2 us
  other arithmetic: 2.78 us -> 1.7 us
    ppermute x18 -> x25, waiting for transfers between devices: 34.3 us -> 18.3 us  [the longest x9 7.52 us: local(): backward[k] = lax.ppermute(behind_of, 'row', behind)]
    ppermute x18 -> x25, starting transfers between devices: 18.4 us -> 31.4 us  [the longest x9 17.2 us: local(): forward[k] = lax.ppermute(ahead_of, 'row', ahead)]
    pallas_call x2 -> x5, Pallas kernels: 22.3 us -> 33.2 us  [the longest x4 31.3 us: gram(): pl.pallas_call(functools.partial(gram_kernel, scale, shards, lists, piece...]
    mul x2 -> x0, other arithmetic: 2.11 us -> none  [pair_half(): masked = values * live_mask]
    ppermute x4 -> x6, waiting for transfers between devices: 2.67 us -> 1.54 us  [local(): lax.ppermute(g, 'col', swap)]
    select_n x2 -> x1, other arithmetic: 0.11 us -> 1 us  [local(): jnp.where(col == 0, keep, other)]
  transfers between devices with their start and end apart: 22 -> 31, of which waited for: 11 -> 16; matrix products, arithmetic and copies ran while one was open for 2% -> 1% of each run, Pallas kernels for 4% -> 20%
where the time goes in v2:
time: 88.6 us; the launch traced here: 88.3 us
  Pallas kernels  33.2 us (37%)
  starting transfers between devices  31.7 us (36%)
  waiting for transfers between devices  19.8 us (22%)
  other arithmetic  1.7 us (2%)
  between operations  1.62 us (2%)
    pallas_call x4, Pallas kernels, gram(): pl.pallas_call(functools.partial(gram_kernel, scale, shards, lists, piece...  31.3 us
    ppermute x9, starting transfers between devices, local(): forward[k] = lax.ppermute(ahead_of, 'row', ahead)  17.2 us
    ppermute x9, waiting for transfers between devices, local(): backward[k] = lax.ppermute(behind_of, 'row', behind)  7.52 us
    ppermute x9, starting transfers between devices, local(): backward[k] = lax.ppermute(behind_of, 'row', behind)  6.79 us
    ppermute x3, starting transfers between devices, local(): upper = lax.ppermute(ahead_of[:, :middle], 'row', ahead)  4.48 us
    ppermute x9, waiting for transfers between devices, local(): forward[k] = lax.ppermute(ahead_of, 'row', ahead)  3.87 us
    ppermute x3, waiting for transfers between devices, local(): lower = lax.ppermute(behind_of[:, middle:], 'row', behind)  3.74 us
    ppermute x3, starting transfers between devices, local(): lower = lax.ppermute(behind_of[:, middle:], 'row', behind)  2.45 us
  transfers between devices with their start and end apart: 31, of which 16 were waited for; matrix products, arithmetic and copies ran while one was open for 1% of the time, Pallas kernels for 20%

profile of v2, /device:TPU:0, one launch (start us, length us, event | category | flops | bytes accessed | tf_op | source)
XLA Modules:
  0.0 88.3 jit_solution(18022715192358472571)
XLA Ops:
  1.3 2.0 %shard_map.50 = (bf16[12,9216]{1,0:T(8,128)(2,1)}, bf16[12,9216]{1,0:T(8,128)(2,1)}) custom-call(s32[1]{0:T(128)} %bitcast.half_ref, s32[1]{0:T(128)S(6)} %copy.24.count_ref, bf16[12,14336]{1,0:T(8,128)(2,1)} %act_ref.1, bf16[12,4096]{1,0:T(8,128)(2,1)} %grad_ref.1), custom_call_target="tpu_custom_call" | custom-call | tf_op jit(solution)/shard_map/pallas_call | solution.py:114
  3.2 0.4 collective-permute-start
  3.7 1.4 %collective-permute-done = bf16[12,9216]{1,0:T(8,128)(2,1)S(1)} collective-permute-done((bf16[12,9216]{1,0:T(8,128)(2,1)}, bf16[12,9216]{1,0:T(8,128)(2,1)S(1)}, u32[]{:S(2)}, u32[]{:S(2)}) %collective-permute-start) | collective-permute-done | bytes 221216 | tf_op jit(solution)/shard_map/ppermute | solution.py:120
  5.1 1.0 %broadcast_select_fusion.1 = (bf16[12,9216]{1,0:T(8,128)(2,1)S(1)}, bf16[12,9216]{1,0:T(8,128)(2,1)S(1)}) fusion(bf16[12,9216]{1,0:T(8,128)(2,1)} %get-tuple-element.28, bf16[12,9216]{1,0:T(8,128)(2,1)S(1)} %collective-permute-done, pred[]{:T(512)S(6)} %eq.9), kind=kLoop, calls=%fused_computation.3 | loop fusion | flops 221184 | bytes 884737 | tf_op jit(solution)/shard_map/jit(_where)/select_n | solution.py:121
  6.2 0.1 constant_dynamic-update-slice_fusion.4
  6.4 0.1 constant_dynamic-update-slice_fusion.13
  6.5 3.0 %collective-permute-start.1 = (bf16[24,3584]{1,0:T(8,128)(2,1)S(1)}, bf16[24,3584]{1,0:T(8,128)(2,1)S(1)}, u32[]{:S(2)}, u32[]{:S(2)}) collective-permute-start(bf16[24,3584]{1,0:T(8,128)(2,1)S(1)} %pad_maximum_fusion.3.refs_0_.refs_8_), channel_id=1, source_target_pairs={{0,4},{4,8},{8,12},{12,14},{14,10},{10,6},{6,2},{2,0},{1,5},{5,9},... | collective-permute-start | bytes 516104 | tf_op jit(solution)/shard_map/ppermute | solution.py:138
  9.5 0.0 collective-permute-start.2
  9.5 2.0 %collective-permute-start.3 = (bf16[24,2048]{1,0:T(8,128)(2,1)S(1)}, bf16[24,2048]{1,0:T(8,128)(2,1)S(1)}, u32[]{:S(2)}, u32[]{:S(2)}) collective-permute-start(bf16[24,2048]{1,0:T(8,128)(2,1)S(1)} %pad_maximum_fusion.7.refs_0_), channel_id=1, source_target_pairs={{0,4},{4,8},{8,12},{12,14},{14,10},{10,6},{6,2},{2,0},{1,5},{5,9},... | collective-permute-start | bytes 294920 | tf_op jit(solution)/shard_map/ppermute | solution.py:138
  11.5 0.0 collective-permute-start.4
  11.5 2.0 %collective-permute-start.10 = (bf16[24,3584]{1,0:T(8,128)(2,1)S(1)}, bf16[24,3584]{1,0:T(8,128)(2,1)S(1)}, u32[]{:S(2)}, u32[]{:S(2)}) collective-permute-start(bf16[24,3584]{1,0:T(8,128)(2,1)S(1)} %pad_maximum_fusion.4.refs_0_), channel_id=1, source_target_pairs={{0,4},{4,8},{8,12},{12,14},{14,10},{10,6},{6,2},{2,0},{1,5},{5,9},... | collective-permute-start | bytes 516104 | tf_op jit(solution)/shard_map/ppermute | solution.py:138
  13.6 0.1 constant_dynamic-update-slice_fusion.18
  13.7 3.0 %collective-permute-done.3.refs_1_ = bf16[24,2048]{1,0:T(8,128)(2,1)S(1)} collective-permute-done((bf16[24,2048]{1,0:T(8,128)(2,1)S(1)}, bf16[24,2048]{1,0:T(8,128)(2,1)S(1)}, u32[]{:S(2)}, u32[]{:S(2)}) %collective-permute-start.3) | collective-permute-done | bytes 98336 | tf_op jit(solution)/shard_map/ppermute | solution.py:138
  16.7 2.1 %collective-permute-start.11 = (bf16[24,3584]{1,0:T(8,128)(2,1)S(1)}, bf16[24,3584]{1,0:T(8,128)(2,1)S(1)}, u32[]{:S(2)}, u32[]{:S(2)}) collective-permute-start(bf16[24,3584]{1,0:T(8,128)(2,1)S(1)} %pad_maximum_fusion.4.refs_0_), channel_id=1, source_target_pairs={{4,0},{8,4},{12,8},{14,12},{10,14},{6,10},{2,6},{0,2},{5,1},{9,5},... | collective-permute-start | bytes 516104 | tf_op jit(solution)/shard_map/ppermute | solution.py:139
  18.8 0.0 collective-permute-done.4.refs_2_
  18.8 0.6 collective-permute-start.5
  19.3 0.8 collective-permute-done.10.refs_1_
  20.2 1.9 %collective-permute-start.6 = (bf16[24,2048]{1,0:T(8,128)(2,1)S(1)}, bf16[24,2048]{1,0:T(8,128)(2,1)S(1)}, u32[]{:S(2)}, u32[]{:S(2)}) collective-permute-start(bf16[24,2048]{1,0:T(8,128)(2,1)S(1)} %collective-permute-done.4.refs_2_), channel_id=1, source_target_pairs={{4,0},{8,4},{12,8},{14,12},{10,14},{6,10},{2,6},{0,2},{5,1},{9,5},... | collective-permute-start | bytes 294920 | tf_op jit(solution)/shard_map/ppermute | solution.py:139
  22.1 0.2 collective-permute-done.11.refs_2_
  22.3 2.6 %collective-permute-start.16 = (bf16[24,3584]{1,0:T(8,128)(2,1)S(1)}, bf16[24,3584]{1,0:T(8,128)(2,1)S(1)}, u32[]{:S(2)}, u32[]{:S(2)}) collective-permute-start(bf16[24,3584]{1,0:T(8,128)(2,1)S(1)} %collective-permute-done.10.refs_1_), channel_id=1, source_target_pairs={{0,4},{4,8},{8,12},{12,14},{14,10},{10,6},{6,2},{2,0},{1,5},{5,9},... | collective-permute-start | bytes 516104 | tf_op jit(solution)/shard_map/ppermute | solution.py:138
  24.9 0.0 collective-permute-done.1.refs_1_.refs_9_
  24.9 0.1 collective-permute-start.17
  25.0 0.0 collective-permute-done.5.refs_3_
  25.0 1.0 %collective-permute-done.6.refs_4_ = bf16[24,2048]{1,0:T(8,128)(2,1)S(1)} collective-permute-done((bf16[24,2048]{1,0:T(8,128)(2,1)S(1)}, bf16[24,2048]{1,0:T(8,128)(2,1)S(1)}, u32[]{:S(2)}, u32[]{:S(2)}) %collective-permute-start.6) | collective-permute-done | bytes 98336 | tf_op jit(solution)/shard_map/ppermute | solution.py:139
  25.9 2.2 %collective-permute-start.7 = (bf16[24,3584]{1,0:T(8,128)(2,1)S(1)}, bf16[24,3584]{1,0:T(8,128)(2,1)S(1)}, u32[]{:S(2)}, u32[]{:S(2)}) collective-permute-start(bf16[24,3584]{1,0:T(8,128)(2,1)S(1)} %collective-permute-done.1.refs_1_.refs_9_), channel_id=1, source_target_pairs={{0,4},{4,8},{8,12},{12,14},{14,10},{10,6},{6,2},{2,0},{1,5},{5,9},... | collective-permute-start | bytes 516104 | tf_op jit(solution)/shard_map/ppermute | solution.py:138
  28.2 1.6 %collective-permute-start.12 = (bf16[24,2048]{1,0:T(8,128)(2,1)S(1)}, bf16[24,2048]{1,0:T(8,128)(2,1)S(1)}, u32[]{:S(2)}, u32[]{:S(2)}) collective-permute-start(bf16[24,2048]{1,0:T(8,128)(2,1)S(1)} %collective-permute-done.5.refs_3_), channel_id=1, source_target_pairs={{0,4},{4,8},{8,12},{12,14},{14,10},{10,6},{6,2},{2,0},{1,5},{5,9},... | collective-permute-start | bytes 294920 | tf_op jit(solution)/shard_map/ppermute | solution.py:138
  29.8 0.4 collective-permute-start.13
  30.2 4.2 %collective-permute-done.13.refs_6_ = bf16[24,2048]{1,0:T(8,128)(2,1)S(1)} collective-permute-done((bf16[24,2048]{1,0:T(8,128)(2,1)S(1)}, bf16[24,2048]{1,0:T(8,128)(2,1)S(1)}, u32[]{:S(2)}, u32[]{:S(2)}) %collective-permute-start.13) | collective-permute-done | bytes 98336 | tf_op jit(solution)/shard_map/ppermute | solution.py:139
  34.4 1.0 %collective-permute-start.8 = (bf16[24,3584]{1,0:T(8,128)(2,1)S(1)}, bf16[24,3584]{1,0:T(8,128)(2,1)S(1)}, u32[]{:S(2)}, u32[]{:S(2)}) collective-permute-start(bf16[24,3584]{1,0:T(8,128)(2,1)S(1)} %collective-permute-done.2.refs_2_.refs_10_), channel_id=1, source_target_pairs={{4,0},{8,4},{12,8},{14,12},{10,14},{6,10},{2,6},{0,2},{5,1},{9,5},... | collective-permute-start | bytes 516104 | tf_op jit(solution)/shard_map/ppermute | solution.py:139
  35.4 0.3 collective-permute-done.27
  35.8 0.0 collective-permute-done.17.refs_4_
  35.8 1.6 %collective-permute-start.18 = (bf16[24,3584]{1,0:T(8,128)(2,1)S(1)}, bf16[24,3584]{1,0:T(8,128)(2,1)S(1)}, u32[]{:S(2)}, u32[]{:S(2)}) collective-permute-start(bf16[24,3584]{1,0:T(8,128)(2,1)S(1)} %collective-permute-done.16.refs_3_), channel_id=1, source_target_pairs={{0,4},{4,8},{8,12},{12,14},{14,10},{10,6},{6,2},{2,0},{1,5},{5,9},... | collective-permute-start | bytes 516104 | tf_op jit(solution)/shard_map/ppermute | solution.py:138
  37.4 0.5 collective-permute-start.19
  37.9 0.1 collective-permute-start.25
  38.0 0.0 collective-permute-done.7.refs_3_.refs_11_
  38.0 1.6 %collective-permute-start.28 = (bf16[24,1024]{1,0:T(8,128)(2,1)S(1)}, bf16[24,1024]{1,0:T(8,128)(2,1)S(1)}, u32[]{:S(2)}, u32[]{:S(2)}) collective-permute-start(bf16[24,1024]{1,0:T(8,128)(2,1)S(1)} %slice.46), channel_id=1, source_target_pairs={{0,4},{4,8},{8,12},{12,14},{14,10},{10,6},{6,2},{2,0},{1,5},{5,9},... | collective-permute-start | bytes 147464 | tf_op jit(solution)/shard_map/ppermute | solution.py:143
  39.6 2.0 %collective-permute-done.8.refs_4_.refs_12_ = bf16[24,3584]{1,0:T(8,128)(2,1)S(1)} collective-permute-done((bf16[24,3584]{1,0:T(8,128)(2,1)S(1)}, bf16[24,3584]{1,0:T(8,128)(2,1)S(1)}, u32[]{:S(2)}, u32[]{:S(2)}) %collective-permute-start.8) | collective-permute-done | bytes 172064 | tf_op jit(solution)/shard_map/ppermute | solution.py:139
  41.6 1.0 %collective-permute-start.29 = (bf16[24,1024]{1,0:T(8,128)(2,1)S(1)}, bf16[24,1024]{1,0:T(8,128)(2,1)S(1)}, u32[]{:S(2)}, u32[]{:S(2)}) collective-permute-start(bf16[24,1024]{1,0:T(8,128)(2,1)S(1)} %slice.47), channel_id=1, source_target_pairs={{4,0},{8,4},{12,8},{14,12},{10,14},{6,10},{2,6},{0,2},{5,1},{9,5},... | collective-permute-start | bytes 147464 | tf_op jit(solution)/shard_map/ppermute | solution.py:144
  42.7 0.6 collective-permute-done.28
  43.3 1.6 %collective-permute-start.14 = (bf16[24,3584]{1,0:T(8,128)(2,1)S(1)}, bf16[24,3584]{1,0:T(8,128)(2,1)S(1)}, u32[]{:S(2)}, u32[]{:S(2)}) collective-permute-start(bf16[24,3584]{1,0:T(8,128)(2,1)S(1)} %collective-permute-done.7.refs_3_.refs_11_), channel_id=1, source_target_pairs={{0,4},{4,8},{8,12},{12,14},{14,10},{10,6},{6,2},{2,0},{1,5},{5,9},... | collective-permute-start | bytes 516104 | tf_op jit(solution)/shard_map/ppermute | solution.py:138
  44.9 1.0 %collective-permute-done.29 = bf16[24,1024]{1,0:T(8,128)(2,1)S(1)} collective-permute-done((bf16[24,1024]{1,0:T(8,128)(2,1)S(1)}, bf16[24,1024]{1,0:T(8,128)(2,1)S(1)}, u32[]{:S(2)}, u32[]{:S(2)}) %collective-permute-start.29) | collective-permute-done | bytes 49184 | tf_op jit(solution)/shard_map/ppermute | solution.py:144
  46.0 0.1 collective-permute-start.30
  46.1 1.2 %collective-permute-done.30 = bf16[72,512]{1,0:T(8,128)(2,1)S(1)} collective-permute-done((bf16[72,512]{1,0:T(8,128)(2,1)S(1)}, bf16[72,512]{1,0:T(8,128)(2,1)S(1)}, u32[]{:S(2)}, u32[]{:S(2)}) %collective-permute-start.30) | collective-permute-done | bytes 73760 | tf_op jit(solution)/shard_map/ppermute | solution.py:155
  47.3 0.8 collective-permute-start.15
  48.2 3.2 %shard_map.54 = f32[512,2048]{1,0:T(8,128)} custom-call(bf16[192,512]{1,0:T(8,128)(2,1)S(1)} %pad_maximum_fusion.2.left_ref, bf16[24,2048]{1,0:T(8,128)(2,1)S(1)} %pad_maximum_fusion.7.refs_0_, bf16[24,2048]{1,0:T(8,128)(2,1)S(1)} %collective-permute-done.3.refs_1_, bf16[24,2048]{1,0:T(8,128)(2,1)S(1)} %collective-permute-done.4.refs_2_, ...), custom_call_target="tpu_custom_call" | custom-call | flops 402653184 | bytes 4194304 | tf_op jit(solution)/shard_map/pallas_call | solution.py:56
  51.4 0.0 collective-permute-done.18.refs_5_
  51.4 1.2 %collective-permute-start.23 = (bf16[24,1792]{1,0:T(8,128)(2,1)S(1)}, bf16[24,1792]{1,0:T(8,128)(2,1)S(1)}, u32[]{:S(2)}, u32[]{:S(2)}) collective-permute-start(bf16[24,1792]{1,0:T(8,128)(2,1)S(1)} %slice.44), channel_id=1, source_target_pairs={{0,4},{4,8},{8,12},{12,14},{14,10},{10,6},{6,2},{2,0},{1,5},{5,9},... | collective-permute-start | bytes 258056 | tf_op jit(solution)/shard_map/ppermute | solution.py:143
  52.7 0.9 %collective-permute-start.24 = (bf16[24,1792]{1,0:T(8,128)(2,1)S(1)}, bf16[24,1792]{1,0:T(8,128)(2,1)S(1)}, u32[]{:S(2)}, u32[]{:S(2)}) collective-permute-start(bf16[24,1792]{1,0:T(8,128)(2,1)S(1)} %slice.45), channel_id=1, source_target_pairs={{4,0},{8,4},{12,8},{14,12},{10,14},{6,10},{2,6},{0,2},{5,1},{9,5},... | collective-permute-start | bytes 258056 | tf_op jit(solution)/shard_map/ppermute | solution.py:144
  53.6 0.2 collective-permute-done.15.refs_6_.refs_14_
  53.7 1.6 %collective-permute-start.20 = (bf16[24,1792]{1,0:T(8,128)(2,1)S(1)}, bf16[24,1792]{1,0:T(8,128)(2,1)S(1)}, u32[]{:S(2)}, u32[]{:S(2)}) collective-permute-start(bf16[24,1792]{1,0:T(8,128)(2,1)S(1)} %slice.42), channel_id=1, source_target_pairs={{0,4},{4,8},{8,12},{12,14},{14,10},{10,6},{6,2},{2,0},{1,5},{5,9},... | collective-permute-start | bytes 258056 | tf_op jit(solution)/shard_map/ppermute | solution.py:143
  55.4 0.0 collective-permute-done.25
  55.4 0.5 collective-permute-start.21
  55.9 0.0 collective-permute-done.9
  56.0 0.6 collective-permute-done.23
  56.6 1.0 %collective-permute-done.24 = bf16[24,1792]{1,0:T(8,128)(2,1)S(1)} collective-permute-done((bf16[24,1792]{1,0:T(8,128)(2,1)S(1)}, bf16[24,1792]{1,0:T(8,128)(2,1)S(1)}, u32[]{:S(2)}, u32[]{:S(2)}) %collective-permute-start.24) | collective-permute-done | bytes 86048 | tf_op jit(solution)/shard_map/ppermute | solution.py:144
  57.6 0.1 collective-permute-start.26
  57.7 0.5 collective-permute-done.20
  58.3 1.7 %collective-permute-done.21 = bf16[24,1792]{1,0:T(8,128)(2,1)S(1)} collective-permute-done((bf16[24,1792]{1,0:T(8,128)(2,1)S(1)}, bf16[24,1792]{1,0:T(8,128)(2,1)S(1)}, u32[]{:S(2)}, u32[]{:S(2)}) %collective-permute-start.21) | collective-permute-done | bytes 86048 | tf_op jit(solution)/shard_map/ppermute | solution.py:144
  60.0 0.1 collective-permute-start.22
  60.1 0.0 collective-permute-done.26
  60.2 7.2 %shard_map.51.refs_8_ = f32[1792,7168]{1,0:T(8,128)} custom-call(bf16[192,896]{1,0:T(8,128)(2,1)S(1)} %pad_maximum_fusion.1.left_ref, bf16[24,3584]{1,0:T(8,128)(2,1)S(1)} %pad_maximum_fusion.4.refs_0_, bf16[24,3584]{1,0:T(8,128)(2,1)S(1)} %collective-permute-done.10.refs_1_, bf16[24,3584]{1,0:T(8,128)(2,1)S(1)} %collective-permute-done.11.refs_2_, ...), custom_call_target="tpu_custom_call" | custom-call | flops 1233125376 | bytes 12845056 | tf_op jit(solution)/shard_map/pallas_call | solution.py:56
  67.3 7.1 %shard_map.52.refs_16_ = f32[1792,7168]{1,0:T(8,128)} custom-call(bf16[192,896]{1,0:T(8,128)(2,1)S(1)} %pad_maximum_fusion.1.left_ref, bf16[24,3584]{1,0:T(8,128)(2,1)S(1)} %pad_maximum_fusion.3.refs_0_.refs_8_, bf16[24,3584]{1,0:T(8,128)(2,1)S(1)} %collective-permute-done.1.refs_1_.refs_9_, ...), custom_call_target="tpu_custom_call", output_to_operand_aliasing={{}: (9, {})} | custom-call | flops 1233125376 | bytes 12845056 | tf_op jit(solution)/shard_map/pallas_call | solution.py:56
  74.5 0.0 collective-permute-done.22
  74.6 13.8 %shard_map.53 = f32[1792,7168]{1,0:T(8,128)} custom-call(bf16[192,896]{1,0:T(8,128)(2,1)S(1)} %pad_maximum_fusion.left_ref, bf16[24,3584]{1,0:T(8,128)(2,1)S(1)} %pad_maximum_fusion.4.refs_0_, bf16[24,3584]{1,0:T(8,128)(2,1)S(1)} %collective-permute-done.10.refs_1_, ...), custom_call_target="tpu_custom_call", output_to_operand_aliasing={{}: (17, {})} | custom-call | flops 2466250752 | bytes 25690112 | tf_op jit(solution)/shard_map/pallas_call | solution.py:56
  (58 shorter events, 0.7 us)
Async XLA Ops:
  3.2 1.9 %collective-permute-start = (bf16[12,9216]{1,0:T(8,128)(2,1)}, bf16[12,9216]{1,0:T(8,128)(2,1)S(1)}, u32[]{:S(2)}, u32[]{:S(2)}) collective-permute-start(bf16[12,9216]{1,0:T(8,128)(2,1)} %get-tuple-element.29), channel_id=1, source_target_pairs={{0,1},{1,0},{2,3},{3,2},{4,5},{5,4},{6,7},{7,6},{8,9},{9,8},{10,11... | collective-permute-start | bytes 663560 | tf_op jit(solution)/shard_map/ppermute | solution.py:120
  6.5 18.4 %collective-permute-start.1 = (bf16[24,3584]{1,0:T(8,128)(2,1)S(1)}, bf16[24,3584]{1,0:T(8,128)(2,1)S(1)}, u32[]{:S(2)}, u32[]{:S(2)}) collective-permute-start(bf16[24,3584]{1,0:T(8,128)(2,1)S(1)} %pad_maximum_fusion.3.refs_0_.refs_8_), channel_id=1, source_target_pairs={{0,4},{4,8},{8,12},{12,14},{14,10},{10,6},{6,2},{2,0},{1,5},{5,9},... | collective-permute-start | bytes 516104 | tf_op jit(solution)/shard_map/ppermute | solution.py:138
  9.5 15.4 %collective-permute-start.2 = (bf16[24,3584]{1,0:T(8,128)(2,1)S(1)}, bf16[24,3584]{1,0:T(8,128)(2,1)S(1)}, u32[]{:S(2)}, u32[]{:S(2)}) collective-permute-start(bf16[24,3584]{1,0:T(8,128)(2,1)S(1)} %pad_maximum_fusion.3.refs_0_.refs_8_), channel_id=1, source_target_pairs={{4,0},{8,4},{12,8},{14,12},{10,14},{6,10},{2,6},{0,2},{5,1},{9,5},... | collective-permute-start | bytes 516104 | tf_op jit(solution)/shard_map/ppermute | solution.py:139
  9.5 7.2 %collective-permute-start.3 = (bf16[24,2048]{1,0:T(8,128)(2,1)S(1)}, bf16[24,2048]{1,0:T(8,128)(2,1)S(1)}, u32[]{:S(2)}, u32[]{:S(2)}) collective-permute-start(bf16[24,2048]{1,0:T(8,128)(2,1)S(1)} %pad_maximum_fusion.7.refs_0_), channel_id=1, source_target_pairs={{0,4},{4,8},{8,12},{12,14},{14,10},{10,6},{6,2},{2,0},{1,5},{5,9},... | collective-permute-start | bytes 294920 | tf_op jit(solution)/shard_map/ppermute | solution.py:138
  11.5 7.2 %collective-permute-start.4 = (bf16[24,2048]{1,0:T(8,128)(2,1)S(1)}, bf16[24,2048]{1,0:T(8,128)(2,1)S(1)}, u32[]{:S(2)}, u32[]{:S(2)}) collective-permute-start(bf16[24,2048]{1,0:T(8,128)(2,1)S(1)} %pad_maximum_fusion.7.refs_0_), channel_id=1, source_target_pairs={{4,0},{8,4},{12,8},{14,12},{10,14},{6,10},{2,6},{0,2},{5,1},{9,5},... | collective-permute-start | bytes 294920 | tf_op jit(solution)/shard_map/ppermute | solution.py:139
  11.5 8.6 %collective-permute-start.10 = (bf16[24,3584]{1,0:T(8,128)(2,1)S(1)}, bf16[24,3584]{1,0:T(8,128)(2,1)S(1)}, u32[]{:S(2)}, u32[]{:S(2)}) collective-permute-start(bf16[24,3584]{1,0:T(8,128)(2,1)S(1)} %pad_maximum_fusion.4.refs_0_), channel_id=1, source_target_pairs={{0,4},{4,8},{8,12},{12,14},{14,10},{10,6},{6,2},{2,0},{1,5},{5,9},... | collective-permute-start | bytes 516104 | tf_op jit(solution)/shard_map/ppermute | solution.py:138
  16.7 5.6 %collective-permute-start.11 = (bf16[24,3584]{1,0:T(8,128)(2,1)S(1)}, bf16[24,3584]{1,0:T(8,128)(2,1)S(1)}, u32[]{:S(2)}, u32[]{:S(2)}) collective-permute-start(bf16[24,3584]{1,0:T(8,128)(2,1)S(1)} %pad_maximum_fusion.4.refs_0_), channel_id=1, source_target_pairs={{4,0},{8,4},{12,8},{14,12},{10,14},{6,10},{2,6},{0,2},{5,1},{9,5},... | collective-permute-start | bytes 516104 | tf_op jit(solution)/shard_map/ppermute | solution.py:139
  18.8 6.2 %collective-permute-start.5 = (bf16[24,2048]{1,0:T(8,128)(2,1)S(1)}, bf16[24,2048]{1,0:T(8,128)(2,1)S(1)}, u32[]{:S(2)}, u32[]{:S(2)}) collective-permute-start(bf16[24,2048]{1,0:T(8,128)(2,1)S(1)} %collective-permute-done.3.refs_1_), channel_id=1, source_target_pairs={{0,4},{4,8},{8,12},{12,14},{14,10},{10,6},{6,2},{2,0},{1,5},{5,9},... | collective-permute-start | bytes 294920 | tf_op jit(solution)/shard_map/ppermute | solution.py:138
  20.2 5.8 %collective-permute-start.6 = (bf16[24,2048]{1,0:T(8,128)(2,1)S(1)}, bf16[24,2048]{1,0:T(8,128)(2,1)S(1)}, u32[]{:S(2)}, u32[]{:S(2)}) collective-permute-start(bf16[24,2048]{1,0:T(8,128)(2,1)S(1)} %collective-permute-done.4.refs_2_), channel_id=1, source_target_pairs={{4,0},{8,4},{12,8},{14,12},{10,14},{6,10},{2,6},{0,2},{5,1},{9,5},... | collective-permute-start | bytes 294920 | tf_op jit(solution)/shard_map/ppermute | solution.py:139
  22.3 13.5 %collective-permute-start.16 = (bf16[24,3584]{1,0:T(8,128)(2,1)S(1)}, bf16[24,3584]{1,0:T(8,128)(2,1)S(1)}, u32[]{:S(2)}, u32[]{:S(2)}) collective-permute-start(bf16[24,3584]{1,0:T(8,128)(2,1)S(1)} %collective-permute-done.10.refs_1_), channel_id=1, source_target_pairs={{0,4},{4,8},{8,12},{12,14},{14,10},{10,6},{6,2},{2,0},{1,5},{5,9},... | collective-permute-start | bytes 516104 | tf_op jit(solution)/shard_map/ppermute | solution.py:138
  24.9 10.9 %collective-permute-start.17 = (bf16[24,3584]{1,0:T(8,128)(2,1)S(1)}, bf16[24,3584]{1,0:T(8,128)(2,1)S(1)}, u32[]{:S(2)}, u32[]{:S(2)}) collective-permute-start(bf16[24,3584]{1,0:T(8,128)(2,1)S(1)} %collective-permute-done.11.refs_2_), channel_id=1, source_target_pairs={{4,0},{8,4},{12,8},{14,12},{10,14},{6,10},{2,6},{0,2},{5,1},{9,5},... | collective-permute-start | bytes 516104 | tf_op jit(solution)/shard_map/ppermute | solution.py:139
  25.9 12.0 %collective-permute-start.7 = (bf16[24,3584]{1,0:T(8,128)(2,1)S(1)}, bf16[24,3584]{1,0:T(8,128)(2,1)S(1)}, u32[]{:S(2)}, u32[]{:S(2)}) collective-permute-start(bf16[24,3584]{1,0:T(8,128)(2,1)S(1)} %collective-permute-done.1.refs_1_.refs_9_), channel_id=1, source_target_pairs={{0,4},{4,8},{8,12},{12,14},{14,10},{10,6},{6,2},{2,0},{1,5},{5,9},... | collective-permute-start | bytes 516104 | tf_op jit(solution)/shard_map/ppermute | solution.py:138
  28.2 6.2 %collective-permute-start.12 = (bf16[24,2048]{1,0:T(8,128)(2,1)S(1)}, bf16[24,2048]{1,0:T(8,128)(2,1)S(1)}, u32[]{:S(2)}, u32[]{:S(2)}) collective-permute-start(bf16[24,2048]{1,0:T(8,128)(2,1)S(1)} %collective-permute-done.5.refs_3_), channel_id=1, source_target_pairs={{0,4},{4,8},{8,12},{12,14},{14,10},{10,6},{6,2},{2,0},{1,5},{5,9},... | collective-permute-start | bytes 294920 | tf_op jit(solution)/shard_map/ppermute | solution.py:138
  29.8 4.6 %collective-permute-start.13 = (bf16[24,2048]{1,0:T(8,128)(2,1)S(1)}, bf16[24,2048]{1,0:T(8,128)(2,1)S(1)}, u32[]{:S(2)}, u32[]{:S(2)}) collective-permute-start(bf16[24,2048]{1,0:T(8,128)(2,1)S(1)} %collective-permute-done.6.refs_4_), channel_id=1, source_target_pairs={{4,0},{8,4},{12,8},{14,12},{10,14},{6,10},{2,6},{0,2},{5,1},{9,5},... | collective-permute-start | bytes 294920 | tf_op jit(solution)/shard_map/ppermute | solution.py:139
  34.4 1.3 %collective-permute-start.27 = (bf16[120,512]{1,0:T(8,128)(2,1)S(1)}, bf16[120,512]{1,0:T(8,128)(2,1)S(1)}, u32[]{:S(2)}, u32[]{:S(2)}) collective-permute-start(bf16[120,512]{1,0:T(8,128)(2,1)S(1)} %constant_dynamic-update-slice_fusion.14), channel_id=1, source_target_pairs={{0,1},{1,0},{2,3},{3,2},{4,5},{5,4},{6,7},{7,6},{8,9},{9,8},{10,11... | collective-permute-start | bytes 368648 | tf_op jit(solution)/shard_map/ppermute | solution.py:155
  34.4 7.2 %collective-permute-start.8 = (bf16[24,3584]{1,0:T(8,128)(2,1)S(1)}, bf16[24,3584]{1,0:T(8,128)(2,1)S(1)}, u32[]{:S(2)}, u32[]{:S(2)}) collective-permute-start(bf16[24,3584]{1,0:T(8,128)(2,1)S(1)} %collective-permute-done.2.refs_2_.refs_10_), channel_id=1, source_target_pairs={{4,0},{8,4},{12,8},{14,12},{10,14},{6,10},{2,6},{0,2},{5,1},{9,5},... | collective-permute-start | bytes 516104 | tf_op jit(solution)/shard_map/ppermute | solution.py:139
  35.8 15.6 %collective-permute-start.18 = (bf16[24,3584]{1,0:T(8,128)(2,1)S(1)}, bf16[24,3584]{1,0:T(8,128)(2,1)S(1)}, u32[]{:S(2)}, u32[]{:S(2)}) collective-permute-start(bf16[24,3584]{1,0:T(8,128)(2,1)S(1)} %collective-permute-done.16.refs_3_), channel_id=1, source_target_pairs={{0,4},{4,8},{8,12},{12,14},{14,10},{10,6},{6,2},{2,0},{1,5},{5,9},... | collective-permute-start | bytes 516104 | tf_op jit(solution)/shard_map/ppermute | solution.py:138
  37.4 14.0 %collective-permute-start.19 = (bf16[24,3584]{1,0:T(8,128)(2,1)S(1)}, bf16[24,3584]{1,0:T(8,128)(2,1)S(1)}, u32[]{:S(2)}, u32[]{:S(2)}) collective-permute-start(bf16[24,3584]{1,0:T(8,128)(2,1)S(1)} %collective-permute-done.17.refs_4_), channel_id=1, source_target_pairs={{4,0},{8,4},{12,8},{14,12},{10,14},{6,10},{2,6},{0,2},{5,1},{9,5},... | collective-permute-start | bytes 516104 | tf_op jit(solution)/shard_map/ppermute | solution.py:139
  37.9 17.5 %collective-permute-start.25 = (bf16[120,896]{1,0:T(8,128)(2,1)S(1)}, bf16[120,896]{1,0:T(8,128)(2,1)S(1)}, u32[]{:S(2)}, u32[]{:S(2)}) collective-permute-start(bf16[120,896]{1,0:T(8,128)(2,1)S(1)} %constant_dynamic-update-slice_fusion.9), channel_id=1, source_target_pairs={{0,1},{1,0},{2,3},{3,2},{4,5},{5,4},{6,7},{7,6},{8,9},{9,8},{10,11... | collective-permute-start | bytes 645128 | tf_op jit(solution)/shard_map/ppermute | solution.py:155
  38.0 5.3 %collective-permute-start.28 = (bf16[24,1024]{1,0:T(8,128)(2,1)S(1)}, bf16[24,1024]{1,0:T(8,128)(2,1)S(1)}, u32[]{:S(2)}, u32[]{:S(2)}) collective-permute-start(bf16[24,1024]{1,0:T(8,128)(2,1)S(1)} %slice.46), channel_id=1, source_target_pairs={{0,4},{4,8},{8,12},{12,14},{14,10},{10,6},{6,2},{2,0},{1,5},{5,9},... | collective-permute-start | bytes 147464 | tf_op jit(solution)/shard_map/ppermute | solution.py:143
  41.6 4.3 %collective-permute-start.29 = (bf16[24,1024]{1,0:T(8,128)(2,1)S(1)}, bf16[24,1024]{1,0:T(8,128)(2,1)S(1)}, u32[]{:S(2)}, u32[]{:S(2)}) collective-permute-start(bf16[24,1024]{1,0:T(8,128)(2,1)S(1)} %slice.47), channel_id=1, source_target_pairs={{4,0},{8,4},{12,8},{14,12},{10,14},{6,10},{2,6},{0,2},{5,1},{9,5},... | collective-permute-start | bytes 147464 | tf_op jit(solution)/shard_map/ppermute | solution.py:144
  43.3 9.4 %collective-permute-start.14 = (bf16[24,3584]{1,0:T(8,128)(2,1)S(1)}, bf16[24,3584]{1,0:T(8,128)(2,1)S(1)}, u32[]{:S(2)}, u32[]{:S(2)}) collective-permute-start(bf16[24,3584]{1,0:T(8,128)(2,1)S(1)} %collective-permute-done.7.refs_3_.refs_11_), channel_id=1, source_target_pairs={{0,4},{4,8},{8,12},{12,14},{14,10},{10,6},{6,2},{2,0},{1,5},{5,9},... | collective-permute-start | bytes 516104 | tf_op jit(solution)/shard_map/ppermute | solution.py:138
  46.0 1.3 %collective-permute-start.30 = (bf16[72,512]{1,0:T(8,128)(2,1)S(1)}, bf16[72,512]{1,0:T(8,128)(2,1)S(1)}, u32[]{:S(2)}, u32[]{:S(2)}) collective-permute-start(bf16[72,512]{1,0:T(8,128)(2,1)S(1)} %pad_maximum_fusion.8), channel_id=1, source_target_pairs={{0,1},{1,0},{2,3},{3,2},{4,5},{5,4},{6,7},{7,6},{8,9},{9,8},{10,11... | collective-permute-start | bytes 221192 | tf_op jit(solution)/shard_map/ppermute | solution.py:155
  47.3 6.4 %collective-permute-start.15 = (bf16[24,3584]{1,0:T(8,128)(2,1)S(1)}, bf16[24,3584]{1,0:T(8,128)(2,1)S(1)}, u32[]{:S(2)}, u32[]{:S(2)}) collective-permute-start(bf16[24,3584]{1,0:T(8,128)(2,1)S(1)} %collective-permute-done.8.refs_4_.refs_12_), channel_id=1, source_target_pairs={{4,0},{8,4},{12,8},{14,12},{10,14},{6,10},{2,6},{0,2},{5,1},{9,5},... | collective-permute-start | bytes 516104 | tf_op jit(solution)/shard_map/ppermute | solution.py:139
  51.4 4.6 %collective-permute-start.9 = (bf16[120,896]{1,0:T(8,128)(2,1)S(1)}, bf16[120,896]{1,0:T(8,128)(2,1)S(1)}, u32[]{:S(2)}, u32[]{:S(2)}) collective-permute-start(bf16[120,896]{1,0:T(8,128)(2,1)S(1)} %constant_dynamic-update-slice_fusion), channel_id=1, source_target_pairs={{0,1},{1,0},{2,3},{3,2},{4,5},{5,4},{6,7},{7,6},{8,9},{9,8},{10,11... | collective-permute-start | bytes 645128 | tf_op jit(solution)/shard_map/ppermute | solution.py:155
  51.4 5.2 %collective-permute-start.23 = (bf16[24,1792]{1,0:T(8,128)(2,1)S(1)}, bf16[24,1792]{1,0:T(8,128)(2,1)S(1)}, u32[]{:S(2)}, u32[]{:S(2)}) collective-permute-start(bf16[24,1792]{1,0:T(8,128)(2,1)S(1)} %slice.44), channel_id=1, source_target_pairs={{0,4},{4,8},{8,12},{12,14},{14,10},{10,6},{6,2},{2,0},{1,5},{5,9},... | collective-permute-start | bytes 258056 | tf_op jit(solution)/shard_map/ppermute | solution.py:143
  52.7 4.9 %collective-permute-start.24 = (bf16[24,1792]{1,0:T(8,128)(2,1)S(1)}, bf16[24,1792]{1,0:T(8,128)(2,1)S(1)}, u32[]{:S(2)}, u32[]{:S(2)}) collective-permute-start(bf16[24,1792]{1,0:T(8,128)(2,1)S(1)} %slice.45), channel_id=1, source_target_pairs={{4,0},{8,4},{12,8},{14,12},{10,14},{6,10},{2,6},{0,2},{5,1},{9,5},... | collective-permute-start | bytes 258056 | tf_op jit(solution)/shard_map/ppermute | solution.py:144
  53.7 4.5 %collective-permute-start.20 = (bf16[24,1792]{1,0:T(8,128)(2,1)S(1)}, bf16[24,1792]{1,0:T(8,128)(2,1)S(1)}, u32[]{:S(2)}, u32[]{:S(2)}) collective-permute-start(bf16[24,1792]{1,0:T(8,128)(2,1)S(1)} %slice.42), channel_id=1, source_target_pairs={{0,4},{4,8},{8,12},{12,14},{14,10},{10,6},{6,2},{2,0},{1,5},{5,9},... | collective-permute-start | bytes 258056 | tf_op jit(solution)/shard_map/ppermute | solution.py:143
  55.4 4.5 %collective-permute-start.21 = (bf16[24,1792]{1,0:T(8,128)(2,1)S(1)}, bf16[24,1792]{1,0:T(8,128)(2,1)S(1)}, u32[]{:S(2)}, u32[]{:S(2)}) collective-permute-start(bf16[24,1792]{1,0:T(8,128)(2,1)S(1)} %slice.43), channel_id=1, source_target_pairs={{4,0},{8,4},{12,8},{14,12},{10,14},{6,10},{2,6},{0,2},{5,1},{9,5},... | collective-permute-start | bytes 258056 | tf_op jit(solution)/shard_map/ppermute | solution.py:144
  57.6 2.4 %collective-permute-start.26 = (bf16[72,896]{1,0:T(8,128)(2,1)S(1)}, bf16[72,896]{1,0:T(8,128)(2,1)S(1)}, u32[]{:S(2)}, u32[]{:S(2)}) collective-permute-start(bf16[72,896]{1,0:T(8,128)(2,1)S(1)} %pad_maximum_fusion.6), channel_id=1, source_target_pairs={{0,1},{1,0},{2,3},{3,2},{4,5},{5,4},{6,7},{7,6},{8,9},{9,8},{10,11... | collective-permute-start | bytes 387080 | tf_op jit(solution)/shard_map/ppermute | solution.py:155
  60.0 14.5 %collective-permute-start.22 = (bf16[72,896]{1,0:T(8,128)(2,1)S(1)}, bf16[72,896]{1,0:T(8,128)(2,1)S(1)}, u32[]{:S(2)}, u32[]{:S(2)}) collective-permute-start(bf16[72,896]{1,0:T(8,128)(2,1)S(1)} %pad_maximum_fusion.5), channel_id=1, source_target_pairs={{0,1},{1,0},{2,3},{3,2},{4,5},{5,4},{6,7},{7,6},{8,9},{9,8},{10,11... | collective-permute-start | bytes 387080 | tf_op jit(solution)/shard_map/ppermute | solution.py:155

commit v3 on v2

v3 whole, which is shorter than its diff:
```python
import functools

import jax
import jax.numpy as jnp
from jax import lax
from jax.experimental import pallas as pl
from jax.experimental.pallas import tpu as pltpu
from jax.sharding import PartitionSpec as P


SLOTS = 4


def chip_ring(rows):
    width = 2 if rows <= 8 else 4
    depth = rows // width
    order = [z * width for z in range(depth)]
    for step, z in enumerate(reversed(range(depth))):
        columns = range(1, width) if step % 2 == 0 else range(width - 1, 0, -1)
        order += [z * width + x for x in columns]
    return order


def gram_kernel(scale, left_ref, *refs):
    right_refs, out_ref, turned = refs[:-2], refs[-2], refs[-1]

    @pl.when(pl.program_id(0) == 0)
    def _():
        turned[...] = left_ref[...].T

    right = jnp.concatenate([ref[...] for ref in right_refs], axis=0)
    out_ref[...] = jnp.dot(turned[...], right, preferred_element_type=jnp.float32) * scale


def gram(left, rights, scale, steps, tile):
    tokens, height = left.shape
    return pl.pallas_call(
        functools.partial(gram_kernel, scale),
        grid=(steps,),
        in_specs=[pl.BlockSpec((tokens, height), lambda j: (0, 0))]
        + [pl.BlockSpec((part.shape[0], tile), lambda j: (0, j)) for part in rights],
        out_specs=pl.BlockSpec((height, tile), lambda j: (0, j)),
        out_shape=jax.ShapeDtypeStruct((height, steps * tile), jnp.float32),
        scratch_shapes=[pltpu.VMEM((height, tokens), jnp.bfloat16)],
        compiler_params=pltpu.CompilerParams(vmem_limit_bytes=32 * 1024 * 1024),
    )(left, *rights)


def tiles_kernel(scale, groups, lefts, lists, outs, aliased, *refs):
    left_refs, refs = refs[:lefts], refs[lefts:]
    sources = []
    for shards in lists:
        sources.append(refs[:shards])
        refs = refs[shards:]
    out_refs = refs[aliased : aliased + outs]
    turned, buffer, sems = refs[aliased + outs : -2], refs[-2], refs[-1]
    for left_ref, turned_ref in zip(left_refs, turned):
        turned_ref[...] = left_ref[...].T

    def copy(group, slot, j):
        _, _, _, _, height, width, which, row, column, stride, _ = group
        return pltpu.make_async_copy(
            buffer.at[slot, pl.ds(0, height), pl.ds(0, width)],
            out_refs[which].at[pl.ds(row, height), pl.ds(pl.multiple_of(column + j * stride, 128), width)],
            sems.at[slot],
        )

    earlier = None
    for group in groups:

        def step(j, carry, group=group, earlier=earlier):
            left, source, first, apart, height, width, _, _, _, _, _ = group
            slot = lax.rem(j, SLOTS)

            @pl.when(j >= SLOTS)
            def _():
                copy(group, slot, j - SLOTS).wait()

            if earlier is not None:

                @pl.when(j < SLOTS)
                def _():
                    copy(earlier, slot, j + earlier[-1] - SLOTS).wait()

            here = pl.ds(pl.multiple_of(first + j * apart, 128), width)
            right = jnp.concatenate([ref[:, here] for ref in sources[source]], axis=0)
            product = jnp.dot(turned[left][...], right, preferred_element_type=jnp.float32)
            buffer[slot, :height, :width] = product * scale
            copy(group, slot, j).start()
            return carry

        lax.fori_loop(0, group[-1], step, 0)
        earlier = group
    for slot in range(SLOTS):
        copy(earlier, slot, earlier[-1] - SLOTS + slot).wait()


def tiles(scale, groups, lefts, lists, out_shapes, out=None):
    tokens = lefts[0].shape[0]
    whole, anywhere = pl.BlockSpec(memory_space=pltpu.VMEM), pl.BlockSpec(memory_space=pl.ANY)
    operands = [*lefts, *[part for parts in lists for part in parts]]
    specs, aliases = [whole] * len(operands), {}
    if out is not None:
        aliases = {len(operands): 0}
        operands.append(out)
        specs.append(anywhere)
    area = sum(g[4] * g[5] * g[10] for g in groups)
    return pl.pallas_call(
        functools.partial(
            tiles_kernel, scale, groups, len(lefts), [len(parts) for parts in lists], len(out_shapes), len(aliases)
        ),
        in_specs=specs,
        out_specs=[anywhere] * len(out_shapes),
        out_shape=[jax.ShapeDtypeStruct(shape, jnp.float32) for shape in out_shapes],
        scratch_shapes=[pltpu.VMEM((left.shape[1], tokens), jnp.bfloat16) for left in lefts]
        + [
            pltpu.VMEM((SLOTS, max(g[4] for g in groups), max(g[5] for g in groups)), jnp.float32),
            pltpu.SemaphoreType.DMA((SLOTS,)),
        ],
        input_output_aliases=aliases,
        compiler_params=pltpu.CompilerParams(vmem_limit_bytes=32 * 1024 * 1024),
        cost_estimate=pl.CostEstimate(flops=2 * tokens * area, bytes_accessed=4 * area, transcendentals=0),
    )(*operands)


def split_kernel(halves, order, half_ref, count_ref, act_ref, grad_ref, keep_ref, send_ref):
    live = lax.broadcasted_iota(jnp.int32, (act_ref.shape[0], 128), 0) < count_ref[0]
    for half in range(halves):
        for flip, out_ref in ((0, keep_ref), (1, send_ref)):

            @pl.when((half_ref[0] + flip) % halves == half)
            def _(half=half, out_ref=out_ref):
                for source, start, width, target in order:
                    ref = (grad_ref, act_ref)[source]
                    first = half * (ref.shape[1] // halves) + start
                    values = ref[:, first : first + width]
                    mask = jnp.concatenate([live] * (width // 128), axis=1)
                    out_ref[:, target : target + width] = jnp.where(mask, values, jnp.zeros_like(values))


def solution(mesh):
    rows, cols = mesh.shape["row"], mesh.shape["col"]
    order = chip_ring(rows)
    ahead = [(order[p], order[(p + 1) % rows]) for p in range(rows)]
    behind = [(target, source) for source, target in ahead]
    swap = [(0, 1), (1, 0)]
    half_rows = rows // cols
    scale = 1.0 / (9.0 * rows * cols)

    def local(activations, pseudo_grads, row_counts):
        row, col = lax.axis_index("row"), lax.axis_index("col")
        slots, act_width = activations.shape
        grad_width = pseudo_grads.shape[1]
        act_half, grad_half = act_width // cols, grad_width // cols
        act_block, grad_block = act_width // rows, grad_width // rows
        cut = act_block * 4 // 7 if act_block % 1792 == 0 else act_block
        rest = act_block - cut
        widths = [half_rows * cut, half_rows * rest + grad_half]
        layout = [(1, j * act_block, cut, j * cut) for j in range(half_rows)]
        if rest == 0:
            layout = [(1, 0, act_half, 0)]
        else:
            layout += [(1, j * act_block + cut, rest, widths[0] + j * rest) for j in range(half_rows)]
        layout.append((0, 0, grad_half, widths[0] + half_rows * rest))
        half_shape = jax.ShapeDtypeStruct((slots, grad_half + act_half), jnp.bfloat16)
        keep, send = pl.pallas_call(
            functools.partial(split_kernel, cols, layout),
            in_specs=[pl.BlockSpec(memory_space=pltpu.SMEM)] * 2 + [pl.BlockSpec(memory_space=pltpu.VMEM)] * 2,
            out_specs=[pl.BlockSpec(memory_space=pltpu.VMEM)] * 2,
            out_shape=[half_shape, half_shape],
        )(col[None], row_counts, activations, pseudo_grads)
        other = lax.ppermute(send, "col", swap)
        first, second = jnp.where(col == 0, keep, other), jnp.where(col == 0, other, keep)

        chains = []
        for start, width in ((0, widths[0]), (widths[0], widths[1])):
            own = jnp.concatenate([first[:, start : start + width], second[:, start : start + width]], axis=0)
            chains.append([own])
        forward = [chain[0] for chain in chains]
        backward = list(forward)
        steps, halfway = [0] * len(chains), rows // 2
        sequence = [0, 1] * halfway
        previous = ()
        for k in sequence:
            chain, latest = chains[k], (forward[k], backward[k])
            (ahead_of, behind_of), _ = lax.optimization_barrier((latest, previous))
            previous = latest
            steps[k] += 1
            if steps[k] < halfway:
                forward[k] = lax.ppermute(ahead_of, "row", ahead)
                backward[k] = lax.ppermute(behind_of, "row", behind)
                chain += [forward[k], backward[k]]
            else:
                middle = widths[k] // 2
                upper = lax.ppermute(ahead_of[:, :middle], "row", ahead)
                lower = lax.ppermute(behind_of[:, middle:], "row", behind)
                chain.append(jnp.concatenate([upper, lower], axis=1))

        def left_part(chain, pieces):
            own = []
            for part in chain:
                cuts = [
                    lax.dynamic_slice_in_dim(part, base + (row % half_rows) * size, size, 1) for base, size in pieces
                ]
                own.append(cuts[0] if len(cuts) == 1 else jnp.concatenate(cuts, axis=1))
            early = len(own) - 3
            groups = [jnp.concatenate(own[:early], axis=0), jnp.concatenate(own[early:], axis=0)]
            mine = col == row // half_rows
            return jnp.concatenate([jnp.where(mine, g, lax.ppermute(g, "col", swap)) for g in groups], axis=0)

        act_shape, grad_shape = (act_block, act_half), (grad_block, grad_half)
        left_first = left_part(chains[0], [(0, cut)])
        if rest == 0:
            left_grad = left_part(chains[1], [(0, grad_block)])
            act_cov = gram(left_first, chains[0], scale, act_half // 256, 256)
            grad_cov = gram(left_grad, chains[1], scale, grad_half // 256, 256)
        else:
            grad_first = half_rows * rest
            left_second = left_part(chains[1], [(0, rest), (grad_first, grad_block)])
            half_cut = cut // 2
            (act_cov,) = tiles(
                scale,
                [
                    (0, 0, part * half_cut, cut, cut, half_cut, 0, 0, part * half_cut, act_block, half_rows)
                    for part in (0, 1)
                ],
                [left_first], [chains[0]], [act_shape],
            )
            lefts = [left_first, left_second[:, :rest], left_second[:, rest:]]
            act_cov, grad_cov = tiles(
                scale,
                [
                    (0, 1, 0, rest, cut, rest, 0, 0, cut, act_block, half_rows),
                    (1, 0, 0, cut, rest, cut, 0, cut, 0, act_block, half_rows),
                    (1, 1, 0, rest, rest, rest, 0, cut, cut, act_block, half_rows),
                    (2, 1, grad_first, grad_block, grad_block, grad_block, 1, 0, 0, grad_block, half_rows),
                ],
                lefts, chains, [act_shape, grad_shape], act_cov,
            )
        return act_cov, grad_cov

    return jax.shard_map(
        local,
        mesh=mesh,
        in_specs=(
            P(("groups", "row", "col"), None),
            P(("groups", "row", "col"), None),
            P(("groups", "row", "col")),
        ),
        out_specs=(P(("groups", "row"), "col"), P(("groups", "row"), "col")),
        check_vma=False,
    )
```

time: 88.6 us -> 69.5 us (0.78)
  starting transfers between devices: 31.7 us -> 18 us
  Pallas kernels: 33.2 us -> 22 us
  waiting for transfers between devices: 19.8 us -> 25.7 us
    pallas_call x4 -> x2, Pallas kernels: 31.3 us -> 20 us  [tiles(): pl.pallas_call(functools.partial(tiles_kernel, scale, groups, len(lefts),...]
    ppermute x9 -> x6, starting transfers between devices: 17.2 us -> 11.4 us  [local(): forward[k] = lax.ppermute(ahead_of, 'row', ahead)]
    ppermute x3 -> x2, waiting for transfers between devices: 1.73 us -> 6.8 us  [local(): upper = lax.ppermute(ahead_of[:, :middle], 'row', ahead)]
    ppermute x9 -> x6, starting transfers between devices: 6.79 us -> 1.8 us  [local(): backward[k] = lax.ppermute(behind_of, 'row', behind)]
    ppermute x9 -> x6, waiting for transfers between devices: 3.87 us -> 7.02 us  [local(): forward[k] = lax.ppermute(ahead_of, 'row', ahead)]
    ppermute x3 -> x2, waiting for transfers between devices: 3.74 us -> 1.29 us  [local(): lower = lax.ppermute(behind_of[:, middle:], 'row', behind)]
    ppermute x9 -> x6, waiting for transfers between devices: 7.52 us -> 9.17 us  [local(): backward[k] = lax.ppermute(behind_of, 'row', behind)]
    ppermute x6 -> x4, waiting for transfers between devices: 1.54 us -> 0.01 us  [left_part(): lax.ppermute(g, 'col', swap)]
  transfers between devices with their start and end apart: 31 -> 21, of which waited for: 16 -> 14; matrix products, arithmetic and copies ran while one was open for 1% -> 1% of each run, Pallas kernels for 20% -> 9%
where the time goes in v3:
time: 69.5 us; the launch traced here: 69.2 us
  waiting for transfers between devices  25.7 us (37%)
  Pallas kernels  22 us (32%)
  starting transfers between devices  18 us (26%)
  other arithmetic  1.68 us (2%)
  between operations  1.63 us (2%)
    pallas_call x2, Pallas kernels, tiles(): pl.pallas_call(functools.partial(tiles_kernel, scale, groups, len(lefts),...  20 us
    ppermute x6, starting transfers between devices, local(): forward[k] = lax.ppermute(ahead_of, 'row', ahead)  11.4 us
    ppermute x6, waiting for transfers between devices, local(): backward[k] = lax.ppermute(behind_of, 'row', behind)  9.17 us
    ppermute x6, waiting for transfers between devices, local(): forward[k] = lax.ppermute(ahead_of, 'row', ahead)  7.02 us
    ppermute x2, waiting for transfers between devices, local(): upper = lax.ppermute(ahead_of[:, :middle], 'row', ahead)  6.8 us
    ppermute x2, starting transfers between devices, local(): upper = lax.ppermute(ahead_of[:, :middle], 'row', ahead)  3.21 us
    pallas_call x1, Pallas kernels, local(): pl.pallas_call(functools.partial(split_kernel, cols, layout), in_specs=[p...  1.95 us
    ppermute x6, starting transfers between devices, local(): backward[k] = lax.ppermute(behind_of, 'row', behind)  1.8 us
  transfers between devices with their start and end apart: 21, of which 14 were waited for; matrix products, arithmetic and copies ran while one was open for 1% of the time, Pallas kernels for 9%

profile of v3, /device:TPU:0, one launch (start us, length us, event | category | flops | bytes accessed | tf_op | source)
XLA Modules:
  0.0 69.2 jit_solution(13535247534010227102)
XLA Ops:
  1.3 1.9 %shard_map.50 = (bf16[12,9216]{1,0:T(8,128)(2,1)}, bf16[12,9216]{1,0:T(8,128)(2,1)}) custom-call(s32[1]{0:T(128)} %bitcast.half_ref, s32[1]{0:T(128)S(6)} %copy.17.count_ref, bf16[12,14336]{1,0:T(8,128)(2,1)} %act_ref.1, bf16[12,4096]{1,0:T(8,128)(2,1)} %grad_ref.1), custom_call_target="tpu_custom_call" | custom-call | tf_op jit(solution)/shard_map/pallas_call | solution.py:166
  3.2 0.4 collective-permute-start
  3.7 1.4 %collective-permute-done = bf16[12,9216]{1,0:T(8,128)(2,1)S(1)} collective-permute-done((bf16[12,9216]{1,0:T(8,128)(2,1)}, bf16[12,9216]{1,0:T(8,128)(2,1)S(1)}, u32[]{:S(2)}, u32[]{:S(2)}) %collective-permute-start) | collective-permute-done | bytes 221216 | tf_op jit(solution)/shard_map/ppermute | solution.py:172
  5.1 1.0 %broadcast_select_fusion.2 = (bf16[12,9216]{1,0:T(8,128)(2,1)S(1)}, bf16[12,9216]{1,0:T(8,128)(2,1)S(1)}) fusion(bf16[12,9216]{1,0:T(8,128)(2,1)} %get-tuple-element.20, bf16[12,9216]{1,0:T(8,128)(2,1)S(1)} %collective-permute-done, pred[]{:T(512)S(6)} %eq.34), kind=kLoop, calls=%fused_computation.6 | loop fusion | flops 221184 | bytes 884737 | tf_op jit(solution)/shard_map/jit(_where)/select_n | solution.py:173
  6.2 0.1 pad_maximum_fusion.1.refs_11_
  6.2 0.1 fusion.4
  6.3 0.1 fusion.3
  6.4 0.1 pad_maximum_fusion.2.refs_1_.refs_3_
  6.5 3.0 %collective-permute-start.1 = (bf16[24,4096]{1,0:T(8,128)(2,1)S(1)}, bf16[24,4096]{1,0:T(8,128)(2,1)S(1)}, u32[]{:S(2)}, u32[]{:S(2)}) collective-permute-start(bf16[24,4096]{1,0:T(8,128)(2,1)S(1)} %pad_maximum_fusion.2.refs_1_.refs_3_), channel_id=1, source_target_pairs={{0,4},{4,8},{8,12},{12,14},{14,10},{10,6},{6,2},{2,0},{1,5},{5,9},... | collective-permute-start | bytes 589832 | tf_op jit(solution)/shard_map/ppermute | solution.py:190
  9.5 0.0 collective-permute-start.2
  9.5 2.0 %collective-permute-start.6 = (bf16[24,5120]{1,0:T(8,128)(2,1)S(1)}, bf16[24,5120]{1,0:T(8,128)(2,1)S(1)}, u32[]{:S(2)}, u32[]{:S(2)}) collective-permute-start(bf16[24,5120]{1,0:T(8,128)(2,1)S(1)} %pad_maximum_fusion.1.refs_11_), channel_id=1, source_target_pairs={{0,4},{4,8},{8,12},{12,14},{14,10},{10,6},{6,2},{2,0},{1,5},{5,9},... | collective-permute-start | bytes 737288 | tf_op jit(solution)/shard_map/ppermute | solution.py:190
  11.5 0.0 collective-permute-start.7
  11.5 0.1 fusion.2
  11.6 3.5 %collective-permute-done.1.refs_2_.refs_4_ = bf16[24,4096]{1,0:T(8,128)(2,1)S(1)} collective-permute-done((bf16[24,4096]{1,0:T(8,128)(2,1)S(1)}, bf16[24,4096]{1,0:T(8,128)(2,1)S(1)}, u32[]{:S(2)}, u32[]{:S(2)}) %collective-permute-start.1) | collective-permute-done | bytes 196640 | tf_op jit(solution)/shard_map/ppermute | solution.py:190
  15.1 2.2 %collective-permute-done.2.refs_3_.refs_5_ = bf16[24,4096]{1,0:T(8,128)(2,1)S(1)} collective-permute-done((bf16[24,4096]{1,0:T(8,128)(2,1)S(1)}, bf16[24,4096]{1,0:T(8,128)(2,1)S(1)}, u32[]{:S(2)}, u32[]{:S(2)}) %collective-permute-start.2) | collective-permute-done | bytes 196640 | tf_op jit(solution)/shard_map/ppermute | solution.py:191
  17.3 1.6 %collective-permute-start.3 = (bf16[24,4096]{1,0:T(8,128)(2,1)S(1)}, bf16[24,4096]{1,0:T(8,128)(2,1)S(1)}, u32[]{:S(2)}, u32[]{:S(2)}) collective-permute-start(bf16[24,4096]{1,0:T(8,128)(2,1)S(1)} %collective-permute-done.1.refs_2_.refs_4_), channel_id=1, source_target_pairs={{0,4},{4,8},{8,12},{12,14},{14,10},{10,6},{6,2},{2,0},{1,5},{5,9},... | collective-permute-start | bytes 589832 | tf_op jit(solution)/shard_map/ppermute | solution.py:190
  18.8 0.4 collective-permute-start.4
  19.3 1.0 %collective-permute-done.6.refs_12_ = bf16[24,5120]{1,0:T(8,128)(2,1)S(1)} collective-permute-done((bf16[24,5120]{1,0:T(8,128)(2,1)S(1)}, bf16[24,5120]{1,0:T(8,128)(2,1)S(1)}, u32[]{:S(2)}, u32[]{:S(2)}) %collective-permute-start.6) | collective-permute-done | bytes 245792 | tf_op jit(solution)/shard_map/ppermute | solution.py:190
  20.4 2.2 %collective-permute-done.7.refs_13_ = bf16[24,5120]{1,0:T(8,128)(2,1)S(1)} collective-permute-done((bf16[24,5120]{1,0:T(8,128)(2,1)S(1)}, bf16[24,5120]{1,0:T(8,128)(2,1)S(1)}, u32[]{:S(2)}, u32[]{:S(2)}) %collective-permute-start.7) | collective-permute-done | bytes 245792 | tf_op jit(solution)/shard_map/ppermute | solution.py:191
  22.5 1.6 %collective-permute-start.10 = (bf16[24,5120]{1,0:T(8,128)(2,1)S(1)}, bf16[24,5120]{1,0:T(8,128)(2,1)S(1)}, u32[]{:S(2)}, u32[]{:S(2)}) collective-permute-start(bf16[24,5120]{1,0:T(8,128)(2,1)S(1)} %collective-permute-done.6.refs_12_), channel_id=1, source_target_pairs={{0,4},{4,8},{8,12},{12,14},{14,10},{10,6},{6,2},{2,0},{1,5},{5,9},... | collective-permute-start | bytes 737288 | tf_op jit(solution)/shard_map/ppermute | solution.py:190
  24.1 0.4 collective-permute-start.11
  24.6 0.5 collective-permute-done.3.refs_4_.refs_6_
  25.1 1.6 %collective-permute-done.4.refs_5_.refs_7_ = bf16[24,4096]{1,0:T(8,128)(2,1)S(1)} collective-permute-done((bf16[24,4096]{1,0:T(8,128)(2,1)S(1)}, bf16[24,4096]{1,0:T(8,128)(2,1)S(1)}, u32[]{:S(2)}, u32[]{:S(2)}) %collective-permute-start.4) | collective-permute-done | bytes 196640 | tf_op jit(solution)/shard_map/ppermute | solution.py:191
  26.8 0.0 collective-permute-start.5
  26.8 1.6 %collective-permute-start.8 = (bf16[24,4096]{1,0:T(8,128)(2,1)S(1)}, bf16[24,4096]{1,0:T(8,128)(2,1)S(1)}, u32[]{:S(2)}, u32[]{:S(2)}) collective-permute-start(bf16[24,4096]{1,0:T(8,128)(2,1)S(1)} %collective-permute-done.3.refs_4_.refs_6_), channel_id=1, source_target_pairs={{0,4},{4,8},{8,12},{12,14},{14,10},{10,6},{6,2},{2,0},{1,5},{5,9},... | collective-permute-start | bytes 589832 | tf_op jit(solution)/shard_map/ppermute | solution.py:190
  28.4 0.4 collective-permute-start.9
  28.8 0.5 collective-permute-done.10.refs_14_
  29.3 1.5 %collective-permute-done.11.refs_15_ = bf16[24,5120]{1,0:T(8,128)(2,1)S(1)} collective-permute-done((bf16[24,5120]{1,0:T(8,128)(2,1)S(1)}, bf16[24,5120]{1,0:T(8,128)(2,1)S(1)}, u32[]{:S(2)}, u32[]{:S(2)}) %collective-permute-start.11) | collective-permute-done | bytes 245792 | tf_op jit(solution)/shard_map/ppermute | solution.py:191
  30.9 1.6 %collective-permute-start.16 = (bf16[24,5120]{1,0:T(8,128)(2,1)S(1)}, bf16[24,5120]{1,0:T(8,128)(2,1)S(1)}, u32[]{:S(2)}, u32[]{:S(2)}) collective-permute-start(bf16[24,5120]{1,0:T(8,128)(2,1)S(1)} %collective-permute-done.10.refs_14_), channel_id=1, source_target_pairs={{0,4},{4,8},{8,12},{12,14},{14,10},{10,6},{6,2},{2,0},{1,5},{5,9},... | collective-permute-start | bytes 737288 | tf_op jit(solution)/shard_map/ppermute | solution.py:190
  32.5 0.4 collective-permute-start.17
  33.0 1.5 %collective-permute-done.8.refs_6_.refs_8_ = bf16[24,4096]{1,0:T(8,128)(2,1)S(1)} collective-permute-done((bf16[24,4096]{1,0:T(8,128)(2,1)S(1)}, bf16[24,4096]{1,0:T(8,128)(2,1)S(1)}, u32[]{:S(2)}, u32[]{:S(2)}) %collective-permute-start.8) | collective-permute-done | bytes 196640 | tf_op jit(solution)/shard_map/ppermute | solution.py:190
  34.5 0.0 collective-permute-start.15
  34.5 1.6 %collective-permute-done.9.refs_7_.refs_9_ = bf16[24,4096]{1,0:T(8,128)(2,1)S(1)} collective-permute-done((bf16[24,4096]{1,0:T(8,128)(2,1)S(1)}, bf16[24,4096]{1,0:T(8,128)(2,1)S(1)}, u32[]{:S(2)}, u32[]{:S(2)}) %collective-permute-start.9) | collective-permute-done | bytes 196640 | tf_op jit(solution)/shard_map/ppermute | solution.py:191
  36.2 0.5 collective-permute-start.13
  36.7 0.0 collective-permute-done.5
  36.7 1.6 %collective-permute-start.12 = (bf16[24,2048]{1,0:T(8,128)(2,1)S(1)}, bf16[24,2048]{1,0:T(8,128)(2,1)S(1)}, u32[]{:S(2)}, u32[]{:S(2)}) collective-permute-start(bf16[24,2048]{1,0:T(8,128)(2,1)S(1)} %slice.34), channel_id=1, source_target_pairs={{0,4},{4,8},{8,12},{12,14},{14,10},{10,6},{6,2},{2,0},{1,5},{5,9},... | collective-permute-start | bytes 294920 | tf_op jit(solution)/shard_map/ppermute | solution.py:195
  38.3 3.1 %collective-permute-done.12 = bf16[24,2048]{1,0:T(8,128)(2,1)S(1)} collective-permute-done((bf16[24,2048]{1,0:T(8,128)(2,1)S(1)}, bf16[24,2048]{1,0:T(8,128)(2,1)S(1)}, u32[]{:S(2)}, u32[]{:S(2)}) %collective-permute-start.12) | collective-permute-done | bytes 98336 | tf_op jit(solution)/shard_map/ppermute | solution.py:195
  41.5 1.3 %collective-permute-done.13 = bf16[24,2048]{1,0:T(8,128)(2,1)S(1)} collective-permute-done((bf16[24,2048]{1,0:T(8,128)(2,1)S(1)}, bf16[24,2048]{1,0:T(8,128)(2,1)S(1)}, u32[]{:S(2)}, u32[]{:S(2)}) %collective-permute-start.13) | collective-permute-done | bytes 98336 | tf_op jit(solution)/shard_map/ppermute | solution.py:196
  42.8 0.1 collective-permute-start.14
  42.9 0.0 collective-permute-done.16.refs_16_
  42.9 0.0 collective-permute-done.17.refs_17_
  42.9 0.5 collective-permute-start.19
  43.4 1.6 %collective-permute-start.18 = (bf16[24,2560]{1,0:T(8,128)(2,1)S(1)}, bf16[24,2560]{1,0:T(8,128)(2,1)S(1)}, u32[]{:S(2)}, u32[]{:S(2)}) collective-permute-start(bf16[24,2560]{1,0:T(8,128)(2,1)S(1)} %slice.36), channel_id=1, source_target_pairs={{0,4},{4,8},{8,12},{12,14},{14,10},{10,6},{6,2},{2,0},{1,5},{5,9},... | collective-permute-start | bytes 368648 | tf_op jit(solution)/shard_map/ppermute | solution.py:195
  45.0 0.0 collective-permute-done.15
  45.1 0.0 collective-permute-done.14
  45.2 3.7 %collective-permute-done.18 = bf16[24,2560]{1,0:T(8,128)(2,1)S(1)} collective-permute-done((bf16[24,2560]{1,0:T(8,128)(2,1)S(1)}, bf16[24,2560]{1,0:T(8,128)(2,1)S(1)}, u32[]{:S(2)}, u32[]{:S(2)}) %collective-permute-start.18) | collective-permute-done | bytes 122912 | tf_op jit(solution)/shard_map/ppermute | solution.py:195
  48.9 0.0 collective-permute-done.19
  49.0 0.1 collective-permute-start.20
  49.1 6.5 %shard_map.51.refs_19_ = f32[1792,7168]{1,0:T(8,128)} custom-call(bf16[192,1024]{1,0:T(8,128)(2,1)S(1)} %pad_maximum_fusion.refs_0_, bf16[24,4096]{1,0:T(8,128)(2,1)S(1)} %pad_maximum_fusion.2.refs_1_.refs_3_, bf16[24,4096]{1,0:T(8,128)(2,1)S(1)} %collective-permute-done.1.refs_2_.refs_4_, bf16[24,4096]{1,0:T(8,128)(2,1)S(1)} %collective-permute-done.2.refs_3_.refs_5_, ...), custom_call_target="tpu_custom_call" | custom-call | flops 1610612736 | bytes 16777216 | tf_op jit(solution)/shard_map/pallas_call | solution.py:108
  55.6 0.0 collective-permute-done.20
  55.6 0.1 broadcast_select_fusion.4
  55.7 13.5 %shard_map.52 = (f32[1792,7168]{1,0:T(8,128)}, f32[512,2048]{1,0:T(8,128)}) custom-call(bf16[192,1024]{1,0:T(8,128)(2,1)S(1)} %pad_maximum_fusion.refs_0_, bf16[192,768]{1,0:T(8,128)(2,1)S(1)} %fusion.refs_1_, bf16[192,512]{1,0:T(8,128)(2,1)S(1)} %pad_maximum_fusion.3.refs_2_, ...), custom_call_target="tpu_custom_call", output_to_operand_aliasing={{0}: (19, {})} | custom-call | flops 3724541952 | bytes 38797312 | tf_op jit(solution)/shard_map/pallas_call | solution.py:108
  (46 shorter events, 0.5 us)
Async XLA Ops:
  3.2 1.9 %collective-permute-start = (bf16[12,9216]{1,0:T(8,128)(2,1)}, bf16[12,9216]{1,0:T(8,128)(2,1)S(1)}, u32[]{:S(2)}, u32[]{:S(2)}) collective-permute-start(bf16[12,9216]{1,0:T(8,128)(2,1)} %get-tuple-element.21), channel_id=1, source_target_pairs={{0,1},{1,0},{2,3},{3,2},{4,5},{5,4},{6,7},{7,6},{8,9},{9,8},{10,11... | collective-permute-start | bytes 663560 | tf_op jit(solution)/shard_map/ppermute | solution.py:172
  6.5 8.6 %collective-permute-start.1 = (bf16[24,4096]{1,0:T(8,128)(2,1)S(1)}, bf16[24,4096]{1,0:T(8,128)(2,1)S(1)}, u32[]{:S(2)}, u32[]{:S(2)}) collective-permute-start(bf16[24,4096]{1,0:T(8,128)(2,1)S(1)} %pad_maximum_fusion.2.refs_1_.refs_3_), channel_id=1, source_target_pairs={{0,4},{4,8},{8,12},{12,14},{14,10},{10,6},{6,2},{2,0},{1,5},{5,9},... | collective-permute-start | bytes 589832 | tf_op jit(solution)/shard_map/ppermute | solution.py:190
  9.5 7.8 %collective-permute-start.2 = (bf16[24,4096]{1,0:T(8,128)(2,1)S(1)}, bf16[24,4096]{1,0:T(8,128)(2,1)S(1)}, u32[]{:S(2)}, u32[]{:S(2)}) collective-permute-start(bf16[24,4096]{1,0:T(8,128)(2,1)S(1)} %pad_maximum_fusion.2.refs_1_.refs_3_), channel_id=1, source_target_pairs={{4,0},{8,4},{12,8},{14,12},{10,14},{6,10},{2,6},{0,2},{5,1},{9,5},... | collective-permute-start | bytes 589832 | tf_op jit(solution)/shard_map/ppermute | solution.py:191
  9.5 10.9 %collective-permute-start.6 = (bf16[24,5120]{1,0:T(8,128)(2,1)S(1)}, bf16[24,5120]{1,0:T(8,128)(2,1)S(1)}, u32[]{:S(2)}, u32[]{:S(2)}) collective-permute-start(bf16[24,5120]{1,0:T(8,128)(2,1)S(1)} %pad_maximum_fusion.1.refs_11_), channel_id=1, source_target_pairs={{0,4},{4,8},{8,12},{12,14},{14,10},{10,6},{6,2},{2,0},{1,5},{5,9},... | collective-permute-start | bytes 737288 | tf_op jit(solution)/shard_map/ppermute | solution.py:190
  11.5 11.0 %collective-permute-start.7 = (bf16[24,5120]{1,0:T(8,128)(2,1)S(1)}, bf16[24,5120]{1,0:T(8,128)(2,1)S(1)}, u32[]{:S(2)}, u32[]{:S(2)}) collective-permute-start(bf16[24,5120]{1,0:T(8,128)(2,1)S(1)} %pad_maximum_fusion.1.refs_11_), channel_id=1, source_target_pairs={{4,0},{8,4},{12,8},{14,12},{10,14},{6,10},{2,6},{0,2},{5,1},{9,5},... | collective-permute-start | bytes 737288 | tf_op jit(solution)/shard_map/ppermute | solution.py:191
  17.3 7.8 %collective-permute-start.3 = (bf16[24,4096]{1,0:T(8,128)(2,1)S(1)}, bf16[24,4096]{1,0:T(8,128)(2,1)S(1)}, u32[]{:S(2)}, u32[]{:S(2)}) collective-permute-start(bf16[24,4096]{1,0:T(8,128)(2,1)S(1)} %collective-permute-done.1.refs_2_.refs_4_), channel_id=1, source_target_pairs={{0,4},{4,8},{8,12},{12,14},{14,10},{10,6},{6,2},{2,0},{1,5},{5,9},... | collective-permute-start | bytes 589832 | tf_op jit(solution)/shard_map/ppermute | solution.py:190
  18.8 7.9 %collective-permute-start.4 = (bf16[24,4096]{1,0:T(8,128)(2,1)S(1)}, bf16[24,4096]{1,0:T(8,128)(2,1)S(1)}, u32[]{:S(2)}, u32[]{:S(2)}) collective-permute-start(bf16[24,4096]{1,0:T(8,128)(2,1)S(1)} %collective-permute-done.2.refs_3_.refs_5_), channel_id=1, source_target_pairs={{4,0},{8,4},{12,8},{14,12},{10,14},{6,10},{2,6},{0,2},{5,1},{9,5},... | collective-permute-start | bytes 589832 | tf_op jit(solution)/shard_map/ppermute | solution.py:191
  22.5 6.8 %collective-permute-start.10 = (bf16[24,5120]{1,0:T(8,128)(2,1)S(1)}, bf16[24,5120]{1,0:T(8,128)(2,1)S(1)}, u32[]{:S(2)}, u32[]{:S(2)}) collective-permute-start(bf16[24,5120]{1,0:T(8,128)(2,1)S(1)} %collective-permute-done.6.refs_12_), channel_id=1, source_target_pairs={{0,4},{4,8},{8,12},{12,14},{14,10},{10,6},{6,2},{2,0},{1,5},{5,9},... | collective-permute-start | bytes 737288 | tf_op jit(solution)/shard_map/ppermute | solution.py:190
  24.1 6.8 %collective-permute-start.11 = (bf16[24,5120]{1,0:T(8,128)(2,1)S(1)}, bf16[24,5120]{1,0:T(8,128)(2,1)S(1)}, u32[]{:S(2)}, u32[]{:S(2)}) collective-permute-start(bf16[24,5120]{1,0:T(8,128)(2,1)S(1)} %collective-permute-done.7.refs_13_), channel_id=1, source_target_pairs={{4,0},{8,4},{12,8},{14,12},{10,14},{6,10},{2,6},{0,2},{5,1},{9,5},... | collective-permute-start | bytes 737288 | tf_op jit(solution)/shard_map/ppermute | solution.py:191
  26.8 9.9 %collective-permute-start.5 = (bf16[120,1024]{1,0:T(8,128)(2,1)S(1)}, bf16[120,1024]{1,0:T(8,128)(2,1)S(1)}, u32[]{:S(2)}, u32[]{:S(2)}) collective-permute-start(bf16[120,1024]{1,0:T(8,128)(2,1)S(1)} %dynamic-slice_dynamic-update-slice_fusion), channel_id=1, source_target_pairs={{0,1},{1,0},{2,3},{3,2},{4,5},{5,4},{6,7},{7,6},{8,9},{9,8},{10,11... | collective-permute-start | bytes 737288 | tf_op jit(solution)/shard_map/ppermute | solution.py:209
  26.8 7.8 %collective-permute-start.8 = (bf16[24,4096]{1,0:T(8,128)(2,1)S(1)}, bf16[24,4096]{1,0:T(8,128)(2,1)S(1)}, u32[]{:S(2)}, u32[]{:S(2)}) collective-permute-start(bf16[24,4096]{1,0:T(8,128)(2,1)S(1)} %collective-permute-done.3.refs_4_.refs_6_), channel_id=1, source_target_pairs={{0,4},{4,8},{8,12},{12,14},{14,10},{10,6},{6,2},{2,0},{1,5},{5,9},... | collective-permute-start | bytes 589832 | tf_op jit(solution)/shard_map/ppermute | solution.py:190
  28.4 7.7 %collective-permute-start.9 = (bf16[24,4096]{1,0:T(8,128)(2,1)S(1)}, bf16[24,4096]{1,0:T(8,128)(2,1)S(1)}, u32[]{:S(2)}, u32[]{:S(2)}) collective-permute-start(bf16[24,4096]{1,0:T(8,128)(2,1)S(1)} %collective-permute-done.4.refs_5_.refs_7_), channel_id=1, source_target_pairs={{4,0},{8,4},{12,8},{14,12},{10,14},{6,10},{2,6},{0,2},{5,1},{9,5},... | collective-permute-start | bytes 589832 | tf_op jit(solution)/shard_map/ppermute | solution.py:191
  30.9 12.0 %collective-permute-start.16 = (bf16[24,5120]{1,0:T(8,128)(2,1)S(1)}, bf16[24,5120]{1,0:T(8,128)(2,1)S(1)}, u32[]{:S(2)}, u32[]{:S(2)}) collective-permute-start(bf16[24,5120]{1,0:T(8,128)(2,1)S(1)} %collective-permute-done.10.refs_14_), channel_id=1, source_target_pairs={{0,4},{4,8},{8,12},{12,14},{14,10},{10,6},{6,2},{2,0},{1,5},{5,9},... | collective-permute-start | bytes 737288 | tf_op jit(solution)/shard_map/ppermute | solution.py:190
  32.5 10.4 %collective-permute-start.17 = (bf16[24,5120]{1,0:T(8,128)(2,1)S(1)}, bf16[24,5120]{1,0:T(8,128)(2,1)S(1)}, u32[]{:S(2)}, u32[]{:S(2)}) collective-permute-start(bf16[24,5120]{1,0:T(8,128)(2,1)S(1)} %collective-permute-done.11.refs_15_), channel_id=1, source_target_pairs={{4,0},{8,4},{12,8},{14,12},{10,14},{6,10},{2,6},{0,2},{5,1},{9,5},... | collective-permute-start | bytes 737288 | tf_op jit(solution)/shard_map/ppermute | solution.py:191
  34.5 10.5 %collective-permute-start.15 = (bf16[120,1280]{1,0:T(8,128)(2,1)S(1)}, bf16[120,1280]{1,0:T(8,128)(2,1)S(1)}, u32[]{:S(2)}, u32[]{:S(2)}) collective-permute-start(bf16[120,1280]{1,0:T(8,128)(2,1)S(1)} %maximum_dynamic-update-slice_fusion), channel_id=1, source_target_pairs={{0,1},{1,0},{2,3},{3,2},{4,5},{5,4},{6,7},{7,6},{8,9},{9,8},{10,11... | collective-permute-start | bytes 921608 | tf_op jit(solution)/shard_map/ppermute | solution.py:209
  36.2 6.6 %collective-permute-start.13 = (bf16[24,2048]{1,0:T(8,128)(2,1)S(1)}, bf16[24,2048]{1,0:T(8,128)(2,1)S(1)}, u32[]{:S(2)}, u32[]{:S(2)}) collective-permute-start(bf16[24,2048]{1,0:T(8,128)(2,1)S(1)} %slice.35), channel_id=1, source_target_pairs={{4,0},{8,4},{12,8},{14,12},{10,14},{6,10},{2,6},{0,2},{5,1},{9,5},... | collective-permute-start | bytes 294920 | tf_op jit(solution)/shard_map/ppermute | solution.py:196
  36.7 4.8 %collective-permute-start.12 = (bf16[24,2048]{1,0:T(8,128)(2,1)S(1)}, bf16[24,2048]{1,0:T(8,128)(2,1)S(1)}, u32[]{:S(2)}, u32[]{:S(2)}) collective-permute-start(bf16[24,2048]{1,0:T(8,128)(2,1)S(1)} %slice.34), channel_id=1, source_target_pairs={{0,4},{4,8},{8,12},{12,14},{14,10},{10,6},{6,2},{2,0},{1,5},{5,9},... | collective-permute-start | bytes 294920 | tf_op jit(solution)/shard_map/ppermute | solution.py:195
  42.8 2.3 %collective-permute-start.14 = (bf16[72,1024]{1,0:T(8,128)(2,1)S(1)}, bf16[72,1024]{1,0:T(8,128)(2,1)S(1)}, u32[]{:S(2)}, u32[]{:S(2)}) collective-permute-start(bf16[72,1024]{1,0:T(8,128)(2,1)S(1)} %pad_maximum_fusion.4), channel_id=1, source_target_pairs={{0,1},{1,0},{2,3},{3,2},{4,5},{5,4},{6,7},{7,6},{8,9},{9,8},{10,11... | collective-permute-start | bytes 442376 | tf_op jit(solution)/shard_map/ppermute | solution.py:209
  42.9 5.9 %collective-permute-start.19 = (bf16[24,2560]{1,0:T(8,128)(2,1)S(1)}, bf16[24,2560]{1,0:T(8,128)(2,1)S(1)}, u32[]{:S(2)}, u32[]{:S(2)}) collective-permute-start(bf16[24,2560]{1,0:T(8,128)(2,1)S(1)} %slice.37), channel_id=1, source_target_pairs={{4,0},{8,4},{12,8},{14,12},{10,14},{6,10},{2,6},{0,2},{5,1},{9,5},... | collective-permute-start | bytes 368648 | tf_op jit(solution)/shard_map/ppermute | solution.py:196
  43.4 5.4 %collective-permute-start.18 = (bf16[24,2560]{1,0:T(8,128)(2,1)S(1)}, bf16[24,2560]{1,0:T(8,128)(2,1)S(1)}, u32[]{:S(2)}, u32[]{:S(2)}) collective-permute-start(bf16[24,2560]{1,0:T(8,128)(2,1)S(1)} %slice.36), channel_id=1, source_target_pairs={{0,4},{4,8},{8,12},{12,14},{14,10},{10,6},{6,2},{2,0},{1,5},{5,9},... | collective-permute-start | bytes 368648 | tf_op jit(solution)/shard_map/ppermute | solution.py:195
  49.0 6.6 %collective-permute-start.20 = (bf16[72,1280]{1,0:T(8,128)(2,1)S(1)}, bf16[72,1280]{1,0:T(8,128)(2,1)S(1)}, u32[]{:S(2)}, u32[]{:S(2)}) collective-permute-start(bf16[72,1280]{1,0:T(8,128)(2,1)S(1)} %maximum_maximum_fusion), channel_id=1, source_target_pairs={{0,1},{1,0},{2,3},{3,2},{4,5},{5,4},{6,7},{7,6},{8,9},{9,8},{10,11... | collective-permute-start | bytes 552968 | tf_op jit(solution)/shard_map/ppermute | solution.py:209

commit v4 on v3

--- a/solution.py
+++ b/solution.py
@@ -8,7 +8,7 @@
 from jax.sharding import PartitionSpec as P
 
 
-SLOTS = 4
+SLOTS, COPIES = 4, 2
 
 
 def chip_ring(rows):
@@ -54,19 +54,21 @@
         refs = refs[shards:]
     out_refs = refs[aliased : aliased + outs]
     turned, buffer, sems = refs[aliased + outs : -2], refs[-2], refs[-1]
-    for left_ref, turned_ref in zip(left_refs, turned):
-        turned_ref[...] = left_ref[...].T
-
-    def copy(group, slot, j):
+
+    def copy(group, slot, j, start=0, rows=None):
         _, _, _, _, height, width, which, row, column, stride, _ = group
+        rows = rows or height
         return pltpu.make_async_copy(
-            buffer.at[slot, pl.ds(0, height), pl.ds(0, width)],
-            out_refs[which].at[pl.ds(row, height), pl.ds(pl.multiple_of(column + j * stride, 128), width)],
+            buffer.at[slot, pl.ds(start, rows), pl.ds(0, width)],
+            out_refs[which].at[pl.ds(row + start, rows), pl.ds(pl.multiple_of(column + j * stride, 128), width)],
             sems.at[slot],
         )
 
-    earlier = None
+    earlier, ready = None, set()
     for group in groups:
+        if group[0] not in ready:
+            ready.add(group[0])
+            turned[group[0]][...] = left_refs[group[0]][...].T
 
         def step(j, carry, group=group, earlier=earlier):
             left, source, first, apart, height, width, _, _, _, _, _ = group
@@ -86,7 +88,8 @@
             right = jnp.concatenate([ref[:, here] for ref in sources[source]], axis=0)
             product = jnp.dot(turned[left][...], right, preferred_element_type=jnp.float32)
             buffer[slot, :height, :width] = product * scale
-            copy(group, slot, j).start()
+            for start in range(0, height, height // COPIES):
+                copy(group, slot, j, start, height // COPIES).start()
             return carry
 
         lax.fori_loop(0, group[-1], step, 0)
@@ -123,19 +126,28 @@
     )(*operands)
 
 
-def split_kernel(halves, order, half_ref, count_ref, act_ref, grad_ref, keep_ref, send_ref):
-    live = lax.broadcasted_iota(jnp.int32, (act_ref.shape[0], 128), 0) < count_ref[0]
+def split_kernel(halves, layouts, half_ref, count_ref, act_ref, grad_ref, *out_refs):
+    slots = act_ref.shape[0]
+    live = lax.broadcasted_iota(jnp.int32, (slots, 128), 0) < count_ref[0]
     for half in range(halves):
-        for flip, out_ref in ((0, keep_ref), (1, send_ref)):
+        for flip in (1, 0):
 
             @pl.when((half_ref[0] + flip) % halves == half)
-            def _(half=half, out_ref=out_ref):
-                for source, start, width, target in order:
-                    ref = (grad_ref, act_ref)[source]
-                    first = half * (ref.shape[1] // halves) + start
-                    values = ref[:, first : first + width]
-                    mask = jnp.concatenate([live] * (width // 128), axis=1)
-                    out_ref[:, target : target + width] = jnp.where(mask, values, jnp.zeros_like(values))
+            def _(half=half, flip=flip):
+                for chain, layout in enumerate(layouts):
+                    target = 0
+                    for source, start, width in layout:
+                        ref = (grad_ref, act_ref)[source]
+                        first = half * (ref.shape[1] // halves) + start
+                        values = ref[:, first : first + width]
+                        mask = jnp.concatenate([live] * (width // 128), axis=1)
+                        masked = jnp.where(mask, values, jnp.zeros_like(values))
+                        own = (half + flip) % halves * slots
+                        out_ref, columns = out_refs[2 * chain + flip], slice(target, target + width)
+                        out_ref[own : own + slots, columns] = masked
+                        other = slots - own
+                        out_ref[other : other + slots, columns] = jnp.zeros_like(values)
+                        target += width
 
 
 def solution(mesh):
@@ -156,31 +168,25 @@
         cut = act_block * 4 // 7 if act_block % 1792 == 0 else act_block
         rest = act_block - cut
         widths = [half_rows * cut, half_rows * rest + grad_half]
-        layout = [(1, j * act_block, cut, j * cut) for j in range(half_rows)]
         if rest == 0:
-            layout = [(1, 0, act_half, 0)]
+            layouts = [[(1, 0, act_half)], [(0, 0, grad_half)]]
         else:
-            layout += [(1, j * act_block + cut, rest, widths[0] + j * rest) for j in range(half_rows)]
-        layout.append((0, 0, grad_half, widths[0] + half_rows * rest))
-        half_shape = jax.ShapeDtypeStruct((slots, grad_half + act_half), jnp.bfloat16)
-        keep, send = pl.pallas_call(
-            functools.partial(split_kernel, cols, layout),
+            layouts = [
+                [(1, j * act_block, cut) for j in range(half_rows)],
+                [(1, j * act_block + cut, rest) for j in range(half_rows)] + [(0, 0, grad_half)],
+            ]
+        pieces = pl.pallas_call(
+            functools.partial(split_kernel, cols, layouts),
             in_specs=[pl.BlockSpec(memory_space=pltpu.SMEM)] * 2 + [pl.BlockSpec(memory_space=pltpu.VMEM)] * 2,
-            out_specs=[pl.BlockSpec(memory_space=pltpu.VMEM)] * 2,
-            out_shape=[half_shape, half_shape],
+            out_specs=[pl.BlockSpec(memory_space=pltpu.VMEM)] * 4,
+            out_shape=[jax.ShapeDtypeStruct((2 * slots, width), jnp.bfloat16) for width in widths for _ in (0, 1)],
         )(col[None], row_counts, activations, pseudo_grads)
-        other = lax.ppermute(send, "col", swap)
-        first, second = jnp.where(col == 0, keep, other), jnp.where(col == 0, other, keep)
-
-        chains = []
-        for start, width in ((0, widths[0]), (widths[0], widths[1])):
-            own = jnp.concatenate([first[:, start : start + width], second[:, start : start + width]], axis=0)
-            chains.append([own])
+        chains = [[pieces[2 * k] + lax.ppermute(pieces[2 * k + 1], "col", swap)] for k in (0, 1)]
         forward = [chain[0] for chain in chains]
         backward = list(forward)
         steps, halfway = [0] * len(chains), rows // 2
         sequence = [0, 1] * halfway
-        previous = ()
+        previous, last = (), []
         for k in sequence:
             chain, latest = chains[k], (forward[k], backward[k])
             (ahead_of, behind_of), _ = lax.optimization_barrier((latest, previous))
@@ -194,7 +200,7 @@
                 middle = widths[k] // 2
                 upper = lax.ppermute(ahead_of[:, :middle], "row", ahead)
                 lower = lax.ppermute(behind_of[:, middle:], "row", behind)
-                chain.append(jnp.concatenate([upper, lower], axis=1))
+                last.append((upper, lower))
 
         def left_part(chain, pieces):
             own = []
@@ -209,23 +215,27 @@
             return jnp.concatenate([jnp.where(mine, g, lax.ppermute(g, "col", swap)) for g in groups], axis=0)
 
         act_shape, grad_shape = (act_block, act_half), (grad_block, grad_half)
+        last_first, _ = lax.optimization_barrier((last[0], (forward[1], backward[1])))
+        chains[0].append(jnp.concatenate(last_first, axis=1))
         left_first = left_part(chains[0], [(0, cut)])
         if rest == 0:
+            chains[1].append(jnp.concatenate(last[1], axis=1))
             left_grad = left_part(chains[1], [(0, grad_block)])
             act_cov = gram(left_first, chains[0], scale, act_half // 256, 256)
             grad_cov = gram(left_grad, chains[1], scale, grad_half // 256, 256)
         else:
-            grad_first = half_rows * rest
+            tile, grad_first = cut // 4, half_rows * rest
+
+            def square(part, out):
+                group_of = lambda start: (0, 0, start, cut, cut, tile, 0, 0, start, act_block, half_rows)
+                groups = [group_of(part * cut // 2), group_of(part * cut // 2 + tile)]
+                return tiles(scale, groups, [left_first], [chains[0]], [act_shape], out)[0]
+
+            act_cov = square(0, None)
+            last_second, act_cov = lax.optimization_barrier((last[1], act_cov))
+            chains[1].append(jnp.concatenate(last_second, axis=1))
             left_second = left_part(chains[1], [(0, rest), (grad_first, grad_block)])
-            half_cut = cut // 2
-            (act_cov,) = tiles(
-                scale,
-                [
-                    (0, 0, part * half_cut, cut, cut, half_cut, 0, 0, part * half_cut, act_block, half_rows)
-                    for part in (0, 1)
-                ],
-                [left_first], [chains[0]], [act_shape],
-            )
+            act_cov = square(1, act_cov)
             lefts = [left_first, left_second[:, :rest], left_second[:, rest:]]
             act_cov, grad_cov = tiles(
                 scale,

time: 69.5 us -> 67.6 us (0.973)
  waiting for transfers between devices: 25.7 us -> 22.1 us
  Pallas kernels: 22 us -> 22.9 us
    ppermute x2, waiting for transfers between devices: 6.8 us -> 0.01 us  [local(): upper = lax.ppermute(ahead_of[:, :middle], 'row', ahead)]
    add x0 -> x2, other arithmetic: none -> 1.98 us  [local(): pieces[2 * k] + lax.ppermute(pieces[2 * k + 1], 'col', swap)]
    ppermute x6, waiting for transfers between devices: 9.17 us -> 11 us  [local(): backward[k] = lax.ppermute(behind_of, 'row', behind)]
    ppermute x4, waiting for transfers between devices: 0.01 us -> 1.29 us  [left_part(): lax.ppermute(g, 'col', swap)]
    select_n x1 -> x0, other arithmetic: 1 us -> none  [local(): jnp.where(col == 0, keep, other)]
    pallas_call x2 -> x3, Pallas kernels: 20 us -> 20.9 us  [tiles(): pl.pallas_call(functools.partial(tiles_kernel, scale, groups, len(lefts),...]
    ppermute x1 -> x2, waiting for transfers between devices: 1.42 us -> 1.26 us  [local(): lax.ppermute(pieces[2 * k + 1], 'col', swap)]
  transfers between devices with their start and end apart: 21 -> 22, of which waited for: 14 -> 15; matrix products, arithmetic and copies ran while one was open for 1% -> 4% of each run, Pallas kernels for 9% -> 11%
where the time goes in v4:
time: 67.6 us; the launch traced here: 67.4 us
  Pallas kernels  22.9 us (34%)
  waiting for transfers between devices  22.1 us (33%)
  starting transfers between devices  18.2 us (27%)
  other arithmetic  2.27 us (3%)
  between operations  1.6 us (2%)
    pallas_call x3, Pallas kernels, tiles(): pl.pallas_call(functools.partial(tiles_kernel, scale, groups, len(lefts),...  20.9 us
    ppermute x6, starting transfers between devices, local(): forward[k] = lax.ppermute(ahead_of, 'row', ahead)  11.4 us
    ppermute x6, waiting for transfers between devices, local(): backward[k] = lax.ppermute(behind_of, 'row', behind)  11 us
    ppermute x6, waiting for transfers between devices, local(): forward[k] = lax.ppermute(ahead_of, 'row', ahead)  7.19 us
    ppermute x2, starting transfers between devices, local(): upper = lax.ppermute(ahead_of[:, :middle], 'row', ahead)  3.21 us
    pallas_call x1, Pallas kernels, local(): pl.pallas_call(functools.partial(split_kernel, cols, layouts), in_specs=[...  2.05 us
    add x2, other arithmetic, local(): pieces[2 * k] + lax.ppermute(pieces[2 * k + 1], 'col', swap)  1.98 us
    ppermute x6, starting transfers between devices, local(): backward[k] = lax.ppermute(behind_of, 'row', behind)  1.81 us
  transfers between devices with their start and end apart: 22, of which 15 were waited for; matrix products, arithmetic and copies ran while one was open for 4% of the time, Pallas kernels for 11%

profile of v4, /device:TPU:0, one launch (start us, length us, event | category | flops | bytes accessed | tf_op | source)
XLA Modules:
  0.0 67.4 jit_solution(13206208565780139490)
XLA Ops:
  1.3 2.1 %shard_map.50 = (bf16[24,4096]{1,0:T(8,128)(2,1)}, bf16[24,4096]{1,0:T(8,128)(2,1)}, bf16[24,5120]{1,0:T(8,128)(2,1)}, bf16[24,5120]{1,0:T(8,128)(2,1)}) custom-call(s32[1]{0:T(128)} %bitcast.half_ref, s32[1]{0:T(128)S(6)} %copy.19.count_ref, bf16[12,14336]{1,0:T(8,128)(2,1)} %act_ref.1, bf16[12,4096]{1,0:T(8,128)(2,1)} %grad_ref.1), custom_call_target="tpu_custom_call" | custom-call | tf_op jit(solution)/shard_map/pallas_call | solution.py:178
  3.3 0.5 collective-permute-start
  3.8 0.0 collective-permute-start.3
  3.8 1.3 %collective-permute-done = bf16[24,4096]{1,0:T(8,128)(2,1)S(1)} collective-permute-done((bf16[24,4096]{1,0:T(8,128)(2,1)}, bf16[24,4096]{1,0:T(8,128)(2,1)S(1)}, u32[]{:S(2)}, u32[]{:S(2)}) %collective-permute-start) | collective-permute-done | bytes 196640 | tf_op jit(solution)/shard_map/ppermute | solution.py:184
  5.1 1.0 %add.76.refs_1_.refs_3_ = bf16[24,4096]{1,0:T(8,128)(2,1)S(1)} add(bf16[24,4096]{1,0:T(8,128)(2,1)} %get-tuple-element.27, bf16[24,4096]{1,0:T(8,128)(2,1)S(1)} %collective-permute-done) | non-fusion elementwise | flops 98304 | bytes 589824 | tf_op jit(solution)/shard_map/add | solution.py:184
  6.1 3.0 %collective-permute-start.1 = (bf16[24,4096]{1,0:T(8,128)(2,1)S(1)}, bf16[24,4096]{1,0:T(8,128)(2,1)S(1)}, u32[]{:S(2)}, u32[]{:S(2)}) collective-permute-start(bf16[24,4096]{1,0:T(8,128)(2,1)S(1)} %add.76.refs_1_.refs_3_), channel_id=1, source_target_pairs={{0,4},{4,8},{8,12},{12,14},{14,10},{10,6},{6,2},{2,0},{1,5},{5,9},... | collective-permute-start | bytes 589832 | tf_op jit(solution)/shard_map/ppermute | solution.py:196
  9.0 0.0 collective-permute-start.2
  9.0 0.0 collective-permute-done.3
  9.1 1.0 %add.79.refs_11_ = bf16[24,5120]{1,0:T(8,128)(2,1)S(1)} add(bf16[24,5120]{1,0:T(8,128)(2,1)} %get-tuple-element.31, bf16[24,5120]{1,0:T(8,128)(2,1)S(1)} %collective-permute-done.3) | non-fusion elementwise | flops 122880 | bytes 737280 | tf_op jit(solution)/shard_map/add | solution.py:184
  10.1 2.1 %collective-permute-start.7 = (bf16[24,5120]{1,0:T(8,128)(2,1)S(1)}, bf16[24,5120]{1,0:T(8,128)(2,1)S(1)}, u32[]{:S(2)}, u32[]{:S(2)}) collective-permute-start(bf16[24,5120]{1,0:T(8,128)(2,1)S(1)} %add.79.refs_11_), channel_id=1, source_target_pairs={{0,4},{4,8},{8,12},{12,14},{14,10},{10,6},{6,2},{2,0},{1,5},{5,9},... | collective-permute-start | bytes 737288 | tf_op jit(solution)/shard_map/ppermute | solution.py:196
  12.2 0.0 collective-permute-start.8
  12.2 2.5 %collective-permute-done.1.refs_2_.refs_4_ = bf16[24,4096]{1,0:T(8,128)(2,1)S(1)} collective-permute-done((bf16[24,4096]{1,0:T(8,128)(2,1)S(1)}, bf16[24,4096]{1,0:T(8,128)(2,1)S(1)}, u32[]{:S(2)}, u32[]{:S(2)}) %collective-permute-start.1) | collective-permute-done | bytes 196640 | tf_op jit(solution)/shard_map/ppermute | solution.py:196
  14.6 2.2 %collective-permute-done.2.refs_3_.refs_5_ = bf16[24,4096]{1,0:T(8,128)(2,1)S(1)} collective-permute-done((bf16[24,4096]{1,0:T(8,128)(2,1)S(1)}, bf16[24,4096]{1,0:T(8,128)(2,1)S(1)}, u32[]{:S(2)}, u32[]{:S(2)}) %collective-permute-start.2) | collective-permute-done | bytes 196640 | tf_op jit(solution)/shard_map/ppermute | solution.py:197
  16.8 1.6 %collective-permute-start.4 = (bf16[24,4096]{1,0:T(8,128)(2,1)S(1)}, bf16[24,4096]{1,0:T(8,128)(2,1)S(1)}, u32[]{:S(2)}, u32[]{:S(2)}) collective-permute-start(bf16[24,4096]{1,0:T(8,128)(2,1)S(1)} %collective-permute-done.1.refs_2_.refs_4_), channel_id=1, source_target_pairs={{0,4},{4,8},{8,12},{12,14},{14,10},{10,6},{6,2},{2,0},{1,5},{5,9},... | collective-permute-start | bytes 589832 | tf_op jit(solution)/shard_map/ppermute | solution.py:196
  18.4 0.4 collective-permute-start.5
  18.9 1.0 %collective-permute-done.7.refs_12_ = bf16[24,5120]{1,0:T(8,128)(2,1)S(1)} collective-permute-done((bf16[24,5120]{1,0:T(8,128)(2,1)S(1)}, bf16[24,5120]{1,0:T(8,128)(2,1)S(1)}, u32[]{:S(2)}, u32[]{:S(2)}) %collective-permute-start.7) | collective-permute-done | bytes 245792 | tf_op jit(solution)/shard_map/ppermute | solution.py:196
  19.9 2.2 %collective-permute-done.8.refs_13_ = bf16[24,5120]{1,0:T(8,128)(2,1)S(1)} collective-permute-done((bf16[24,5120]{1,0:T(8,128)(2,1)S(1)}, bf16[24,5120]{1,0:T(8,128)(2,1)S(1)}, u32[]{:S(2)}, u32[]{:S(2)}) %collective-permute-start.8) | collective-permute-done | bytes 245792 | tf_op jit(solution)/shard_map/ppermute | solution.py:197
  22.1 1.6 %collective-permute-start.11 = (bf16[24,5120]{1,0:T(8,128)(2,1)S(1)}, bf16[24,5120]{1,0:T(8,128)(2,1)S(1)}, u32[]{:S(2)}, u32[]{:S(2)}) collective-permute-start(bf16[24,5120]{1,0:T(8,128)(2,1)S(1)} %collective-permute-done.7.refs_12_), channel_id=1, source_target_pairs={{0,4},{4,8},{8,12},{12,14},{14,10},{10,6},{6,2},{2,0},{1,5},{5,9},... | collective-permute-start | bytes 737288 | tf_op jit(solution)/shard_map/ppermute | solution.py:196
  23.7 0.4 collective-permute-start.12
  24.2 0.5 collective-permute-done.4.refs_4_.refs_6_
  24.7 1.6 %collective-permute-done.5.refs_5_.refs_7_ = bf16[24,4096]{1,0:T(8,128)(2,1)S(1)} collective-permute-done((bf16[24,4096]{1,0:T(8,128)(2,1)S(1)}, bf16[24,4096]{1,0:T(8,128)(2,1)S(1)}, u32[]{:S(2)}, u32[]{:S(2)}) %collective-permute-start.5) | collective-permute-done | bytes 196640 | tf_op jit(solution)/shard_map/ppermute | solution.py:197
  26.3 0.0 collective-permute-start.6
  26.3 1.6 %collective-permute-start.9 = (bf16[24,4096]{1,0:T(8,128)(2,1)S(1)}, bf16[24,4096]{1,0:T(8,128)(2,1)S(1)}, u32[]{:S(2)}, u32[]{:S(2)}) collective-permute-start(bf16[24,4096]{1,0:T(8,128)(2,1)S(1)} %collective-permute-done.4.refs_4_.refs_6_), channel_id=1, source_target_pairs={{0,4},{4,8},{8,12},{12,14},{14,10},{10,6},{6,2},{2,0},{1,5},{5,9},... | collective-permute-start | bytes 589832 | tf_op jit(solution)/shard_map/ppermute | solution.py:196
  27.9 0.4 collective-permute-start.10
  28.4 0.5 collective-permute-done.11.refs_14_
  28.9 1.5 %collective-permute-done.12.refs_15_ = bf16[24,5120]{1,0:T(8,128)(2,1)S(1)} collective-permute-done((bf16[24,5120]{1,0:T(8,128)(2,1)S(1)}, bf16[24,5120]{1,0:T(8,128)(2,1)S(1)}, u32[]{:S(2)}, u32[]{:S(2)}) %collective-permute-start.12) | collective-permute-done | bytes 245792 | tf_op jit(solution)/shard_map/ppermute | solution.py:197
  30.4 1.6 %collective-permute-start.15 = (bf16[24,5120]{1,0:T(8,128)(2,1)S(1)}, bf16[24,5120]{1,0:T(8,128)(2,1)S(1)}, u32[]{:S(2)}, u32[]{:S(2)}) collective-permute-start(bf16[24,5120]{1,0:T(8,128)(2,1)S(1)} %collective-permute-done.11.refs_14_), channel_id=1, source_target_pairs={{0,4},{4,8},{8,12},{12,14},{14,10},{10,6},{6,2},{2,0},{1,5},{5,9},... | collective-permute-start | bytes 737288 | tf_op jit(solution)/shard_map/ppermute | solution.py:196
  32.0 0.4 collective-permute-start.16
  32.5 1.5 %collective-permute-done.9.refs_6_.refs_8_ = bf16[24,4096]{1,0:T(8,128)(2,1)S(1)} collective-permute-done((bf16[24,4096]{1,0:T(8,128)(2,1)S(1)}, bf16[24,4096]{1,0:T(8,128)(2,1)S(1)}, u32[]{:S(2)}, u32[]{:S(2)}) %collective-permute-start.9) | collective-permute-done | bytes 196640 | tf_op jit(solution)/shard_map/ppermute | solution.py:196
  34.1 0.0 collective-permute-start.18
  34.1 1.6 %collective-permute-done.10.refs_7_.refs_9_ = bf16[24,4096]{1,0:T(8,128)(2,1)S(1)} collective-permute-done((bf16[24,4096]{1,0:T(8,128)(2,1)S(1)}, bf16[24,4096]{1,0:T(8,128)(2,1)S(1)}, u32[]{:S(2)}, u32[]{:S(2)}) %collective-permute-start.10) | collective-permute-done | bytes 196640 | tf_op jit(solution)/shard_map/ppermute | solution.py:197
  35.7 0.5 collective-permute-start.14
  36.2 0.0 collective-permute-done.6
  36.2 1.6 %collective-permute-start.13 = (bf16[24,2048]{1,0:T(8,128)(2,1)S(1)}, bf16[24,2048]{1,0:T(8,128)(2,1)S(1)}, u32[]{:S(2)}, u32[]{:S(2)}) collective-permute-start(bf16[24,2048]{1,0:T(8,128)(2,1)S(1)} %slice.18), channel_id=1, source_target_pairs={{0,4},{4,8},{8,12},{12,14},{14,10},{10,6},{6,2},{2,0},{1,5},{5,9},... | collective-permute-start | bytes 294920 | tf_op jit(solution)/shard_map/ppermute | solution.py:201
  37.9 1.2 %collective-permute-done.15.refs_16_ = bf16[24,5120]{1,0:T(8,128)(2,1)S(1)} collective-permute-done((bf16[24,5120]{1,0:T(8,128)(2,1)S(1)}, bf16[24,5120]{1,0:T(8,128)(2,1)S(1)}, u32[]{:S(2)}, u32[]{:S(2)}) %collective-permute-start.15) | collective-permute-done | bytes 245792 | tf_op jit(solution)/shard_map/ppermute | solution.py:196
  39.1 1.9 %collective-permute-done.16.refs_17_ = bf16[24,5120]{1,0:T(8,128)(2,1)S(1)} collective-permute-done((bf16[24,5120]{1,0:T(8,128)(2,1)S(1)}, bf16[24,5120]{1,0:T(8,128)(2,1)S(1)}, u32[]{:S(2)}, u32[]{:S(2)}) %collective-permute-start.16) | collective-permute-done | bytes 245792 | tf_op jit(solution)/shard_map/ppermute | solution.py:197
  41.0 1.3 %collective-permute-done.14 = bf16[24,2048]{1,0:T(8,128)(2,1)S(1)} collective-permute-done((bf16[24,2048]{1,0:T(8,128)(2,1)S(1)}, bf16[24,2048]{1,0:T(8,128)(2,1)S(1)}, u32[]{:S(2)}, u32[]{:S(2)}) %collective-permute-start.14) | collective-permute-done | bytes 98336 | tf_op jit(solution)/shard_map/ppermute | solution.py:202
  42.3 0.0 collective-permute-done.13
  42.4 0.5 collective-permute-start.20
  42.9 1.6 %collective-permute-start.19 = (bf16[24,2560]{1,0:T(8,128)(2,1)S(1)}, bf16[24,2560]{1,0:T(8,128)(2,1)S(1)}, u32[]{:S(2)}, u32[]{:S(2)}) collective-permute-start(bf16[24,2560]{1,0:T(8,128)(2,1)S(1)} %slice.20), channel_id=1, source_target_pairs={{0,4},{4,8},{8,12},{12,14},{14,10},{10,6},{6,2},{2,0},{1,5},{5,9},... | collective-permute-start | bytes 368648 | tf_op jit(solution)/shard_map/ppermute | solution.py:201
  44.5 0.1 collective-permute-start.17
  44.6 1.3 %collective-permute-done.17 = bf16[72,1024]{1,0:T(8,128)(2,1)S(1)} collective-permute-done((bf16[72,1024]{1,0:T(8,128)(2,1)S(1)}, bf16[72,1024]{1,0:T(8,128)(2,1)S(1)}, u32[]{:S(2)}, u32[]{:S(2)}) %collective-permute-start.17) | collective-permute-done | bytes 147488 | tf_op jit(solution)/shard_map/ppermute | solution.py:215
  46.0 3.8 %shard_map.51.refs_9_ = f32[1792,7168]{1,0:T(8,128)} custom-call(bf16[192,1024]{1,0:T(8,128)(2,1)S(1)} %pad_maximum_fusion.refs_0_, bf16[24,4096]{1,0:T(8,128)(2,1)S(1)} %add.76.refs_1_.refs_3_, bf16[24,4096]{1,0:T(8,128)(2,1)S(1)} %collective-permute-done.1.refs_2_.refs_4_, bf16[24,4096]{1,0:T(8,128)(2,1)S(1)} %collective-permute-done.2.refs_3_.refs_5_, ...), custom_call_target="tpu_custom_call" | custom-call | flops 805306368 | bytes 8388608 | tf_op jit(solution)/shard_map/pallas_call | solution.py:111
  49.8 0.0 collective-permute-done.20
  49.8 0.0 collective-permute-done.19
  49.9 0.2 collective-permute-start.21
  50.1 0.0 collective-permute-done.18
  50.2 3.8 %shard_map.52.refs_19_ = f32[1792,7168]{1,0:T(8,128)} custom-call(bf16[192,1024]{1,0:T(8,128)(2,1)S(1)} %pad_maximum_fusion.refs_0_, bf16[24,4096]{1,0:T(8,128)(2,1)S(1)} %add.76.refs_1_.refs_3_, bf16[24,4096]{1,0:T(8,128)(2,1)S(1)} %collective-permute-done.1.refs_2_.refs_4_, ...), custom_call_target="tpu_custom_call", output_to_operand_aliasing={{}: (9, {})} | custom-call | flops 805306368 | bytes 8388608 | tf_op jit(solution)/shard_map/pallas_call | solution.py:111
  54.0 0.0 collective-permute-done.21
  54.0 0.1 broadcast_select_fusion.2
  54.1 13.2 %shard_map.53 = (f32[1792,7168]{1,0:T(8,128)}, f32[512,2048]{1,0:T(8,128)}) custom-call(bf16[192,1024]{1,0:T(8,128)(2,1)S(1)} %pad_maximum_fusion.refs_0_, bf16[192,768]{1,0:T(8,128)(2,1)S(1)} %fusion.refs_1_, bf16[192,512]{1,0:T(8,128)(2,1)S(1)} %pad_maximum_fusion.1.refs_2_, ...), custom_call_target="tpu_custom_call", output_to_operand_aliasing={{0}: (19, {})} | custom-call | flops 3724541952 | bytes 38797312 | tf_op jit(solution)/shard_map/pallas_call | solution.py:111
  (45 shorter events, 0.5 us)
Async XLA Ops:
  3.3 1.8 %collective-permute-start = (bf16[24,4096]{1,0:T(8,128)(2,1)}, bf16[24,4096]{1,0:T(8,128)(2,1)S(1)}, u32[]{:S(2)}, u32[]{:S(2)}) collective-permute-start(bf16[24,4096]{1,0:T(8,128)(2,1)} %get-tuple-element.28), channel_id=1, source_target_pairs={{0,1},{1,0},{2,3},{3,2},{4,5},{5,4},{6,7},{7,6},{8,9},{9,8},{10,11... | collective-permute-start | bytes 589832 | tf_op jit(solution)/shard_map/ppermute | solution.py:184
  3.8 5.2 %collective-permute-start.3 = (bf16[24,5120]{1,0:T(8,128)(2,1)}, bf16[24,5120]{1,0:T(8,128)(2,1)S(1)}, u32[]{:S(2)}, u32[]{:S(2)}) collective-permute-start(bf16[24,5120]{1,0:T(8,128)(2,1)} %get-tuple-element.32), channel_id=1, source_target_pairs={{0,1},{1,0},{2,3},{3,2},{4,5},{5,4},{6,7},{7,6},{8,9},{9,8},{10,11... | collective-permute-start | bytes 737288 | tf_op jit(solution)/shard_map/ppermute | solution.py:184
  6.1 8.6 %collective-permute-start.1 = (bf16[24,4096]{1,0:T(8,128)(2,1)S(1)}, bf16[24,4096]{1,0:T(8,128)(2,1)S(1)}, u32[]{:S(2)}, u32[]{:S(2)}) collective-permute-start(bf16[24,4096]{1,0:T(8,128)(2,1)S(1)} %add.76.refs_1_.refs_3_), channel_id=1, source_target_pairs={{0,4},{4,8},{8,12},{12,14},{14,10},{10,6},{6,2},{2,0},{1,5},{5,9},... | collective-permute-start | bytes 589832 | tf_op jit(solution)/shard_map/ppermute | solution.py:196
  9.0 7.8 %collective-permute-start.2 = (bf16[24,4096]{1,0:T(8,128)(2,1)S(1)}, bf16[24,4096]{1,0:T(8,128)(2,1)S(1)}, u32[]{:S(2)}, u32[]{:S(2)}) collective-permute-start(bf16[24,4096]{1,0:T(8,128)(2,1)S(1)} %add.76.refs_1_.refs_3_), channel_id=1, source_target_pairs={{4,0},{8,4},{12,8},{14,12},{10,14},{6,10},{2,6},{0,2},{5,1},{9,5},... | collective-permute-start | bytes 589832 | tf_op jit(solution)/shard_map/ppermute | solution.py:197
  10.1 9.8 %collective-permute-start.7 = (bf16[24,5120]{1,0:T(8,128)(2,1)S(1)}, bf16[24,5120]{1,0:T(8,128)(2,1)S(1)}, u32[]{:S(2)}, u32[]{:S(2)}) collective-permute-start(bf16[24,5120]{1,0:T(8,128)(2,1)S(1)} %add.79.refs_11_), channel_id=1, source_target_pairs={{0,4},{4,8},{8,12},{12,14},{14,10},{10,6},{6,2},{2,0},{1,5},{5,9},... | collective-permute-start | bytes 737288 | tf_op jit(solution)/shard_map/ppermute | solution.py:196
  12.2 9.9 %collective-permute-start.8 = (bf16[24,5120]{1,0:T(8,128)(2,1)S(1)}, bf16[24,5120]{1,0:T(8,128)(2,1)S(1)}, u32[]{:S(2)}, u32[]{:S(2)}) collective-permute-start(bf16[24,5120]{1,0:T(8,128)(2,1)S(1)} %add.79.refs_11_), channel_id=1, source_target_pairs={{4,0},{8,4},{12,8},{14,12},{10,14},{6,10},{2,6},{0,2},{5,1},{9,5},... | collective-permute-start | bytes 737288 | tf_op jit(solution)/shard_map/ppermute | solution.py:197
  16.8 7.8 %collective-permute-start.4 = (bf16[24,4096]{1,0:T(8,128)(2,1)S(1)}, bf16[24,4096]{1,0:T(8,128)(2,1)S(1)}, u32[]{:S(2)}, u32[]{:S(2)}) collective-permute-start(bf16[24,4096]{1,0:T(8,128)(2,1)S(1)} %collective-permute-done.1.refs_2_.refs_4_), channel_id=1, source_target_pairs={{0,4},{4,8},{8,12},{12,14},{14,10},{10,6},{6,2},{2,0},{1,5},{5,9},... | collective-permute-start | bytes 589832 | tf_op jit(solution)/shard_map/ppermute | solution.py:196
  18.4 7.9 %collective-permute-start.5 = (bf16[24,4096]{1,0:T(8,128)(2,1)S(1)}, bf16[24,4096]{1,0:T(8,128)(2,1)S(1)}, u32[]{:S(2)}, u32[]{:S(2)}) collective-permute-start(bf16[24,4096]{1,0:T(8,128)(2,1)S(1)} %collective-permute-done.2.refs_3_.refs_5_), channel_id=1, source_target_pairs={{4,0},{8,4},{12,8},{14,12},{10,14},{6,10},{2,6},{0,2},{5,1},{9,5},... | collective-permute-start | bytes 589832 | tf_op jit(solution)/shard_map/ppermute | solution.py:197
  22.1 6.8 %collective-permute-start.11 = (bf16[24,5120]{1,0:T(8,128)(2,1)S(1)}, bf16[24,5120]{1,0:T(8,128)(2,1)S(1)}, u32[]{:S(2)}, u32[]{:S(2)}) collective-permute-start(bf16[24,5120]{1,0:T(8,128)(2,1)S(1)} %collective-permute-done.7.refs_12_), channel_id=1, source_target_pairs={{0,4},{4,8},{8,12},{12,14},{14,10},{10,6},{6,2},{2,0},{1,5},{5,9},... | collective-permute-start | bytes 737288 | tf_op jit(solution)/shard_map/ppermute | solution.py:196
  23.7 6.8 %collective-permute-start.12 = (bf16[24,5120]{1,0:T(8,128)(2,1)S(1)}, bf16[24,5120]{1,0:T(8,128)(2,1)S(1)}, u32[]{:S(2)}, u32[]{:S(2)}) collective-permute-start(bf16[24,5120]{1,0:T(8,128)(2,1)S(1)} %collective-permute-done.8.refs_13_), channel_id=1, source_target_pairs={{4,0},{8,4},{12,8},{14,12},{10,14},{6,10},{2,6},{0,2},{5,1},{9,5},... | collective-permute-start | bytes 737288 | tf_op jit(solution)/shard_map/ppermute | solution.py:197
  26.3 9.9 %collective-permute-start.6 = (bf16[120,1024]{1,0:T(8,128)(2,1)S(1)}, bf16[120,1024]{1,0:T(8,128)(2,1)S(1)}, u32[]{:S(2)}, u32[]{:S(2)}) collective-permute-start(bf16[120,1024]{1,0:T(8,128)(2,1)S(1)} %dynamic-slice_dynamic-update-slice_fusion), channel_id=1, source_target_pairs={{0,1},{1,0},{2,3},{3,2},{4,5},{5,4},{6,7},{7,6},{8,9},{9,8},{10,11... | collective-permute-start | bytes 737288 | tf_op jit(solution)/shard_map/ppermute | solution.py:215
  26.3 7.8 %collective-permute-start.9 = (bf16[24,4096]{1,0:T(8,128)(2,1)S(1)}, bf16[24,4096]{1,0:T(8,128)(2,1)S(1)}, u32[]{:S(2)}, u32[]{:S(2)}) collective-permute-start(bf16[24,4096]{1,0:T(8,128)(2,1)S(1)} %collective-permute-done.4.refs_4_.refs_6_), channel_id=1, source_target_pairs={{0,4},{4,8},{8,12},{12,14},{14,10},{10,6},{6,2},{2,0},{1,5},{5,9},... | collective-permute-start | bytes 589832 | tf_op jit(solution)/shard_map/ppermute | solution.py:196
  27.9 7.7 %collective-permute-start.10 = (bf16[24,4096]{1,0:T(8,128)(2,1)S(1)}, bf16[24,4096]{1,0:T(8,128)(2,1)S(1)}, u32[]{:S(2)}, u32[]{:S(2)}) collective-permute-start(bf16[24,4096]{1,0:T(8,128)(2,1)S(1)} %collective-permute-done.5.refs_5_.refs_7_), channel_id=1, source_target_pairs={{4,0},{8,4},{12,8},{14,12},{10,14},{6,10},{2,6},{0,2},{5,1},{9,5},... | collective-permute-start | bytes 589832 | tf_op jit(solution)/shard_map/ppermute | solution.py:197
  30.4 8.6 %collective-permute-start.15 = (bf16[24,5120]{1,0:T(8,128)(2,1)S(1)}, bf16[24,5120]{1,0:T(8,128)(2,1)S(1)}, u32[]{:S(2)}, u32[]{:S(2)}) collective-permute-start(bf16[24,5120]{1,0:T(8,128)(2,1)S(1)} %collective-permute-done.11.refs_14_), channel_id=1, source_target_pairs={{0,4},{4,8},{8,12},{12,14},{14,10},{10,6},{6,2},{2,0},{1,5},{5,9},... | collective-permute-start | bytes 737288 | tf_op jit(solution)/shard_map/ppermute | solution.py:196
  32.0 8.9 %collective-permute-start.16 = (bf16[24,5120]{1,0:T(8,128)(2,1)S(1)}, bf16[24,5120]{1,0:T(8,128)(2,1)S(1)}, u32[]{:S(2)}, u32[]{:S(2)}) collective-permute-start(bf16[24,5120]{1,0:T(8,128)(2,1)S(1)} %collective-permute-done.12.refs_15_), channel_id=1, source_target_pairs={{4,0},{8,4},{12,8},{14,12},{10,14},{6,10},{2,6},{0,2},{5,1},{9,5},... | collective-permute-start | bytes 737288 | tf_op jit(solution)/shard_map/ppermute | solution.py:197
  34.1 16.1 %collective-permute-start.18 = (bf16[120,1280]{1,0:T(8,128)(2,1)S(1)}, bf16[120,1280]{1,0:T(8,128)(2,1)S(1)}, u32[]{:S(2)}, u32[]{:S(2)}) collective-permute-start(bf16[120,1280]{1,0:T(8,128)(2,1)S(1)} %maximum_dynamic-update-slice_fusion), channel_id=1, source_target_pairs={{0,1},{1,0},{2,3},{3,2},{4,5},{5,4},{6,7},{7,6},{8,9},{9,8},{10,11... | collective-permute-start | bytes 921608 | tf_op jit(solution)/shard_map/ppermute | solution.py:215
  35.7 6.6 %collective-permute-start.14 = (bf16[24,2048]{1,0:T(8,128)(2,1)S(1)}, bf16[24,2048]{1,0:T(8,128)(2,1)S(1)}, u32[]{:S(2)}, u32[]{:S(2)}) collective-permute-start(bf16[24,2048]{1,0:T(8,128)(2,1)S(1)} %slice.19), channel_id=1, source_target_pairs={{4,0},{8,4},{12,8},{14,12},{10,14},{6,10},{2,6},{0,2},{5,1},{9,5},... | collective-permute-start | bytes 294920 | tf_op jit(solution)/shard_map/ppermute | solution.py:202
  36.2 6.1 %collective-permute-start.13 = (bf16[24,2048]{1,0:T(8,128)(2,1)S(1)}, bf16[24,2048]{1,0:T(8,128)(2,1)S(1)}, u32[]{:S(2)}, u32[]{:S(2)}) collective-permute-start(bf16[24,2048]{1,0:T(8,128)(2,1)S(1)} %slice.18), channel_id=1, source_target_pairs={{0,4},{4,8},{8,12},{12,14},{14,10},{10,6},{6,2},{2,0},{1,5},{5,9},... | collective-permute-start | bytes 294920 | tf_op jit(solution)/shard_map/ppermute | solution.py:201
  42.4 7.4 %collective-permute-start.20 = (bf16[24,2560]{1,0:T(8,128)(2,1)S(1)}, bf16[24,2560]{1,0:T(8,128)(2,1)S(1)}, u32[]{:S(2)}, u32[]{:S(2)}) collective-permute-start(bf16[24,2560]{1,0:T(8,128)(2,1)S(1)} %slice.21), channel_id=1, source_target_pairs={{4,0},{8,4},{12,8},{14,12},{10,14},{6,10},{2,6},{0,2},{5,1},{9,5},... | collective-permute-start | bytes 368648 | tf_op jit(solution)/shard_map/ppermute | solution.py:202
  42.9 6.9 %collective-permute-start.19 = (bf16[24,2560]{1,0:T(8,128)(2,1)S(1)}, bf16[24,2560]{1,0:T(8,128)(2,1)S(1)}, u32[]{:S(2)}, u32[]{:S(2)}) collective-permute-start(bf16[24,2560]{1,0:T(8,128)(2,1)S(1)} %slice.20), channel_id=1, source_target_pairs={{0,4},{4,8},{8,12},{12,14},{14,10},{10,6},{6,2},{2,0},{1,5},{5,9},... | collective-permute-start | bytes 368648 | tf_op jit(solution)/shard_map/ppermute | solution.py:201
  44.5 1.4 %collective-permute-start.17 = (bf16[72,1024]{1,0:T(8,128)(2,1)S(1)}, bf16[72,1024]{1,0:T(8,128)(2,1)S(1)}, u32[]{:S(2)}, u32[]{:S(2)}) collective-permute-start(bf16[72,1024]{1,0:T(8,128)(2,1)S(1)} %pad_maximum_fusion.2), channel_id=1, source_target_pairs={{0,1},{1,0},{2,3},{3,2},{4,5},{5,4},{6,7},{7,6},{8,9},{9,8},{10,11... | collective-permute-start | bytes 442376 | tf_op jit(solution)/shard_map/ppermute | solution.py:215
  49.9 4.1 %collective-permute-start.21 = (bf16[72,1280]{1,0:T(8,128)(2,1)S(1)}, bf16[72,1280]{1,0:T(8,128)(2,1)S(1)}, u32[]{:S(2)}, u32[]{:S(2)}) collective-permute-start(bf16[72,1280]{1,0:T(8,128)(2,1)S(1)} %maximum_maximum_fusion), channel_id=1, source_target_pairs={{0,1},{1,0},{2,3},{3,2},{4,5},{5,4},{6,7},{7,6},{8,9},{9,8},{10,11... | collective-permute-start | bytes 552968 | tf_op jit(solution)/shard_map/ppermute | solution.py:215

commit v5 on v4

--- a/solution.py
+++ b/solution.py
@@ -179,7 +179,7 @@
             functools.partial(split_kernel, cols, layouts),
             in_specs=[pl.BlockSpec(memory_space=pltpu.SMEM)] * 2 + [pl.BlockSpec(memory_space=pltpu.VMEM)] * 2,
             out_specs=[pl.BlockSpec(memory_space=pltpu.VMEM)] * 4,
-            out_shape=[jax.ShapeDtypeStruct((2 * slots, width), jnp.bfloat16) for width in widths for _ in (0, 1)],
+            out_shape=[pltpu.VMEM((2 * slots, width), jnp.bfloat16) for width in widths for _ in (0, 1)],
         )(col[None], row_counts, activations, pseudo_grads)
         chains = [[pieces[2 * k] + lax.ppermute(pieces[2 * k + 1], "col", swap)] for k in (0, 1)]
         forward = [chain[0] for chain in chains]
@@ -188,19 +188,21 @@
         sequence = [0, 1] * halfway
         previous, last = (), []
         for k in sequence:
-            chain, latest = chains[k], (forward[k], backward[k])
-            (ahead_of, behind_of), _ = lax.optimization_barrier((latest, previous))
-            previous = latest
+            chain, middle = chains[k], widths[k] // 2
             steps[k] += 1
-            if steps[k] < halfway:
-                forward[k] = lax.ppermute(ahead_of, "row", ahead)
-                backward[k] = lax.ppermute(behind_of, "row", behind)
+            final = steps[k] == halfway
+            ahead_of, _ = lax.optimization_barrier((forward[k], previous))
+            behind_of, _ = lax.optimization_barrier((backward[k], previous))
+            previous = forward[k]
+            if final:
+                ahead_of, behind_of = ahead_of[:, :middle], behind_of[:, middle:]
+            forward[k] = lax.ppermute(ahead_of, "row", ahead)
+            backward[k] = lax.ppermute(behind_of, "row", behind)
+            if final:
+                last.append((forward[k], backward[k]))
+            else:
                 chain += [forward[k], backward[k]]
-            else:
-                middle = widths[k] // 2
-                upper = lax.ppermute(ahead_of[:, :middle], "row", ahead)
-                lower = lax.ppermute(behind_of[:, middle:], "row", behind)
-                last.append((upper, lower))
+                latest = (forward[k], backward[k])
 
         def left_part(chain, pieces):
             own = []
@@ -215,7 +217,7 @@
             return jnp.concatenate([jnp.where(mine, g, lax.ppermute(g, "col", swap)) for g in groups], axis=0)
 
         act_shape, grad_shape = (act_block, act_half), (grad_block, grad_half)
-        last_first, _ = lax.optimization_barrier((last[0], (forward[1], backward[1])))
+        last_first, _ = lax.optimization_barrier((last[0], latest))
         chains[0].append(jnp.concatenate(last_first, axis=1))
         left_first = left_part(chains[0], [(0, cut)])
         if rest == 0:

time: 67.6 us -> 64.1 us (0.948)
  other arithmetic: 2.27 us -> 0.39 us
  waiting for transfers between devices: 22.1 us -> 20.6 us
  starting transfers between devices: 18.2 us -> 19.1 us
  Pallas kernels: 22.9 us -> 22 us
    ppermute x6 -> x8, starting transfers between devices: 1.81 us -> 15.3 us  [local(): backward[k] = lax.ppermute(behind_of, 'row', behind)]
    ppermute x6 -> x8, starting transfers between devices: 11.4 us -> 2.79 us  [local(): forward[k] = lax.ppermute(ahead_of, 'row', ahead)]
    ppermute x4 -> x0, starting transfers between devices: 4.21 us -> none  [the longest x2 3.21 us: local(): upper = lax.ppermute(ahead_of[:, :middle], 'row', ahead)]
    add x2, other arithmetic: 1.98 us -> 0.11 us  [local(): pieces[2 * k] + lax.ppermute(pieces[2 * k + 1], 'col', swap)]
    ppermute x4 -> x0, waiting for transfers between devices: 1.35 us -> none  [the longest x2 1.35 us: local(): lower = lax.ppermute(behind_of[:, middle:], 'row', behind)]
    pallas_call x1, Pallas kernels: 2.05 us -> 1.15 us  [local(): pl.pallas_call(functools.partial(split_kernel, cols, layouts), in_specs=[...]
    ppermute x6 -> x8, waiting for transfers between devices: 7.19 us -> 8.06 us  [local(): forward[k] = lax.ppermute(ahead_of, 'row', ahead)]
    ppermute x6 -> x8, waiting for transfers between devices: 11 us -> 10.3 us  [local(): backward[k] = lax.ppermute(behind_of, 'row', behind)]
  transfers between devices with their start and end apart: 22 -> 22, of which waited for: 15 -> 12; matrix products, arithmetic and copies ran while one was open for 4% -> 1% of each run, Pallas kernels for 11% -> 12%
where the time goes in v5:
time: 64.1 us; the launch traced here: 63.9 us
  Pallas kernels  22 us (34%)
  waiting for transfers between devices  20.6 us (32%)
  starting transfers between devices  19.1 us (30%)
  between operations  1.6 us (2%)
    pallas_call x3, Pallas kernels, tiles(): pl.pallas_call(functools.partial(tiles_kernel, scale, groups, len(lefts),...  20.9 us
    ppermute x8, starting transfers between devices, local(): backward[k] = lax.ppermute(behind_of, 'row', behind)  15.3 us
    ppermute x8, waiting for transfers between devices, local(): backward[k] = lax.ppermute(behind_of, 'row', behind)  10.3 us
    ppermute x8, waiting for transfers between devices, local(): forward[k] = lax.ppermute(ahead_of, 'row', ahead)  8.06 us
    ppermute x8, starting transfers between devices, local(): forward[k] = lax.ppermute(ahead_of, 'row', ahead)  2.79 us
    ppermute x4, waiting for transfers between devices, left_part(): lax.ppermute(g, 'col', swap)  1.29 us
  transfers between devices with their start and end apart: 22, of which 12 were waited for; matrix products, arithmetic and copies ran while one was open for 1% of the time, Pallas kernels for 12%

profile of v5, /device:TPU:0, one launch (start us, length us, event | category | flops | bytes accessed | tf_op | source)
XLA Modules:
  0.0 63.9 jit_solution(16069133362428073379)
XLA Ops:
  1.3 1.1 %shard_map.50 = (bf16[24,4096]{1,0:T(8,128)(2,1)S(1)}, bf16[24,4096]{1,0:T(8,128)(2,1)S(1)}, bf16[24,5120]{1,0:T(8,128)(2,1)S(1)}, bf16[24,5120]{1,0:T(8,128)(2,1)S(1)}) custom-call(s32[1]{0:T(128)} %bitcast.half_ref, s32[1]{0:T(128)S(6)} %copy.19.count_ref, bf16[12,14336]{1,0:T(8,128)(2,1)} %act_ref.1, bf16[12,4096]{1,0:T(8,128)(2,1)} %grad_ref.1), custom_call_target="tpu_custom_call" | custom-call | tf_op jit(solution)/shard_map/pallas_call | solution.py:178
  2.4 0.6 collective-permute-start
  3.0 0.1 collective-permute-start.3
  3.1 1.0 %collective-permute-done = bf16[24,4096]{1,0:T(8,128)(2,1)S(1)} collective-permute-done((bf16[24,4096]{1,0:T(8,128)(2,1)S(1)}, bf16[24,4096]{1,0:T(8,128)(2,1)S(1)}, u32[]{:S(2)}, u32[]{:S(2)}) %collective-permute-start) | collective-permute-done | bytes 196640 | tf_op jit(solution)/shard_map/ppermute | solution.py:184
  4.1 2.9 %collective-permute-start.2 = (bf16[24,4096]{1,0:T(8,128)(2,1)S(1)}, bf16[24,4096]{1,0:T(8,128)(2,1)S(1)}, u32[]{:S(2)}, u32[]{:S(2)}) collective-permute-start(bf16[24,4096]{1,0:T(8,128)(2,1)S(1)} %add.76.refs_1_.refs_3_), channel_id=1, source_target_pairs={{4,0},{8,4},{12,8},{14,12},{10,14},{6,10},{2,6},{0,2},{5,1},{9,5},... | collective-permute-start | bytes 589832 | tf_op jit(solution)/shard_map/ppermute | solution.py:200
  7.0 0.2 collective-permute-start.1
  7.1 0.0 collective-permute-done.3
  7.1 0.1 add.79.refs_11_
  7.2 1.9 %collective-permute-start.14 = (bf16[24,5120]{1,0:T(8,128)(2,1)S(1)}, bf16[24,5120]{1,0:T(8,128)(2,1)S(1)}, u32[]{:S(2)}, u32[]{:S(2)}) collective-permute-start(bf16[24,5120]{1,0:T(8,128)(2,1)S(1)} %add.79.refs_11_), channel_id=1, source_target_pairs={{4,0},{8,4},{12,8},{14,12},{10,14},{6,10},{2,6},{0,2},{5,1},{9,5},... | collective-permute-start | bytes 737288 | tf_op jit(solution)/shard_map/ppermute | solution.py:200
  9.1 0.2 collective-permute-start.7
  9.3 3.5 %collective-permute-done.2.refs_3_.refs_5_ = bf16[24,4096]{1,0:T(8,128)(2,1)S(1)} collective-permute-done((bf16[24,4096]{1,0:T(8,128)(2,1)S(1)}, bf16[24,4096]{1,0:T(8,128)(2,1)S(1)}, u32[]{:S(2)}, u32[]{:S(2)}) %collective-permute-start.2) | collective-permute-done | bytes 196640 | tf_op jit(solution)/shard_map/ppermute | solution.py:200
  12.8 2.0 %collective-permute-done.1.refs_2_.refs_4_ = bf16[24,4096]{1,0:T(8,128)(2,1)S(1)} collective-permute-done((bf16[24,4096]{1,0:T(8,128)(2,1)S(1)}, bf16[24,4096]{1,0:T(8,128)(2,1)S(1)}, u32[]{:S(2)}, u32[]{:S(2)}) %collective-permute-start.1) | collective-permute-done | bytes 196640 | tf_op jit(solution)/shard_map/ppermute | solution.py:199
  14.8 0.1 collective-permute-start.4
  14.9 1.9 %collective-permute-start.5 = (bf16[24,4096]{1,0:T(8,128)(2,1)S(1)}, bf16[24,4096]{1,0:T(8,128)(2,1)S(1)}, u32[]{:S(2)}, u32[]{:S(2)}) collective-permute-start(bf16[24,4096]{1,0:T(8,128)(2,1)S(1)} %collective-permute-done.2.refs_3_.refs_5_), channel_id=1, source_target_pairs={{4,0},{8,4},{12,8},{14,12},{10,14},{6,10},{2,6},{0,2},{5,1},{9,5},... | collective-permute-start | bytes 589832 | tf_op jit(solution)/shard_map/ppermute | solution.py:200
  16.8 1.2 %collective-permute-done.14.refs_13_ = bf16[24,5120]{1,0:T(8,128)(2,1)S(1)} collective-permute-done((bf16[24,5120]{1,0:T(8,128)(2,1)S(1)}, bf16[24,5120]{1,0:T(8,128)(2,1)S(1)}, u32[]{:S(2)}, u32[]{:S(2)}) %collective-permute-start.14) | collective-permute-done | bytes 245792 | tf_op jit(solution)/shard_map/ppermute | solution.py:200
  18.0 2.0 %collective-permute-start.15 = (bf16[24,5120]{1,0:T(8,128)(2,1)S(1)}, bf16[24,5120]{1,0:T(8,128)(2,1)S(1)}, u32[]{:S(2)}, u32[]{:S(2)}) collective-permute-start(bf16[24,5120]{1,0:T(8,128)(2,1)S(1)} %collective-permute-done.14.refs_13_), channel_id=1, source_target_pairs={{4,0},{8,4},{12,8},{14,12},{10,14},{6,10},{2,6},{0,2},{5,1},{9,5},... | collective-permute-start | bytes 737288 | tf_op jit(solution)/shard_map/ppermute | solution.py:200
  20.0 0.0 collective-permute-done.7.refs_12_
  20.0 0.1 collective-permute-start.10
  20.2 4.0 %collective-permute-done.4.refs_4_.refs_6_ = bf16[24,4096]{1,0:T(8,128)(2,1)S(1)} collective-permute-done((bf16[24,4096]{1,0:T(8,128)(2,1)S(1)}, bf16[24,4096]{1,0:T(8,128)(2,1)S(1)}, u32[]{:S(2)}, u32[]{:S(2)}) %collective-permute-start.4) | collective-permute-done | bytes 196640 | tf_op jit(solution)/shard_map/ppermute | solution.py:199
  24.3 0.0 collective-permute-done.5.refs_5_.refs_7_
  24.3 0.1 collective-permute-start.6
  24.4 0.4 collective-permute-start.8
  24.8 1.7 %collective-permute-start.9 = (bf16[24,4096]{1,0:T(8,128)(2,1)S(1)}, bf16[24,4096]{1,0:T(8,128)(2,1)S(1)}, u32[]{:S(2)}, u32[]{:S(2)}) collective-permute-start(bf16[24,4096]{1,0:T(8,128)(2,1)S(1)} %collective-permute-done.5.refs_5_.refs_7_), channel_id=1, source_target_pairs={{4,0},{8,4},{12,8},{14,12},{10,14},{6,10},{2,6},{0,2},{5,1},{9,5},... | collective-permute-start | bytes 589832 | tf_op jit(solution)/shard_map/ppermute | solution.py:200
  26.4 0.6 collective-permute-done.15.refs_15_
  27.0 1.7 %collective-permute-start.16 = (bf16[24,5120]{1,0:T(8,128)(2,1)S(1)}, bf16[24,5120]{1,0:T(8,128)(2,1)S(1)}, u32[]{:S(2)}, u32[]{:S(2)}) collective-permute-start(bf16[24,5120]{1,0:T(8,128)(2,1)S(1)} %collective-permute-done.15.refs_15_), channel_id=1, source_target_pairs={{4,0},{8,4},{12,8},{14,12},{10,14},{6,10},{2,6},{0,2},{5,1},{9,5},... | collective-permute-start | bytes 737288 | tf_op jit(solution)/shard_map/ppermute | solution.py:200
  28.7 0.6 collective-permute-done.10.refs_14_
  29.3 0.4 collective-permute-start.13
  29.7 2.8 %collective-permute-done.9.refs_7_.refs_9_ = bf16[24,4096]{1,0:T(8,128)(2,1)S(1)} collective-permute-done((bf16[24,4096]{1,0:T(8,128)(2,1)S(1)}, bf16[24,4096]{1,0:T(8,128)(2,1)S(1)}, u32[]{:S(2)}, u32[]{:S(2)}) %collective-permute-start.9) | collective-permute-done | bytes 196640 | tf_op jit(solution)/shard_map/ppermute | solution.py:200
  32.5 0.0 collective-permute-start.18
  32.6 0.9 %collective-permute-done.8.refs_6_.refs_8_ = bf16[24,4096]{1,0:T(8,128)(2,1)S(1)} collective-permute-done((bf16[24,4096]{1,0:T(8,128)(2,1)S(1)}, bf16[24,4096]{1,0:T(8,128)(2,1)S(1)}, u32[]{:S(2)}, u32[]{:S(2)}) %collective-permute-start.8) | collective-permute-done | bytes 196640 | tf_op jit(solution)/shard_map/ppermute | solution.py:199
  33.5 1.6 %collective-permute-start.12 = (bf16[24,2048]{1,0:T(8,128)(2,1)S(1)}, bf16[24,2048]{1,0:T(8,128)(2,1)S(1)}, u32[]{:S(2)}, u32[]{:S(2)}) collective-permute-start(bf16[24,2048]{1,0:T(8,128)(2,1)S(1)} %slice.19), channel_id=1, source_target_pairs={{4,0},{8,4},{12,8},{14,12},{10,14},{6,10},{2,6},{0,2},{5,1},{9,5},... | collective-permute-start | bytes 294920 | tf_op jit(solution)/shard_map/ppermute | solution.py:200
  35.1 0.0 collective-permute-done.6
  35.1 0.5 collective-permute-start.11
  35.6 2.2 %collective-permute-done.16.refs_17_ = bf16[24,5120]{1,0:T(8,128)(2,1)S(1)} collective-permute-done((bf16[24,5120]{1,0:T(8,128)(2,1)S(1)}, bf16[24,5120]{1,0:T(8,128)(2,1)S(1)}, u32[]{:S(2)}, u32[]{:S(2)}) %collective-permute-start.16) | collective-permute-done | bytes 245792 | tf_op jit(solution)/shard_map/ppermute | solution.py:200
  37.8 1.7 %collective-permute-start.20 = (bf16[24,2560]{1,0:T(8,128)(2,1)S(1)}, bf16[24,2560]{1,0:T(8,128)(2,1)S(1)}, u32[]{:S(2)}, u32[]{:S(2)}) collective-permute-start(bf16[24,2560]{1,0:T(8,128)(2,1)S(1)} %slice.21), channel_id=1, source_target_pairs={{4,0},{8,4},{12,8},{14,12},{10,14},{6,10},{2,6},{0,2},{5,1},{9,5},... | collective-permute-start | bytes 368648 | tf_op jit(solution)/shard_map/ppermute | solution.py:200
  39.5 0.0 collective-permute-done.13.refs_16_
  39.5 0.0 collective-permute-done.12
  39.5 0.5 collective-permute-done.11
  40.0 1.0 %collective-permute-start.19 = (bf16[24,2560]{1,0:T(8,128)(2,1)S(1)}, bf16[24,2560]{1,0:T(8,128)(2,1)S(1)}, u32[]{:S(2)}, u32[]{:S(2)}) collective-permute-start(bf16[24,2560]{1,0:T(8,128)(2,1)S(1)} %slice.20), channel_id=1, source_target_pairs={{0,4},{4,8},{8,12},{12,14},{14,10},{10,6},{6,2},{2,0},{1,5},{5,9},... | collective-permute-start | bytes 368648 | tf_op jit(solution)/shard_map/ppermute | solution.py:199
  41.0 0.1 collective-permute-start.17
  41.2 1.3 %collective-permute-done.17 = bf16[72,1024]{1,0:T(8,128)(2,1)S(1)} collective-permute-done((bf16[72,1024]{1,0:T(8,128)(2,1)S(1)}, bf16[72,1024]{1,0:T(8,128)(2,1)S(1)}, u32[]{:S(2)}, u32[]{:S(2)}) %collective-permute-start.17) | collective-permute-done | bytes 147488 | tf_op jit(solution)/shard_map/ppermute | solution.py:217
  42.6 3.8 %shard_map.51.refs_9_ = f32[1792,7168]{1,0:T(8,128)} custom-call(bf16[192,1024]{1,0:T(8,128)(2,1)S(1)} %pad_maximum_fusion.refs_0_, bf16[24,4096]{1,0:T(8,128)(2,1)S(1)} %add.76.refs_1_.refs_3_, bf16[24,4096]{1,0:T(8,128)(2,1)S(1)} %collective-permute-done.1.refs_2_.refs_4_, bf16[24,4096]{1,0:T(8,128)(2,1)S(1)} %collective-permute-done.2.refs_3_.refs_5_, ...), custom_call_target="tpu_custom_call" | custom-call | flops 805306368 | bytes 8388608 | tf_op jit(solution)/shard_map/pallas_call | solution.py:111
  46.4 0.0 collective-permute-done.20
  46.4 0.0 collective-permute-done.19
  46.5 0.2 collective-permute-start.21
  46.7 0.0 collective-permute-done.18
  46.7 3.8 %shard_map.52.refs_19_ = f32[1792,7168]{1,0:T(8,128)} custom-call(bf16[192,1024]{1,0:T(8,128)(2,1)S(1)} %pad_maximum_fusion.refs_0_, bf16[24,4096]{1,0:T(8,128)(2,1)S(1)} %add.76.refs_1_.refs_3_, bf16[24,4096]{1,0:T(8,128)(2,1)S(1)} %collective-permute-done.1.refs_2_.refs_4_, ...), custom_call_target="tpu_custom_call", output_to_operand_aliasing={{}: (9, {})} | custom-call | flops 805306368 | bytes 8388608 | tf_op jit(solution)/shard_map/pallas_call | solution.py:111
  50.6 0.0 collective-permute-done.21
  50.6 0.1 broadcast_select_fusion.2
  50.7 13.2 %shard_map.53 = (f32[1792,7168]{1,0:T(8,128)}, f32[512,2048]{1,0:T(8,128)}) custom-call(bf16[192,1024]{1,0:T(8,128)(2,1)S(1)} %pad_maximum_fusion.refs_0_, bf16[192,768]{1,0:T(8,128)(2,1)S(1)} %fusion.refs_1_, bf16[192,512]{1,0:T(8,128)(2,1)S(1)} %pad_maximum_fusion.1.refs_2_, ...), custom_call_target="tpu_custom_call", output_to_operand_aliasing={{0}: (19, {})} | custom-call | flops 3724541952 | bytes 38797312 | tf_op jit(solution)/shard_map/pallas_call | solution.py:111
  (46 shorter events, 0.5 us)
Async XLA Ops:
  2.4 1.6 %collective-permute-start = (bf16[24,4096]{1,0:T(8,128)(2,1)S(1)}, bf16[24,4096]{1,0:T(8,128)(2,1)S(1)}, u32[]{:S(2)}, u32[]{:S(2)}) collective-permute-start(bf16[24,4096]{1,0:T(8,128)(2,1)S(1)} %get-tuple-element.25), channel_id=1, source_target_pairs={{0,1},{1,0},{2,3},{3,2},{4,5},{5,4},{6,7},{7,6},{8,9},{9,8},{10,11... | collective-permute-start | bytes 589832 | tf_op jit(solution)/shard_map/ppermute | solution.py:184
  3.0 4.1 %collective-permute-start.3 = (bf16[24,5120]{1,0:T(8,128)(2,1)S(1)}, bf16[24,5120]{1,0:T(8,128)(2,1)S(1)}, u32[]{:S(2)}, u32[]{:S(2)}) collective-permute-start(bf16[24,5120]{1,0:T(8,128)(2,1)S(1)} %get-tuple-element.27), channel_id=1, source_target_pairs={{0,1},{1,0},{2,3},{3,2},{4,5},{5,4},{6,7},{7,6},{8,9},{9,8},{10,11... | collective-permute-start | bytes 737288 | tf_op jit(solution)/shard_map/ppermute | solution.py:184
  4.1 8.6 %collective-permute-start.2 = (bf16[24,4096]{1,0:T(8,128)(2,1)S(1)}, bf16[24,4096]{1,0:T(8,128)(2,1)S(1)}, u32[]{:S(2)}, u32[]{:S(2)}) collective-permute-start(bf16[24,4096]{1,0:T(8,128)(2,1)S(1)} %add.76.refs_1_.refs_3_), channel_id=1, source_target_pairs={{4,0},{8,4},{12,8},{14,12},{10,14},{6,10},{2,6},{0,2},{5,1},{9,5},... | collective-permute-start | bytes 589832 | tf_op jit(solution)/shard_map/ppermute | solution.py:200
  7.0 7.8 %collective-permute-start.1 = (bf16[24,4096]{1,0:T(8,128)(2,1)S(1)}, bf16[24,4096]{1,0:T(8,128)(2,1)S(1)}, u32[]{:S(2)}, u32[]{:S(2)}) collective-permute-start(bf16[24,4096]{1,0:T(8,128)(2,1)S(1)} %add.76.refs_1_.refs_3_), channel_id=1, source_target_pairs={{0,4},{4,8},{8,12},{12,14},{14,10},{10,6},{6,2},{2,0},{1,5},{5,9},... | collective-permute-start | bytes 589832 | tf_op jit(solution)/shard_map/ppermute | solution.py:199
  7.2 10.8 %collective-permute-start.14 = (bf16[24,5120]{1,0:T(8,128)(2,1)S(1)}, bf16[24,5120]{1,0:T(8,128)(2,1)S(1)}, u32[]{:S(2)}, u32[]{:S(2)}) collective-permute-start(bf16[24,5120]{1,0:T(8,128)(2,1)S(1)} %add.79.refs_11_), channel_id=1, source_target_pairs={{4,0},{8,4},{12,8},{14,12},{10,14},{6,10},{2,6},{0,2},{5,1},{9,5},... | collective-permute-start | bytes 737288 | tf_op jit(solution)/shard_map/ppermute | solution.py:200
  9.1 10.9 %collective-permute-start.7 = (bf16[24,5120]{1,0:T(8,128)(2,1)S(1)}, bf16[24,5120]{1,0:T(8,128)(2,1)S(1)}, u32[]{:S(2)}, u32[]{:S(2)}) collective-permute-start(bf16[24,5120]{1,0:T(8,128)(2,1)S(1)} %add.79.refs_11_), channel_id=1, source_target_pairs={{0,4},{4,8},{8,12},{12,14},{14,10},{10,6},{6,2},{2,0},{1,5},{5,9},... | collective-permute-start | bytes 737288 | tf_op jit(solution)/shard_map/ppermute | solution.py:199
  14.8 9.5 %collective-permute-start.4 = (bf16[24,4096]{1,0:T(8,128)(2,1)S(1)}, bf16[24,4096]{1,0:T(8,128)(2,1)S(1)}, u32[]{:S(2)}, u32[]{:S(2)}) collective-permute-start(bf16[24,4096]{1,0:T(8,128)(2,1)S(1)} %collective-permute-done.1.refs_2_.refs_4_), channel_id=1, source_target_pairs={{0,4},{4,8},{8,12},{12,14},{14,10},{10,6},{6,2},{2,0},{1,5},{5,9},... | collective-permute-start | bytes 589832 | tf_op jit(solution)/shard_map/ppermute | solution.py:199
  14.9 9.4 %collective-permute-start.5 = (bf16[24,4096]{1,0:T(8,128)(2,1)S(1)}, bf16[24,4096]{1,0:T(8,128)(2,1)S(1)}, u32[]{:S(2)}, u32[]{:S(2)}) collective-permute-start(bf16[24,4096]{1,0:T(8,128)(2,1)S(1)} %collective-permute-done.2.refs_3_.refs_5_), channel_id=1, source_target_pairs={{4,0},{8,4},{12,8},{14,12},{10,14},{6,10},{2,6},{0,2},{5,1},{9,5},... | collective-permute-start | bytes 589832 | tf_op jit(solution)/shard_map/ppermute | solution.py:200
  18.0 9.0 %collective-permute-start.15 = (bf16[24,5120]{1,0:T(8,128)(2,1)S(1)}, bf16[24,5120]{1,0:T(8,128)(2,1)S(1)}, u32[]{:S(2)}, u32[]{:S(2)}) collective-permute-start(bf16[24,5120]{1,0:T(8,128)(2,1)S(1)} %collective-permute-done.14.refs_13_), channel_id=1, source_target_pairs={{4,0},{8,4},{12,8},{14,12},{10,14},{6,10},{2,6},{0,2},{5,1},{9,5},... | collective-permute-start | bytes 737288 | tf_op jit(solution)/shard_map/ppermute | solution.py:200
  20.0 9.2 %collective-permute-start.10 = (bf16[24,5120]{1,0:T(8,128)(2,1)S(1)}, bf16[24,5120]{1,0:T(8,128)(2,1)S(1)}, u32[]{:S(2)}, u32[]{:S(2)}) collective-permute-start(bf16[24,5120]{1,0:T(8,128)(2,1)S(1)} %collective-permute-done.7.refs_12_), channel_id=1, source_target_pairs={{0,4},{4,8},{8,12},{12,14},{14,10},{10,6},{6,2},{2,0},{1,5},{5,9},... | collective-permute-start | bytes 737288 | tf_op jit(solution)/shard_map/ppermute | solution.py:199
  24.3 10.8 %collective-permute-start.6 = (bf16[120,1024]{1,0:T(8,128)(2,1)S(1)}, bf16[120,1024]{1,0:T(8,128)(2,1)S(1)}, u32[]{:S(2)}, u32[]{:S(2)}) collective-permute-start(bf16[120,1024]{1,0:T(8,128)(2,1)S(1)} %dynamic-slice_dynamic-update-slice_fusion), channel_id=1, source_target_pairs={{0,1},{1,0},{2,3},{3,2},{4,5},{5,4},{6,7},{7,6},{8,9},{9,8},{10,11... | collective-permute-start | bytes 737288 | tf_op jit(solution)/shard_map/ppermute | solution.py:217
  24.4 9.1 %collective-permute-start.8 = (bf16[24,4096]{1,0:T(8,128)(2,1)S(1)}, bf16[24,4096]{1,0:T(8,128)(2,1)S(1)}, u32[]{:S(2)}, u32[]{:S(2)}) collective-permute-start(bf16[24,4096]{1,0:T(8,128)(2,1)S(1)} %collective-permute-done.4.refs_4_.refs_6_), channel_id=1, source_target_pairs={{0,4},{4,8},{8,12},{12,14},{14,10},{10,6},{6,2},{2,0},{1,5},{5,9},... | collective-permute-start | bytes 589832 | tf_op jit(solution)/shard_map/ppermute | solution.py:199
  24.8 7.7 %collective-permute-start.9 = (bf16[24,4096]{1,0:T(8,128)(2,1)S(1)}, bf16[24,4096]{1,0:T(8,128)(2,1)S(1)}, u32[]{:S(2)}, u32[]{:S(2)}) collective-permute-start(bf16[24,4096]{1,0:T(8,128)(2,1)S(1)} %collective-permute-done.5.refs_5_.refs_7_), channel_id=1, source_target_pairs={{4,0},{8,4},{12,8},{14,12},{10,14},{6,10},{2,6},{0,2},{5,1},{9,5},... | collective-permute-start | bytes 589832 | tf_op jit(solution)/shard_map/ppermute | solution.py:200
  27.0 10.8 %collective-permute-start.16 = (bf16[24,5120]{1,0:T(8,128)(2,1)S(1)}, bf16[24,5120]{1,0:T(8,128)(2,1)S(1)}, u32[]{:S(2)}, u32[]{:S(2)}) collective-permute-start(bf16[24,5120]{1,0:T(8,128)(2,1)S(1)} %collective-permute-done.15.refs_15_), channel_id=1, source_target_pairs={{4,0},{8,4},{12,8},{14,12},{10,14},{6,10},{2,6},{0,2},{5,1},{9,5},... | collective-permute-start | bytes 737288 | tf_op jit(solution)/shard_map/ppermute | solution.py:200
  29.3 10.2 %collective-permute-start.13 = (bf16[24,5120]{1,0:T(8,128)(2,1)S(1)}, bf16[24,5120]{1,0:T(8,128)(2,1)S(1)}, u32[]{:S(2)}, u32[]{:S(2)}) collective-permute-start(bf16[24,5120]{1,0:T(8,128)(2,1)S(1)} %collective-permute-done.10.refs_14_), channel_id=1, source_target_pairs={{0,4},{4,8},{8,12},{12,14},{14,10},{10,6},{6,2},{2,0},{1,5},{5,9},... | collective-permute-start | bytes 737288 | tf_op jit(solution)/shard_map/ppermute | solution.py:199
  32.5 14.2 %collective-permute-start.18 = (bf16[120,1280]{1,0:T(8,128)(2,1)S(1)}, bf16[120,1280]{1,0:T(8,128)(2,1)S(1)}, u32[]{:S(2)}, u32[]{:S(2)}) collective-permute-start(bf16[120,1280]{1,0:T(8,128)(2,1)S(1)} %maximum_dynamic-update-slice_fusion), channel_id=1, source_target_pairs={{0,1},{1,0},{2,3},{3,2},{4,5},{5,4},{6,7},{7,6},{8,9},{9,8},{10,11... | collective-permute-start | bytes 921608 | tf_op jit(solution)/shard_map/ppermute | solution.py:217
  33.5 6.0 %collective-permute-start.12 = (bf16[24,2048]{1,0:T(8,128)(2,1)S(1)}, bf16[24,2048]{1,0:T(8,128)(2,1)S(1)}, u32[]{:S(2)}, u32[]{:S(2)}) collective-permute-start(bf16[24,2048]{1,0:T(8,128)(2,1)S(1)} %slice.19), channel_id=1, source_target_pairs={{4,0},{8,4},{12,8},{14,12},{10,14},{6,10},{2,6},{0,2},{5,1},{9,5},... | collective-permute-start | bytes 294920 | tf_op jit(solution)/shard_map/ppermute | solution.py:200
  35.1 4.9 %collective-permute-start.11 = (bf16[24,2048]{1,0:T(8,128)(2,1)S(1)}, bf16[24,2048]{1,0:T(8,128)(2,1)S(1)}, u32[]{:S(2)}, u32[]{:S(2)}) collective-permute-start(bf16[24,2048]{1,0:T(8,128)(2,1)S(1)} %slice.18), channel_id=1, source_target_pairs={{0,4},{4,8},{8,12},{12,14},{14,10},{10,6},{6,2},{2,0},{1,5},{5,9},... | collective-permute-start | bytes 294920 | tf_op jit(solution)/shard_map/ppermute | solution.py:199
  37.8 8.6 %collective-permute-start.20 = (bf16[24,2560]{1,0:T(8,128)(2,1)S(1)}, bf16[24,2560]{1,0:T(8,128)(2,1)S(1)}, u32[]{:S(2)}, u32[]{:S(2)}) collective-permute-start(bf16[24,2560]{1,0:T(8,128)(2,1)S(1)} %slice.21), channel_id=1, source_target_pairs={{4,0},{8,4},{12,8},{14,12},{10,14},{6,10},{2,6},{0,2},{5,1},{9,5},... | collective-permute-start | bytes 368648 | tf_op jit(solution)/shard_map/ppermute | solution.py:200
  40.0 6.3 %collective-permute-start.19 = (bf16[24,2560]{1,0:T(8,128)(2,1)S(1)}, bf16[24,2560]{1,0:T(8,128)(2,1)S(1)}, u32[]{:S(2)}, u32[]{:S(2)}) collective-permute-start(bf16[24,2560]{1,0:T(8,128)(2,1)S(1)} %slice.20), channel_id=1, source_target_pairs={{0,4},{4,8},{8,12},{12,14},{14,10},{10,6},{6,2},{2,0},{1,5},{5,9},... | collective-permute-start | bytes 368648 | tf_op jit(solution)/shard_map/ppermute | solution.py:199
  41.0 1.4 %collective-permute-start.17 = (bf16[72,1024]{1,0:T(8,128)(2,1)S(1)}, bf16[72,1024]{1,0:T(8,128)(2,1)S(1)}, u32[]{:S(2)}, u32[]{:S(2)}) collective-permute-start(bf16[72,1024]{1,0:T(8,128)(2,1)S(1)} %pad_maximum_fusion.2), channel_id=1, source_target_pairs={{0,1},{1,0},{2,3},{3,2},{4,5},{5,4},{6,7},{7,6},{8,9},{9,8},{10,11... | collective-permute-start | bytes 442376 | tf_op jit(solution)/shard_map/ppermute | solution.py:217
  46.5 4.1 %collective-permute-start.21 = (bf16[72,1280]{1,0:T(8,128)(2,1)S(1)}, bf16[72,1280]{1,0:T(8,128)(2,1)S(1)}, u32[]{:S(2)}, u32[]{:S(2)}) collective-permute-start(bf16[72,1280]{1,0:T(8,128)(2,1)S(1)} %maximum_maximum_fusion), channel_id=1, source_target_pairs={{0,1},{1,0},{2,3},{3,2},{4,5},{5,4},{6,7},{7,6},{8,9},{9,8},{10,11... | collective-permute-start | bytes 552968 | tf_op jit(solution)/shard_map/ppermute | solution.py:217

commit v6 on v5

--- a/solution.py
+++ b/solution.py
@@ -186,55 +186,60 @@
         backward = list(forward)
         steps, halfway = [0] * len(chains), rows // 2
         sequence = [0, 1] * halfway
-        previous, last = (), []
-        for k in sequence:
-            chain, middle = chains[k], widths[k] // 2
-            steps[k] += 1
-            final = steps[k] == halfway
-            ahead_of, _ = lax.optimization_barrier((forward[k], previous))
-            behind_of, _ = lax.optimization_barrier((backward[k], previous))
-            previous = forward[k]
-            if final:
-                ahead_of, behind_of = ahead_of[:, :middle], behind_of[:, middle:]
-            forward[k] = lax.ppermute(ahead_of, "row", ahead)
-            backward[k] = lax.ppermute(behind_of, "row", behind)
-            if final:
-                last.append((forward[k], backward[k]))
-            else:
-                chain += [forward[k], backward[k]]
-                latest = (forward[k], backward[k])
-
-        def left_part(chain, pieces):
+        def left_part(chain, pieces, hold=None):
             own = []
             for part in chain:
                 cuts = [
                     lax.dynamic_slice_in_dim(part, base + (row % half_rows) * size, size, 1) for base, size in pieces
                 ]
                 own.append(cuts[0] if len(cuts) == 1 else jnp.concatenate(cuts, axis=1))
-            early = len(own) - 3
-            groups = [jnp.concatenate(own[:early], axis=0), jnp.concatenate(own[early:], axis=0)]
+            groups = [jnp.concatenate(own[:-1], axis=0), own[-1]]
             mine = col == row // half_rows
+            if hold is not None:
+                hold.append(groups[1])
             return jnp.concatenate([jnp.where(mine, g, lax.ppermute(g, "col", swap)) for g in groups], axis=0)
 
+        previous, hold, left_first = (), [], None
+        for k in sequence:
+            chain, middle = chains[k], widths[k] // 2
+            steps[k] += 1
+            final = steps[k] == halfway
+            ahead_of, _ = lax.optimization_barrier((forward[k], previous))
+            behind_of, _ = lax.optimization_barrier((backward[k], (previous, hold)))
+            previous = forward[k]
+            if final:
+                ahead_of, behind_of = ahead_of[:, :middle], behind_of[:, middle:]
+            forward[k] = lax.ppermute(ahead_of, "row", ahead)
+            backward[k] = lax.ppermute(behind_of, "row", behind)
+            if not final:
+                chain += [forward[k], backward[k]]
+                latest = (forward[k], backward[k])
+            elif k == 0:
+                last_first, _ = lax.optimization_barrier(((forward[k], backward[k]), latest))
+                chain.append(jnp.concatenate(last_first, axis=1))
+                left_first = left_part(chain, [(0, cut)], hold)
+
         act_shape, grad_shape = (act_block, act_half), (grad_block, grad_half)
-        last_first, _ = lax.optimization_barrier((last[0], latest))
-        chains[0].append(jnp.concatenate(last_first, axis=1))
-        left_first = left_part(chains[0], [(0, cut)])
         if rest == 0:
-            chains[1].append(jnp.concatenate(last[1], axis=1))
+            chains[1].append(jnp.concatenate((forward[1], backward[1]), axis=1))
             left_grad = left_part(chains[1], [(0, grad_block)])
             act_cov = gram(left_first, chains[0], scale, act_half // 256, 256)
             grad_cov = gram(left_grad, chains[1], scale, grad_half // 256, 256)
         else:
-            tile, grad_first = cut // 4, half_rows * rest
+            grad_first = half_rows * rest
+
+            def group(left, source, base, apart, height, start, width):
+                row_at, column_at = left * cut, source * cut + start
+                return (left, source, base + start, apart, height, width, 0, row_at, column_at, act_block, half_rows)
 
             def square(part, out):
-                group_of = lambda start: (0, 0, start, cut, cut, tile, 0, 0, start, act_block, half_rows)
-                groups = [group_of(part * cut // 2), group_of(part * cut // 2 + tile)]
+                widths_of = (128, 256, 128) if cut == 1024 else (cut // 2,)
+                starts = [part * cut // 2 + sum(widths_of[:n]) for n in range(len(widths_of))]
+                groups = [group(0, 0, 0, cut, cut, start, width) for start, width in zip(starts, widths_of)]
                 return tiles(scale, groups, [left_first], [chains[0]], [act_shape], out)[0]
 
             act_cov = square(0, None)
-            last_second, act_cov = lax.optimization_barrier((last[1], act_cov))
+            last_second, act_cov = lax.optimization_barrier(((forward[1], backward[1]), act_cov))
             chains[1].append(jnp.concatenate(last_second, axis=1))
             left_second = left_part(chains[1], [(0, rest), (grad_first, grad_block)])
             act_cov = square(1, act_cov)
@@ -242,10 +247,10 @@
             act_cov, grad_cov = tiles(
                 scale,
                 [
-                    (0, 1, 0, rest, cut, rest, 0, 0, cut, act_block, half_rows),
-                    (1, 0, 0, cut, rest, cut, 0, cut, 0, act_block, half_rows),
-                    (1, 1, 0, rest, rest, rest, 0, cut, cut, act_block, half_rows),
                     (2, 1, grad_first, grad_block, grad_block, grad_block, 1, 0, 0, grad_block, half_rows),
+                    group(0, 1, 0, rest, cut, 0, rest),
+                    group(1, 0, 0, cut, rest, 0, cut),
+                    *[group(1, 1, 0, rest, rest, start, rest // 3) for start in range(0, rest, rest // 3)],
                 ],
                 lefts, chains, [act_shape, grad_shape], act_cov,
             )

time: 64.1 us -> 66.7 us (1.041)
  Pallas kernels: 22 us -> 24.3 us
    pallas_call x3, Pallas kernels: 20.9 us -> 23.2 us  [tiles(): pl.pallas_call(functools.partial(tiles_kernel, scale, groups, len(lefts),...]
    ppermute x4, waiting for transfers between devices: 1.29 us -> 0.01 us  [left_part(): lax.ppermute(g, 'col', swap)]
    ppermute x8, waiting for transfers between devices: 10.3 us -> 11.4 us  [local(): backward[k] = lax.ppermute(behind_of, 'row', behind)]
    ppermute x8, waiting for transfers between devices: 8.06 us -> 8.82 us  [local(): forward[k] = lax.ppermute(ahead_of, 'row', ahead)]
    ppermute x8, starting transfers between devices: 2.79 us -> 2.06 us  [local(): forward[k] = lax.ppermute(ahead_of, 'row', ahead)]
  transfers between devices with their start and end apart: 22 -> 22, of which waited for: 12 -> 11; matrix products, arithmetic and copies ran while one was open for 1% -> 1% of each run, Pallas kernels for 12% -> 14%
where the time goes in v6:
time: 66.7 us; the launch traced here: 66.5 us
  Pallas kernels  24.3 us (36%)
  waiting for transfers between devices  21.2 us (32%)
  starting transfers between devices  18.8 us (28%)
  between operations  1.61 us (2%)
    pallas_call x3, Pallas kernels, tiles(): pl.pallas_call(functools.partial(tiles_kernel, scale, groups, len(lefts),...  23.2 us
    ppermute x8, starting transfers between devices, local(): backward[k] = lax.ppermute(behind_of, 'row', behind)  15.4 us
    ppermute x8, waiting for transfers between devices, local(): backward[k] = lax.ppermute(behind_of, 'row', behind)  11.4 us
    ppermute x8, waiting for transfers between devices, local(): forward[k] = lax.ppermute(ahead_of, 'row', ahead)  8.82 us
    ppermute x8, starting transfers between devices, local(): forward[k] = lax.ppermute(ahead_of, 'row', ahead)  2.06 us
  transfers between devices with their start and end apart: 22, of which 11 were waited for; matrix products, arithmetic and copies ran while one was open for 1% of the time, Pallas kernels for 14%

profile of v6, /device:TPU:0, one launch (start us, length us, event | category | flops | bytes accessed | tf_op | source)
XLA Modules:
  0.0 66.5 jit_solution(7208979060774983217)
XLA Ops:
  1.3 1.1 %shard_map.50 = (bf16[24,4096]{1,0:T(8,128)(2,1)S(1)}, bf16[24,4096]{1,0:T(8,128)(2,1)S(1)}, bf16[24,5120]{1,0:T(8,128)(2,1)S(1)}, bf16[24,5120]{1,0:T(8,128)(2,1)S(1)}) custom-call(s32[1]{0:T(128)} %bitcast.half_ref, s32[1]{0:T(128)S(6)} %copy.23.count_ref, bf16[12,14336]{1,0:T(8,128)(2,1)} %act_ref.1, bf16[12,4096]{1,0:T(8,128)(2,1)} %grad_ref.1), custom_call_target="tpu_custom_call" | custom-call | tf_op jit(solution)/shard_map/pallas_call | solution.py:178
  2.4 0.6 collective-permute-start
  3.0 0.1 collective-permute-start.3
  3.1 1.0 %collective-permute-done = bf16[24,4096]{1,0:T(8,128)(2,1)S(1)} collective-permute-done((bf16[24,4096]{1,0:T(8,128)(2,1)S(1)}, bf16[24,4096]{1,0:T(8,128)(2,1)S(1)}, u32[]{:S(2)}, u32[]{:S(2)}) %collective-permute-start) | collective-permute-done | bytes 196640 | tf_op jit(solution)/shard_map/ppermute | solution.py:184
  4.1 2.9 %collective-permute-start.2 = (bf16[24,4096]{1,0:T(8,128)(2,1)S(1)}, bf16[24,4096]{1,0:T(8,128)(2,1)S(1)}, u32[]{:S(2)}, u32[]{:S(2)}) collective-permute-start(bf16[24,4096]{1,0:T(8,128)(2,1)S(1)} %add.76.refs_1_.refs_3_), channel_id=1, source_target_pairs={{4,0},{8,4},{12,8},{14,12},{10,14},{6,10},{2,6},{0,2},{5,1},{9,5},... | collective-permute-start | bytes 589832 | tf_op jit(solution)/shard_map/ppermute | solution.py:213
  7.0 0.2 collective-permute-start.1
  7.1 0.0 collective-permute-done.3
  7.1 0.1 add.79.refs_11_
  7.2 1.9 %collective-permute-start.14 = (bf16[24,5120]{1,0:T(8,128)(2,1)S(1)}, bf16[24,5120]{1,0:T(8,128)(2,1)S(1)}, u32[]{:S(2)}, u32[]{:S(2)}) collective-permute-start(bf16[24,5120]{1,0:T(8,128)(2,1)S(1)} %add.79.refs_11_), channel_id=1, source_target_pairs={{4,0},{8,4},{12,8},{14,12},{10,14},{6,10},{2,6},{0,2},{5,1},{9,5},... | collective-permute-start | bytes 737288 | tf_op jit(solution)/shard_map/ppermute | solution.py:213
  9.1 0.2 collective-permute-start.6
  9.3 3.5 %collective-permute-done.2.refs_3_.refs_5_ = bf16[24,4096]{1,0:T(8,128)(2,1)S(1)} collective-permute-done((bf16[24,4096]{1,0:T(8,128)(2,1)S(1)}, bf16[24,4096]{1,0:T(8,128)(2,1)S(1)}, u32[]{:S(2)}, u32[]{:S(2)}) %collective-permute-start.2) | collective-permute-done | bytes 196640 | tf_op jit(solution)/shard_map/ppermute | solution.py:213
  12.8 2.0 %collective-permute-done.1.refs_2_.refs_4_ = bf16[24,4096]{1,0:T(8,128)(2,1)S(1)} collective-permute-done((bf16[24,4096]{1,0:T(8,128)(2,1)S(1)}, bf16[24,4096]{1,0:T(8,128)(2,1)S(1)}, u32[]{:S(2)}, u32[]{:S(2)}) %collective-permute-start.1) | collective-permute-done | bytes 196640 | tf_op jit(solution)/shard_map/ppermute | solution.py:212
  14.8 0.1 collective-permute-start.4
  14.9 1.9 %collective-permute-start.5 = (bf16[24,4096]{1,0:T(8,128)(2,1)S(1)}, bf16[24,4096]{1,0:T(8,128)(2,1)S(1)}, u32[]{:S(2)}, u32[]{:S(2)}) collective-permute-start(bf16[24,4096]{1,0:T(8,128)(2,1)S(1)} %collective-permute-done.2.refs_3_.refs_5_), channel_id=1, source_target_pairs={{4,0},{8,4},{12,8},{14,12},{10,14},{6,10},{2,6},{0,2},{5,1},{9,5},... | collective-permute-start | bytes 589832 | tf_op jit(solution)/shard_map/ppermute | solution.py:213
  16.8 1.2 %collective-permute-done.14.refs_13_ = bf16[24,5120]{1,0:T(8,128)(2,1)S(1)} collective-permute-done((bf16[24,5120]{1,0:T(8,128)(2,1)S(1)}, bf16[24,5120]{1,0:T(8,128)(2,1)S(1)}, u32[]{:S(2)}, u32[]{:S(2)}) %collective-permute-start.14) | collective-permute-done | bytes 245792 | tf_op jit(solution)/shard_map/ppermute | solution.py:213
  18.0 2.0 %collective-permute-start.15 = (bf16[24,5120]{1,0:T(8,128)(2,1)S(1)}, bf16[24,5120]{1,0:T(8,128)(2,1)S(1)}, u32[]{:S(2)}, u32[]{:S(2)}) collective-permute-start(bf16[24,5120]{1,0:T(8,128)(2,1)S(1)} %collective-permute-done.14.refs_13_), channel_id=1, source_target_pairs={{4,0},{8,4},{12,8},{14,12},{10,14},{6,10},{2,6},{0,2},{5,1},{9,5},... | collective-permute-start | bytes 737288 | tf_op jit(solution)/shard_map/ppermute | solution.py:213
  20.0 0.0 collective-permute-done.6.refs_12_
  20.0 0.1 collective-permute-start.10
  20.2 2.5 %collective-permute-done.5.refs_5_.refs_7_ = bf16[24,4096]{1,0:T(8,128)(2,1)S(1)} collective-permute-done((bf16[24,4096]{1,0:T(8,128)(2,1)S(1)}, bf16[24,4096]{1,0:T(8,128)(2,1)S(1)}, u32[]{:S(2)}, u32[]{:S(2)}) %collective-permute-start.5) | collective-permute-done | bytes 196640 | tf_op jit(solution)/shard_map/ppermute | solution.py:213
  22.7 1.5 %collective-permute-done.4.refs_4_.refs_6_ = bf16[24,4096]{1,0:T(8,128)(2,1)S(1)} collective-permute-done((bf16[24,4096]{1,0:T(8,128)(2,1)S(1)}, bf16[24,4096]{1,0:T(8,128)(2,1)S(1)}, u32[]{:S(2)}, u32[]{:S(2)}) %collective-permute-start.4) | collective-permute-done | bytes 196640 | tf_op jit(solution)/shard_map/ppermute | solution.py:212
  24.2 0.5 collective-permute-start.7
  24.7 1.5 %collective-permute-start.8 = (bf16[24,4096]{1,0:T(8,128)(2,1)S(1)}, bf16[24,4096]{1,0:T(8,128)(2,1)S(1)}, u32[]{:S(2)}, u32[]{:S(2)}) collective-permute-start(bf16[24,4096]{1,0:T(8,128)(2,1)S(1)} %collective-permute-done.5.refs_5_.refs_7_), channel_id=1, source_target_pairs={{4,0},{8,4},{12,8},{14,12},{10,14},{6,10},{2,6},{0,2},{5,1},{9,5},... | collective-permute-start | bytes 589832 | tf_op jit(solution)/shard_map/ppermute | solution.py:213
  26.3 1.7 %collective-permute-done.15.refs_15_ = bf16[24,5120]{1,0:T(8,128)(2,1)S(1)} collective-permute-done((bf16[24,5120]{1,0:T(8,128)(2,1)S(1)}, bf16[24,5120]{1,0:T(8,128)(2,1)S(1)}, u32[]{:S(2)}, u32[]{:S(2)}) %collective-permute-start.15) | collective-permute-done | bytes 245792 | tf_op jit(solution)/shard_map/ppermute | solution.py:213
  28.0 1.9 %collective-permute-start.16 = (bf16[24,5120]{1,0:T(8,128)(2,1)S(1)}, bf16[24,5120]{1,0:T(8,128)(2,1)S(1)}, u32[]{:S(2)}, u32[]{:S(2)}) collective-permute-start(bf16[24,5120]{1,0:T(8,128)(2,1)S(1)} %collective-permute-done.15.refs_15_), channel_id=1, source_target_pairs={{4,0},{8,4},{12,8},{14,12},{10,14},{6,10},{2,6},{0,2},{5,1},{9,5},... | collective-permute-start | bytes 737288 | tf_op jit(solution)/shard_map/ppermute | solution.py:213
  29.9 0.0 collective-permute-done.10.refs_14_
  29.9 0.1 collective-permute-start.13
  30.1 2.5 %collective-permute-done.8.refs_7_.refs_9_ = bf16[24,4096]{1,0:T(8,128)(2,1)S(1)} collective-permute-done((bf16[24,4096]{1,0:T(8,128)(2,1)S(1)}, bf16[24,4096]{1,0:T(8,128)(2,1)S(1)}, u32[]{:S(2)}, u32[]{:S(2)}) %collective-permute-start.8) | collective-permute-done | bytes 196640 | tf_op jit(solution)/shard_map/ppermute | solution.py:213
  32.6 1.2 %collective-permute-done.7.refs_6_.refs_8_ = bf16[24,4096]{1,0:T(8,128)(2,1)S(1)} collective-permute-done((bf16[24,4096]{1,0:T(8,128)(2,1)S(1)}, bf16[24,4096]{1,0:T(8,128)(2,1)S(1)}, u32[]{:S(2)}, u32[]{:S(2)}) %collective-permute-start.7) | collective-permute-done | bytes 196640 | tf_op jit(solution)/shard_map/ppermute | solution.py:212
  33.8 1.6 %collective-permute-start.12 = (bf16[24,2048]{1,0:T(8,128)(2,1)S(1)}, bf16[24,2048]{1,0:T(8,128)(2,1)S(1)}, u32[]{:S(2)}, u32[]{:S(2)}) collective-permute-start(bf16[24,2048]{1,0:T(8,128)(2,1)S(1)} %slice.19), channel_id=1, source_target_pairs={{4,0},{8,4},{12,8},{14,12},{10,14},{6,10},{2,6},{0,2},{5,1},{9,5},... | collective-permute-start | bytes 294920 | tf_op jit(solution)/shard_map/ppermute | solution.py:213
  35.4 0.4 collective-permute-start.11
  35.8 0.1 collective-permute-start.9
  35.9 3.0 %collective-permute-done.13.refs_16_ = bf16[24,5120]{1,0:T(8,128)(2,1)S(1)} collective-permute-done((bf16[24,5120]{1,0:T(8,128)(2,1)S(1)}, bf16[24,5120]{1,0:T(8,128)(2,1)S(1)}, u32[]{:S(2)}, u32[]{:S(2)}) %collective-permute-start.13) | collective-permute-done | bytes 245792 | tf_op jit(solution)/shard_map/ppermute | solution.py:212
  38.9 0.0 collective-permute-done.12
  38.9 1.1 %collective-permute-done.11 = bf16[24,2048]{1,0:T(8,128)(2,1)S(1)} collective-permute-done((bf16[24,2048]{1,0:T(8,128)(2,1)S(1)}, bf16[24,2048]{1,0:T(8,128)(2,1)S(1)}, u32[]{:S(2)}, u32[]{:S(2)}) %collective-permute-start.11) | collective-permute-done | bytes 98336 | tf_op jit(solution)/shard_map/ppermute | solution.py:212
  40.0 0.0 collective-permute-done.16.refs_17_
  40.1 0.1 collective-permute-start.17
  40.2 0.5 collective-permute-start.19
  40.7 1.6 %collective-permute-start.20 = (bf16[24,2560]{1,0:T(8,128)(2,1)S(1)}, bf16[24,2560]{1,0:T(8,128)(2,1)S(1)}, u32[]{:S(2)}, u32[]{:S(2)}) collective-permute-start(bf16[24,2560]{1,0:T(8,128)(2,1)S(1)} %slice.21), channel_id=1, source_target_pairs={{4,0},{8,4},{12,8},{14,12},{10,14},{6,10},{2,6},{0,2},{5,1},{9,5},... | collective-permute-start | bytes 368648 | tf_op jit(solution)/shard_map/ppermute | solution.py:213
  42.3 0.1 collective-permute-start.18
  42.4 0.0 collective-permute-done.17
  42.4 0.0 collective-permute-done.9
  42.4 0.1 broadcast_select_fusion.1
  42.5 4.7 %shard_map.51.refs_9_ = f32[1792,7168]{1,0:T(8,128)} custom-call(bf16[192,1024]{1,0:T(8,128)(2,1)S(1)} %pad_maximum_fusion.refs_0_, bf16[24,4096]{1,0:T(8,128)(2,1)S(1)} %add.76.refs_1_.refs_3_, bf16[24,4096]{1,0:T(8,128)(2,1)S(1)} %collective-permute-done.1.refs_2_.refs_4_, bf16[24,4096]{1,0:T(8,128)(2,1)S(1)} %collective-permute-done.2.refs_3_.refs_5_, ...), custom_call_target="tpu_custom_call" | custom-call | flops 805306368 | bytes 8388608 | tf_op jit(solution)/shard_map/pallas_call | solution.py:111
  47.3 0.0 collective-permute-done.19
  47.3 0.0 collective-permute-done.20
  47.4 0.5 collective-permute-start.21
  47.9 4.7 %shard_map.52.refs_19_ = f32[1792,7168]{1,0:T(8,128)} custom-call(bf16[192,1024]{1,0:T(8,128)(2,1)S(1)} %pad_maximum_fusion.refs_0_, bf16[24,4096]{1,0:T(8,128)(2,1)S(1)} %add.76.refs_1_.refs_3_, bf16[24,4096]{1,0:T(8,128)(2,1)S(1)} %collective-permute-done.1.refs_2_.refs_4_, ...), custom_call_target="tpu_custom_call", output_to_operand_aliasing={{}: (9, {})} | custom-call | flops 805306368 | bytes 8388608 | tf_op jit(solution)/shard_map/pallas_call | solution.py:111
  52.7 0.0 collective-permute-done.21
  52.7 0.0 collective-permute-done.18
  52.7 0.1 broadcast_select_fusion
  52.8 13.7 %shard_map.53 = (f32[1792,7168]{1,0:T(8,128)}, f32[512,2048]{1,0:T(8,128)}) custom-call(bf16[192,1024]{1,0:T(8,128)(2,1)S(1)} %pad_maximum_fusion.refs_0_, bf16[192,768]{1,0:T(8,128)(2,1)S(1)} %fusion.refs_1_, bf16[192,512]{1,0:T(8,128)(2,1)S(1)} %pad_maximum_fusion.1.refs_2_, ...), custom_call_target="tpu_custom_call", output_to_operand_aliasing={{0}: (19, {})} | custom-call | flops 3724541952 | bytes 38797312 | tf_op jit(solution)/shard_map/pallas_call | solution.py:111
  (46 shorter events, 0.5 us)
Async XLA Ops:
  2.4 1.6 %collective-permute-start = (bf16[24,4096]{1,0:T(8,128)(2,1)S(1)}, bf16[24,4096]{1,0:T(8,128)(2,1)S(1)}, u32[]{:S(2)}, u32[]{:S(2)}) collective-permute-start(bf16[24,4096]{1,0:T(8,128)(2,1)S(1)} %get-tuple-element.25), channel_id=1, source_target_pairs={{0,1},{1,0},{2,3},{3,2},{4,5},{5,4},{6,7},{7,6},{8,9},{9,8},{10,11... | collective-permute-start | bytes 589832 | tf_op jit(solution)/shard_map/ppermute | solution.py:184
  3.0 4.1 %collective-permute-start.3 = (bf16[24,5120]{1,0:T(8,128)(2,1)S(1)}, bf16[24,5120]{1,0:T(8,128)(2,1)S(1)}, u32[]{:S(2)}, u32[]{:S(2)}) collective-permute-start(bf16[24,5120]{1,0:T(8,128)(2,1)S(1)} %get-tuple-element.27), channel_id=1, source_target_pairs={{0,1},{1,0},{2,3},{3,2},{4,5},{5,4},{6,7},{7,6},{8,9},{9,8},{10,11... | collective-permute-start | bytes 737288 | tf_op jit(solution)/shard_map/ppermute | solution.py:184
  4.1 8.6 %collective-permute-start.2 = (bf16[24,4096]{1,0:T(8,128)(2,1)S(1)}, bf16[24,4096]{1,0:T(8,128)(2,1)S(1)}, u32[]{:S(2)}, u32[]{:S(2)}) collective-permute-start(bf16[24,4096]{1,0:T(8,128)(2,1)S(1)} %add.76.refs_1_.refs_3_), channel_id=1, source_target_pairs={{4,0},{8,4},{12,8},{14,12},{10,14},{6,10},{2,6},{0,2},{5,1},{9,5},... | collective-permute-start | bytes 589832 | tf_op jit(solution)/shard_map/ppermute | solution.py:213
  7.0 7.8 %collective-permute-start.1 = (bf16[24,4096]{1,0:T(8,128)(2,1)S(1)}, bf16[24,4096]{1,0:T(8,128)(2,1)S(1)}, u32[]{:S(2)}, u32[]{:S(2)}) collective-permute-start(bf16[24,4096]{1,0:T(8,128)(2,1)S(1)} %add.76.refs_1_.refs_3_), channel_id=1, source_target_pairs={{0,4},{4,8},{8,12},{12,14},{14,10},{10,6},{6,2},{2,0},{1,5},{5,9},... | collective-permute-start | bytes 589832 | tf_op jit(solution)/shard_map/ppermute | solution.py:212
  7.2 10.8 %collective-permute-start.14 = (bf16[24,5120]{1,0:T(8,128)(2,1)S(1)}, bf16[24,5120]{1,0:T(8,128)(2,1)S(1)}, u32[]{:S(2)}, u32[]{:S(2)}) collective-permute-start(bf16[24,5120]{1,0:T(8,128)(2,1)S(1)} %add.79.refs_11_), channel_id=1, source_target_pairs={{4,0},{8,4},{12,8},{14,12},{10,14},{6,10},{2,6},{0,2},{5,1},{9,5},... | collective-permute-start | bytes 737288 | tf_op jit(solution)/shard_map/ppermute | solution.py:213
  9.1 10.9 %collective-permute-start.6 = (bf16[24,5120]{1,0:T(8,128)(2,1)S(1)}, bf16[24,5120]{1,0:T(8,128)(2,1)S(1)}, u32[]{:S(2)}, u32[]{:S(2)}) collective-permute-start(bf16[24,5120]{1,0:T(8,128)(2,1)S(1)} %add.79.refs_11_), channel_id=1, source_target_pairs={{0,4},{4,8},{8,12},{12,14},{14,10},{10,6},{6,2},{2,0},{1,5},{5,9},... | collective-permute-start | bytes 737288 | tf_op jit(solution)/shard_map/ppermute | solution.py:212
  14.8 9.5 %collective-permute-start.4 = (bf16[24,4096]{1,0:T(8,128)(2,1)S(1)}, bf16[24,4096]{1,0:T(8,128)(2,1)S(1)}, u32[]{:S(2)}, u32[]{:S(2)}) collective-permute-start(bf16[24,4096]{1,0:T(8,128)(2,1)S(1)} %collective-permute-done.1.refs_2_.refs_4_), channel_id=1, source_target_pairs={{0,4},{4,8},{8,12},{12,14},{14,10},{10,6},{6,2},{2,0},{1,5},{5,9},... | collective-permute-start | bytes 589832 | tf_op jit(solution)/shard_map/ppermute | solution.py:212
  14.9 7.8 %collective-permute-start.5 = (bf16[24,4096]{1,0:T(8,128)(2,1)S(1)}, bf16[24,4096]{1,0:T(8,128)(2,1)S(1)}, u32[]{:S(2)}, u32[]{:S(2)}) collective-permute-start(bf16[24,4096]{1,0:T(8,128)(2,1)S(1)} %collective-permute-done.2.refs_3_.refs_5_), channel_id=1, source_target_pairs={{4,0},{8,4},{12,8},{14,12},{10,14},{6,10},{2,6},{0,2},{5,1},{9,5},... | collective-permute-start | bytes 589832 | tf_op jit(solution)/shard_map/ppermute | solution.py:213
  18.0 10.0 %collective-permute-start.15 = (bf16[24,5120]{1,0:T(8,128)(2,1)S(1)}, bf16[24,5120]{1,0:T(8,128)(2,1)S(1)}, u32[]{:S(2)}, u32[]{:S(2)}) collective-permute-start(bf16[24,5120]{1,0:T(8,128)(2,1)S(1)} %collective-permute-done.14.refs_13_), channel_id=1, source_target_pairs={{4,0},{8,4},{12,8},{14,12},{10,14},{6,10},{2,6},{0,2},{5,1},{9,5},... | collective-permute-start | bytes 737288 | tf_op jit(solution)/shard_map/ppermute | solution.py:213
  20.0 9.9 %collective-permute-start.10 = (bf16[24,5120]{1,0:T(8,128)(2,1)S(1)}, bf16[24,5120]{1,0:T(8,128)(2,1)S(1)}, u32[]{:S(2)}, u32[]{:S(2)}) collective-permute-start(bf16[24,5120]{1,0:T(8,128)(2,1)S(1)} %collective-permute-done.6.refs_12_), channel_id=1, source_target_pairs={{0,4},{4,8},{8,12},{12,14},{14,10},{10,6},{6,2},{2,0},{1,5},{5,9},... | collective-permute-start | bytes 737288 | tf_op jit(solution)/shard_map/ppermute | solution.py:212
  24.2 9.5 %collective-permute-start.7 = (bf16[24,4096]{1,0:T(8,128)(2,1)S(1)}, bf16[24,4096]{1,0:T(8,128)(2,1)S(1)}, u32[]{:S(2)}, u32[]{:S(2)}) collective-permute-start(bf16[24,4096]{1,0:T(8,128)(2,1)S(1)} %collective-permute-done.4.refs_4_.refs_6_), channel_id=1, source_target_pairs={{0,4},{4,8},{8,12},{12,14},{14,10},{10,6},{6,2},{2,0},{1,5},{5,9},... | collective-permute-start | bytes 589832 | tf_op jit(solution)/shard_map/ppermute | solution.py:212
  24.7 7.8 %collective-permute-start.8 = (bf16[24,4096]{1,0:T(8,128)(2,1)S(1)}, bf16[24,4096]{1,0:T(8,128)(2,1)S(1)}, u32[]{:S(2)}, u32[]{:S(2)}) collective-permute-start(bf16[24,4096]{1,0:T(8,128)(2,1)S(1)} %collective-permute-done.5.refs_5_.refs_7_), channel_id=1, source_target_pairs={{4,0},{8,4},{12,8},{14,12},{10,14},{6,10},{2,6},{0,2},{5,1},{9,5},... | collective-permute-start | bytes 589832 | tf_op jit(solution)/shard_map/ppermute | solution.py:213
  28.0 12.0 %collective-permute-start.16 = (bf16[24,5120]{1,0:T(8,128)(2,1)S(1)}, bf16[24,5120]{1,0:T(8,128)(2,1)S(1)}, u32[]{:S(2)}, u32[]{:S(2)}) collective-permute-start(bf16[24,5120]{1,0:T(8,128)(2,1)S(1)} %collective-permute-done.15.refs_15_), channel_id=1, source_target_pairs={{4,0},{8,4},{12,8},{14,12},{10,14},{6,10},{2,6},{0,2},{5,1},{9,5},... | collective-permute-start | bytes 737288 | tf_op jit(solution)/shard_map/ppermute | solution.py:213
  29.9 9.0 %collective-permute-start.13 = (bf16[24,5120]{1,0:T(8,128)(2,1)S(1)}, bf16[24,5120]{1,0:T(8,128)(2,1)S(1)}, u32[]{:S(2)}, u32[]{:S(2)}) collective-permute-start(bf16[24,5120]{1,0:T(8,128)(2,1)S(1)} %collective-permute-done.10.refs_14_), channel_id=1, source_target_pairs={{0,4},{4,8},{8,12},{12,14},{14,10},{10,6},{6,2},{2,0},{1,5},{5,9},... | collective-permute-start | bytes 737288 | tf_op jit(solution)/shard_map/ppermute | solution.py:212
  33.8 5.2 %collective-permute-start.12 = (bf16[24,2048]{1,0:T(8,128)(2,1)S(1)}, bf16[24,2048]{1,0:T(8,128)(2,1)S(1)}, u32[]{:S(2)}, u32[]{:S(2)}) collective-permute-start(bf16[24,2048]{1,0:T(8,128)(2,1)S(1)} %slice.19), channel_id=1, source_target_pairs={{4,0},{8,4},{12,8},{14,12},{10,14},{6,10},{2,6},{0,2},{5,1},{9,5},... | collective-permute-start | bytes 294920 | tf_op jit(solution)/shard_map/ppermute | solution.py:213
  35.4 4.6 %collective-permute-start.11 = (bf16[24,2048]{1,0:T(8,128)(2,1)S(1)}, bf16[24,2048]{1,0:T(8,128)(2,1)S(1)}, u32[]{:S(2)}, u32[]{:S(2)}) collective-permute-start(bf16[24,2048]{1,0:T(8,128)(2,1)S(1)} %slice.18), channel_id=1, source_target_pairs={{0,4},{4,8},{8,12},{12,14},{14,10},{10,6},{6,2},{2,0},{1,5},{5,9},... | collective-permute-start | bytes 294920 | tf_op jit(solution)/shard_map/ppermute | solution.py:212
  35.8 6.6 %collective-permute-start.9 = (bf16[168,1024]{1,0:T(8,128)(2,1)S(1)}, bf16[168,1024]{1,0:T(8,128)(2,1)S(1)}, u32[]{:S(2)}, u32[]{:S(2)}) collective-permute-start(bf16[168,1024]{1,0:T(8,128)(2,1)S(1)} %dynamic-slice_dynamic-update-slice_fusion), channel_id=1, source_target_pairs={{0,1},{1,0},{2,3},{3,2},{4,5},{5,4},{6,7},{7,6},{8,9},{9,8},{10,11... | collective-permute-start | bytes 1032200 | tf_op jit(solution)/shard_map/ppermute | solution.py:200
  40.1 2.3 %collective-permute-start.17 = (bf16[24,1024]{1,0:T(8,128)(2,1)S(1)}, bf16[24,1024]{1,0:T(8,128)(2,1)S(1)}, u32[]{:S(2)}, u32[]{:S(2)}) collective-permute-start(bf16[24,1024]{1,0:T(8,128)(2,1)S(1)} %constant_dynamic-slice_fusion.16), channel_id=1, source_target_pairs={{0,1},{1,0},{2,3},{3,2},{4,5},{5,4},{6,7},{7,6},{8,9},{9,8},{10,11... | collective-permute-start | bytes 147464 | tf_op jit(solution)/shard_map/ppermute | solution.py:200
  40.2 7.1 %collective-permute-start.19 = (bf16[24,2560]{1,0:T(8,128)(2,1)S(1)}, bf16[24,2560]{1,0:T(8,128)(2,1)S(1)}, u32[]{:S(2)}, u32[]{:S(2)}) collective-permute-start(bf16[24,2560]{1,0:T(8,128)(2,1)S(1)} %slice.20), channel_id=1, source_target_pairs={{0,4},{4,8},{8,12},{12,14},{14,10},{10,6},{6,2},{2,0},{1,5},{5,9},... | collective-permute-start | bytes 368648 | tf_op jit(solution)/shard_map/ppermute | solution.py:212
  40.7 6.6 %collective-permute-start.20 = (bf16[24,2560]{1,0:T(8,128)(2,1)S(1)}, bf16[24,2560]{1,0:T(8,128)(2,1)S(1)}, u32[]{:S(2)}, u32[]{:S(2)}) collective-permute-start(bf16[24,2560]{1,0:T(8,128)(2,1)S(1)} %slice.21), channel_id=1, source_target_pairs={{4,0},{8,4},{12,8},{14,12},{10,14},{6,10},{2,6},{0,2},{5,1},{9,5},... | collective-permute-start | bytes 368648 | tf_op jit(solution)/shard_map/ppermute | solution.py:213
  42.3 10.4 %collective-permute-start.18 = (bf16[168,1280]{1,0:T(8,128)(2,1)S(1)}, bf16[168,1280]{1,0:T(8,128)(2,1)S(1)}, u32[]{:S(2)}, u32[]{:S(2)}) collective-permute-start(bf16[168,1280]{1,0:T(8,128)(2,1)S(1)} %maximum_dynamic-update-slice_fusion), channel_id=1, source_target_pairs={{0,1},{1,0},{2,3},{3,2},{4,5},{5,4},{6,7},{7,6},{8,9},{9,8},{10,11... | collective-permute-start | bytes 1290248 | tf_op jit(solution)/shard_map/ppermute | solution.py:200
  47.4 5.3 %collective-permute-start.21 = (bf16[24,1280]{1,0:T(8,128)(2,1)S(1)}, bf16[24,1280]{1,0:T(8,128)(2,1)S(1)}, u32[]{:S(2)}, u32[]{:S(2)}) collective-permute-start(bf16[24,1280]{1,0:T(8,128)(2,1)S(1)} %pad_maximum_fusion.2), channel_id=1, source_target_pairs={{0,1},{1,0},{2,3},{3,2},{4,5},{5,4},{6,7},{7,6},{8,9},{9,8},{10,11... | collective-permute-start | bytes 184328 | tf_op jit(solution)/shard_map/ppermute | solution.py:200

commit v7 on v6

--- a/solution.py
+++ b/solution.py
@@ -8,7 +8,7 @@
 from jax.sharding import PartitionSpec as P
 
 
-SLOTS, COPIES = 4, 2
+SLOTS, HEIGHT = 4, 256
 
 
 def chip_ring(rows):
@@ -46,60 +46,72 @@
     )(left, *rights)
 
 
-def tiles_kernel(scale, groups, lefts, lists, outs, aliased, *refs):
-    left_refs, refs = refs[:lefts], refs[lefts:]
+def tiles_kernel(scale, groups, ready, lists, outs, aliased, *refs):
+    left_refs, refs = refs[: len(ready)], refs[len(ready) :]
     sources = []
     for shards in lists:
         sources.append(refs[:shards])
         refs = refs[shards:]
-    out_refs = refs[aliased : aliased + outs]
-    turned, buffer, sems = refs[aliased + outs : -2], refs[-2], refs[-1]
-
-    def copy(group, slot, j, start=0, rows=None):
-        _, _, _, _, height, width, which, row, column, stride, _ = group
-        rows = rows or height
+    refs = refs[aliased:]
+    out_refs, turned = refs[:outs], list(refs[outs:-3])
+    joined, buffer, sems = refs[-3:]
+    turned = [left_ref if done else turned.pop(0) for left_ref, done in zip(left_refs, ready)]
+
+    def copy(group, slot, j, m):
+        _, height, _, width, which, row, column, stride, _, _ = group
         return pltpu.make_async_copy(
-            buffer.at[slot, pl.ds(start, rows), pl.ds(0, width)],
-            out_refs[which].at[pl.ds(row + start, rows), pl.ds(pl.multiple_of(column + j * stride, 128), width)],
+            buffer.at[slot, pl.ds(0, height), pl.ds(0, width)],
+            out_refs[which].at[
+                pl.ds(pl.multiple_of(row + m * height, 8), height),
+                pl.ds(pl.multiple_of(column + j * stride, 128), width),
+            ],
             sems.at[slot],
         )
 
-    earlier, ready = None, set()
+    earlier, done = None, [index for index, is_ready in enumerate(ready) if is_ready]
     for group in groups:
-        if group[0] not in ready:
-            ready.add(group[0])
-            turned[group[0]][...] = left_refs[group[0]][...].T
-
-        def step(j, carry, group=group, earlier=earlier):
-            left, source, first, apart, height, width, _, _, _, _, _ = group
-            slot = lax.rem(j, SLOTS)
-
-            @pl.when(j >= SLOTS)
+        left, height, parts, width, _, _, _, _, blocks, pieces = group
+        if left not in done:
+            done.append(left)
+            turned[left][...] = left_refs[left][...].T
+
+        def step(n, carry, group=group, earlier=earlier):
+            left, height, parts, width, _, _, _, _, blocks, pieces = group
+            slot, j, m = lax.rem(n, SLOTS), lax.div(n, pieces), lax.rem(n, pieces)
+
+            @pl.when(m == 0)
             def _():
-                copy(group, slot, j - SLOTS).wait()
+                at = 0
+                for source, first, apart, wide in parts:
+                    here = pl.ds(pl.multiple_of(first + j * apart, 128), wide)
+                    joined[:, at : at + wide] = jnp.concatenate([ref[:, here] for ref in sources[source]], axis=0)
+                    at += wide
+
+            @pl.when(n >= SLOTS)
+            def _():
+                copy(group, slot, 0, 0).wait()
 
             if earlier is not None:
 
-                @pl.when(j < SLOTS)
+                @pl.when(n < SLOTS)
                 def _():
-                    copy(earlier, slot, j + earlier[-1] - SLOTS).wait()
-
-            here = pl.ds(pl.multiple_of(first + j * apart, 128), width)
-            right = jnp.concatenate([ref[:, here] for ref in sources[source]], axis=0)
-            product = jnp.dot(turned[left][...], right, preferred_element_type=jnp.float32)
+                    copy(earlier, slot, 0, 0).wait()
+
+            rows = turned[left][pl.ds(pl.multiple_of(m * height, height), height), :]
+            product = jnp.dot(rows, joined[:, :width], preferred_element_type=jnp.float32)
             buffer[slot, :height, :width] = product * scale
-            for start in range(0, height, height // COPIES):
-                copy(group, slot, j, start, height // COPIES).start()
+            copy(group, slot, j, m).start()
             return carry
 
-        lax.fori_loop(0, group[-1], step, 0)
+        lax.fori_loop(0, blocks * pieces, step, 0)
         earlier = group
     for slot in range(SLOTS):
-        copy(earlier, slot, earlier[-1] - SLOTS + slot).wait()
-
-
-def tiles(scale, groups, lefts, lists, out_shapes, out=None):
-    tokens = lefts[0].shape[0]
+        copy(earlier, slot, 0, 0).wait()
+
+
+def tiles(scale, groups, lefts, lists, out_shapes, out=None, ready=(), hand_on=False):
+    ready = tuple(ready) or (False,) * len(lefts)
+    tokens = lists[0][0].shape[0] * len(lists[0])
     whole, anywhere = pl.BlockSpec(memory_space=pltpu.VMEM), pl.BlockSpec(memory_space=pl.ANY)
     operands = [*lefts, *[part for parts in lists for part in parts]]
     specs, aliases = [whole] * len(operands), {}
@@ -107,17 +119,24 @@
         aliases = {len(operands): 0}
         operands.append(out)
         specs.append(anywhere)
-    area = sum(g[4] * g[5] * g[10] for g in groups)
+    area = sum(g[1] * g[3] * g[8] * g[9] for g in groups)
+    turned = [(left.shape[1], tokens) for left, done in zip(lefts, ready) if not done]
+    results = [jax.ShapeDtypeStruct(shape, jnp.float32) for shape in out_shapes]
+    result_specs = [anywhere] * len(results)
+    if hand_on:
+        results.append(pltpu.VMEM(turned[0], jnp.bfloat16))
+        result_specs.append(whole)
     return pl.pallas_call(
         functools.partial(
-            tiles_kernel, scale, groups, len(lefts), [len(parts) for parts in lists], len(out_shapes), len(aliases)
+            tiles_kernel, scale, groups, ready, [len(parts) for parts in lists], len(out_shapes), len(aliases)
         ),
         in_specs=specs,
-        out_specs=[anywhere] * len(out_shapes),
-        out_shape=[jax.ShapeDtypeStruct(shape, jnp.float32) for shape in out_shapes],
-        scratch_shapes=[pltpu.VMEM((left.shape[1], tokens), jnp.bfloat16) for left in lefts]
+        out_specs=result_specs,
+        out_shape=results,
+        scratch_shapes=[pltpu.VMEM(shape, jnp.bfloat16) for shape in turned[int(hand_on) :]]
         + [
-            pltpu.VMEM((SLOTS, max(g[4] for g in groups), max(g[5] for g in groups)), jnp.float32),
+            pltpu.VMEM((tokens, max(g[3] for g in groups)), jnp.bfloat16),
+            pltpu.VMEM((SLOTS, max(g[1] for g in groups), max(g[3] for g in groups)), jnp.float32),
             pltpu.SemaphoreType.DMA((SLOTS,)),
         ],
         input_output_aliases=aliases,
@@ -227,32 +246,30 @@
             grad_cov = gram(left_grad, chains[1], scale, grad_half // 256, 256)
         else:
             grad_first = half_rows * rest
-
-            def group(left, source, base, apart, height, start, width):
-                row_at, column_at = left * cut, source * cut + start
-                return (left, source, base + start, apart, height, width, 0, row_at, column_at, act_block, half_rows)
-
-            def square(part, out):
-                widths_of = (128, 256, 128) if cut == 1024 else (cut // 2,)
-                starts = [part * cut // 2 + sum(widths_of[:n]) for n in range(len(widths_of))]
-                groups = [group(0, 0, 0, cut, cut, start, width) for start, width in zip(starts, widths_of)]
-                return tiles(scale, groups, [left_first], [chains[0]], [act_shape], out)[0]
-
-            act_cov = square(0, None)
+            first_part, second_part = (0, 0, cut, cut), (1, 0, rest, rest)
+            grad_part = (1, grad_first, grad_block, grad_block)
+
+            def square(part, lefts, out, **more):
+                blocks = half_rows // 2
+                start = part * blocks
+                parts = [(0, start * cut, cut, cut)]
+                group = (0, HEIGHT, parts, cut, 0, 0, start * act_block, act_block, blocks, cut // HEIGHT)
+                return tiles(scale, [group], lefts, [chains[0]], [act_shape], out, **more)
+
+            act_cov, turned_first = square(0, [left_first], None, hand_on=True)
             last_second, act_cov = lax.optimization_barrier(((forward[1], backward[1]), act_cov))
             chains[1].append(jnp.concatenate(last_second, axis=1))
             left_second = left_part(chains[1], [(0, rest), (grad_first, grad_block)])
-            act_cov = square(1, act_cov)
-            lefts = [left_first, left_second[:, :rest], left_second[:, rest:]]
+            (act_cov,) = square(1, [turned_first], act_cov, ready=[True])
             act_cov, grad_cov = tiles(
                 scale,
                 [
-                    (2, 1, grad_first, grad_block, grad_block, grad_block, 1, 0, 0, grad_block, half_rows),
-                    group(0, 1, 0, rest, cut, 0, rest),
-                    group(1, 0, 0, cut, rest, 0, cut),
-                    *[group(1, 1, 0, rest, rest, start, rest // 3) for start in range(0, rest, rest // 3)],
+                    (2, HEIGHT, [grad_part], grad_block, 1, 0, 0, grad_block, half_rows, grad_block // HEIGHT),
+                    (1, HEIGHT, [first_part, second_part], act_block, 0, cut, 0, act_block, half_rows, rest // HEIGHT),
+                    (0, HEIGHT, [second_part], rest, 0, 0, cut, act_block, half_rows, cut // HEIGHT),
                 ],
-                lefts, chains, [act_shape, grad_shape], act_cov,
+                [turned_first, left_second[:, :rest], left_second[:, rest:]],
+                chains, [act_shape, grad_shape], act_cov, ready=[True, False, False],
             )
         return act_cov, grad_cov
 

time: 66.7 us -> 65.6 us (0.984)
  Pallas kernels: 24.3 us -> 23.2 us
    pallas_call x3, Pallas kernels: 23.2 us -> 22 us  [tiles(): pl.pallas_call(functools.partial(tiles_kernel, scale, groups, ready, [len...]
  transfers between devices with their start and end apart: 22 -> 22, of which waited for: 11 -> 11; matrix products, arithmetic and copies ran while one was open for 1% -> 1% of each run, Pallas kernels for 14% -> 11%
where the time goes in v7:
time: 65.6 us; the launch traced here: 65.4 us
  Pallas kernels  23.2 us (35%)
  waiting for transfers between devices  21.2 us (32%)
  starting transfers between devices  18.8 us (29%)
  between operations  1.62 us (2%)
    pallas_call x3, Pallas kernels, tiles(): pl.pallas_call(functools.partial(tiles_kernel, scale, groups, ready, [len...  22 us
    ppermute x8, starting transfers between devices, local(): backward[k] = lax.ppermute(behind_of, 'row', behind)  15.4 us
    ppermute x8, waiting for transfers between devices, local(): backward[k] = lax.ppermute(behind_of, 'row', behind)  11.4 us
    ppermute x8, waiting for transfers between devices, local(): forward[k] = lax.ppermute(ahead_of, 'row', ahead)  8.82 us
    ppermute x8, starting transfers between devices, local(): forward[k] = lax.ppermute(ahead_of, 'row', ahead)  2.06 us
  transfers between devices with their start and end apart: 22, of which 11 were waited for; matrix products, arithmetic and copies ran while one was open for 1% of the time, Pallas kernels for 11%

profile of v7, /device:TPU:0, one launch (start us, length us, event | category | flops | bytes accessed | tf_op | source)
XLA Modules:
  0.0 65.4 jit_solution(4972409174759128825)
XLA Ops:
  1.3 1.1 %shard_map.50 = (bf16[24,4096]{1,0:T(8,128)(2,1)S(1)}, bf16[24,4096]{1,0:T(8,128)(2,1)S(1)}, bf16[24,5120]{1,0:T(8,128)(2,1)S(1)}, bf16[24,5120]{1,0:T(8,128)(2,1)S(1)}) custom-call(s32[1]{0:T(128)} %bitcast.half_ref, s32[1]{0:T(128)S(6)} %copy.23.count_ref, bf16[12,14336]{1,0:T(8,128)(2,1)} %act_ref.1, bf16[12,4096]{1,0:T(8,128)(2,1)} %grad_ref.1), custom_call_target="tpu_custom_call" | custom-call | tf_op jit(solution)/shard_map/pallas_call | solution.py:197
  2.4 0.6 collective-permute-start
  3.0 0.1 collective-permute-start.3
  3.1 1.0 %collective-permute-done = bf16[24,4096]{1,0:T(8,128)(2,1)S(1)} collective-permute-done((bf16[24,4096]{1,0:T(8,128)(2,1)S(1)}, bf16[24,4096]{1,0:T(8,128)(2,1)S(1)}, u32[]{:S(2)}, u32[]{:S(2)}) %collective-permute-start) | collective-permute-done | bytes 196640 | tf_op jit(solution)/shard_map/ppermute | solution.py:203
  4.1 2.9 %collective-permute-start.2 = (bf16[24,4096]{1,0:T(8,128)(2,1)S(1)}, bf16[24,4096]{1,0:T(8,128)(2,1)S(1)}, u32[]{:S(2)}, u32[]{:S(2)}) collective-permute-start(bf16[24,4096]{1,0:T(8,128)(2,1)S(1)} %add.76.refs_1_.refs_3_), channel_id=1, source_target_pairs={{4,0},{8,4},{12,8},{14,12},{10,14},{6,10},{2,6},{0,2},{5,1},{9,5},... | collective-permute-start | bytes 589832 | tf_op jit(solution)/shard_map/ppermute | solution.py:232
  7.0 0.2 collective-permute-start.1
  7.1 0.0 collective-permute-done.3
  7.1 0.1 add.79.refs_11_
  7.2 1.9 %collective-permute-start.14 = (bf16[24,5120]{1,0:T(8,128)(2,1)S(1)}, bf16[24,5120]{1,0:T(8,128)(2,1)S(1)}, u32[]{:S(2)}, u32[]{:S(2)}) collective-permute-start(bf16[24,5120]{1,0:T(8,128)(2,1)S(1)} %add.79.refs_11_), channel_id=1, source_target_pairs={{4,0},{8,4},{12,8},{14,12},{10,14},{6,10},{2,6},{0,2},{5,1},{9,5},... | collective-permute-start | bytes 737288 | tf_op jit(solution)/shard_map/ppermute | solution.py:232
  9.1 0.2 collective-permute-start.6
  9.3 3.5 %collective-permute-done.2.refs_3_.refs_5_ = bf16[24,4096]{1,0:T(8,128)(2,1)S(1)} collective-permute-done((bf16[24,4096]{1,0:T(8,128)(2,1)S(1)}, bf16[24,4096]{1,0:T(8,128)(2,1)S(1)}, u32[]{:S(2)}, u32[]{:S(2)}) %collective-permute-start.2) | collective-permute-done | bytes 196640 | tf_op jit(solution)/shard_map/ppermute | solution.py:232
  12.8 2.0 %collective-permute-done.1.refs_2_.refs_4_ = bf16[24,4096]{1,0:T(8,128)(2,1)S(1)} collective-permute-done((bf16[24,4096]{1,0:T(8,128)(2,1)S(1)}, bf16[24,4096]{1,0:T(8,128)(2,1)S(1)}, u32[]{:S(2)}, u32[]{:S(2)}) %collective-permute-start.1) | collective-permute-done | bytes 196640 | tf_op jit(solution)/shard_map/ppermute | solution.py:231
  14.8 0.1 collective-permute-start.4
  14.9 1.9 %collective-permute-start.5 = (bf16[24,4096]{1,0:T(8,128)(2,1)S(1)}, bf16[24,4096]{1,0:T(8,128)(2,1)S(1)}, u32[]{:S(2)}, u32[]{:S(2)}) collective-permute-start(bf16[24,4096]{1,0:T(8,128)(2,1)S(1)} %collective-permute-done.2.refs_3_.refs_5_), channel_id=1, source_target_pairs={{4,0},{8,4},{12,8},{14,12},{10,14},{6,10},{2,6},{0,2},{5,1},{9,5},... | collective-permute-start | bytes 589832 | tf_op jit(solution)/shard_map/ppermute | solution.py:232
  16.8 1.2 %collective-permute-done.14.refs_13_ = bf16[24,5120]{1,0:T(8,128)(2,1)S(1)} collective-permute-done((bf16[24,5120]{1,0:T(8,128)(2,1)S(1)}, bf16[24,5120]{1,0:T(8,128)(2,1)S(1)}, u32[]{:S(2)}, u32[]{:S(2)}) %collective-permute-start.14) | collective-permute-done | bytes 245792 | tf_op jit(solution)/shard_map/ppermute | solution.py:232
  18.0 2.0 %collective-permute-start.15 = (bf16[24,5120]{1,0:T(8,128)(2,1)S(1)}, bf16[24,5120]{1,0:T(8,128)(2,1)S(1)}, u32[]{:S(2)}, u32[]{:S(2)}) collective-permute-start(bf16[24,5120]{1,0:T(8,128)(2,1)S(1)} %collective-permute-done.14.refs_13_), channel_id=1, source_target_pairs={{4,0},{8,4},{12,8},{14,12},{10,14},{6,10},{2,6},{0,2},{5,1},{9,5},... | collective-permute-start | bytes 737288 | tf_op jit(solution)/shard_map/ppermute | solution.py:232
  20.0 0.0 collective-permute-done.6.refs_12_
  20.0 0.1 collective-permute-start.10
  20.2 2.5 %collective-permute-done.5.refs_5_.refs_7_ = bf16[24,4096]{1,0:T(8,128)(2,1)S(1)} collective-permute-done((bf16[24,4096]{1,0:T(8,128)(2,1)S(1)}, bf16[24,4096]{1,0:T(8,128)(2,1)S(1)}, u32[]{:S(2)}, u32[]{:S(2)}) %collective-permute-start.5) | collective-permute-done | bytes 196640 | tf_op jit(solution)/shard_map/ppermute | solution.py:232
  22.7 1.5 %collective-permute-done.4.refs_4_.refs_6_ = bf16[24,4096]{1,0:T(8,128)(2,1)S(1)} collective-permute-done((bf16[24,4096]{1,0:T(8,128)(2,1)S(1)}, bf16[24,4096]{1,0:T(8,128)(2,1)S(1)}, u32[]{:S(2)}, u32[]{:S(2)}) %collective-permute-start.4) | collective-permute-done | bytes 196640 | tf_op jit(solution)/shard_map/ppermute | solution.py:231
  24.2 0.5 collective-permute-start.7
  24.7 1.5 %collective-permute-start.8 = (bf16[24,4096]{1,0:T(8,128)(2,1)S(1)}, bf16[24,4096]{1,0:T(8,128)(2,1)S(1)}, u32[]{:S(2)}, u32[]{:S(2)}) collective-permute-start(bf16[24,4096]{1,0:T(8,128)(2,1)S(1)} %collective-permute-done.5.refs_5_.refs_7_), channel_id=1, source_target_pairs={{4,0},{8,4},{12,8},{14,12},{10,14},{6,10},{2,6},{0,2},{5,1},{9,5},... | collective-permute-start | bytes 589832 | tf_op jit(solution)/shard_map/ppermute | solution.py:232
  26.3 1.7 %collective-permute-done.15.refs_15_ = bf16[24,5120]{1,0:T(8,128)(2,1)S(1)} collective-permute-done((bf16[24,5120]{1,0:T(8,128)(2,1)S(1)}, bf16[24,5120]{1,0:T(8,128)(2,1)S(1)}, u32[]{:S(2)}, u32[]{:S(2)}) %collective-permute-start.15) | collective-permute-done | bytes 245792 | tf_op jit(solution)/shard_map/ppermute | solution.py:232
  28.0 1.9 %collective-permute-start.16 = (bf16[24,5120]{1,0:T(8,128)(2,1)S(1)}, bf16[24,5120]{1,0:T(8,128)(2,1)S(1)}, u32[]{:S(2)}, u32[]{:S(2)}) collective-permute-start(bf16[24,5120]{1,0:T(8,128)(2,1)S(1)} %collective-permute-done.15.refs_15_), channel_id=1, source_target_pairs={{4,0},{8,4},{12,8},{14,12},{10,14},{6,10},{2,6},{0,2},{5,1},{9,5},... | collective-permute-start | bytes 737288 | tf_op jit(solution)/shard_map/ppermute | solution.py:232
  29.9 0.0 collective-permute-done.10.refs_14_
  29.9 0.1 collective-permute-start.13
  30.1 2.5 %collective-permute-done.8.refs_7_.refs_9_ = bf16[24,4096]{1,0:T(8,128)(2,1)S(1)} collective-permute-done((bf16[24,4096]{1,0:T(8,128)(2,1)S(1)}, bf16[24,4096]{1,0:T(8,128)(2,1)S(1)}, u32[]{:S(2)}, u32[]{:S(2)}) %collective-permute-start.8) | collective-permute-done | bytes 196640 | tf_op jit(solution)/shard_map/ppermute | solution.py:232
  32.6 1.2 %collective-permute-done.7.refs_6_.refs_8_ = bf16[24,4096]{1,0:T(8,128)(2,1)S(1)} collective-permute-done((bf16[24,4096]{1,0:T(8,128)(2,1)S(1)}, bf16[24,4096]{1,0:T(8,128)(2,1)S(1)}, u32[]{:S(2)}, u32[]{:S(2)}) %collective-permute-start.7) | collective-permute-done | bytes 196640 | tf_op jit(solution)/shard_map/ppermute | solution.py:231
  33.8 1.6 %collective-permute-start.12 = (bf16[24,2048]{1,0:T(8,128)(2,1)S(1)}, bf16[24,2048]{1,0:T(8,128)(2,1)S(1)}, u32[]{:S(2)}, u32[]{:S(2)}) collective-permute-start(bf16[24,2048]{1,0:T(8,128)(2,1)S(1)} %slice.19), channel_id=1, source_target_pairs={{4,0},{8,4},{12,8},{14,12},{10,14},{6,10},{2,6},{0,2},{5,1},{9,5},... | collective-permute-start | bytes 294920 | tf_op jit(solution)/shard_map/ppermute | solution.py:232
  35.4 0.4 collective-permute-start.11
  35.8 0.1 collective-permute-start.9
  35.9 3.0 %collective-permute-done.13.refs_16_ = bf16[24,5120]{1,0:T(8,128)(2,1)S(1)} collective-permute-done((bf16[24,5120]{1,0:T(8,128)(2,1)S(1)}, bf16[24,5120]{1,0:T(8,128)(2,1)S(1)}, u32[]{:S(2)}, u32[]{:S(2)}) %collective-permute-start.13) | collective-permute-done | bytes 245792 | tf_op jit(solution)/shard_map/ppermute | solution.py:231
  38.9 0.0 collective-permute-done.12
  38.9 1.1 %collective-permute-done.11 = bf16[24,2048]{1,0:T(8,128)(2,1)S(1)} collective-permute-done((bf16[24,2048]{1,0:T(8,128)(2,1)S(1)}, bf16[24,2048]{1,0:T(8,128)(2,1)S(1)}, u32[]{:S(2)}, u32[]{:S(2)}) %collective-permute-start.11) | collective-permute-done | bytes 98336 | tf_op jit(solution)/shard_map/ppermute | solution.py:231
  40.0 0.0 collective-permute-done.16.refs_17_
  40.1 0.1 collective-permute-start.17
  40.2 0.5 collective-permute-start.19
  40.7 1.6 %collective-permute-start.20 = (bf16[24,2560]{1,0:T(8,128)(2,1)S(1)}, bf16[24,2560]{1,0:T(8,128)(2,1)S(1)}, u32[]{:S(2)}, u32[]{:S(2)}) collective-permute-start(bf16[24,2560]{1,0:T(8,128)(2,1)S(1)} %slice.21), channel_id=1, source_target_pairs={{4,0},{8,4},{12,8},{14,12},{10,14},{6,10},{2,6},{0,2},{5,1},{9,5},... | collective-permute-start | bytes 368648 | tf_op jit(solution)/shard_map/ppermute | solution.py:232
  42.3 0.1 collective-permute-start.18
  42.4 0.0 collective-permute-done.17
  42.4 0.0 collective-permute-done.9
  42.4 0.1 broadcast_select_fusion.1
  42.5 3.8 %shard_map.51 = (f32[1792,7168]{1,0:T(8,128)}, bf16[1024,192]{1,0:T(8,128)(2,1)S(1)}) custom-call(bf16[192,1024]{1,0:T(8,128)(2,1)S(1)} %pad_maximum_fusion.refs_0_, bf16[24,4096]{1,0:T(8,128)(2,1)S(1)} %add.76.refs_1_.refs_3_, bf16[24,4096]{1,0:T(8,128)(2,1)S(1)} %collective-permute-done.1.refs_2_.refs_4_, ...), custom_call_target="tpu_custom_call" | custom-call | flops 805306368 | bytes 8388608 | tf_op jit(solution)/shard_map/pallas_call | solution.py:129
  46.4 0.0 collective-permute-done.19
  46.4 0.0 collective-permute-done.20
  46.5 0.5 collective-permute-start.21
  47.0 3.6 %shard_map.52.refs_19_ = f32[1792,7168]{1,0:T(8,128)} custom-call(bf16[1024,192]{1,0:T(8,128)(2,1)S(1)} %get-tuple-element.43.refs_0_, bf16[24,4096]{1,0:T(8,128)(2,1)S(1)} %add.76.refs_1_.refs_3_, bf16[24,4096]{1,0:T(8,128)(2,1)S(1)} %collective-permute-done.1.refs_2_.refs_4_, ...), custom_call_target="tpu_custom_call", output_to_operand_aliasing={{}: (9, {})} | custom-call | flops 805306368 | bytes 8388608 | tf_op jit(solution)/shard_map/pallas_call | solution.py:129
  50.7 0.0 collective-permute-done.21
  50.7 0.0 collective-permute-done.18
  50.9 14.6 %shard_map.53 = (f32[1792,7168]{1,0:T(8,128)}, f32[512,2048]{1,0:T(8,128)}) custom-call(bf16[1024,192]{1,0:T(8,128)(2,1)S(1)} %get-tuple-element.43.refs_0_, bf16[192,768]{1,0:T(8,128)(2,1)S(1)} %fusion.refs_1_, bf16[192,512]{1,0:T(8,128)(2,1)S(1)} %pad_maximum_fusion.1.refs_2_, ...), custom_call_target="tpu_custom_call", output_to_operand_aliasing={{0}: (19, {})} | custom-call | flops 3724541952 | bytes 38797312 | tf_op jit(solution)/shard_map/pallas_call | solution.py:129
  (47 shorter events, 0.5 us)
Async XLA Ops:
  2.4 1.6 %collective-permute-start = (bf16[24,4096]{1,0:T(8,128)(2,1)S(1)}, bf16[24,4096]{1,0:T(8,128)(2,1)S(1)}, u32[]{:S(2)}, u32[]{:S(2)}) collective-permute-start(bf16[24,4096]{1,0:T(8,128)(2,1)S(1)} %get-tuple-element.27), channel_id=1, source_target_pairs={{0,1},{1,0},{2,3},{3,2},{4,5},{5,4},{6,7},{7,6},{8,9},{9,8},{10,11... | collective-permute-start | bytes 589832 | tf_op jit(solution)/shard_map/ppermute | solution.py:203
  3.0 4.1 %collective-permute-start.3 = (bf16[24,5120]{1,0:T(8,128)(2,1)S(1)}, bf16[24,5120]{1,0:T(8,128)(2,1)S(1)}, u32[]{:S(2)}, u32[]{:S(2)}) collective-permute-start(bf16[24,5120]{1,0:T(8,128)(2,1)S(1)} %get-tuple-element.29), channel_id=1, source_target_pairs={{0,1},{1,0},{2,3},{3,2},{4,5},{5,4},{6,7},{7,6},{8,9},{9,8},{10,11... | collective-permute-start | bytes 737288 | tf_op jit(solution)/shard_map/ppermute | solution.py:203
  4.1 8.6 %collective-permute-start.2 = (bf16[24,4096]{1,0:T(8,128)(2,1)S(1)}, bf16[24,4096]{1,0:T(8,128)(2,1)S(1)}, u32[]{:S(2)}, u32[]{:S(2)}) collective-permute-start(bf16[24,4096]{1,0:T(8,128)(2,1)S(1)} %add.76.refs_1_.refs_3_), channel_id=1, source_target_pairs={{4,0},{8,4},{12,8},{14,12},{10,14},{6,10},{2,6},{0,2},{5,1},{9,5},... | collective-permute-start | bytes 589832 | tf_op jit(solution)/shard_map/ppermute | solution.py:232
  7.0 7.8 %collective-permute-start.1 = (bf16[24,4096]{1,0:T(8,128)(2,1)S(1)}, bf16[24,4096]{1,0:T(8,128)(2,1)S(1)}, u32[]{:S(2)}, u32[]{:S(2)}) collective-permute-start(bf16[24,4096]{1,0:T(8,128)(2,1)S(1)} %add.76.refs_1_.refs_3_), channel_id=1, source_target_pairs={{0,4},{4,8},{8,12},{12,14},{14,10},{10,6},{6,2},{2,0},{1,5},{5,9},... | collective-permute-start | bytes 589832 | tf_op jit(solution)/shard_map/ppermute | solution.py:231
  7.2 10.8 %collective-permute-start.14 = (bf16[24,5120]{1,0:T(8,128)(2,1)S(1)}, bf16[24,5120]{1,0:T(8,128)(2,1)S(1)}, u32[]{:S(2)}, u32[]{:S(2)}) collective-permute-start(bf16[24,5120]{1,0:T(8,128)(2,1)S(1)} %add.79.refs_11_), channel_id=1, source_target_pairs={{4,0},{8,4},{12,8},{14,12},{10,14},{6,10},{2,6},{0,2},{5,1},{9,5},... | collective-permute-start | bytes 737288 | tf_op jit(solution)/shard_map/ppermute | solution.py:232
  9.1 10.9 %collective-permute-start.6 = (bf16[24,5120]{1,0:T(8,128)(2,1)S(1)}, bf16[24,5120]{1,0:T(8,128)(2,1)S(1)}, u32[]{:S(2)}, u32[]{:S(2)}) collective-permute-start(bf16[24,5120]{1,0:T(8,128)(2,1)S(1)} %add.79.refs_11_), channel_id=1, source_target_pairs={{0,4},{4,8},{8,12},{12,14},{14,10},{10,6},{6,2},{2,0},{1,5},{5,9},... | collective-permute-start | bytes 737288 | tf_op jit(solution)/shard_map/ppermute | solution.py:231
  14.8 9.5 %collective-permute-start.4 = (bf16[24,4096]{1,0:T(8,128)(2,1)S(1)}, bf16[24,4096]{1,0:T(8,128)(2,1)S(1)}, u32[]{:S(2)}, u32[]{:S(2)}) collective-permute-start(bf16[24,4096]{1,0:T(8,128)(2,1)S(1)} %collective-permute-done.1.refs_2_.refs_4_), channel_id=1, source_target_pairs={{0,4},{4,8},{8,12},{12,14},{14,10},{10,6},{6,2},{2,0},{1,5},{5,9},... | collective-permute-start | bytes 589832 | tf_op jit(solution)/shard_map/ppermute | solution.py:231
  14.9 7.8 %collective-permute-start.5 = (bf16[24,4096]{1,0:T(8,128)(2,1)S(1)}, bf16[24,4096]{1,0:T(8,128)(2,1)S(1)}, u32[]{:S(2)}, u32[]{:S(2)}) collective-permute-start(bf16[24,4096]{1,0:T(8,128)(2,1)S(1)} %collective-permute-done.2.refs_3_.refs_5_), channel_id=1, source_target_pairs={{4,0},{8,4},{12,8},{14,12},{10,14},{6,10},{2,6},{0,2},{5,1},{9,5},... | collective-permute-start | bytes 589832 | tf_op jit(solution)/shard_map/ppermute | solution.py:232
  18.0 10.0 %collective-permute-start.15 = (bf16[24,5120]{1,0:T(8,128)(2,1)S(1)}, bf16[24,5120]{1,0:T(8,128)(2,1)S(1)}, u32[]{:S(2)}, u32[]{:S(2)}) collective-permute-start(bf16[24,5120]{1,0:T(8,128)(2,1)S(1)} %collective-permute-done.14.refs_13_), channel_id=1, source_target_pairs={{4,0},{8,4},{12,8},{14,12},{10,14},{6,10},{2,6},{0,2},{5,1},{9,5},... | collective-permute-start | bytes 737288 | tf_op jit(solution)/shard_map/ppermute | solution.py:232
  20.0 9.9 %collective-permute-start.10 = (bf16[24,5120]{1,0:T(8,128)(2,1)S(1)}, bf16[24,5120]{1,0:T(8,128)(2,1)S(1)}, u32[]{:S(2)}, u32[]{:S(2)}) collective-permute-start(bf16[24,5120]{1,0:T(8,128)(2,1)S(1)} %collective-permute-done.6.refs_12_), channel_id=1, source_target_pairs={{0,4},{4,8},{8,12},{12,14},{14,10},{10,6},{6,2},{2,0},{1,5},{5,9},... | collective-permute-start | bytes 737288 | tf_op jit(solution)/shard_map/ppermute | solution.py:231
  24.2 9.5 %collective-permute-start.7 = (bf16[24,4096]{1,0:T(8,128)(2,1)S(1)}, bf16[24,4096]{1,0:T(8,128)(2,1)S(1)}, u32[]{:S(2)}, u32[]{:S(2)}) collective-permute-start(bf16[24,4096]{1,0:T(8,128)(2,1)S(1)} %collective-permute-done.4.refs_4_.refs_6_), channel_id=1, source_target_pairs={{0,4},{4,8},{8,12},{12,14},{14,10},{10,6},{6,2},{2,0},{1,5},{5,9},... | collective-permute-start | bytes 589832 | tf_op jit(solution)/shard_map/ppermute | solution.py:231
  24.7 7.8 %collective-permute-start.8 = (bf16[24,4096]{1,0:T(8,128)(2,1)S(1)}, bf16[24,4096]{1,0:T(8,128)(2,1)S(1)}, u32[]{:S(2)}, u32[]{:S(2)}) collective-permute-start(bf16[24,4096]{1,0:T(8,128)(2,1)S(1)} %collective-permute-done.5.refs_5_.refs_7_), channel_id=1, source_target_pairs={{4,0},{8,4},{12,8},{14,12},{10,14},{6,10},{2,6},{0,2},{5,1},{9,5},... | collective-permute-start | bytes 589832 | tf_op jit(solution)/shard_map/ppermute | solution.py:232
  28.0 12.0 %collective-permute-start.16 = (bf16[24,5120]{1,0:T(8,128)(2,1)S(1)}, bf16[24,5120]{1,0:T(8,128)(2,1)S(1)}, u32[]{:S(2)}, u32[]{:S(2)}) collective-permute-start(bf16[24,5120]{1,0:T(8,128)(2,1)S(1)} %collective-permute-done.15.refs_15_), channel_id=1, source_target_pairs={{4,0},{8,4},{12,8},{14,12},{10,14},{6,10},{2,6},{0,2},{5,1},{9,5},... | collective-permute-start | bytes 737288 | tf_op jit(solution)/shard_map/ppermute | solution.py:232
  29.9 9.0 %collective-permute-start.13 = (bf16[24,5120]{1,0:T(8,128)(2,1)S(1)}, bf16[24,5120]{1,0:T(8,128)(2,1)S(1)}, u32[]{:S(2)}, u32[]{:S(2)}) collective-permute-start(bf16[24,5120]{1,0:T(8,128)(2,1)S(1)} %collective-permute-done.10.refs_14_), channel_id=1, source_target_pairs={{0,4},{4,8},{8,12},{12,14},{14,10},{10,6},{6,2},{2,0},{1,5},{5,9},... | collective-permute-start | bytes 737288 | tf_op jit(solution)/shard_map/ppermute | solution.py:231
  33.8 5.2 %collective-permute-start.12 = (bf16[24,2048]{1,0:T(8,128)(2,1)S(1)}, bf16[24,2048]{1,0:T(8,128)(2,1)S(1)}, u32[]{:S(2)}, u32[]{:S(2)}) collective-permute-start(bf16[24,2048]{1,0:T(8,128)(2,1)S(1)} %slice.19), channel_id=1, source_target_pairs={{4,0},{8,4},{12,8},{14,12},{10,14},{6,10},{2,6},{0,2},{5,1},{9,5},... | collective-permute-start | bytes 294920 | tf_op jit(solution)/shard_map/ppermute | solution.py:232
  35.4 4.6 %collective-permute-start.11 = (bf16[24,2048]{1,0:T(8,128)(2,1)S(1)}, bf16[24,2048]{1,0:T(8,128)(2,1)S(1)}, u32[]{:S(2)}, u32[]{:S(2)}) collective-permute-start(bf16[24,2048]{1,0:T(8,128)(2,1)S(1)} %slice.18), channel_id=1, source_target_pairs={{0,4},{4,8},{8,12},{12,14},{14,10},{10,6},{6,2},{2,0},{1,5},{5,9},... | collective-permute-start | bytes 294920 | tf_op jit(solution)/shard_map/ppermute | solution.py:231
  35.8 6.6 %collective-permute-start.9 = (bf16[168,1024]{1,0:T(8,128)(2,1)S(1)}, bf16[168,1024]{1,0:T(8,128)(2,1)S(1)}, u32[]{:S(2)}, u32[]{:S(2)}) collective-permute-start(bf16[168,1024]{1,0:T(8,128)(2,1)S(1)} %dynamic-slice_dynamic-update-slice_fusion), channel_id=1, source_target_pairs={{0,1},{1,0},{2,3},{3,2},{4,5},{5,4},{6,7},{7,6},{8,9},{9,8},{10,11... | collective-permute-start | bytes 1032200 | tf_op jit(solution)/shard_map/ppermute | solution.py:219
  40.1 2.3 %collective-permute-start.17 = (bf16[24,1024]{1,0:T(8,128)(2,1)S(1)}, bf16[24,1024]{1,0:T(8,128)(2,1)S(1)}, u32[]{:S(2)}, u32[]{:S(2)}) collective-permute-start(bf16[24,1024]{1,0:T(8,128)(2,1)S(1)} %constant_dynamic-slice_fusion.16), channel_id=1, source_target_pairs={{0,1},{1,0},{2,3},{3,2},{4,5},{5,4},{6,7},{7,6},{8,9},{9,8},{10,11... | collective-permute-start | bytes 147464 | tf_op jit(solution)/shard_map/ppermute | solution.py:219
  40.2 6.2 %collective-permute-start.19 = (bf16[24,2560]{1,0:T(8,128)(2,1)S(1)}, bf16[24,2560]{1,0:T(8,128)(2,1)S(1)}, u32[]{:S(2)}, u32[]{:S(2)}) collective-permute-start(bf16[24,2560]{1,0:T(8,128)(2,1)S(1)} %slice.20), channel_id=1, source_target_pairs={{0,4},{4,8},{8,12},{12,14},{14,10},{10,6},{6,2},{2,0},{1,5},{5,9},... | collective-permute-start | bytes 368648 | tf_op jit(solution)/shard_map/ppermute | solution.py:231
  40.7 5.7 %collective-permute-start.20 = (bf16[24,2560]{1,0:T(8,128)(2,1)S(1)}, bf16[24,2560]{1,0:T(8,128)(2,1)S(1)}, u32[]{:S(2)}, u32[]{:S(2)}) collective-permute-start(bf16[24,2560]{1,0:T(8,128)(2,1)S(1)} %slice.21), channel_id=1, source_target_pairs={{4,0},{8,4},{12,8},{14,12},{10,14},{6,10},{2,6},{0,2},{5,1},{9,5},... | collective-permute-start | bytes 368648 | tf_op jit(solution)/shard_map/ppermute | solution.py:232
  42.3 8.4 %collective-permute-start.18 = (bf16[168,1280]{1,0:T(8,128)(2,1)S(1)}, bf16[168,1280]{1,0:T(8,128)(2,1)S(1)}, u32[]{:S(2)}, u32[]{:S(2)}) collective-permute-start(bf16[168,1280]{1,0:T(8,128)(2,1)S(1)} %maximum_dynamic-update-slice_fusion), channel_id=1, source_target_pairs={{0,1},{1,0},{2,3},{3,2},{4,5},{5,4},{6,7},{7,6},{8,9},{9,8},{10,11... | collective-permute-start | bytes 1290248 | tf_op jit(solution)/shard_map/ppermute | solution.py:219
  46.5 4.2 %collective-permute-start.21 = (bf16[24,1280]{1,0:T(8,128)(2,1)S(1)}, bf16[24,1280]{1,0:T(8,128)(2,1)S(1)}, u32[]{:S(2)}, u32[]{:S(2)}) collective-permute-start(bf16[24,1280]{1,0:T(8,128)(2,1)S(1)} %pad_maximum_fusion.2), channel_id=1, source_target_pairs={{0,1},{1,0},{2,3},{3,2},{4,5},{5,4},{6,7},{7,6},{8,9},{9,8},{10,11... | collective-permute-start | bytes 184328 | tf_op jit(solution)/shard_map/ppermute | solution.py:219

commit v8 on v7

--- a/solution.py
+++ b/solution.py
@@ -8,7 +8,7 @@
 from jax.sharding import PartitionSpec as P
 
 
-SLOTS, HEIGHT = 4, 256
+SLOTS, PIECE = 4, 128
 
 
 def chip_ring(rows):
@@ -57,56 +57,50 @@
     joined, buffer, sems = refs[-3:]
     turned = [left_ref if done else turned.pop(0) for left_ref, done in zip(left_refs, ready)]
 
-    def copy(group, slot, j, m):
-        _, height, _, width, which, row, column, stride, _, _ = group
+    def copy(group, slot, j):
+        _, height, (_, _, _, width), which, row, column, stride, _ = group
         return pltpu.make_async_copy(
             buffer.at[slot, pl.ds(0, height), pl.ds(0, width)],
-            out_refs[which].at[
-                pl.ds(pl.multiple_of(row + m * height, 8), height),
-                pl.ds(pl.multiple_of(column + j * stride, 128), width),
-            ],
+            out_refs[which].at[pl.ds(row, height), pl.ds(pl.multiple_of(column + j * stride, 128), width)],
             sems.at[slot],
         )
 
     earlier, done = None, [index for index, is_ready in enumerate(ready) if is_ready]
     for group in groups:
-        left, height, parts, width, _, _, _, _, blocks, pieces = group
+        left = group[0]
         if left not in done:
             done.append(left)
             turned[left][...] = left_refs[left][...].T
 
-        def step(n, carry, group=group, earlier=earlier):
-            left, height, parts, width, _, _, _, _, blocks, pieces = group
-            slot, j, m = lax.rem(n, SLOTS), lax.div(n, pieces), lax.rem(n, pieces)
-
-            @pl.when(m == 0)
+        def step(j, carry, group=group, earlier=earlier):
+            left, height, (source, first, apart, width), _, _, _, _, _ = group
+            slot = lax.rem(j, SLOTS)
+            here = pl.ds(pl.multiple_of(first + j * apart, 128), width)
+            joined[:, :width] = jnp.concatenate([ref[:, here] for ref in sources[source]], axis=0)
+
+            @pl.when(j >= SLOTS)
             def _():
-                at = 0
-                for source, first, apart, wide in parts:
-                    here = pl.ds(pl.multiple_of(first + j * apart, 128), wide)
-                    joined[:, at : at + wide] = jnp.concatenate([ref[:, here] for ref in sources[source]], axis=0)
-                    at += wide
-
-            @pl.when(n >= SLOTS)
-            def _():
-                copy(group, slot, 0, 0).wait()
+                copy(group, slot, 0).wait()
 
             if earlier is not None:
 
-                @pl.when(n < SLOTS)
+                @pl.when(j < SLOTS)
                 def _():
-                    copy(earlier, slot, 0, 0).wait()
-
-            rows = turned[left][pl.ds(pl.multiple_of(m * height, height), height), :]
-            product = jnp.dot(rows, joined[:, :width], preferred_element_type=jnp.float32)
-            buffer[slot, :height, :width] = product * scale
-            copy(group, slot, j, m).start()
+                    copy(earlier, slot, 0).wait()
+
+            for across in range(0, width, 256):
+                right = joined[:, across : across + 256]
+                for down in range(0, height, PIECE):
+                    rows = turned[left][down : down + PIECE, :]
+                    product = jnp.dot(rows, right, preferred_element_type=jnp.float32)
+                    buffer[slot, down : down + PIECE, across : across + 256] = product * scale
+            copy(group, slot, j).start()
             return carry
 
-        lax.fori_loop(0, blocks * pieces, step, 0)
+        lax.fori_loop(0, group[-1], step, 0)
         earlier = group
     for slot in range(SLOTS):
-        copy(earlier, slot, 0, 0).wait()
+        copy(earlier, slot, 0).wait()
 
 
 def tiles(scale, groups, lefts, lists, out_shapes, out=None, ready=(), hand_on=False):
@@ -119,7 +113,7 @@
         aliases = {len(operands): 0}
         operands.append(out)
         specs.append(anywhere)
-    area = sum(g[1] * g[3] * g[8] * g[9] for g in groups)
+    area = sum(g[1] * g[2][3] * g[7] for g in groups)
     turned = [(left.shape[1], tokens) for left, done in zip(lefts, ready) if not done]
     results = [jax.ShapeDtypeStruct(shape, jnp.float32) for shape in out_shapes]
     result_specs = [anywhere] * len(results)
@@ -135,8 +129,8 @@
         out_shape=results,
         scratch_shapes=[pltpu.VMEM(shape, jnp.bfloat16) for shape in turned[int(hand_on) :]]
         + [
-            pltpu.VMEM((tokens, max(g[3] for g in groups)), jnp.bfloat16),
-            pltpu.VMEM((SLOTS, max(g[1] for g in groups), max(g[3] for g in groups)), jnp.float32),
+            pltpu.VMEM((tokens, max(g[2][3] for g in groups)), jnp.bfloat16),
+            pltpu.VMEM((SLOTS, max(g[1] for g in groups), max(g[2][3] for g in groups)), jnp.float32),
             pltpu.SemaphoreType.DMA((SLOTS,)),
         ],
         input_output_aliases=aliases,
@@ -250,11 +244,9 @@
             grad_part = (1, grad_first, grad_block, grad_block)
 
             def square(part, lefts, out, **more):
-                blocks = half_rows // 2
-                start = part * blocks
-                parts = [(0, start * cut, cut, cut)]
-                group = (0, HEIGHT, parts, cut, 0, 0, start * act_block, act_block, blocks, cut // HEIGHT)
-                return tiles(scale, [group], lefts, [chains[0]], [act_shape], out, **more)
+                starts = [part * cut // 2, part * cut // 2 + cut // 4]
+                groups = [(0, cut, (0, at, cut, cut // 4), 0, 0, at, act_block, half_rows) for at in starts]
+                return tiles(scale, groups, lefts, [chains[0]], [act_shape], out, **more)
 
             act_cov, turned_first = square(0, [left_first], None, hand_on=True)
             last_second, act_cov = lax.optimization_barrier(((forward[1], backward[1]), act_cov))
@@ -264,9 +256,10 @@
             act_cov, grad_cov = tiles(
                 scale,
                 [
-                    (2, HEIGHT, [grad_part], grad_block, 1, 0, 0, grad_block, half_rows, grad_block // HEIGHT),
-                    (1, HEIGHT, [first_part, second_part], act_block, 0, cut, 0, act_block, half_rows, rest // HEIGHT),
-                    (0, HEIGHT, [second_part], rest, 0, 0, cut, act_block, half_rows, cut // HEIGHT),
+                    (2, grad_block, grad_part, 1, 0, 0, grad_block, half_rows),
+                    (0, cut, second_part, 0, 0, cut, act_block, half_rows),
+                    (1, rest, first_part, 0, cut, 0, act_block, half_rows),
+                    (1, rest, second_part, 0, cut, cut, act_block, half_rows),
                 ],
                 [turned_first, left_second[:, :rest], left_second[:, rest:]],
                 chains, [act_shape, grad_shape], act_cov, ready=[True, False, False],

time: 65.6 us -> 64.1 us (0.977)
  Pallas kernels: 23.2 us -> 21.8 us
    pallas_call x3, Pallas kernels: 22 us -> 20.6 us  [tiles(): pl.pallas_call(functools.partial(tiles_kernel, scale, groups, ready, [len...]
  transfers between devices with their start and end apart: 22 -> 22, of which waited for: 11 -> 11; matrix products, arithmetic and copies ran while one was open for 1% -> 1% of each run, Pallas kernels for 11% -> 12%
where the time goes in v8:
time: 64.1 us; the launch traced here: 64 us
  Pallas kernels  21.8 us (34%)
  waiting for transfers between devices  21.2 us (33%)
  starting transfers between devices  18.8 us (29%)
  between operations  1.62 us (3%)
    pallas_call x3, Pallas kernels, tiles(): pl.pallas_call(functools.partial(tiles_kernel, scale, groups, ready, [len...  20.6 us
    ppermute x8, starting transfers between devices, local(): backward[k] = lax.ppermute(behind_of, 'row', behind)  15.4 us
    ppermute x8, waiting for transfers between devices, local(): backward[k] = lax.ppermute(behind_of, 'row', behind)  11.4 us
    ppermute x8, waiting for transfers between devices, local(): forward[k] = lax.ppermute(ahead_of, 'row', ahead)  8.82 us
    ppermute x8, starting transfers between devices, local(): forward[k] = lax.ppermute(ahead_of, 'row', ahead)  2.06 us
  transfers between devices with their start and end apart: 22, of which 11 were waited for; matrix products, arithmetic and copies ran while one was open for 1% of the time, Pallas kernels for 12%

profile of v8, /device:TPU:0, one launch (start us, length us, event | category | flops | bytes accessed | tf_op | source)
XLA Modules:
  0.0 64.0 jit_solution(17246038550648830303)
XLA Ops:
  1.3 1.1 %shard_map.50 = (bf16[24,4096]{1,0:T(8,128)(2,1)S(1)}, bf16[24,4096]{1,0:T(8,128)(2,1)S(1)}, bf16[24,5120]{1,0:T(8,128)(2,1)S(1)}, bf16[24,5120]{1,0:T(8,128)(2,1)S(1)}) custom-call(s32[1]{0:T(128)} %bitcast.half_ref, s32[1]{0:T(128)S(6)} %copy.23.count_ref, bf16[12,14336]{1,0:T(8,128)(2,1)} %act_ref.1, bf16[12,4096]{1,0:T(8,128)(2,1)} %grad_ref.1), custom_call_target="tpu_custom_call" | custom-call | tf_op jit(solution)/shard_map/pallas_call | solution.py:191
  2.4 0.6 collective-permute-start
  3.0 0.1 collective-permute-start.3
  3.1 1.0 %collective-permute-done = bf16[24,4096]{1,0:T(8,128)(2,1)S(1)} collective-permute-done((bf16[24,4096]{1,0:T(8,128)(2,1)S(1)}, bf16[24,4096]{1,0:T(8,128)(2,1)S(1)}, u32[]{:S(2)}, u32[]{:S(2)}) %collective-permute-start) | collective-permute-done | bytes 196640 | tf_op jit(solution)/shard_map/ppermute | solution.py:197
  4.1 2.9 %collective-permute-start.2 = (bf16[24,4096]{1,0:T(8,128)(2,1)S(1)}, bf16[24,4096]{1,0:T(8,128)(2,1)S(1)}, u32[]{:S(2)}, u32[]{:S(2)}) collective-permute-start(bf16[24,4096]{1,0:T(8,128)(2,1)S(1)} %add.76.refs_1_.refs_3_), channel_id=1, source_target_pairs={{4,0},{8,4},{12,8},{14,12},{10,14},{6,10},{2,6},{0,2},{5,1},{9,5},... | collective-permute-start | bytes 589832 | tf_op jit(solution)/shard_map/ppermute | solution.py:226
  7.0 0.2 collective-permute-start.1
  7.1 0.0 collective-permute-done.3
  7.1 0.1 add.79.refs_11_
  7.2 1.9 %collective-permute-start.14 = (bf16[24,5120]{1,0:T(8,128)(2,1)S(1)}, bf16[24,5120]{1,0:T(8,128)(2,1)S(1)}, u32[]{:S(2)}, u32[]{:S(2)}) collective-permute-start(bf16[24,5120]{1,0:T(8,128)(2,1)S(1)} %add.79.refs_11_), channel_id=1, source_target_pairs={{4,0},{8,4},{12,8},{14,12},{10,14},{6,10},{2,6},{0,2},{5,1},{9,5},... | collective-permute-start | bytes 737288 | tf_op jit(solution)/shard_map/ppermute | solution.py:226
  9.1 0.2 collective-permute-start.6
  9.3 3.5 %collective-permute-done.2.refs_3_.refs_5_ = bf16[24,4096]{1,0:T(8,128)(2,1)S(1)} collective-permute-done((bf16[24,4096]{1,0:T(8,128)(2,1)S(1)}, bf16[24,4096]{1,0:T(8,128)(2,1)S(1)}, u32[]{:S(2)}, u32[]{:S(2)}) %collective-permute-start.2) | collective-permute-done | bytes 196640 | tf_op jit(solution)/shard_map/ppermute | solution.py:226
  12.8 2.0 %collective-permute-done.1.refs_2_.refs_4_ = bf16[24,4096]{1,0:T(8,128)(2,1)S(1)} collective-permute-done((bf16[24,4096]{1,0:T(8,128)(2,1)S(1)}, bf16[24,4096]{1,0:T(8,128)(2,1)S(1)}, u32[]{:S(2)}, u32[]{:S(2)}) %collective-permute-start.1) | collective-permute-done | bytes 196640 | tf_op jit(solution)/shard_map/ppermute | solution.py:225
  14.8 0.1 collective-permute-start.4
  14.9 1.9 %collective-permute-start.5 = (bf16[24,4096]{1,0:T(8,128)(2,1)S(1)}, bf16[24,4096]{1,0:T(8,128)(2,1)S(1)}, u32[]{:S(2)}, u32[]{:S(2)}) collective-permute-start(bf16[24,4096]{1,0:T(8,128)(2,1)S(1)} %collective-permute-done.2.refs_3_.refs_5_), channel_id=1, source_target_pairs={{4,0},{8,4},{12,8},{14,12},{10,14},{6,10},{2,6},{0,2},{5,1},{9,5},... | collective-permute-start | bytes 589832 | tf_op jit(solution)/shard_map/ppermute | solution.py:226
  16.8 1.2 %collective-permute-done.14.refs_13_ = bf16[24,5120]{1,0:T(8,128)(2,1)S(1)} collective-permute-done((bf16[24,5120]{1,0:T(8,128)(2,1)S(1)}, bf16[24,5120]{1,0:T(8,128)(2,1)S(1)}, u32[]{:S(2)}, u32[]{:S(2)}) %collective-permute-start.14) | collective-permute-done | bytes 245792 | tf_op jit(solution)/shard_map/ppermute | solution.py:226
  18.0 2.0 %collective-permute-start.15 = (bf16[24,5120]{1,0:T(8,128)(2,1)S(1)}, bf16[24,5120]{1,0:T(8,128)(2,1)S(1)}, u32[]{:S(2)}, u32[]{:S(2)}) collective-permute-start(bf16[24,5120]{1,0:T(8,128)(2,1)S(1)} %collective-permute-done.14.refs_13_), channel_id=1, source_target_pairs={{4,0},{8,4},{12,8},{14,12},{10,14},{6,10},{2,6},{0,2},{5,1},{9,5},... | collective-permute-start | bytes 737288 | tf_op jit(solution)/shard_map/ppermute | solution.py:226
  20.0 0.0 collective-permute-done.6.refs_12_
  20.0 0.1 collective-permute-start.10
  20.2 2.5 %collective-permute-done.5.refs_5_.refs_7_ = bf16[24,4096]{1,0:T(8,128)(2,1)S(1)} collective-permute-done((bf16[24,4096]{1,0:T(8,128)(2,1)S(1)}, bf16[24,4096]{1,0:T(8,128)(2,1)S(1)}, u32[]{:S(2)}, u32[]{:S(2)}) %collective-permute-start.5) | collective-permute-done | bytes 196640 | tf_op jit(solution)/shard_map/ppermute | solution.py:226
  22.7 1.5 %collective-permute-done.4.refs_4_.refs_6_ = bf16[24,4096]{1,0:T(8,128)(2,1)S(1)} collective-permute-done((bf16[24,4096]{1,0:T(8,128)(2,1)S(1)}, bf16[24,4096]{1,0:T(8,128)(2,1)S(1)}, u32[]{:S(2)}, u32[]{:S(2)}) %collective-permute-start.4) | collective-permute-done | bytes 196640 | tf_op jit(solution)/shard_map/ppermute | solution.py:225
  24.2 0.5 collective-permute-start.7
  24.7 1.5 %collective-permute-start.8 = (bf16[24,4096]{1,0:T(8,128)(2,1)S(1)}, bf16[24,4096]{1,0:T(8,128)(2,1)S(1)}, u32[]{:S(2)}, u32[]{:S(2)}) collective-permute-start(bf16[24,4096]{1,0:T(8,128)(2,1)S(1)} %collective-permute-done.5.refs_5_.refs_7_), channel_id=1, source_target_pairs={{4,0},{8,4},{12,8},{14,12},{10,14},{6,10},{2,6},{0,2},{5,1},{9,5},... | collective-permute-start | bytes 589832 | tf_op jit(solution)/shard_map/ppermute | solution.py:226
  26.3 1.7 %collective-permute-done.15.refs_15_ = bf16[24,5120]{1,0:T(8,128)(2,1)S(1)} collective-permute-done((bf16[24,5120]{1,0:T(8,128)(2,1)S(1)}, bf16[24,5120]{1,0:T(8,128)(2,1)S(1)}, u32[]{:S(2)}, u32[]{:S(2)}) %collective-permute-start.15) | collective-permute-done | bytes 245792 | tf_op jit(solution)/shard_map/ppermute | solution.py:226
  28.0 1.9 %collective-permute-start.16 = (bf16[24,5120]{1,0:T(8,128)(2,1)S(1)}, bf16[24,5120]{1,0:T(8,128)(2,1)S(1)}, u32[]{:S(2)}, u32[]{:S(2)}) collective-permute-start(bf16[24,5120]{1,0:T(8,128)(2,1)S(1)} %collective-permute-done.15.refs_15_), channel_id=1, source_target_pairs={{4,0},{8,4},{12,8},{14,12},{10,14},{6,10},{2,6},{0,2},{5,1},{9,5},... | collective-permute-start | bytes 737288 | tf_op jit(solution)/shard_map/ppermute | solution.py:226
  29.9 0.0 collective-permute-done.10.refs_14_
  29.9 0.1 collective-permute-start.13
  30.1 2.5 %collective-permute-done.8.refs_7_.refs_9_ = bf16[24,4096]{1,0:T(8,128)(2,1)S(1)} collective-permute-done((bf16[24,4096]{1,0:T(8,128)(2,1)S(1)}, bf16[24,4096]{1,0:T(8,128)(2,1)S(1)}, u32[]{:S(2)}, u32[]{:S(2)}) %collective-permute-start.8) | collective-permute-done | bytes 196640 | tf_op jit(solution)/shard_map/ppermute | solution.py:226
  32.6 1.2 %collective-permute-done.7.refs_6_.refs_8_ = bf16[24,4096]{1,0:T(8,128)(2,1)S(1)} collective-permute-done((bf16[24,4096]{1,0:T(8,128)(2,1)S(1)}, bf16[24,4096]{1,0:T(8,128)(2,1)S(1)}, u32[]{:S(2)}, u32[]{:S(2)}) %collective-permute-start.7) | collective-permute-done | bytes 196640 | tf_op jit(solution)/shard_map/ppermute | solution.py:225
  33.8 1.6 %collective-permute-start.12 = (bf16[24,2048]{1,0:T(8,128)(2,1)S(1)}, bf16[24,2048]{1,0:T(8,128)(2,1)S(1)}, u32[]{:S(2)}, u32[]{:S(2)}) collective-permute-start(bf16[24,2048]{1,0:T(8,128)(2,1)S(1)} %slice.19), channel_id=1, source_target_pairs={{4,0},{8,4},{12,8},{14,12},{10,14},{6,10},{2,6},{0,2},{5,1},{9,5},... | collective-permute-start | bytes 294920 | tf_op jit(solution)/shard_map/ppermute | solution.py:226
  35.4 0.4 collective-permute-start.11
  35.8 0.1 collective-permute-start.9
  35.9 3.0 %collective-permute-done.13.refs_16_ = bf16[24,5120]{1,0:T(8,128)(2,1)S(1)} collective-permute-done((bf16[24,5120]{1,0:T(8,128)(2,1)S(1)}, bf16[24,5120]{1,0:T(8,128)(2,1)S(1)}, u32[]{:S(2)}, u32[]{:S(2)}) %collective-permute-start.13) | collective-permute-done | bytes 245792 | tf_op jit(solution)/shard_map/ppermute | solution.py:225
  38.9 0.0 collective-permute-done.12
  38.9 1.1 %collective-permute-done.11 = bf16[24,2048]{1,0:T(8,128)(2,1)S(1)} collective-permute-done((bf16[24,2048]{1,0:T(8,128)(2,1)S(1)}, bf16[24,2048]{1,0:T(8,128)(2,1)S(1)}, u32[]{:S(2)}, u32[]{:S(2)}) %collective-permute-start.11) | collective-permute-done | bytes 98336 | tf_op jit(solution)/shard_map/ppermute | solution.py:225
  40.0 0.0 collective-permute-done.16.refs_17_
  40.1 0.1 collective-permute-start.17
  40.2 0.5 collective-permute-start.19
  40.7 1.6 %collective-permute-start.20 = (bf16[24,2560]{1,0:T(8,128)(2,1)S(1)}, bf16[24,2560]{1,0:T(8,128)(2,1)S(1)}, u32[]{:S(2)}, u32[]{:S(2)}) collective-permute-start(bf16[24,2560]{1,0:T(8,128)(2,1)S(1)} %slice.21), channel_id=1, source_target_pairs={{4,0},{8,4},{12,8},{14,12},{10,14},{6,10},{2,6},{0,2},{5,1},{9,5},... | collective-permute-start | bytes 368648 | tf_op jit(solution)/shard_map/ppermute | solution.py:226
  42.3 0.1 collective-permute-start.18
  42.4 0.0 collective-permute-done.17
  42.4 0.0 collective-permute-done.9
  42.4 0.1 broadcast_select_fusion.1
  42.5 3.8 %shard_map.51 = (f32[1792,7168]{1,0:T(8,128)}, bf16[1024,192]{1,0:T(8,128)(2,1)S(1)}) custom-call(bf16[192,1024]{1,0:T(8,128)(2,1)S(1)} %pad_maximum_fusion.refs_0_, bf16[24,4096]{1,0:T(8,128)(2,1)S(1)} %add.76.refs_1_.refs_3_, bf16[24,4096]{1,0:T(8,128)(2,1)S(1)} %collective-permute-done.1.refs_2_.refs_4_, ...), custom_call_target="tpu_custom_call" | custom-call | flops 805306368 | bytes 8388608 | tf_op jit(solution)/shard_map/pallas_call | solution.py:123
  46.4 0.0 collective-permute-done.19
  46.4 0.0 collective-permute-done.20
  46.5 0.5 collective-permute-start.21
  47.0 3.7 %shard_map.52.refs_19_ = f32[1792,7168]{1,0:T(8,128)} custom-call(bf16[1024,192]{1,0:T(8,128)(2,1)S(1)} %get-tuple-element.43.refs_0_, bf16[24,4096]{1,0:T(8,128)(2,1)S(1)} %add.76.refs_1_.refs_3_, bf16[24,4096]{1,0:T(8,128)(2,1)S(1)} %collective-permute-done.1.refs_2_.refs_4_, ...), custom_call_target="tpu_custom_call", output_to_operand_aliasing={{}: (9, {})} | custom-call | flops 805306368 | bytes 8388608 | tf_op jit(solution)/shard_map/pallas_call | solution.py:123
  50.7 0.0 collective-permute-done.21
  50.7 0.0 collective-permute-done.18
  50.9 13.1 %shard_map.53 = (f32[1792,7168]{1,0:T(8,128)}, f32[512,2048]{1,0:T(8,128)}) custom-call(bf16[1024,192]{1,0:T(8,128)(2,1)S(1)} %get-tuple-element.43.refs_0_, bf16[192,768]{1,0:T(8,128)(2,1)S(1)} %fusion.refs_1_, bf16[192,512]{1,0:T(8,128)(2,1)S(1)} %pad_maximum_fusion.1.refs_2_, ...), custom_call_target="tpu_custom_call", output_to_operand_aliasing={{0}: (19, {})} | custom-call | flops 3724541952 | bytes 38797312 | tf_op jit(solution)/shard_map/pallas_call | solution.py:123
  (47 shorter events, 0.5 us)
Async XLA Ops:
  2.4 1.6 %collective-permute-start = (bf16[24,4096]{1,0:T(8,128)(2,1)S(1)}, bf16[24,4096]{1,0:T(8,128)(2,1)S(1)}, u32[]{:S(2)}, u32[]{:S(2)}) collective-permute-start(bf16[24,4096]{1,0:T(8,128)(2,1)S(1)} %get-tuple-element.27), channel_id=1, source_target_pairs={{0,1},{1,0},{2,3},{3,2},{4,5},{5,4},{6,7},{7,6},{8,9},{9,8},{10,11... | collective-permute-start | bytes 589832 | tf_op jit(solution)/shard_map/ppermute | solution.py:197
  3.0 4.1 %collective-permute-start.3 = (bf16[24,5120]{1,0:T(8,128)(2,1)S(1)}, bf16[24,5120]{1,0:T(8,128)(2,1)S(1)}, u32[]{:S(2)}, u32[]{:S(2)}) collective-permute-start(bf16[24,5120]{1,0:T(8,128)(2,1)S(1)} %get-tuple-element.29), channel_id=1, source_target_pairs={{0,1},{1,0},{2,3},{3,2},{4,5},{5,4},{6,7},{7,6},{8,9},{9,8},{10,11... | collective-permute-start | bytes 737288 | tf_op jit(solution)/shard_map/ppermute | solution.py:197
  4.1 8.6 %collective-permute-start.2 = (bf16[24,4096]{1,0:T(8,128)(2,1)S(1)}, bf16[24,4096]{1,0:T(8,128)(2,1)S(1)}, u32[]{:S(2)}, u32[]{:S(2)}) collective-permute-start(bf16[24,4096]{1,0:T(8,128)(2,1)S(1)} %add.76.refs_1_.refs_3_), channel_id=1, source_target_pairs={{4,0},{8,4},{12,8},{14,12},{10,14},{6,10},{2,6},{0,2},{5,1},{9,5},... | collective-permute-start | bytes 589832 | tf_op jit(solution)/shard_map/ppermute | solution.py:226
  7.0 7.8 %collective-permute-start.1 = (bf16[24,4096]{1,0:T(8,128)(2,1)S(1)}, bf16[24,4096]{1,0:T(8,128)(2,1)S(1)}, u32[]{:S(2)}, u32[]{:S(2)}) collective-permute-start(bf16[24,4096]{1,0:T(8,128)(2,1)S(1)} %add.76.refs_1_.refs_3_), channel_id=1, source_target_pairs={{0,4},{4,8},{8,12},{12,14},{14,10},{10,6},{6,2},{2,0},{1,5},{5,9},... | collective-permute-start | bytes 589832 | tf_op jit(solution)/shard_map/ppermute | solution.py:225
  7.2 10.8 %collective-permute-start.14 = (bf16[24,5120]{1,0:T(8,128)(2,1)S(1)}, bf16[24,5120]{1,0:T(8,128)(2,1)S(1)}, u32[]{:S(2)}, u32[]{:S(2)}) collective-permute-start(bf16[24,5120]{1,0:T(8,128)(2,1)S(1)} %add.79.refs_11_), channel_id=1, source_target_pairs={{4,0},{8,4},{12,8},{14,12},{10,14},{6,10},{2,6},{0,2},{5,1},{9,5},... | collective-permute-start | bytes 737288 | tf_op jit(solution)/shard_map/ppermute | solution.py:226
  9.1 10.9 %collective-permute-start.6 = (bf16[24,5120]{1,0:T(8,128)(2,1)S(1)}, bf16[24,5120]{1,0:T(8,128)(2,1)S(1)}, u32[]{:S(2)}, u32[]{:S(2)}) collective-permute-start(bf16[24,5120]{1,0:T(8,128)(2,1)S(1)} %add.79.refs_11_), channel_id=1, source_target_pairs={{0,4},{4,8},{8,12},{12,14},{14,10},{10,6},{6,2},{2,0},{1,5},{5,9},... | collective-permute-start | bytes 737288 | tf_op jit(solution)/shard_map/ppermute | solution.py:225
  14.8 9.5 %collective-permute-start.4 = (bf16[24,4096]{1,0:T(8,128)(2,1)S(1)}, bf16[24,4096]{1,0:T(8,128)(2,1)S(1)}, u32[]{:S(2)}, u32[]{:S(2)}) collective-permute-start(bf16[24,4096]{1,0:T(8,128)(2,1)S(1)} %collective-permute-done.1.refs_2_.refs_4_), channel_id=1, source_target_pairs={{0,4},{4,8},{8,12},{12,14},{14,10},{10,6},{6,2},{2,0},{1,5},{5,9},... | collective-permute-start | bytes 589832 | tf_op jit(solution)/shard_map/ppermute | solution.py:225
  14.9 7.8 %collective-permute-start.5 = (bf16[24,4096]{1,0:T(8,128)(2,1)S(1)}, bf16[24,4096]{1,0:T(8,128)(2,1)S(1)}, u32[]{:S(2)}, u32[]{:S(2)}) collective-permute-start(bf16[24,4096]{1,0:T(8,128)(2,1)S(1)} %collective-permute-done.2.refs_3_.refs_5_), channel_id=1, source_target_pairs={{4,0},{8,4},{12,8},{14,12},{10,14},{6,10},{2,6},{0,2},{5,1},{9,5},... | collective-permute-start | bytes 589832 | tf_op jit(solution)/shard_map/ppermute | solution.py:226
  18.0 10.0 %collective-permute-start.15 = (bf16[24,5120]{1,0:T(8,128)(2,1)S(1)}, bf16[24,5120]{1,0:T(8,128)(2,1)S(1)}, u32[]{:S(2)}, u32[]{:S(2)}) collective-permute-start(bf16[24,5120]{1,0:T(8,128)(2,1)S(1)} %collective-permute-done.14.refs_13_), channel_id=1, source_target_pairs={{4,0},{8,4},{12,8},{14,12},{10,14},{6,10},{2,6},{0,2},{5,1},{9,5},... | collective-permute-start | bytes 737288 | tf_op jit(solution)/shard_map/ppermute | solution.py:226
  20.0 9.9 %collective-permute-start.10 = (bf16[24,5120]{1,0:T(8,128)(2,1)S(1)}, bf16[24,5120]{1,0:T(8,128)(2,1)S(1)}, u32[]{:S(2)}, u32[]{:S(2)}) collective-permute-start(bf16[24,5120]{1,0:T(8,128)(2,1)S(1)} %collective-permute-done.6.refs_12_), channel_id=1, source_target_pairs={{0,4},{4,8},{8,12},{12,14},{14,10},{10,6},{6,2},{2,0},{1,5},{5,9},... | collective-permute-start | bytes 737288 | tf_op jit(solution)/shard_map/ppermute | solution.py:225
  24.2 9.5 %collective-permute-start.7 = (bf16[24,4096]{1,0:T(8,128)(2,1)S(1)}, bf16[24,4096]{1,0:T(8,128)(2,1)S(1)}, u32[]{:S(2)}, u32[]{:S(2)}) collective-permute-start(bf16[24,4096]{1,0:T(8,128)(2,1)S(1)} %collective-permute-done.4.refs_4_.refs_6_), channel_id=1, source_target_pairs={{0,4},{4,8},{8,12},{12,14},{14,10},{10,6},{6,2},{2,0},{1,5},{5,9},... | collective-permute-start | bytes 589832 | tf_op jit(solution)/shard_map/ppermute | solution.py:225
  24.7 7.8 %collective-permute-start.8 = (bf16[24,4096]{1,0:T(8,128)(2,1)S(1)}, bf16[24,4096]{1,0:T(8,128)(2,1)S(1)}, u32[]{:S(2)}, u32[]{:S(2)}) collective-permute-start(bf16[24,4096]{1,0:T(8,128)(2,1)S(1)} %collective-permute-done.5.refs_5_.refs_7_), channel_id=1, source_target_pairs={{4,0},{8,4},{12,8},{14,12},{10,14},{6,10},{2,6},{0,2},{5,1},{9,5},... | collective-permute-start | bytes 589832 | tf_op jit(solution)/shard_map/ppermute | solution.py:226
  28.0 12.0 %collective-permute-start.16 = (bf16[24,5120]{1,0:T(8,128)(2,1)S(1)}, bf16[24,5120]{1,0:T(8,128)(2,1)S(1)}, u32[]{:S(2)}, u32[]{:S(2)}) collective-permute-start(bf16[24,5120]{1,0:T(8,128)(2,1)S(1)} %collective-permute-done.15.refs_15_), channel_id=1, source_target_pairs={{4,0},{8,4},{12,8},{14,12},{10,14},{6,10},{2,6},{0,2},{5,1},{9,5},... | collective-permute-start | bytes 737288 | tf_op jit(solution)/shard_map/ppermute | solution.py:226
  29.9 9.0 %collective-permute-start.13 = (bf16[24,5120]{1,0:T(8,128)(2,1)S(1)}, bf16[24,5120]{1,0:T(8,128)(2,1)S(1)}, u32[]{:S(2)}, u32[]{:S(2)}) collective-permute-start(bf16[24,5120]{1,0:T(8,128)(2,1)S(1)} %collective-permute-done.10.refs_14_), channel_id=1, source_target_pairs={{0,4},{4,8},{8,12},{12,14},{14,10},{10,6},{6,2},{2,0},{1,5},{5,9},... | collective-permute-start | bytes 737288 | tf_op jit(solution)/shard_map/ppermute | solution.py:225
  33.8 5.2 %collective-permute-start.12 = (bf16[24,2048]{1,0:T(8,128)(2,1)S(1)}, bf16[24,2048]{1,0:T(8,128)(2,1)S(1)}, u32[]{:S(2)}, u32[]{:S(2)}) collective-permute-start(bf16[24,2048]{1,0:T(8,128)(2,1)S(1)} %slice.19), channel_id=1, source_target_pairs={{4,0},{8,4},{12,8},{14,12},{10,14},{6,10},{2,6},{0,2},{5,1},{9,5},... | collective-permute-start | bytes 294920 | tf_op jit(solution)/shard_map/ppermute | solution.py:226
  35.4 4.6 %collective-permute-start.11 = (bf16[24,2048]{1,0:T(8,128)(2,1)S(1)}, bf16[24,2048]{1,0:T(8,128)(2,1)S(1)}, u32[]{:S(2)}, u32[]{:S(2)}) collective-permute-start(bf16[24,2048]{1,0:T(8,128)(2,1)S(1)} %slice.18), channel_id=1, source_target_pairs={{0,4},{4,8},{8,12},{12,14},{14,10},{10,6},{6,2},{2,0},{1,5},{5,9},... | collective-permute-start | bytes 294920 | tf_op jit(solution)/shard_map/ppermute | solution.py:225
  35.8 6.6 %collective-permute-start.9 = (bf16[168,1024]{1,0:T(8,128)(2,1)S(1)}, bf16[168,1024]{1,0:T(8,128)(2,1)S(1)}, u32[]{:S(2)}, u32[]{:S(2)}) collective-permute-start(bf16[168,1024]{1,0:T(8,128)(2,1)S(1)} %dynamic-slice_dynamic-update-slice_fusion), channel_id=1, source_target_pairs={{0,1},{1,0},{2,3},{3,2},{4,5},{5,4},{6,7},{7,6},{8,9},{9,8},{10,11... | collective-permute-start | bytes 1032200 | tf_op jit(solution)/shard_map/ppermute | solution.py:213
  40.1 2.3 %collective-permute-start.17 = (bf16[24,1024]{1,0:T(8,128)(2,1)S(1)}, bf16[24,1024]{1,0:T(8,128)(2,1)S(1)}, u32[]{:S(2)}, u32[]{:S(2)}) collective-permute-start(bf16[24,1024]{1,0:T(8,128)(2,1)S(1)} %constant_dynamic-slice_fusion.16), channel_id=1, source_target_pairs={{0,1},{1,0},{2,3},{3,2},{4,5},{5,4},{6,7},{7,6},{8,9},{9,8},{10,11... | collective-permute-start | bytes 147464 | tf_op jit(solution)/shard_map/ppermute | solution.py:213
  40.2 6.2 %collective-permute-start.19 = (bf16[24,2560]{1,0:T(8,128)(2,1)S(1)}, bf16[24,2560]{1,0:T(8,128)(2,1)S(1)}, u32[]{:S(2)}, u32[]{:S(2)}) collective-permute-start(bf16[24,2560]{1,0:T(8,128)(2,1)S(1)} %slice.20), channel_id=1, source_target_pairs={{0,4},{4,8},{8,12},{12,14},{14,10},{10,6},{6,2},{2,0},{1,5},{5,9},... | collective-permute-start | bytes 368648 | tf_op jit(solution)/shard_map/ppermute | solution.py:225
  40.7 5.7 %collective-permute-start.20 = (bf16[24,2560]{1,0:T(8,128)(2,1)S(1)}, bf16[24,2560]{1,0:T(8,128)(2,1)S(1)}, u32[]{:S(2)}, u32[]{:S(2)}) collective-permute-start(bf16[24,2560]{1,0:T(8,128)(2,1)S(1)} %slice.21), channel_id=1, source_target_pairs={{4,0},{8,4},{12,8},{14,12},{10,14},{6,10},{2,6},{0,2},{5,1},{9,5},... | collective-permute-start | bytes 368648 | tf_op jit(solution)/shard_map/ppermute | solution.py:226
  42.3 8.4 %collective-permute-start.18 = (bf16[168,1280]{1,0:T(8,128)(2,1)S(1)}, bf16[168,1280]{1,0:T(8,128)(2,1)S(1)}, u32[]{:S(2)}, u32[]{:S(2)}) collective-permute-start(bf16[168,1280]{1,0:T(8,128)(2,1)S(1)} %maximum_dynamic-update-slice_fusion), channel_id=1, source_target_pairs={{0,1},{1,0},{2,3},{3,2},{4,5},{5,4},{6,7},{7,6},{8,9},{9,8},{10,11... | collective-permute-start | bytes 1290248 | tf_op jit(solution)/shard_map/ppermute | solution.py:213
  46.5 4.2 %collective-permute-start.21 = (bf16[24,1280]{1,0:T(8,128)(2,1)S(1)}, bf16[24,1280]{1,0:T(8,128)(2,1)S(1)}, u32[]{:S(2)}, u32[]{:S(2)}) collective-permute-start(bf16[24,1280]{1,0:T(8,128)(2,1)S(1)} %pad_maximum_fusion.2), channel_id=1, source_target_pairs={{0,1},{1,0},{2,3},{3,2},{4,5},{5,4},{6,7},{7,6},{8,9},{9,8},{10,11... | collective-permute-start | bytes 184328 | tf_op jit(solution)/shard_map/ppermute | solution.py:213

commit v9 on v8

v9 whole, which is shorter than its diff:
```python
import functools

import jax
import jax.numpy as jnp
from jax import lax
from jax.experimental import pallas as pl
from jax.experimental.pallas import tpu as pltpu
from jax.sharding import PartitionSpec as P


SLOTS, PIECE = 4, 128


def chip_ring(rows):
    width = 2 if rows <= 8 else 4
    depth = rows // width
    order = [z * width for z in range(depth)]
    for step, z in enumerate(reversed(range(depth))):
        columns = range(1, width) if step % 2 == 0 else range(width - 1, 0, -1)
        order += [z * width + x for x in columns]
    return order


def gram_kernel(scale, left_ref, *refs):
    right_refs, out_ref, turned = refs[:-2], refs[-2], refs[-1]

    @pl.when(pl.program_id(0) == 0)
    def _():
        turned[...] = left_ref[...].T

    right = jnp.concatenate([ref[...] for ref in right_refs], axis=0)
    out_ref[...] = jnp.dot(turned[...], right, preferred_element_type=jnp.float32) * scale


def gram(left, rights, scale, steps, tile):
    tokens, height = left.shape
    return pl.pallas_call(
        functools.partial(gram_kernel, scale),
        grid=(steps,),
        in_specs=[pl.BlockSpec((tokens, height), lambda j: (0, 0))]
        + [pl.BlockSpec((part.shape[0], tile), lambda j: (0, j)) for part in rights],
        out_specs=pl.BlockSpec((height, tile), lambda j: (0, j)),
        out_shape=jax.ShapeDtypeStruct((height, steps * tile), jnp.float32),
        scratch_shapes=[pltpu.VMEM((height, tokens), jnp.bfloat16)],
        compiler_params=pltpu.CompilerParams(vmem_limit_bytes=32 * 1024 * 1024),
    )(left, *rights)


def tiles_kernel(scale, cut, rest, grad_tile, shards, *refs):
    first_left, second_left = refs[:2]
    first, second = refs[2 : 2 + shards], refs[2 + shards : 2 + 2 * shards]
    act_out, grad_out, turned, turned_grad, joined, buffer, sems = refs[2 + 2 * shards :]
    act_block, blocks = cut + rest, first[0].shape[1] // cut
    groups = [(turned_grad, second, blocks * rest, grad_tile, grad_tile, grad_out, 0, grad_tile, blocks)]
    groups.append((turned, second, 0, rest, rest, act_out, cut, act_block, blocks))
    for start in range(0, cut, 256):
        groups.append((turned, first, start, cut, 256, act_out, start, act_block, blocks))

    def copy(group, slot, j):
        left, _, _, _, width, out, column, stride, _ = group
        return pltpu.make_async_copy(
            buffer.at[slot, pl.ds(0, left.shape[0]), pl.ds(0, width)],
            out.at[:, pl.ds(pl.multiple_of(column + j * stride, 128), width)],
            sems.at[slot],
        )

    turned_grad[...] = second_left[:, rest:].T
    earlier = None
    for group in groups:

        def step(j, carry, group=group, earlier=earlier):
            left, sources, start, apart, width, _, _, _, _ = group
            height, slot = left.shape[0], lax.rem(j, SLOTS)
            here = pl.ds(pl.multiple_of(start + j * apart, 128), width)
            joined[:, :width] = jnp.concatenate([ref[:, here] for ref in sources], axis=0)

            @pl.when(j >= SLOTS)
            def _():
                copy(group, slot, 0).wait()

            if earlier is not None:

                @pl.when(j < SLOTS)
                def _():
                    copy(earlier, slot, 0).wait()

            for across in range(0, width, 256):
                right = joined[:, across : across + 256]
                for down in range(0, height, PIECE):
                    product = jnp.dot(left[down : down + PIECE, :], right, preferred_element_type=jnp.float32)
                    buffer[slot, down : down + PIECE, across : across + 256] = product * scale
            copy(group, slot, j).start()
            return carry

        lax.fori_loop(0, group[-1], step, 0)
        if earlier is None:
            turned[:cut, :] = first_left[...].T
            turned[cut:, :] = second_left[:, :rest].T
        earlier = group
    for slot in range(SLOTS):
        copy(earlier, slot, 0).wait()


def tiles(scale, cut, rest, first_left, second_left, chains):
    shards = len(chains[0])
    tokens, blocks = first_left.shape[0], chains[0][0].shape[1] // cut
    act_block, grad_block = cut + rest, second_left.shape[1] - rest
    grad_half = chains[1][0].shape[1] - blocks * rest
    act_shape, grad_shape = (act_block, blocks * act_block), (grad_block, grad_half)
    area = act_shape[0] * act_shape[1] + grad_shape[0] * grad_shape[1]
    whole = pl.BlockSpec(memory_space=pltpu.VMEM)
    return pl.pallas_call(
        functools.partial(tiles_kernel, scale, cut, rest, grad_half // blocks, shards),
        in_specs=[whole] * (2 + 2 * shards),
        out_specs=[pl.BlockSpec(memory_space=pl.ANY)] * 2,
        out_shape=[jax.ShapeDtypeStruct(shape, jnp.float32) for shape in (act_shape, grad_shape)],
        scratch_shapes=[
            pltpu.VMEM((act_block, tokens), jnp.bfloat16),
            pltpu.VMEM((grad_block, tokens), jnp.bfloat16),
            pltpu.VMEM((tokens, rest), jnp.bfloat16),
            pltpu.VMEM((SLOTS, act_block, rest), jnp.float32),
            pltpu.SemaphoreType.DMA((SLOTS,)),
        ],
        compiler_params=pltpu.CompilerParams(vmem_limit_bytes=40 * 1024 * 1024),
        cost_estimate=pl.CostEstimate(flops=2 * tokens * area, bytes_accessed=4 * area, transcendentals=0),
    )(first_left, second_left, *chains[0], *chains[1])


def split_kernel(halves, layouts, half_ref, count_ref, act_ref, grad_ref, *out_refs):
    slots = act_ref.shape[0]
    live = lax.broadcasted_iota(jnp.int32, (slots, 128), 0) < count_ref[0]
    for half in range(halves):
        for flip in (1, 0):

            @pl.when((half_ref[0] + flip) % halves == half)
            def _(half=half, flip=flip):
                for chain, layout in enumerate(layouts):
                    target = 0
                    for source, start, width in layout:
                        ref = (grad_ref, act_ref)[source]
                        first = half * (ref.shape[1] // halves) + start
                        values = ref[:, first : first + width]
                        mask = jnp.concatenate([live] * (width // 128), axis=1)
                        masked = jnp.where(mask, values, jnp.zeros_like(values))
                        own = (half + flip) % halves * slots
                        out_ref, columns = out_refs[2 * chain + flip], slice(target, target + width)
                        out_ref[own : own + slots, columns] = masked
                        other = slots - own
                        out_ref[other : other + slots, columns] = jnp.zeros_like(values)
                        target += width


def solution(mesh):
    rows, cols = mesh.shape["row"], mesh.shape["col"]
    order = chip_ring(rows)
    ahead = [(order[p], order[(p + 1) % rows]) for p in range(rows)]
    behind = [(target, source) for source, target in ahead]
    swap = [(0, 1), (1, 0)]
    half_rows = rows // cols
    scale = 1.0 / (9.0 * rows * cols)

    def local(activations, pseudo_grads, row_counts):
        row, col = lax.axis_index("row"), lax.axis_index("col")
        slots, act_width = activations.shape
        grad_width = pseudo_grads.shape[1]
        act_half, grad_half = act_width // cols, grad_width // cols
        act_block, grad_block = act_width // rows, grad_width // rows
        cut = act_block * 4 // 7 if act_block % 1792 == 0 else act_block
        rest = act_block - cut
        widths = [half_rows * cut, half_rows * rest + grad_half]
        if rest == 0:
            layouts = [[(1, 0, act_half)], [(0, 0, grad_half)]]
        else:
            layouts = [
                [(1, j * act_block, cut) for j in range(half_rows)],
                [(1, j * act_block + cut, rest) for j in range(half_rows)] + [(0, 0, grad_half)],
            ]
        pieces = pl.pallas_call(
            functools.partial(split_kernel, cols, layouts),
            in_specs=[pl.BlockSpec(memory_space=pltpu.SMEM)] * 2 + [pl.BlockSpec(memory_space=pltpu.VMEM)] * 2,
            out_specs=[pl.BlockSpec(memory_space=pltpu.VMEM)] * 4,
            out_shape=[pltpu.VMEM((2 * slots, width), jnp.bfloat16) for width in widths for _ in (0, 1)],
        )(col[None], row_counts, activations, pseudo_grads)
        chains = [[pieces[2 * k] + lax.ppermute(pieces[2 * k + 1], "col", swap)] for k in (0, 1)]
        forward = [chain[0] for chain in chains]
        backward = list(forward)
        steps, halfway = [0] * len(chains), rows // 2
        sequence = [0, 1] * halfway
        def left_part(chain, pieces):
            own = []
            for part in chain:
                cuts = [
                    lax.dynamic_slice_in_dim(part, base + (row % half_rows) * size, size, 1) for base, size in pieces
                ]
                own.append(cuts[0] if len(cuts) == 1 else jnp.concatenate(cuts, axis=1))
            groups = [jnp.concatenate(own[:-1], axis=0), own[-1]]
            mine = col == row // half_rows
            return jnp.concatenate([jnp.where(mine, g, lax.ppermute(g, "col", swap)) for g in groups], axis=0)

        previous = ()
        for k in sequence:
            chain = chains[k]
            steps[k] += 1
            ahead_of, _ = lax.optimization_barrier((forward[k], previous))
            behind_of, _ = lax.optimization_barrier((backward[k], previous))
            previous = forward[k]
            if steps[k] < halfway or k == 0:
                forward[k] = lax.ppermute(ahead_of, "row", ahead)
                chain.append(forward[k])
            if steps[k] < halfway or k == 1:
                backward[k] = lax.ppermute(behind_of, "row", behind)
                chain.append(backward[k])

        left_first = left_part(chains[0], [(0, cut)])
        if rest == 0:
            left_grad = left_part(chains[1], [(0, grad_block)])
            act_cov = gram(left_first, chains[0], scale, act_half // 256, 256)
            grad_cov = gram(left_grad, chains[1], scale, grad_half // 256, 256)
        else:
            left_second = left_part(chains[1], [(0, rest), (half_rows * rest, grad_block)])
            act_cov, grad_cov = tiles(scale, cut, rest, left_first, left_second, chains)
        return act_cov, grad_cov

    return jax.shard_map(
        local,
        mesh=mesh,
        in_specs=(
            P(("groups", "row", "col"), None),
            P(("groups", "row", "col"), None),
            P(("groups", "row", "col")),
        ),
        out_specs=(P(("groups", "row"), "col"), P(("groups", "row"), "col")),
        check_vma=False,
    )
```

time: 64.1 us -> 64 us (level)
  waiting for transfers between devices: 21.2 us -> 25.2 us
  starting transfers between devices: 18.8 us -> 16.5 us
  Pallas kernels: 21.8 us -> 20 us
    ppermute x8 -> x7, waiting for transfers between devices: 8.82 us -> 11.2 us  [local(): forward[k] = lax.ppermute(ahead_of, 'row', ahead)]
    pallas_call x3 -> x1, Pallas kernels: 20.6 us -> 18.9 us  [tiles(): pl.pallas_call(functools.partial(tiles_kernel, scale, cut, rest, grad_hal...]
    ppermute x4, waiting for transfers between devices: 0.01 us -> 1.64 us  [left_part(): lax.ppermute(g, 'col', swap)]
    ppermute x8 -> x7, starting transfers between devices: 15.4 us -> 13.8 us  [local(): backward[k] = lax.ppermute(behind_of, 'row', behind)]
    ppermute x8 -> x7, starting transfers between devices: 2.06 us -> 1.22 us  [local(): forward[k] = lax.ppermute(ahead_of, 'row', ahead)]
    ppermute x8 -> x7, waiting for transfers between devices: 11.4 us -> 11.4 us  [local(): backward[k] = lax.ppermute(behind_of, 'row', behind)]
  transfers between devices with their start and end apart: 22 -> 20, of which waited for: 11 -> 12; matrix products, arithmetic and copies ran while one was open for 1% -> 1% of each run, Pallas kernels for 12% -> 0%
where the time goes in v9:
time: 64 us; the launch traced here: 63.8 us
  waiting for transfers between devices  25.2 us (39%)
  Pallas kernels  20 us (31%)
  starting transfers between devices  16.5 us (26%)
  between operations  1.52 us (2%)
    pallas_call x1, Pallas kernels, tiles(): pl.pallas_call(functools.partial(tiles_kernel, scale, cut, rest, grad_hal...  18.9 us
    ppermute x7, starting transfers between devices, local(): backward[k] = lax.ppermute(behind_of, 'row', behind)  13.8 us
    ppermute x7, waiting for transfers between devices, local(): backward[k] = lax.ppermute(behind_of, 'row', behind)  11.4 us
    ppermute x7, waiting for transfers between devices, local(): forward[k] = lax.ppermute(ahead_of, 'row', ahead)  11.2 us
    ppermute x4, waiting for transfers between devices, left_part(): lax.ppermute(g, 'col', swap)  1.64 us
  transfers between devices with their start and end apart: 20, of which 12 were waited for; matrix products, arithmetic and copies ran while one was open for 1% of the time, Pallas kernels for 0%

profile of v9, /device:TPU:0, one launch (start us, length us, event | category | flops | bytes accessed | tf_op | source)
XLA Modules:
  0.0 63.8 jit_solution(2706490871397614111)
XLA Ops:
  1.3 1.1 %shard_map.50 = (bf16[24,4096]{1,0:T(8,128)(2,1)S(1)}, bf16[24,4096]{1,0:T(8,128)(2,1)S(1)}, bf16[24,5120]{1,0:T(8,128)(2,1)S(1)}, bf16[24,5120]{1,0:T(8,128)(2,1)S(1)}) custom-call(s32[1]{0:T(128)} %bitcast.half_ref, s32[1]{0:T(128)S(6)} %copy.17.count_ref, bf16[12,14336]{1,0:T(8,128)(2,1)} %act_ref.1, bf16[12,4096]{1,0:T(8,128)(2,1)} %grad_ref.1), custom_call_target="tpu_custom_call" | custom-call | tf_op jit(solution)/shard_map/pallas_call | solution.py:178
  2.4 0.6 collective-permute-start
  3.0 0.1 collective-permute-start.3
  3.1 1.0 %collective-permute-done = bf16[24,4096]{1,0:T(8,128)(2,1)S(1)} collective-permute-done((bf16[24,4096]{1,0:T(8,128)(2,1)S(1)}, bf16[24,4096]{1,0:T(8,128)(2,1)S(1)}, u32[]{:S(2)}, u32[]{:S(2)}) %collective-permute-start) | collective-permute-done | bytes 196640 | tf_op jit(solution)/shard_map/ppermute | solution.py:184
  4.1 2.9 %collective-permute-start.2 = (bf16[24,4096]{1,0:T(8,128)(2,1)S(1)}, bf16[24,4096]{1,0:T(8,128)(2,1)S(1)}, u32[]{:S(2)}, u32[]{:S(2)}) collective-permute-start(bf16[24,4096]{1,0:T(8,128)(2,1)S(1)} %add.76.refs_2_), channel_id=1, source_target_pairs={{4,0},{8,4},{12,8},{14,12},{10,14},{6,10},{2,6},{0,2},{5,1},{9,5},... | collective-permute-start | bytes 589832 | tf_op jit(solution)/shard_map/ppermute | solution.py:211
  7.0 0.2 collective-permute-start.1
  7.1 0.0 collective-permute-done.3
  7.1 0.1 add.79.refs_10_
  7.2 1.9 %collective-permute-start.13 = (bf16[24,5120]{1,0:T(8,128)(2,1)S(1)}, bf16[24,5120]{1,0:T(8,128)(2,1)S(1)}, u32[]{:S(2)}, u32[]{:S(2)}) collective-permute-start(bf16[24,5120]{1,0:T(8,128)(2,1)S(1)} %add.79.refs_10_), channel_id=1, source_target_pairs={{4,0},{8,4},{12,8},{14,12},{10,14},{6,10},{2,6},{0,2},{5,1},{9,5},... | collective-permute-start | bytes 737288 | tf_op jit(solution)/shard_map/ppermute | solution.py:211
  9.1 0.2 collective-permute-start.6
  9.3 3.5 %collective-permute-done.2.refs_4_ = bf16[24,4096]{1,0:T(8,128)(2,1)S(1)} collective-permute-done((bf16[24,4096]{1,0:T(8,128)(2,1)S(1)}, bf16[24,4096]{1,0:T(8,128)(2,1)S(1)}, u32[]{:S(2)}, u32[]{:S(2)}) %collective-permute-start.2) | collective-permute-done | bytes 196640 | tf_op jit(solution)/shard_map/ppermute | solution.py:211
  12.8 2.0 %collective-permute-done.1.refs_3_ = bf16[24,4096]{1,0:T(8,128)(2,1)S(1)} collective-permute-done((bf16[24,4096]{1,0:T(8,128)(2,1)S(1)}, bf16[24,4096]{1,0:T(8,128)(2,1)S(1)}, u32[]{:S(2)}, u32[]{:S(2)}) %collective-permute-start.1) | collective-permute-done | bytes 196640 | tf_op jit(solution)/shard_map/ppermute | solution.py:208
  14.8 0.1 collective-permute-start.4
  14.9 1.9 %collective-permute-start.5 = (bf16[24,4096]{1,0:T(8,128)(2,1)S(1)}, bf16[24,4096]{1,0:T(8,128)(2,1)S(1)}, u32[]{:S(2)}, u32[]{:S(2)}) collective-permute-start(bf16[24,4096]{1,0:T(8,128)(2,1)S(1)} %collective-permute-done.2.refs_4_), channel_id=1, source_target_pairs={{4,0},{8,4},{12,8},{14,12},{10,14},{6,10},{2,6},{0,2},{5,1},{9,5},... | collective-permute-start | bytes 589832 | tf_op jit(solution)/shard_map/ppermute | solution.py:211
  16.8 1.2 %collective-permute-done.13.refs_12_ = bf16[24,5120]{1,0:T(8,128)(2,1)S(1)} collective-permute-done((bf16[24,5120]{1,0:T(8,128)(2,1)S(1)}, bf16[24,5120]{1,0:T(8,128)(2,1)S(1)}, u32[]{:S(2)}, u32[]{:S(2)}) %collective-permute-start.13) | collective-permute-done | bytes 245792 | tf_op jit(solution)/shard_map/ppermute | solution.py:211
  18.0 2.0 %collective-permute-start.14 = (bf16[24,5120]{1,0:T(8,128)(2,1)S(1)}, bf16[24,5120]{1,0:T(8,128)(2,1)S(1)}, u32[]{:S(2)}, u32[]{:S(2)}) collective-permute-start(bf16[24,5120]{1,0:T(8,128)(2,1)S(1)} %collective-permute-done.13.refs_12_), channel_id=1, source_target_pairs={{4,0},{8,4},{12,8},{14,12},{10,14},{6,10},{2,6},{0,2},{5,1},{9,5},... | collective-permute-start | bytes 737288 | tf_op jit(solution)/shard_map/ppermute | solution.py:211
  20.0 0.0 collective-permute-done.6.refs_11_
  20.0 0.1 collective-permute-start.10
  20.2 2.5 %collective-permute-done.5.refs_6_ = bf16[24,4096]{1,0:T(8,128)(2,1)S(1)} collective-permute-done((bf16[24,4096]{1,0:T(8,128)(2,1)S(1)}, bf16[24,4096]{1,0:T(8,128)(2,1)S(1)}, u32[]{:S(2)}, u32[]{:S(2)}) %collective-permute-start.5) | collective-permute-done | bytes 196640 | tf_op jit(solution)/shard_map/ppermute | solution.py:211
  22.7 1.5 %collective-permute-done.4.refs_5_ = bf16[24,4096]{1,0:T(8,128)(2,1)S(1)} collective-permute-done((bf16[24,4096]{1,0:T(8,128)(2,1)S(1)}, bf16[24,4096]{1,0:T(8,128)(2,1)S(1)}, u32[]{:S(2)}, u32[]{:S(2)}) %collective-permute-start.4) | collective-permute-done | bytes 196640 | tf_op jit(solution)/shard_map/ppermute | solution.py:208
  24.2 0.5 collective-permute-start.7
  24.7 1.5 %collective-permute-start.8 = (bf16[24,4096]{1,0:T(8,128)(2,1)S(1)}, bf16[24,4096]{1,0:T(8,128)(2,1)S(1)}, u32[]{:S(2)}, u32[]{:S(2)}) collective-permute-start(bf16[24,4096]{1,0:T(8,128)(2,1)S(1)} %collective-permute-done.5.refs_6_), channel_id=1, source_target_pairs={{4,0},{8,4},{12,8},{14,12},{10,14},{6,10},{2,6},{0,2},{5,1},{9,5},... | collective-permute-start | bytes 589832 | tf_op jit(solution)/shard_map/ppermute | solution.py:211
  26.3 1.7 %collective-permute-done.14.refs_14_ = bf16[24,5120]{1,0:T(8,128)(2,1)S(1)} collective-permute-done((bf16[24,5120]{1,0:T(8,128)(2,1)S(1)}, bf16[24,5120]{1,0:T(8,128)(2,1)S(1)}, u32[]{:S(2)}, u32[]{:S(2)}) %collective-permute-start.14) | collective-permute-done | bytes 245792 | tf_op jit(solution)/shard_map/ppermute | solution.py:211
  28.0 1.9 %collective-permute-start.16 = (bf16[24,5120]{1,0:T(8,128)(2,1)S(1)}, bf16[24,5120]{1,0:T(8,128)(2,1)S(1)}, u32[]{:S(2)}, u32[]{:S(2)}) collective-permute-start(bf16[24,5120]{1,0:T(8,128)(2,1)S(1)} %collective-permute-done.14.refs_14_), channel_id=1, source_target_pairs={{4,0},{8,4},{12,8},{14,12},{10,14},{6,10},{2,6},{0,2},{5,1},{9,5},... | collective-permute-start | bytes 737288 | tf_op jit(solution)/shard_map/ppermute | solution.py:211
  29.9 0.0 collective-permute-done.10.refs_13_
  29.9 0.1 collective-permute-start.15
  30.1 3.6 %collective-permute-done.7.refs_7_ = bf16[24,4096]{1,0:T(8,128)(2,1)S(1)} collective-permute-done((bf16[24,4096]{1,0:T(8,128)(2,1)S(1)}, bf16[24,4096]{1,0:T(8,128)(2,1)S(1)}, u32[]{:S(2)}, u32[]{:S(2)}) %collective-permute-start.7) | collective-permute-done | bytes 196640 | tf_op jit(solution)/shard_map/ppermute | solution.py:208
  33.7 0.1 collective-permute-start.11
  33.8 0.0 collective-permute-done.8.refs_8_
  33.9 0.1 collective-permute-start.9
  33.9 2.6 %collective-permute-done.16.refs_16_ = bf16[24,5120]{1,0:T(8,128)(2,1)S(1)} collective-permute-done((bf16[24,5120]{1,0:T(8,128)(2,1)S(1)}, bf16[24,5120]{1,0:T(8,128)(2,1)S(1)}, u32[]{:S(2)}, u32[]{:S(2)}) %collective-permute-start.16) | collective-permute-done | bytes 245792 | tf_op jit(solution)/shard_map/ppermute | solution.py:211
  36.5 1.7 %collective-permute-start.18 = (bf16[24,5120]{1,0:T(8,128)(2,1)S(1)}, bf16[24,5120]{1,0:T(8,128)(2,1)S(1)}, u32[]{:S(2)}, u32[]{:S(2)}) collective-permute-start(bf16[24,5120]{1,0:T(8,128)(2,1)S(1)} %collective-permute-done.16.refs_16_), channel_id=1, source_target_pairs={{4,0},{8,4},{12,8},{14,12},{10,14},{6,10},{2,6},{0,2},{5,1},{9,5},... | collective-permute-start | bytes 737288 | tf_op jit(solution)/shard_map/ppermute | solution.py:211
  38.2 3.9 %collective-permute-done.11.refs_9_ = bf16[24,4096]{1,0:T(8,128)(2,1)S(1)} collective-permute-done((bf16[24,4096]{1,0:T(8,128)(2,1)S(1)}, bf16[24,4096]{1,0:T(8,128)(2,1)S(1)}, u32[]{:S(2)}, u32[]{:S(2)}) %collective-permute-start.11) | collective-permute-done | bytes 196640 | tf_op jit(solution)/shard_map/ppermute | solution.py:208
  42.1 0.0 collective-permute-start.12
  42.1 0.0 collective-permute-done.15.refs_15_
  42.2 0.5 collective-permute-start.17
  42.8 0.6 collective-permute-done.12
  43.3 0.0 collective-permute-done.9
  43.4 0.0 collective-permute-done.18.refs_17_
  43.5 0.2 collective-permute-start.19
  43.7 1.1 %collective-permute-done.19 = bf16[24,1280]{1,0:T(8,128)(2,1)S(1)} collective-permute-done((bf16[24,1280]{1,0:T(8,128)(2,1)S(1)}, bf16[24,1280]{1,0:T(8,128)(2,1)S(1)}, u32[]{:S(2)}, u32[]{:S(2)}) %collective-permute-start.19) | collective-permute-done | bytes 61472 | tf_op jit(solution)/shard_map/ppermute | solution.py:198
  44.8 0.0 collective-permute-done.17
  44.8 0.1 broadcast_select_fusion
  44.9 18.9 %shard_map.51 = (f32[1792,7168]{1,0:T(8,128)}, f32[512,2048]{1,0:T(8,128)}) custom-call(bf16[192,1024]{1,0:T(8,128)(2,1)S(1)} %pad_maximum_fusion.1.refs_0_, bf16[192,1280]{1,0:T(8,128)(2,1)S(1)} %pad_maximum_fusion.refs_1_, bf16[24,4096]{1,0:T(8,128)(2,1)S(1)} %add.76.refs_2_, bf16[24,4096]{1,0:T(8,128)(2,1)S(1)} %collective-permute-done.1.refs_3_, ...), custom_call_target="tpu_custom_call" | custom-call | flops 5335154688 | bytes 55574528 | tf_op jit(solution)/shard_map/pallas_call | solution.py:112
  (38 shorter events, 0.4 us)
Async XLA Ops:
  2.4 1.6 %collective-permute-start = (bf16[24,4096]{1,0:T(8,128)(2,1)S(1)}, bf16[24,4096]{1,0:T(8,128)(2,1)S(1)}, u32[]{:S(2)}, u32[]{:S(2)}) collective-permute-start(bf16[24,4096]{1,0:T(8,128)(2,1)S(1)} %get-tuple-element.18), channel_id=1, source_target_pairs={{0,1},{1,0},{2,3},{3,2},{4,5},{5,4},{6,7},{7,6},{8,9},{9,8},{10,11... | collective-permute-start | bytes 589832 | tf_op jit(solution)/shard_map/ppermute | solution.py:184
  3.0 4.1 %collective-permute-start.3 = (bf16[24,5120]{1,0:T(8,128)(2,1)S(1)}, bf16[24,5120]{1,0:T(8,128)(2,1)S(1)}, u32[]{:S(2)}, u32[]{:S(2)}) collective-permute-start(bf16[24,5120]{1,0:T(8,128)(2,1)S(1)} %get-tuple-element.20), channel_id=1, source_target_pairs={{0,1},{1,0},{2,3},{3,2},{4,5},{5,4},{6,7},{7,6},{8,9},{9,8},{10,11... | collective-permute-start | bytes 737288 | tf_op jit(solution)/shard_map/ppermute | solution.py:184
  4.1 8.6 %collective-permute-start.2 = (bf16[24,4096]{1,0:T(8,128)(2,1)S(1)}, bf16[24,4096]{1,0:T(8,128)(2,1)S(1)}, u32[]{:S(2)}, u32[]{:S(2)}) collective-permute-start(bf16[24,4096]{1,0:T(8,128)(2,1)S(1)} %add.76.refs_2_), channel_id=1, source_target_pairs={{4,0},{8,4},{12,8},{14,12},{10,14},{6,10},{2,6},{0,2},{5,1},{9,5},... | collective-permute-start | bytes 589832 | tf_op jit(solution)/shard_map/ppermute | solution.py:211
  7.0 7.8 %collective-permute-start.1 = (bf16[24,4096]{1,0:T(8,128)(2,1)S(1)}, bf16[24,4096]{1,0:T(8,128)(2,1)S(1)}, u32[]{:S(2)}, u32[]{:S(2)}) collective-permute-start(bf16[24,4096]{1,0:T(8,128)(2,1)S(1)} %add.76.refs_2_), channel_id=1, source_target_pairs={{0,4},{4,8},{8,12},{12,14},{14,10},{10,6},{6,2},{2,0},{1,5},{5,9},... | collective-permute-start | bytes 589832 | tf_op jit(solution)/shard_map/ppermute | solution.py:208
  7.2 10.8 %collective-permute-start.13 = (bf16[24,5120]{1,0:T(8,128)(2,1)S(1)}, bf16[24,5120]{1,0:T(8,128)(2,1)S(1)}, u32[]{:S(2)}, u32[]{:S(2)}) collective-permute-start(bf16[24,5120]{1,0:T(8,128)(2,1)S(1)} %add.79.refs_10_), channel_id=1, source_target_pairs={{4,0},{8,4},{12,8},{14,12},{10,14},{6,10},{2,6},{0,2},{5,1},{9,5},... | collective-permute-start | bytes 737288 | tf_op jit(solution)/shard_map/ppermute | solution.py:211
  9.1 10.9 %collective-permute-start.6 = (bf16[24,5120]{1,0:T(8,128)(2,1)S(1)}, bf16[24,5120]{1,0:T(8,128)(2,1)S(1)}, u32[]{:S(2)}, u32[]{:S(2)}) collective-permute-start(bf16[24,5120]{1,0:T(8,128)(2,1)S(1)} %add.79.refs_10_), channel_id=1, source_target_pairs={{0,4},{4,8},{8,12},{12,14},{14,10},{10,6},{6,2},{2,0},{1,5},{5,9},... | collective-permute-start | bytes 737288 | tf_op jit(solution)/shard_map/ppermute | solution.py:208
  14.8 9.5 %collective-permute-start.4 = (bf16[24,4096]{1,0:T(8,128)(2,1)S(1)}, bf16[24,4096]{1,0:T(8,128)(2,1)S(1)}, u32[]{:S(2)}, u32[]{:S(2)}) collective-permute-start(bf16[24,4096]{1,0:T(8,128)(2,1)S(1)} %collective-permute-done.1.refs_3_), channel_id=1, source_target_pairs={{0,4},{4,8},{8,12},{12,14},{14,10},{10,6},{6,2},{2,0},{1,5},{5,9},... | collective-permute-start | bytes 589832 | tf_op jit(solution)/shard_map/ppermute | solution.py:208
  14.9 7.8 %collective-permute-start.5 = (bf16[24,4096]{1,0:T(8,128)(2,1)S(1)}, bf16[24,4096]{1,0:T(8,128)(2,1)S(1)}, u32[]{:S(2)}, u32[]{:S(2)}) collective-permute-start(bf16[24,4096]{1,0:T(8,128)(2,1)S(1)} %collective-permute-done.2.refs_4_), channel_id=1, source_target_pairs={{4,0},{8,4},{12,8},{14,12},{10,14},{6,10},{2,6},{0,2},{5,1},{9,5},... | collective-permute-start | bytes 589832 | tf_op jit(solution)/shard_map/ppermute | solution.py:211
  18.0 10.0 %collective-permute-start.14 = (bf16[24,5120]{1,0:T(8,128)(2,1)S(1)}, bf16[24,5120]{1,0:T(8,128)(2,1)S(1)}, u32[]{:S(2)}, u32[]{:S(2)}) collective-permute-start(bf16[24,5120]{1,0:T(8,128)(2,1)S(1)} %collective-permute-done.13.refs_12_), channel_id=1, source_target_pairs={{4,0},{8,4},{12,8},{14,12},{10,14},{6,10},{2,6},{0,2},{5,1},{9,5},... | collective-permute-start | bytes 737288 | tf_op jit(solution)/shard_map/ppermute | solution.py:211
  20.0 9.9 %collective-permute-start.10 = (bf16[24,5120]{1,0:T(8,128)(2,1)S(1)}, bf16[24,5120]{1,0:T(8,128)(2,1)S(1)}, u32[]{:S(2)}, u32[]{:S(2)}) collective-permute-start(bf16[24,5120]{1,0:T(8,128)(2,1)S(1)} %collective-permute-done.6.refs_11_), channel_id=1, source_target_pairs={{0,4},{4,8},{8,12},{12,14},{14,10},{10,6},{6,2},{2,0},{1,5},{5,9},... | collective-permute-start | bytes 737288 | tf_op jit(solution)/shard_map/ppermute | solution.py:208
  24.2 9.5 %collective-permute-start.7 = (bf16[24,4096]{1,0:T(8,128)(2,1)S(1)}, bf16[24,4096]{1,0:T(8,128)(2,1)S(1)}, u32[]{:S(2)}, u32[]{:S(2)}) collective-permute-start(bf16[24,4096]{1,0:T(8,128)(2,1)S(1)} %collective-permute-done.4.refs_5_), channel_id=1, source_target_pairs={{0,4},{4,8},{8,12},{12,14},{14,10},{10,6},{6,2},{2,0},{1,5},{5,9},... | collective-permute-start | bytes 589832 | tf_op jit(solution)/shard_map/ppermute | solution.py:208
  24.7 9.1 %collective-permute-start.8 = (bf16[24,4096]{1,0:T(8,128)(2,1)S(1)}, bf16[24,4096]{1,0:T(8,128)(2,1)S(1)}, u32[]{:S(2)}, u32[]{:S(2)}) collective-permute-start(bf16[24,4096]{1,0:T(8,128)(2,1)S(1)} %collective-permute-done.5.refs_6_), channel_id=1, source_target_pairs={{4,0},{8,4},{12,8},{14,12},{10,14},{6,10},{2,6},{0,2},{5,1},{9,5},... | collective-permute-start | bytes 589832 | tf_op jit(solution)/shard_map/ppermute | solution.py:211
  28.0 8.5 %collective-permute-start.16 = (bf16[24,5120]{1,0:T(8,128)(2,1)S(1)}, bf16[24,5120]{1,0:T(8,128)(2,1)S(1)}, u32[]{:S(2)}, u32[]{:S(2)}) collective-permute-start(bf16[24,5120]{1,0:T(8,128)(2,1)S(1)} %collective-permute-done.14.refs_14_), channel_id=1, source_target_pairs={{4,0},{8,4},{12,8},{14,12},{10,14},{6,10},{2,6},{0,2},{5,1},{9,5},... | collective-permute-start | bytes 737288 | tf_op jit(solution)/shard_map/ppermute | solution.py:211
  29.9 12.2 %collective-permute-start.15 = (bf16[24,5120]{1,0:T(8,128)(2,1)S(1)}, bf16[24,5120]{1,0:T(8,128)(2,1)S(1)}, u32[]{:S(2)}, u32[]{:S(2)}) collective-permute-start(bf16[24,5120]{1,0:T(8,128)(2,1)S(1)} %collective-permute-done.10.refs_13_), channel_id=1, source_target_pairs={{0,4},{4,8},{8,12},{12,14},{14,10},{10,6},{6,2},{2,0},{1,5},{5,9},... | collective-permute-start | bytes 737288 | tf_op jit(solution)/shard_map/ppermute | solution.py:208
  33.7 8.4 %collective-permute-start.11 = (bf16[24,4096]{1,0:T(8,128)(2,1)S(1)}, bf16[24,4096]{1,0:T(8,128)(2,1)S(1)}, u32[]{:S(2)}, u32[]{:S(2)}) collective-permute-start(bf16[24,4096]{1,0:T(8,128)(2,1)S(1)} %collective-permute-done.7.refs_7_), channel_id=1, source_target_pairs={{0,4},{4,8},{8,12},{12,14},{14,10},{10,6},{6,2},{2,0},{1,5},{5,9},... | collective-permute-start | bytes 589832 | tf_op jit(solution)/shard_map/ppermute | solution.py:208
  33.9 9.5 %collective-permute-start.9 = (bf16[168,1024]{1,0:T(8,128)(2,1)S(1)}, bf16[168,1024]{1,0:T(8,128)(2,1)S(1)}, u32[]{:S(2)}, u32[]{:S(2)}) collective-permute-start(bf16[168,1024]{1,0:T(8,128)(2,1)S(1)} %dynamic-slice_dynamic-update-slice_fusion), channel_id=1, source_target_pairs={{0,1},{1,0},{2,3},{3,2},{4,5},{5,4},{6,7},{7,6},{8,9},{9,8},{10,11... | collective-permute-start | bytes 1032200 | tf_op jit(solution)/shard_map/ppermute | solution.py:198
  36.5 6.9 %collective-permute-start.18 = (bf16[24,5120]{1,0:T(8,128)(2,1)S(1)}, bf16[24,5120]{1,0:T(8,128)(2,1)S(1)}, u32[]{:S(2)}, u32[]{:S(2)}) collective-permute-start(bf16[24,5120]{1,0:T(8,128)(2,1)S(1)} %collective-permute-done.16.refs_16_), channel_id=1, source_target_pairs={{4,0},{8,4},{12,8},{14,12},{10,14},{6,10},{2,6},{0,2},{5,1},{9,5},... | collective-permute-start | bytes 737288 | tf_op jit(solution)/shard_map/ppermute | solution.py:211
  42.1 1.2 %collective-permute-start.12 = (bf16[24,1024]{1,0:T(8,128)(2,1)S(1)}, bf16[24,1024]{1,0:T(8,128)(2,1)S(1)}, u32[]{:S(2)}, u32[]{:S(2)}) collective-permute-start(bf16[24,1024]{1,0:T(8,128)(2,1)S(1)} %constant_dynamic-slice_fusion.16), channel_id=1, source_target_pairs={{0,1},{1,0},{2,3},{3,2},{4,5},{5,4},{6,7},{7,6},{8,9},{9,8},{10,11... | collective-permute-start | bytes 147464 | tf_op jit(solution)/shard_map/ppermute | solution.py:198
  42.2 2.6 %collective-permute-start.17 = (bf16[168,1280]{1,0:T(8,128)(2,1)S(1)}, bf16[168,1280]{1,0:T(8,128)(2,1)S(1)}, u32[]{:S(2)}, u32[]{:S(2)}) collective-permute-start(bf16[168,1280]{1,0:T(8,128)(2,1)S(1)} %maximum_dynamic-update-slice_fusion), channel_id=1, source_target_pairs={{0,1},{1,0},{2,3},{3,2},{4,5},{5,4},{6,7},{7,6},{8,9},{9,8},{10,11... | collective-permute-start | bytes 1290248 | tf_op jit(solution)/shard_map/ppermute | solution.py:198
  43.5 1.3 %collective-permute-start.19 = (bf16[24,1280]{1,0:T(8,128)(2,1)S(1)}, bf16[24,1280]{1,0:T(8,128)(2,1)S(1)}, u32[]{:S(2)}, u32[]{:S(2)}) collective-permute-start(bf16[24,1280]{1,0:T(8,128)(2,1)S(1)} %pad_maximum_fusion.2), channel_id=1, source_target_pairs={{0,1},{1,0},{2,3},{3,2},{4,5},{5,4},{6,7},{7,6},{8,9},{9,8},{10,11... | collective-permute-start | bytes 184328 | tf_op jit(solution)/shard_map/ppermute | solution.py:198

commit v10 on v8

--- a/solution.py
+++ b/solution.py
@@ -170,6 +170,9 @@
     behind = [(target, source) for source, target in ahead]
     swap = [(0, 1), (1, 0)]
     half_rows = rows // cols
+    across = [
+        (source * cols + target // half_rows, target * cols + 1 - target // half_rows) for source, target in behind
+    ]
     scale = 1.0 / (9.0 * rows * cols)
 
     def local(activations, pseudo_grads, row_counts):
@@ -199,60 +202,55 @@
         backward = list(forward)
         steps, halfway = [0] * len(chains), rows // 2
         sequence = [0, 1] * halfway
-        def left_part(chain, pieces, hold=None):
-            own = []
-            for part in chain:
-                cuts = [
-                    lax.dynamic_slice_in_dim(part, base + (row % half_rows) * size, size, 1) for base, size in pieces
-                ]
-                own.append(cuts[0] if len(cuts) == 1 else jnp.concatenate(cuts, axis=1))
-            groups = [jnp.concatenate(own[:-1], axis=0), own[-1]]
-            mine = col == row // half_rows
-            if hold is not None:
-                hold.append(groups[1])
-            return jnp.concatenate([jnp.where(mine, g, lax.ppermute(g, "col", swap)) for g in groups], axis=0)
-
-        previous, hold, left_first = (), [], None
+        mine = col == row // half_rows
+
+        def block_of(part, pieces, block_row):
+            cuts = [
+                lax.dynamic_slice_in_dim(part, base + (block_row % half_rows) * size, size, 1) for base, size in pieces
+            ]
+            return cuts[0] if len(cuts) == 1 else jnp.concatenate(cuts, axis=1)
+
+        def left_part(chain, pieces, direct=None):
+            own = [block_of(part, pieces, row) for part in chain]
+            early = jnp.concatenate(own[:-1], axis=0)
+            late = lax.ppermute(own[-1], "col", swap) if direct is None else direct
+            early = jnp.where(mine, early, lax.ppermute(early, "col", swap))
+            return jnp.concatenate([early, jnp.where(mine, own[-1], late)], axis=0)
+
+        first_pieces = [(0, cut)]
+        second_pieces = [(0, rest), (half_rows * rest, grad_block)] if rest else [(0, grad_block)]
+        previous = ()
         for k in sequence:
-            chain, middle = chains[k], widths[k] // 2
+            chain = chains[k]
             steps[k] += 1
-            final = steps[k] == halfway
             ahead_of, _ = lax.optimization_barrier((forward[k], previous))
-            behind_of, _ = lax.optimization_barrier((backward[k], (previous, hold)))
+            behind_of, _ = lax.optimization_barrier((backward[k], previous))
             previous = forward[k]
-            if final:
-                ahead_of, behind_of = ahead_of[:, :middle], behind_of[:, middle:]
-            forward[k] = lax.ppermute(ahead_of, "row", ahead)
-            backward[k] = lax.ppermute(behind_of, "row", behind)
-            if not final:
-                chain += [forward[k], backward[k]]
-                latest = (forward[k], backward[k])
-            elif k == 0:
-                last_first, _ = lax.optimization_barrier(((forward[k], backward[k]), latest))
-                chain.append(jnp.concatenate(last_first, axis=1))
-                left_first = left_part(chain, [(0, cut)], hold)
-
-        act_shape, grad_shape = (act_block, act_half), (grad_block, grad_half)
+            if steps[k] < halfway or k == 0:
+                forward[k] = lax.ppermute(ahead_of, "row", ahead)
+                chain.append(forward[k])
+            if steps[k] < halfway or k == 1:
+                backward[k] = lax.ppermute(behind_of, "row", behind)
+                chain.append(backward[k])
+            if steps[k] == halfway and k == 1:
+                receiver = jnp.asarray([target for _, target in sorted(behind)], jnp.int32)[row]
+                direct = lax.ppermute(block_of(behind_of, second_pieces, receiver), ("row", "col"), across)
+
+        left_first = left_part(chains[0], first_pieces)
         if rest == 0:
-            chains[1].append(jnp.concatenate((forward[1], backward[1]), axis=1))
-            left_grad = left_part(chains[1], [(0, grad_block)])
+            left_grad = left_part(chains[1], second_pieces, direct)
             act_cov = gram(left_first, chains[0], scale, act_half // 256, 256)
             grad_cov = gram(left_grad, chains[1], scale, grad_half // 256, 256)
         else:
-            grad_first = half_rows * rest
             first_part, second_part = (0, 0, cut, cut), (1, 0, rest, rest)
-            grad_part = (1, grad_first, grad_block, grad_block)
-
-            def square(part, lefts, out, **more):
-                starts = [part * cut // 2, part * cut // 2 + cut // 4]
-                groups = [(0, cut, (0, at, cut, cut // 4), 0, 0, at, act_block, half_rows) for at in starts]
-                return tiles(scale, groups, lefts, [chains[0]], [act_shape], out, **more)
-
-            act_cov, turned_first = square(0, [left_first], None, hand_on=True)
-            last_second, act_cov = lax.optimization_barrier(((forward[1], backward[1]), act_cov))
-            chains[1].append(jnp.concatenate(last_second, axis=1))
-            left_second = left_part(chains[1], [(0, rest), (grad_first, grad_block)])
-            (act_cov,) = square(1, [turned_first], act_cov, ready=[True])
+            grad_part = (1, half_rows * rest, grad_block, grad_block)
+            act_shape, grad_shape = (act_block, act_half), (grad_block, grad_half)
+            groups = [
+                (0, cut, (0, start, cut, cut // 2), 0, 0, start, act_block, half_rows) for start in (0, cut // 2)
+            ]
+            act_cov, turned_first = tiles(scale, groups, [left_first], [chains[0]], [act_shape], hand_on=True)
+            (chains[1][-1], direct), act_cov = lax.optimization_barrier(((chains[1][-1], direct), act_cov))
+            left_second = left_part(chains[1], second_pieces, direct)
             act_cov, grad_cov = tiles(
                 scale,
                 [

time: 64.1 us -> 65.8 us (1.027)
  between operations: 1.62 us -> 3.58 us
  local copies, waits for them, and re-layouts: 0.24 us -> 1.42 us
  Pallas kernels: 21.8 us -> 20.8 us
  starting transfers between devices: 18.8 us -> 17.9 us
    ppermute x8 -> x7, starting transfers between devices: 15.4 us -> 13.9 us  [local(): backward[k] = lax.ppermute(behind_of, 'row', behind)]
    ppermute x4, starting transfers between devices: 0.76 us -> 2.22 us  [the longest x1 1.62 us: local(): lax.ppermute(block_of(behind_of, second_pieces, receiver), ('row', 'col')...]
    dynamic_slice x17 -> x20, local copies, waits for them, and re-layouts: 0.14 us -> 1.39 us  [the longest x1 1.24 us: local(): jnp.asarray([target for _, target in sorted(behind)], jnp.int32)[row]]
    ppermute x2, waiting for transfers between devices: 0.99 us -> 0.01 us  [local(): lax.ppermute(pieces[2 * k + 1], 'col', swap)]
    pallas_call x3 -> x2, Pallas kernels: 20.6 us -> 19.7 us  [tiles(): pl.pallas_call(functools.partial(tiles_kernel, scale, groups, ready, [len...]
    ppermute x8 -> x7, starting transfers between devices: 2.06 us -> 1.23 us  [local(): forward[k] = lax.ppermute(ahead_of, 'row', ahead)]
    ppermute x8 -> x7, waiting for transfers between devices: 8.82 us -> 9.51 us  [local(): forward[k] = lax.ppermute(ahead_of, 'row', ahead)]
    ppermute x8 -> x7, waiting for transfers between devices: 11.4 us -> 11.4 us  [local(): backward[k] = lax.ppermute(behind_of, 'row', behind)]
  transfers between devices with their start and end apart: 22 -> 20, of which waited for: 11 -> 10; matrix products, arithmetic and copies ran while one was open for 1% -> 3% of each run, Pallas kernels for 12% -> 10%
where the time goes in v10:
time: 65.8 us; the launch traced here: 65.6 us
  waiting for transfers between devices  21.5 us (33%)
  Pallas kernels  20.8 us (32%)
  starting transfers between devices  17.9 us (27%)
  between operations  3.58 us (5%)
  local copies, waits for them, and re-layouts  1.42 us (2%)
    pallas_call x2, Pallas kernels, tiles(): pl.pallas_call(functools.partial(tiles_kernel, scale, groups, ready, [len...  19.7 us
    ppermute x7, starting transfers between devices, local(): backward[k] = lax.ppermute(behind_of, 'row', behind)  13.9 us
    ppermute x7, waiting for transfers between devices, local(): backward[k] = lax.ppermute(behind_of, 'row', behind)  11.4 us
    ppermute x7, waiting for transfers between devices, local(): forward[k] = lax.ppermute(ahead_of, 'row', ahead)  9.51 us
    ppermute x1, starting transfers between devices, local(): lax.ppermute(block_of(behind_of, second_pieces, receiver), ('row', 'col')...  1.62 us
  transfers between devices with their start and end apart: 20, of which 10 were waited for; matrix products, arithmetic and copies ran while one was open for 3% of the time, Pallas kernels for 10%

profile of v10, /device:TPU:0, one launch (start us, length us, event | category | flops | bytes accessed | tf_op | source)
XLA Modules:
  0.0 65.6 jit_solution(33979727075803838)
XLA Ops:
  1.3 1.1 %shard_map.59 = (bf16[24,4096]{1,0:T(8,128)(2,1)S(1)}, bf16[24,4096]{1,0:T(8,128)(2,1)S(1)}, bf16[24,5120]{1,0:T(8,128)(2,1)S(1)}, bf16[24,5120]{1,0:T(8,128)(2,1)S(1)}) custom-call(s32[1]{0:T(128)} %bitcast.half_ref, s32[1]{0:T(128)S(6)} %copy.20.count_ref, bf16[12,14336]{1,0:T(8,128)(2,1)} %act_ref.1, bf16[12,4096]{1,0:T(8,128)(2,1)} %grad_ref.1), custom_call_target="tpu_custom_call" | custom-call | tf_op jit(solution)/shard_map/pallas_call | solution.py:194
  2.4 0.6 collective-permute-start
  3.0 0.1 collective-permute-start.3
  3.1 1.2 %dynamic_slice.103 = s32[1]{0:T(128)} dynamic-slice(s32[8]{0:T(128)} %constant.106.clone, s32[]{:T(128)S(6)} %select_n.146), dynamic_slice_sizes={1} | dynamic-slice | bytes 12 | tf_op jit(solution)/shard_map/dynamic_slice | solution.py:236
  6.3 0.0 collective-permute-done
  6.4 2.9 %collective-permute-start.2 = (bf16[24,4096]{1,0:T(8,128)(2,1)S(1)}, bf16[24,4096]{1,0:T(8,128)(2,1)S(1)}, u32[]{:S(2)}, u32[]{:S(2)}) collective-permute-start(bf16[24,4096]{1,0:T(8,128)(2,1)S(1)} %add.94.refs_1_.refs_3_), channel_id=1, source_target_pairs={{4,0},{8,4},{12,8},{14,12},{10,14},{6,10},{2,6},{0,2},{5,1},{9,5},... | collective-permute-start | bytes 589832 | tf_op jit(solution)/shard_map/ppermute | solution.py:233
  9.3 0.2 collective-permute-start.1
  9.5 0.0 collective-permute-done.3
  9.5 0.1 add.97.refs_11_
  9.5 1.9 %collective-permute-start.13 = (bf16[24,5120]{1,0:T(8,128)(2,1)S(1)}, bf16[24,5120]{1,0:T(8,128)(2,1)S(1)}, u32[]{:S(2)}, u32[]{:S(2)}) collective-permute-start(bf16[24,5120]{1,0:T(8,128)(2,1)S(1)} %add.97.refs_11_), channel_id=1, source_target_pairs={{4,0},{8,4},{12,8},{14,12},{10,14},{6,10},{2,6},{0,2},{5,1},{9,5},... | collective-permute-start | bytes 737288 | tf_op jit(solution)/shard_map/ppermute | solution.py:233
  11.5 0.2 collective-permute-start.6
  11.6 3.5 %collective-permute-done.2.refs_3_.refs_5_ = bf16[24,4096]{1,0:T(8,128)(2,1)S(1)} collective-permute-done((bf16[24,4096]{1,0:T(8,128)(2,1)S(1)}, bf16[24,4096]{1,0:T(8,128)(2,1)S(1)}, u32[]{:S(2)}, u32[]{:S(2)}) %collective-permute-start.2) | collective-permute-done | bytes 196640 | tf_op jit(solution)/shard_map/ppermute | solution.py:233
  15.1 2.0 %collective-permute-done.1.refs_2_.refs_4_ = bf16[24,4096]{1,0:T(8,128)(2,1)S(1)} collective-permute-done((bf16[24,4096]{1,0:T(8,128)(2,1)S(1)}, bf16[24,4096]{1,0:T(8,128)(2,1)S(1)}, u32[]{:S(2)}, u32[]{:S(2)}) %collective-permute-start.1) | collective-permute-done | bytes 196640 | tf_op jit(solution)/shard_map/ppermute | solution.py:230
  17.1 0.1 collective-permute-start.4
  17.2 1.9 %collective-permute-start.5 = (bf16[24,4096]{1,0:T(8,128)(2,1)S(1)}, bf16[24,4096]{1,0:T(8,128)(2,1)S(1)}, u32[]{:S(2)}, u32[]{:S(2)}) collective-permute-start(bf16[24,4096]{1,0:T(8,128)(2,1)S(1)} %collective-permute-done.2.refs_3_.refs_5_), channel_id=1, source_target_pairs={{4,0},{8,4},{12,8},{14,12},{10,14},{6,10},{2,6},{0,2},{5,1},{9,5},... | collective-permute-start | bytes 589832 | tf_op jit(solution)/shard_map/ppermute | solution.py:233
  19.2 1.2 %collective-permute-done.13.refs_13_ = bf16[24,5120]{1,0:T(8,128)(2,1)S(1)} collective-permute-done((bf16[24,5120]{1,0:T(8,128)(2,1)S(1)}, bf16[24,5120]{1,0:T(8,128)(2,1)S(1)}, u32[]{:S(2)}, u32[]{:S(2)}) %collective-permute-start.13) | collective-permute-done | bytes 245792 | tf_op jit(solution)/shard_map/ppermute | solution.py:233
  20.4 2.0 %collective-permute-start.14 = (bf16[24,5120]{1,0:T(8,128)(2,1)S(1)}, bf16[24,5120]{1,0:T(8,128)(2,1)S(1)}, u32[]{:S(2)}, u32[]{:S(2)}) collective-permute-start(bf16[24,5120]{1,0:T(8,128)(2,1)S(1)} %collective-permute-done.13.refs_13_), channel_id=1, source_target_pairs={{4,0},{8,4},{12,8},{14,12},{10,14},{6,10},{2,6},{0,2},{5,1},{9,5},... | collective-permute-start | bytes 737288 | tf_op jit(solution)/shard_map/ppermute | solution.py:233
  22.3 0.0 collective-permute-done.6.refs_12_
  22.4 0.1 collective-permute-start.10
  22.6 2.5 %collective-permute-done.5.refs_5_.refs_7_ = bf16[24,4096]{1,0:T(8,128)(2,1)S(1)} collective-permute-done((bf16[24,4096]{1,0:T(8,128)(2,1)S(1)}, bf16[24,4096]{1,0:T(8,128)(2,1)S(1)}, u32[]{:S(2)}, u32[]{:S(2)}) %collective-permute-start.5) | collective-permute-done | bytes 196640 | tf_op jit(solution)/shard_map/ppermute | solution.py:233
  25.1 1.5 %collective-permute-done.4.refs_4_.refs_6_ = bf16[24,4096]{1,0:T(8,128)(2,1)S(1)} collective-permute-done((bf16[24,4096]{1,0:T(8,128)(2,1)S(1)}, bf16[24,4096]{1,0:T(8,128)(2,1)S(1)}, u32[]{:S(2)}, u32[]{:S(2)}) %collective-permute-start.4) | collective-permute-done | bytes 196640 | tf_op jit(solution)/shard_map/ppermute | solution.py:230
  26.6 0.5 collective-permute-start.7
  27.1 1.5 %collective-permute-start.8 = (bf16[24,4096]{1,0:T(8,128)(2,1)S(1)}, bf16[24,4096]{1,0:T(8,128)(2,1)S(1)}, u32[]{:S(2)}, u32[]{:S(2)}) collective-permute-start(bf16[24,4096]{1,0:T(8,128)(2,1)S(1)} %collective-permute-done.5.refs_5_.refs_7_), channel_id=1, source_target_pairs={{4,0},{8,4},{12,8},{14,12},{10,14},{6,10},{2,6},{0,2},{5,1},{9,5},... | collective-permute-start | bytes 589832 | tf_op jit(solution)/shard_map/ppermute | solution.py:233
  28.6 1.7 %collective-permute-done.14.refs_15_ = bf16[24,5120]{1,0:T(8,128)(2,1)S(1)} collective-permute-done((bf16[24,5120]{1,0:T(8,128)(2,1)S(1)}, bf16[24,5120]{1,0:T(8,128)(2,1)S(1)}, u32[]{:S(2)}, u32[]{:S(2)}) %collective-permute-start.14) | collective-permute-done | bytes 245792 | tf_op jit(solution)/shard_map/ppermute | solution.py:233
  30.3 1.9 %collective-permute-start.16 = (bf16[24,5120]{1,0:T(8,128)(2,1)S(1)}, bf16[24,5120]{1,0:T(8,128)(2,1)S(1)}, u32[]{:S(2)}, u32[]{:S(2)}) collective-permute-start(bf16[24,5120]{1,0:T(8,128)(2,1)S(1)} %collective-permute-done.14.refs_15_), channel_id=1, source_target_pairs={{4,0},{8,4},{12,8},{14,12},{10,14},{6,10},{2,6},{0,2},{5,1},{9,5},... | collective-permute-start | bytes 737288 | tf_op jit(solution)/shard_map/ppermute | solution.py:233
  32.3 0.0 collective-permute-done.10.refs_14_
  32.3 0.1 collective-permute-start.15
  32.4 3.6 %collective-permute-done.7.refs_6_.refs_8_ = bf16[24,4096]{1,0:T(8,128)(2,1)S(1)} collective-permute-done((bf16[24,4096]{1,0:T(8,128)(2,1)S(1)}, bf16[24,4096]{1,0:T(8,128)(2,1)S(1)}, u32[]{:S(2)}, u32[]{:S(2)}) %collective-permute-start.7) | collective-permute-done | bytes 196640 | tf_op jit(solution)/shard_map/ppermute | solution.py:230
  36.1 0.1 collective-permute-start.11
  36.2 0.0 collective-permute-done.8.refs_7_.refs_9_
  36.2 0.1 collective-permute-start.9
  36.3 2.5 %collective-permute-done.16.refs_17_ = bf16[24,5120]{1,0:T(8,128)(2,1)S(1)} collective-permute-done((bf16[24,5120]{1,0:T(8,128)(2,1)S(1)}, bf16[24,5120]{1,0:T(8,128)(2,1)S(1)}, u32[]{:S(2)}, u32[]{:S(2)}) %collective-permute-start.16) | collective-permute-done | bytes 245792 | tf_op jit(solution)/shard_map/ppermute | solution.py:233
  38.8 1.7 %collective-permute-start.18 = (bf16[24,5120]{1,0:T(8,128)(2,1)S(1)}, bf16[24,5120]{1,0:T(8,128)(2,1)S(1)}, u32[]{:S(2)}, u32[]{:S(2)}) collective-permute-start(bf16[24,5120]{1,0:T(8,128)(2,1)S(1)} %collective-permute-done.16.refs_17_), channel_id=1, source_target_pairs={{4,0},{8,4},{12,8},{14,12},{10,14},{6,10},{2,6},{0,2},{5,1},{9,5},... | collective-permute-start | bytes 737288 | tf_op jit(solution)/shard_map/ppermute | solution.py:233
  40.4 1.6 %collective-permute-start.19 = (bf16[24,1280]{1,0:T(8,128)(2,1)S(1)}, bf16[24,1280]{1,0:T(8,128)(2,1)S(1)}, u32[]{:S(2)}, u32[]{:S(2)}) collective-permute-start(bf16[24,1280]{1,0:T(8,128)(2,1)S(1)} %pad_maximum_fusion.2), channel_id=1, source_target_pairs={{4,1},{8,5},{13,8},{15,12},{11,14},{7,10},{2,7},{0,3},{20,17},{24,... | collective-permute-start | bytes 184328 | tf_op jit(solution)/shard_map/ppermute | solution.py:237
  42.1 2.3 %collective-permute-done.11.refs_8_.refs_10_ = bf16[24,4096]{1,0:T(8,128)(2,1)S(1)} collective-permute-done((bf16[24,4096]{1,0:T(8,128)(2,1)S(1)}, bf16[24,4096]{1,0:T(8,128)(2,1)S(1)}, u32[]{:S(2)}, u32[]{:S(2)}) %collective-permute-start.11) | collective-permute-done | bytes 196640 | tf_op jit(solution)/shard_map/ppermute | solution.py:230
  44.4 0.0 collective-permute-start.12
  44.4 0.0 collective-permute-done.15.refs_16_
  44.5 0.5 collective-permute-start.17
  45.0 0.6 collective-permute-done.12
  45.6 0.0 collective-permute-done.9
  45.7 6.5 %shard_map.60 = (f32[1792,7168]{1,0:T(8,128)}, bf16[1024,192]{1,0:T(8,128)(2,1)S(1)}) custom-call(bf16[192,1024]{1,0:T(8,128)(2,1)S(1)} %pad_maximum_fusion.refs_0_, bf16[24,4096]{1,0:T(8,128)(2,1)S(1)} %add.94.refs_1_.refs_3_, bf16[24,4096]{1,0:T(8,128)(2,1)S(1)} %collective-permute-done.1.refs_2_.refs_4_, ...), custom_call_target="tpu_custom_call" | custom-call | flops 1610612736 | bytes 16777216 | tf_op jit(solution)/shard_map/pallas_call | solution.py:123
  52.3 0.0 collective-permute-done.19
  52.3 0.0 collective-permute-done.18.refs_18_
  52.3 0.0 collective-permute-done.17
  52.3 0.1 broadcast_select_fusion
  52.5 13.1 %shard_map.61 = (f32[1792,7168]{1,0:T(8,128)}, f32[512,2048]{1,0:T(8,128)}) custom-call(bf16[1024,192]{1,0:T(8,128)(2,1)S(1)} %get-tuple-element.33.refs_0_, bf16[192,768]{1,0:T(8,128)(2,1)S(1)} %fusion.refs_1_, bf16[192,512]{1,0:T(8,128)(2,1)S(1)} %pad_maximum_fusion.1.refs_2_, ...), custom_call_target="tpu_custom_call", output_to_operand_aliasing={{0}: (19, {})} | custom-call | flops 3724541952 | bytes 38797312 | tf_op jit(solution)/shard_map/pallas_call | solution.py:123
  (41 shorter events, 0.4 us)
Async XLA Ops:
  2.4 3.9 %collective-permute-start = (bf16[24,4096]{1,0:T(8,128)(2,1)S(1)}, bf16[24,4096]{1,0:T(8,128)(2,1)S(1)}, u32[]{:S(2)}, u32[]{:S(2)}) collective-permute-start(bf16[24,4096]{1,0:T(8,128)(2,1)S(1)} %get-tuple-element.23), channel_id=1, source_target_pairs={{0,1},{1,0},{2,3},{3,2},{4,5},{5,4},{6,7},{7,6},{8,9},{9,8},{10,11... | collective-permute-start | bytes 589832 | tf_op jit(solution)/shard_map/ppermute | solution.py:200
  3.0 6.5 %collective-permute-start.3 = (bf16[24,5120]{1,0:T(8,128)(2,1)S(1)}, bf16[24,5120]{1,0:T(8,128)(2,1)S(1)}, u32[]{:S(2)}, u32[]{:S(2)}) collective-permute-start(bf16[24,5120]{1,0:T(8,128)(2,1)S(1)} %get-tuple-element.25), channel_id=1, source_target_pairs={{0,1},{1,0},{2,3},{3,2},{4,5},{5,4},{6,7},{7,6},{8,9},{9,8},{10,11... | collective-permute-start | bytes 737288 | tf_op jit(solution)/shard_map/ppermute | solution.py:200
  6.4 8.7 %collective-permute-start.2 = (bf16[24,4096]{1,0:T(8,128)(2,1)S(1)}, bf16[24,4096]{1,0:T(8,128)(2,1)S(1)}, u32[]{:S(2)}, u32[]{:S(2)}) collective-permute-start(bf16[24,4096]{1,0:T(8,128)(2,1)S(1)} %add.94.refs_1_.refs_3_), channel_id=1, source_target_pairs={{4,0},{8,4},{12,8},{14,12},{10,14},{6,10},{2,6},{0,2},{5,1},{9,5},... | collective-permute-start | bytes 589832 | tf_op jit(solution)/shard_map/ppermute | solution.py:233
  9.3 7.8 %collective-permute-start.1 = (bf16[24,4096]{1,0:T(8,128)(2,1)S(1)}, bf16[24,4096]{1,0:T(8,128)(2,1)S(1)}, u32[]{:S(2)}, u32[]{:S(2)}) collective-permute-start(bf16[24,4096]{1,0:T(8,128)(2,1)S(1)} %add.94.refs_1_.refs_3_), channel_id=1, source_target_pairs={{0,4},{4,8},{8,12},{12,14},{14,10},{10,6},{6,2},{2,0},{1,5},{5,9},... | collective-permute-start | bytes 589832 | tf_op jit(solution)/shard_map/ppermute | solution.py:230
  9.5 10.8 %collective-permute-start.13 = (bf16[24,5120]{1,0:T(8,128)(2,1)S(1)}, bf16[24,5120]{1,0:T(8,128)(2,1)S(1)}, u32[]{:S(2)}, u32[]{:S(2)}) collective-permute-start(bf16[24,5120]{1,0:T(8,128)(2,1)S(1)} %add.97.refs_11_), channel_id=1, source_target_pairs={{4,0},{8,4},{12,8},{14,12},{10,14},{6,10},{2,6},{0,2},{5,1},{9,5},... | collective-permute-start | bytes 737288 | tf_op jit(solution)/shard_map/ppermute | solution.py:233
  11.5 10.9 %collective-permute-start.6 = (bf16[24,5120]{1,0:T(8,128)(2,1)S(1)}, bf16[24,5120]{1,0:T(8,128)(2,1)S(1)}, u32[]{:S(2)}, u32[]{:S(2)}) collective-permute-start(bf16[24,5120]{1,0:T(8,128)(2,1)S(1)} %add.97.refs_11_), channel_id=1, source_target_pairs={{0,4},{4,8},{8,12},{12,14},{14,10},{10,6},{6,2},{2,0},{1,5},{5,9},... | collective-permute-start | bytes 737288 | tf_op jit(solution)/shard_map/ppermute | solution.py:230
  17.1 9.5 %collective-permute-start.4 = (bf16[24,4096]{1,0:T(8,128)(2,1)S(1)}, bf16[24,4096]{1,0:T(8,128)(2,1)S(1)}, u32[]{:S(2)}, u32[]{:S(2)}) collective-permute-start(bf16[24,4096]{1,0:T(8,128)(2,1)S(1)} %collective-permute-done.1.refs_2_.refs_4_), channel_id=1, source_target_pairs={{0,4},{4,8},{8,12},{12,14},{14,10},{10,6},{6,2},{2,0},{1,5},{5,9},... | collective-permute-start | bytes 589832 | tf_op jit(solution)/shard_map/ppermute | solution.py:230
  17.2 7.8 %collective-permute-start.5 = (bf16[24,4096]{1,0:T(8,128)(2,1)S(1)}, bf16[24,4096]{1,0:T(8,128)(2,1)S(1)}, u32[]{:S(2)}, u32[]{:S(2)}) collective-permute-start(bf16[24,4096]{1,0:T(8,128)(2,1)S(1)} %collective-permute-done.2.refs_3_.refs_5_), channel_id=1, source_target_pairs={{4,0},{8,4},{12,8},{14,12},{10,14},{6,10},{2,6},{0,2},{5,1},{9,5},... | collective-permute-start | bytes 589832 | tf_op jit(solution)/shard_map/ppermute | solution.py:233
  20.4 10.0 %collective-permute-start.14 = (bf16[24,5120]{1,0:T(8,128)(2,1)S(1)}, bf16[24,5120]{1,0:T(8,128)(2,1)S(1)}, u32[]{:S(2)}, u32[]{:S(2)}) collective-permute-start(bf16[24,5120]{1,0:T(8,128)(2,1)S(1)} %collective-permute-done.13.refs_13_), channel_id=1, source_target_pairs={{4,0},{8,4},{12,8},{14,12},{10,14},{6,10},{2,6},{0,2},{5,1},{9,5},... | collective-permute-start | bytes 737288 | tf_op jit(solution)/shard_map/ppermute | solution.py:233
  22.4 9.9 %collective-permute-start.10 = (bf16[24,5120]{1,0:T(8,128)(2,1)S(1)}, bf16[24,5120]{1,0:T(8,128)(2,1)S(1)}, u32[]{:S(2)}, u32[]{:S(2)}) collective-permute-start(bf16[24,5120]{1,0:T(8,128)(2,1)S(1)} %collective-permute-done.6.refs_12_), channel_id=1, source_target_pairs={{0,4},{4,8},{8,12},{12,14},{14,10},{10,6},{6,2},{2,0},{1,5},{5,9},... | collective-permute-start | bytes 737288 | tf_op jit(solution)/shard_map/ppermute | solution.py:230
  26.6 9.5 %collective-permute-start.7 = (bf16[24,4096]{1,0:T(8,128)(2,1)S(1)}, bf16[24,4096]{1,0:T(8,128)(2,1)S(1)}, u32[]{:S(2)}, u32[]{:S(2)}) collective-permute-start(bf16[24,4096]{1,0:T(8,128)(2,1)S(1)} %collective-permute-done.4.refs_4_.refs_6_), channel_id=1, source_target_pairs={{0,4},{4,8},{8,12},{12,14},{14,10},{10,6},{6,2},{2,0},{1,5},{5,9},... | collective-permute-start | bytes 589832 | tf_op jit(solution)/shard_map/ppermute | solution.py:230
  27.1 9.1 %collective-permute-start.8 = (bf16[24,4096]{1,0:T(8,128)(2,1)S(1)}, bf16[24,4096]{1,0:T(8,128)(2,1)S(1)}, u32[]{:S(2)}, u32[]{:S(2)}) collective-permute-start(bf16[24,4096]{1,0:T(8,128)(2,1)S(1)} %collective-permute-done.5.refs_5_.refs_7_), channel_id=1, source_target_pairs={{4,0},{8,4},{12,8},{14,12},{10,14},{6,10},{2,6},{0,2},{5,1},{9,5},... | collective-permute-start | bytes 589832 | tf_op jit(solution)/shard_map/ppermute | solution.py:233
  30.3 8.4 %collective-permute-start.16 = (bf16[24,5120]{1,0:T(8,128)(2,1)S(1)}, bf16[24,5120]{1,0:T(8,128)(2,1)S(1)}, u32[]{:S(2)}, u32[]{:S(2)}) collective-permute-start(bf16[24,5120]{1,0:T(8,128)(2,1)S(1)} %collective-permute-done.14.refs_15_), channel_id=1, source_target_pairs={{4,0},{8,4},{12,8},{14,12},{10,14},{6,10},{2,6},{0,2},{5,1},{9,5},... | collective-permute-start | bytes 737288 | tf_op jit(solution)/shard_map/ppermute | solution.py:233
  32.3 12.1 %collective-permute-start.15 = (bf16[24,5120]{1,0:T(8,128)(2,1)S(1)}, bf16[24,5120]{1,0:T(8,128)(2,1)S(1)}, u32[]{:S(2)}, u32[]{:S(2)}) collective-permute-start(bf16[24,5120]{1,0:T(8,128)(2,1)S(1)} %collective-permute-done.10.refs_14_), channel_id=1, source_target_pairs={{0,4},{4,8},{8,12},{12,14},{14,10},{10,6},{6,2},{2,0},{1,5},{5,9},... | collective-permute-start | bytes 737288 | tf_op jit(solution)/shard_map/ppermute | solution.py:230
  36.1 8.3 %collective-permute-start.11 = (bf16[24,4096]{1,0:T(8,128)(2,1)S(1)}, bf16[24,4096]{1,0:T(8,128)(2,1)S(1)}, u32[]{:S(2)}, u32[]{:S(2)}) collective-permute-start(bf16[24,4096]{1,0:T(8,128)(2,1)S(1)} %collective-permute-done.7.refs_6_.refs_8_), channel_id=1, source_target_pairs={{0,4},{4,8},{8,12},{12,14},{14,10},{10,6},{6,2},{2,0},{1,5},{5,9},... | collective-permute-start | bytes 589832 | tf_op jit(solution)/shard_map/ppermute | solution.py:230
  36.2 9.4 %collective-permute-start.9 = (bf16[168,1024]{1,0:T(8,128)(2,1)S(1)}, bf16[168,1024]{1,0:T(8,128)(2,1)S(1)}, u32[]{:S(2)}, u32[]{:S(2)}) collective-permute-start(bf16[168,1024]{1,0:T(8,128)(2,1)S(1)} %dynamic-slice_dynamic-update-slice_fusion), channel_id=1, source_target_pairs={{0,1},{1,0},{2,3},{3,2},{4,5},{5,4},{6,7},{7,6},{8,9},{9,8},{10,11... | collective-permute-start | bytes 1032200 | tf_op jit(solution)/shard_map/ppermute | solution.py:217
  38.8 13.5 %collective-permute-start.18 = (bf16[24,5120]{1,0:T(8,128)(2,1)S(1)}, bf16[24,5120]{1,0:T(8,128)(2,1)S(1)}, u32[]{:S(2)}, u32[]{:S(2)}) collective-permute-start(bf16[24,5120]{1,0:T(8,128)(2,1)S(1)} %collective-permute-done.16.refs_17_), channel_id=1, source_target_pairs={{4,0},{8,4},{12,8},{14,12},{10,14},{6,10},{2,6},{0,2},{5,1},{9,5},... | collective-permute-start | bytes 737288 | tf_op jit(solution)/shard_map/ppermute | solution.py:233
  40.4 11.8 %collective-permute-start.19 = (bf16[24,1280]{1,0:T(8,128)(2,1)S(1)}, bf16[24,1280]{1,0:T(8,128)(2,1)S(1)}, u32[]{:S(2)}, u32[]{:S(2)}) collective-permute-start(bf16[24,1280]{1,0:T(8,128)(2,1)S(1)} %pad_maximum_fusion.2), channel_id=1, source_target_pairs={{4,1},{8,5},{13,8},{15,12},{11,14},{7,10},{2,7},{0,3},{20,17},{24,... | collective-permute-start | bytes 184328 | tf_op jit(solution)/shard_map/ppermute | solution.py:237
  44.4 1.2 %collective-permute-start.12 = (bf16[24,1024]{1,0:T(8,128)(2,1)S(1)}, bf16[24,1024]{1,0:T(8,128)(2,1)S(1)}, u32[]{:S(2)}, u32[]{:S(2)}) collective-permute-start(bf16[24,1024]{1,0:T(8,128)(2,1)S(1)} %constant_dynamic-slice_fusion.18), channel_id=1, source_target_pairs={{0,1},{1,0},{2,3},{3,2},{4,5},{5,4},{6,7},{7,6},{8,9},{9,8},{10,11... | collective-permute-start | bytes 147464 | tf_op jit(solution)/shard_map/ppermute | solution.py:216
  44.5 7.8 %collective-permute-start.17 = (bf16[168,1280]{1,0:T(8,128)(2,1)S(1)}, bf16[168,1280]{1,0:T(8,128)(2,1)S(1)}, u32[]{:S(2)}, u32[]{:S(2)}) collective-permute-start(bf16[168,1280]{1,0:T(8,128)(2,1)S(1)} %maximum_dynamic-update-slice_fusion), channel_id=1, source_target_pairs={{0,1},{1,0},{2,3},{3,2},{4,5},{5,4},{6,7},{7,6},{8,9},{9,8},{10,11... | collective-permute-start | bytes 1290248 | tf_op jit(solution)/shard_map/ppermute | solution.py:217

commit v11 on v10

--- a/solution.py
+++ b/solution.py
@@ -57,11 +57,14 @@
     joined, buffer, sems = refs[-3:]
     turned = [left_ref if done else turned.pop(0) for left_ref, done in zip(left_refs, ready)]
 
-    def copy(group, slot, j):
+    def copy(group, slot, j, part=0, parts=1):
         _, height, (_, _, _, width), which, row, column, stride, _ = group
+        rows = height // parts
         return pltpu.make_async_copy(
-            buffer.at[slot, pl.ds(0, height), pl.ds(0, width)],
-            out_refs[which].at[pl.ds(row, height), pl.ds(pl.multiple_of(column + j * stride, 128), width)],
+            buffer.at[slot, pl.ds(part * rows, rows), pl.ds(0, width)],
+            out_refs[which].at[
+                pl.ds(row + part * rows, rows), pl.ds(pl.multiple_of(column + j * stride, 128), width)
+            ],
             sems.at[slot],
         )
 
@@ -94,7 +97,8 @@
                     rows = turned[left][down : down + PIECE, :]
                     product = jnp.dot(rows, right, preferred_element_type=jnp.float32)
                     buffer[slot, down : down + PIECE, across : across + 256] = product * scale
-            copy(group, slot, j).start()
+            for part in (0, 1):
+                copy(group, slot, j, part, 2).start(priority=part)
             return carry
 
         lax.fori_loop(0, group[-1], step, 0)
@@ -210,12 +214,16 @@
             ]
             return cuts[0] if len(cuts) == 1 else jnp.concatenate(cuts, axis=1)
 
-        def left_part(chain, pieces, direct=None):
-            own = [block_of(part, pieces, row) for part in chain]
-            early = jnp.concatenate(own[:-1], axis=0)
-            late = lax.ppermute(own[-1], "col", swap) if direct is None else direct
-            early = jnp.where(mine, early, lax.ppermute(early, "col", swap))
-            return jnp.concatenate([early, jnp.where(mine, own[-1], late)], axis=0)
+        def early_part(chain, pieces):
+            early = jnp.concatenate([block_of(part, pieces, row) for part in chain[:-1]], axis=0)
+            return early, lax.ppermute(early, "col", swap)
+
+        def left_part(early, part, pieces, late):
+            own = block_of(part, pieces, row)
+            if late is None:
+                own, early = lax.optimization_barrier((own, early))
+                late = lax.ppermute(own, "col", swap)
+            return jnp.concatenate([jnp.where(mine, *early), jnp.where(mine, own, late)], axis=0)
 
         first_pieces = [(0, cut)]
         second_pieces = [(0, rest), (half_rows * rest, grad_block)] if rest else [(0, grad_block)]
@@ -233,12 +241,14 @@
                 backward[k] = lax.ppermute(behind_of, "row", behind)
                 chain.append(backward[k])
             if steps[k] == halfway and k == 1:
-                receiver = jnp.asarray([target for _, target in sorted(behind)], jnp.int32)[row]
+                receiver = sum(jnp.where(row == source, target, 0) for source, target in behind)
                 direct = lax.ppermute(block_of(behind_of, second_pieces, receiver), ("row", "col"), across)
 
-        left_first = left_part(chains[0], first_pieces)
+        early_first, early_second = early_part(chains[0], first_pieces), early_part(chains[1], second_pieces)
+        early_first, early_second = lax.optimization_barrier((early_first, early_second))
+        left_first = left_part(early_first, chains[0][-1], first_pieces, None)
         if rest == 0:
-            left_grad = left_part(chains[1], second_pieces, direct)
+            left_grad = left_part(early_second, chains[1][-1], second_pieces, direct)
             act_cov = gram(left_first, chains[0], scale, act_half // 256, 256)
             grad_cov = gram(left_grad, chains[1], scale, grad_half // 256, 256)
         else:
@@ -250,7 +260,7 @@
             ]
             act_cov, turned_first = tiles(scale, groups, [left_first], [chains[0]], [act_shape], hand_on=True)
             (chains[1][-1], direct), act_cov = lax.optimization_barrier(((chains[1][-1], direct), act_cov))
-            left_second = left_part(chains[1], second_pieces, direct)
+            left_second = left_part(early_second, chains[1][-1], second_pieces, direct)
             act_cov, grad_cov = tiles(
                 scale,
                 [

time: 65.8 us -> 64.1 us (0.974)
  between operations: 3.58 us -> 1.57 us
  starting transfers between devices: 17.9 us -> 19.4 us
  local copies, waits for them, and re-layouts: 1.42 us -> 0.19 us
    ppermute x1, starting transfers between devices: 1.62 us -> 3.56 us  [local(): lax.ppermute(block_of(behind_of, second_pieces, receiver), ('row', 'col')...]
    ppermute x7, waiting for transfers between devices: 9.51 us -> 8.06 us  [local(): forward[k] = lax.ppermute(ahead_of, 'row', ahead)]
    dynamic_slice x1 -> x0, local copies, waits for them, and re-layouts: 1.24 us -> none  [local(): jnp.asarray([target for _, target in sorted(behind)], jnp.int32)[row]]
    ppermute x2, waiting for transfers between devices: 0.01 us -> 0.99 us  [local(): lax.ppermute(pieces[2 * k + 1], 'col', swap)]
  transfers between devices with their start and end apart: 20 -> 20, of which waited for: 10 -> 11; matrix products, arithmetic and copies ran while one was open for 3% -> 1% of each run, Pallas kernels for 10% -> 10%
where the time goes in v11:
time: 64.1 us; the launch traced here: 63.9 us
  waiting for transfers between devices  21.6 us (34%)
  Pallas kernels  20.8 us (32%)
  starting transfers between devices  19.4 us (30%)
  between operations  1.57 us (2%)
    pallas_call x2, Pallas kernels, tiles(): pl.pallas_call(functools.partial(tiles_kernel, scale, groups, ready, [len...  19.6 us
    ppermute x7, starting transfers between devices, local(): backward[k] = lax.ppermute(behind_of, 'row', behind)  13.8 us
    ppermute x7, waiting for transfers between devices, local(): backward[k] = lax.ppermute(behind_of, 'row', behind)  11.4 us
    ppermute x7, waiting for transfers between devices, local(): forward[k] = lax.ppermute(ahead_of, 'row', ahead)  8.06 us
    ppermute x1, starting transfers between devices, local(): lax.ppermute(block_of(behind_of, second_pieces, receiver), ('row', 'col')...  3.56 us
  transfers between devices with their start and end apart: 20, of which 11 were waited for; matrix products, arithmetic and copies ran while one was open for 1% of the time, Pallas kernels for 10%

profile of v11, /device:TPU:0, one launch (start us, length us, event | category | flops | bytes accessed | tf_op | source)
XLA Modules:
  0.0 63.9 jit_solution(9762203116901586322)
XLA Ops:
  1.3 1.1 %shard_map.50 = (bf16[24,4096]{1,0:T(8,128)(2,1)S(1)}, bf16[24,4096]{1,0:T(8,128)(2,1)S(1)}, bf16[24,5120]{1,0:T(8,128)(2,1)S(1)}, bf16[24,5120]{1,0:T(8,128)(2,1)S(1)}) custom-call(s32[1]{0:T(128)} %bitcast.half_ref, s32[1]{0:T(128)S(6)} %copy.19.count_ref, bf16[12,14336]{1,0:T(8,128)(2,1)} %act_ref.1, bf16[12,4096]{1,0:T(8,128)(2,1)} %grad_ref.1), custom_call_target="tpu_custom_call" | custom-call | tf_op jit(solution)/shard_map/pallas_call | solution.py:198
  2.4 0.6 collective-permute-start
  3.0 0.1 collective-permute-start.2
  3.1 1.0 %collective-permute-done = bf16[24,4096]{1,0:T(8,128)(2,1)S(1)} collective-permute-done((bf16[24,4096]{1,0:T(8,128)(2,1)S(1)}, bf16[24,4096]{1,0:T(8,128)(2,1)S(1)}, u32[]{:S(2)}, u32[]{:S(2)}) %collective-permute-start) | collective-permute-done | bytes 196640 | tf_op jit(solution)/shard_map/ppermute | solution.py:204
  4.1 2.9 %collective-permute-start.8 = (bf16[24,4096]{1,0:T(8,128)(2,1)S(1)}, bf16[24,4096]{1,0:T(8,128)(2,1)S(1)}, u32[]{:S(2)}, u32[]{:S(2)}) collective-permute-start(bf16[24,4096]{1,0:T(8,128)(2,1)S(1)} %add.111.refs_1_.refs_3_), channel_id=1, source_target_pairs={{4,0},{8,4},{12,8},{14,12},{10,14},{6,10},{2,6},{0,2},{5,1},{9,5},... | collective-permute-start | bytes 589832 | tf_op jit(solution)/shard_map/ppermute | solution.py:241
  7.0 0.2 collective-permute-start.1
  7.1 0.0 collective-permute-done.2
  7.1 0.1 add.112.refs_11_
  7.2 1.9 %collective-permute-start.12 = (bf16[24,5120]{1,0:T(8,128)(2,1)S(1)}, bf16[24,5120]{1,0:T(8,128)(2,1)S(1)}, u32[]{:S(2)}, u32[]{:S(2)}) collective-permute-start(bf16[24,5120]{1,0:T(8,128)(2,1)S(1)} %add.112.refs_11_), channel_id=1, source_target_pairs={{4,0},{8,4},{12,8},{14,12},{10,14},{6,10},{2,6},{0,2},{5,1},{9,5},... | collective-permute-start | bytes 737288 | tf_op jit(solution)/shard_map/ppermute | solution.py:241
  9.1 0.2 collective-permute-start.4
  9.3 3.5 %collective-permute-done.8.refs_3_.refs_5_ = bf16[24,4096]{1,0:T(8,128)(2,1)S(1)} collective-permute-done((bf16[24,4096]{1,0:T(8,128)(2,1)S(1)}, bf16[24,4096]{1,0:T(8,128)(2,1)S(1)}, u32[]{:S(2)}, u32[]{:S(2)}) %collective-permute-start.8) | collective-permute-done | bytes 196640 | tf_op jit(solution)/shard_map/ppermute | solution.py:241
  12.8 2.0 %collective-permute-done.1.refs_2_.refs_4_ = bf16[24,4096]{1,0:T(8,128)(2,1)S(1)} collective-permute-done((bf16[24,4096]{1,0:T(8,128)(2,1)S(1)}, bf16[24,4096]{1,0:T(8,128)(2,1)S(1)}, u32[]{:S(2)}, u32[]{:S(2)}) %collective-permute-start.1) | collective-permute-done | bytes 196640 | tf_op jit(solution)/shard_map/ppermute | solution.py:238
  14.8 0.1 collective-permute-start.3
  14.9 1.9 %collective-permute-start.9 = (bf16[24,4096]{1,0:T(8,128)(2,1)S(1)}, bf16[24,4096]{1,0:T(8,128)(2,1)S(1)}, u32[]{:S(2)}, u32[]{:S(2)}) collective-permute-start(bf16[24,4096]{1,0:T(8,128)(2,1)S(1)} %collective-permute-done.8.refs_3_.refs_5_), channel_id=1, source_target_pairs={{4,0},{8,4},{12,8},{14,12},{10,14},{6,10},{2,6},{0,2},{5,1},{9,5},... | collective-permute-start | bytes 589832 | tf_op jit(solution)/shard_map/ppermute | solution.py:241
  16.8 1.2 %collective-permute-done.12.refs_13_ = bf16[24,5120]{1,0:T(8,128)(2,1)S(1)} collective-permute-done((bf16[24,5120]{1,0:T(8,128)(2,1)S(1)}, bf16[24,5120]{1,0:T(8,128)(2,1)S(1)}, u32[]{:S(2)}, u32[]{:S(2)}) %collective-permute-start.12) | collective-permute-done | bytes 245792 | tf_op jit(solution)/shard_map/ppermute | solution.py:241
  18.0 2.0 %collective-permute-start.13 = (bf16[24,5120]{1,0:T(8,128)(2,1)S(1)}, bf16[24,5120]{1,0:T(8,128)(2,1)S(1)}, u32[]{:S(2)}, u32[]{:S(2)}) collective-permute-start(bf16[24,5120]{1,0:T(8,128)(2,1)S(1)} %collective-permute-done.12.refs_13_), channel_id=1, source_target_pairs={{4,0},{8,4},{12,8},{14,12},{10,14},{6,10},{2,6},{0,2},{5,1},{9,5},... | collective-permute-start | bytes 737288 | tf_op jit(solution)/shard_map/ppermute | solution.py:241
  20.0 0.0 collective-permute-done.4.refs_12_
  20.0 0.1 collective-permute-start.6
  20.2 2.5 %collective-permute-done.9.refs_5_.refs_7_ = bf16[24,4096]{1,0:T(8,128)(2,1)S(1)} collective-permute-done((bf16[24,4096]{1,0:T(8,128)(2,1)S(1)}, bf16[24,4096]{1,0:T(8,128)(2,1)S(1)}, u32[]{:S(2)}, u32[]{:S(2)}) %collective-permute-start.9) | collective-permute-done | bytes 196640 | tf_op jit(solution)/shard_map/ppermute | solution.py:241
  22.7 1.5 %collective-permute-done.3.refs_4_.refs_6_ = bf16[24,4096]{1,0:T(8,128)(2,1)S(1)} collective-permute-done((bf16[24,4096]{1,0:T(8,128)(2,1)S(1)}, bf16[24,4096]{1,0:T(8,128)(2,1)S(1)}, u32[]{:S(2)}, u32[]{:S(2)}) %collective-permute-start.3) | collective-permute-done | bytes 196640 | tf_op jit(solution)/shard_map/ppermute | solution.py:238
  24.2 0.5 collective-permute-start.5
  24.7 1.5 %collective-permute-start.10 = (bf16[24,4096]{1,0:T(8,128)(2,1)S(1)}, bf16[24,4096]{1,0:T(8,128)(2,1)S(1)}, u32[]{:S(2)}, u32[]{:S(2)}) collective-permute-start(bf16[24,4096]{1,0:T(8,128)(2,1)S(1)} %collective-permute-done.9.refs_5_.refs_7_), channel_id=1, source_target_pairs={{4,0},{8,4},{12,8},{14,12},{10,14},{6,10},{2,6},{0,2},{5,1},{9,5},... | collective-permute-start | bytes 589832 | tf_op jit(solution)/shard_map/ppermute | solution.py:241
  26.3 1.7 %collective-permute-done.13.refs_15_ = bf16[24,5120]{1,0:T(8,128)(2,1)S(1)} collective-permute-done((bf16[24,5120]{1,0:T(8,128)(2,1)S(1)}, bf16[24,5120]{1,0:T(8,128)(2,1)S(1)}, u32[]{:S(2)}, u32[]{:S(2)}) %collective-permute-start.13) | collective-permute-done | bytes 245792 | tf_op jit(solution)/shard_map/ppermute | solution.py:241
  28.0 1.9 %collective-permute-start.15 = (bf16[24,5120]{1,0:T(8,128)(2,1)S(1)}, bf16[24,5120]{1,0:T(8,128)(2,1)S(1)}, u32[]{:S(2)}, u32[]{:S(2)}) collective-permute-start(bf16[24,5120]{1,0:T(8,128)(2,1)S(1)} %collective-permute-done.13.refs_15_), channel_id=1, source_target_pairs={{4,0},{8,4},{12,8},{14,12},{10,14},{6,10},{2,6},{0,2},{5,1},{9,5},... | collective-permute-start | bytes 737288 | tf_op jit(solution)/shard_map/ppermute | solution.py:241
  29.9 0.0 collective-permute-done.6.refs_14_
  29.9 0.1 collective-permute-start.14
  30.1 3.6 %collective-permute-done.5.refs_6_.refs_8_ = bf16[24,4096]{1,0:T(8,128)(2,1)S(1)} collective-permute-done((bf16[24,4096]{1,0:T(8,128)(2,1)S(1)}, bf16[24,4096]{1,0:T(8,128)(2,1)S(1)}, u32[]{:S(2)}, u32[]{:S(2)}) %collective-permute-start.5) | collective-permute-done | bytes 196640 | tf_op jit(solution)/shard_map/ppermute | solution.py:238
  33.7 0.1 collective-permute-start.7
  33.8 0.0 collective-permute-done.10.refs_7_.refs_9_
  33.9 0.1 collective-permute-start.11
  33.9 2.6 %collective-permute-done.15.refs_17_ = bf16[24,5120]{1,0:T(8,128)(2,1)S(1)} collective-permute-done((bf16[24,5120]{1,0:T(8,128)(2,1)S(1)}, bf16[24,5120]{1,0:T(8,128)(2,1)S(1)}, u32[]{:S(2)}, u32[]{:S(2)}) %collective-permute-start.15) | collective-permute-done | bytes 245792 | tf_op jit(solution)/shard_map/ppermute | solution.py:241
  36.5 1.7 %collective-permute-start.18 = (bf16[24,5120]{1,0:T(8,128)(2,1)S(1)}, bf16[24,5120]{1,0:T(8,128)(2,1)S(1)}, u32[]{:S(2)}, u32[]{:S(2)}) collective-permute-start(bf16[24,5120]{1,0:T(8,128)(2,1)S(1)} %collective-permute-done.15.refs_17_), channel_id=1, source_target_pairs={{4,0},{8,4},{12,8},{14,12},{10,14},{6,10},{2,6},{0,2},{5,1},{9,5},... | collective-permute-start | bytes 737288 | tf_op jit(solution)/shard_map/ppermute | solution.py:241
  38.2 0.8 %collective-permute-done.14.refs_16_ = bf16[24,5120]{1,0:T(8,128)(2,1)S(1)} collective-permute-done((bf16[24,5120]{1,0:T(8,128)(2,1)S(1)}, bf16[24,5120]{1,0:T(8,128)(2,1)S(1)}, u32[]{:S(2)}, u32[]{:S(2)}) %collective-permute-start.14) | collective-permute-done | bytes 245792 | tf_op jit(solution)/shard_map/ppermute | solution.py:238
  39.1 0.1 collective-permute-start.16
  39.2 3.6 %collective-permute-start.19 = (bf16[24,1280]{1,0:T(8,128)(2,1)S(1)}, bf16[24,1280]{1,0:T(8,128)(2,1)S(1)}, u32[]{:S(2)}, u32[]{:S(2)}) collective-permute-start(bf16[24,1280]{1,0:T(8,128)(2,1)S(1)} %pad_maximum_fusion.2), channel_id=1, source_target_pairs={{4,1},{8,5},{13,8},{15,12},{11,14},{7,10},{2,7},{0,3},{20,17},{24,... | collective-permute-start | bytes 184328 | tf_op jit(solution)/shard_map/ppermute | solution.py:245
  42.8 0.0 collective-permute-done.7.refs_8_.refs_10_
  42.8 0.0 collective-permute-done.11
  42.8 0.0 collective-permute-done.16
  42.8 0.1 collective-permute-start.17
  42.9 0.1 broadcast_select_fusion.1
  43.0 1.1 %collective-permute-done.17 = bf16[24,1024]{1,0:T(8,128)(2,1)S(1)} collective-permute-done((bf16[24,1024]{1,0:T(8,128)(2,1)S(1)}, bf16[24,1024]{1,0:T(8,128)(2,1)S(1)}, u32[]{:S(2)}, u32[]{:S(2)}) %collective-permute-start.17) | collective-permute-done | bytes 49184 | tf_op jit(solution)/shard_map/ppermute | solution.py:225
  44.1 6.5 %shard_map.51 = (f32[1792,7168]{1,0:T(8,128)}, bf16[1024,192]{1,0:T(8,128)(2,1)S(1)}) custom-call(bf16[192,1024]{1,0:T(8,128)(2,1)S(1)} %pad_maximum_fusion.refs_0_, bf16[24,4096]{1,0:T(8,128)(2,1)S(1)} %add.111.refs_1_.refs_3_, bf16[24,4096]{1,0:T(8,128)(2,1)S(1)} %collective-permute-done.1.refs_2_.refs_4_, ...), custom_call_target="tpu_custom_call" | custom-call | flops 1610612736 | bytes 16777216 | tf_op jit(solution)/shard_map/pallas_call | solution.py:127
  50.7 0.0 collective-permute-done.19
  50.7 0.0 collective-permute-done.18.refs_18_
  50.8 13.1 %shard_map.52 = (f32[1792,7168]{1,0:T(8,128)}, f32[512,2048]{1,0:T(8,128)}) custom-call(bf16[1024,192]{1,0:T(8,128)(2,1)S(1)} %get-tuple-element.48.refs_0_, bf16[192,768]{1,0:T(8,128)(2,1)S(1)} %fusion.refs_1_, bf16[192,512]{1,0:T(8,128)(2,1)S(1)} %pad_maximum_fusion.1.refs_2_, ...), custom_call_target="tpu_custom_call", output_to_operand_aliasing={{0}: (19, {})} | custom-call | flops 3724541952 | bytes 38797312 | tf_op jit(solution)/shard_map/pallas_call | solution.py:127
  (41 shorter events, 0.4 us)
Async XLA Ops:
  2.4 1.6 %collective-permute-start = (bf16[24,4096]{1,0:T(8,128)(2,1)S(1)}, bf16[24,4096]{1,0:T(8,128)(2,1)S(1)}, u32[]{:S(2)}, u32[]{:S(2)}) collective-permute-start(bf16[24,4096]{1,0:T(8,128)(2,1)S(1)} %get-tuple-element.30), channel_id=1, source_target_pairs={{0,1},{1,0},{2,3},{3,2},{4,5},{5,4},{6,7},{7,6},{8,9},{9,8},{10,11... | collective-permute-start | bytes 589832 | tf_op jit(solution)/shard_map/ppermute | solution.py:204
  3.0 4.1 %collective-permute-start.2 = (bf16[24,5120]{1,0:T(8,128)(2,1)S(1)}, bf16[24,5120]{1,0:T(8,128)(2,1)S(1)}, u32[]{:S(2)}, u32[]{:S(2)}) collective-permute-start(bf16[24,5120]{1,0:T(8,128)(2,1)S(1)} %get-tuple-element.32), channel_id=1, source_target_pairs={{0,1},{1,0},{2,3},{3,2},{4,5},{5,4},{6,7},{7,6},{8,9},{9,8},{10,11... | collective-permute-start | bytes 737288 | tf_op jit(solution)/shard_map/ppermute | solution.py:204
  4.1 8.6 %collective-permute-start.8 = (bf16[24,4096]{1,0:T(8,128)(2,1)S(1)}, bf16[24,4096]{1,0:T(8,128)(2,1)S(1)}, u32[]{:S(2)}, u32[]{:S(2)}) collective-permute-start(bf16[24,4096]{1,0:T(8,128)(2,1)S(1)} %add.111.refs_1_.refs_3_), channel_id=1, source_target_pairs={{4,0},{8,4},{12,8},{14,12},{10,14},{6,10},{2,6},{0,2},{5,1},{9,5},... | collective-permute-start | bytes 589832 | tf_op jit(solution)/shard_map/ppermute | solution.py:241
  7.0 7.8 %collective-permute-start.1 = (bf16[24,4096]{1,0:T(8,128)(2,1)S(1)}, bf16[24,4096]{1,0:T(8,128)(2,1)S(1)}, u32[]{:S(2)}, u32[]{:S(2)}) collective-permute-start(bf16[24,4096]{1,0:T(8,128)(2,1)S(1)} %add.111.refs_1_.refs_3_), channel_id=1, source_target_pairs={{0,4},{4,8},{8,12},{12,14},{14,10},{10,6},{6,2},{2,0},{1,5},{5,9},... | collective-permute-start | bytes 589832 | tf_op jit(solution)/shard_map/ppermute | solution.py:238
  7.2 10.8 %collective-permute-start.12 = (bf16[24,5120]{1,0:T(8,128)(2,1)S(1)}, bf16[24,5120]{1,0:T(8,128)(2,1)S(1)}, u32[]{:S(2)}, u32[]{:S(2)}) collective-permute-start(bf16[24,5120]{1,0:T(8,128)(2,1)S(1)} %add.112.refs_11_), channel_id=1, source_target_pairs={{4,0},{8,4},{12,8},{14,12},{10,14},{6,10},{2,6},{0,2},{5,1},{9,5},... | collective-permute-start | bytes 737288 | tf_op jit(solution)/shard_map/ppermute | solution.py:241
  9.1 10.9 %collective-permute-start.4 = (bf16[24,5120]{1,0:T(8,128)(2,1)S(1)}, bf16[24,5120]{1,0:T(8,128)(2,1)S(1)}, u32[]{:S(2)}, u32[]{:S(2)}) collective-permute-start(bf16[24,5120]{1,0:T(8,128)(2,1)S(1)} %add.112.refs_11_), channel_id=1, source_target_pairs={{0,4},{4,8},{8,12},{12,14},{14,10},{10,6},{6,2},{2,0},{1,5},{5,9},... | collective-permute-start | bytes 737288 | tf_op jit(solution)/shard_map/ppermute | solution.py:238
  14.8 9.5 %collective-permute-start.3 = (bf16[24,4096]{1,0:T(8,128)(2,1)S(1)}, bf16[24,4096]{1,0:T(8,128)(2,1)S(1)}, u32[]{:S(2)}, u32[]{:S(2)}) collective-permute-start(bf16[24,4096]{1,0:T(8,128)(2,1)S(1)} %collective-permute-done.1.refs_2_.refs_4_), channel_id=1, source_target_pairs={{0,4},{4,8},{8,12},{12,14},{14,10},{10,6},{6,2},{2,0},{1,5},{5,9},... | collective-permute-start | bytes 589832 | tf_op jit(solution)/shard_map/ppermute | solution.py:238
  14.9 7.8 %collective-permute-start.9 = (bf16[24,4096]{1,0:T(8,128)(2,1)S(1)}, bf16[24,4096]{1,0:T(8,128)(2,1)S(1)}, u32[]{:S(2)}, u32[]{:S(2)}) collective-permute-start(bf16[24,4096]{1,0:T(8,128)(2,1)S(1)} %collective-permute-done.8.refs_3_.refs_5_), channel_id=1, source_target_pairs={{4,0},{8,4},{12,8},{14,12},{10,14},{6,10},{2,6},{0,2},{5,1},{9,5},... | collective-permute-start | bytes 589832 | tf_op jit(solution)/shard_map/ppermute | solution.py:241
  18.0 10.0 %collective-permute-start.13 = (bf16[24,5120]{1,0:T(8,128)(2,1)S(1)}, bf16[24,5120]{1,0:T(8,128)(2,1)S(1)}, u32[]{:S(2)}, u32[]{:S(2)}) collective-permute-start(bf16[24,5120]{1,0:T(8,128)(2,1)S(1)} %collective-permute-done.12.refs_13_), channel_id=1, source_target_pairs={{4,0},{8,4},{12,8},{14,12},{10,14},{6,10},{2,6},{0,2},{5,1},{9,5},... | collective-permute-start | bytes 737288 | tf_op jit(solution)/shard_map/ppermute | solution.py:241
  20.0 9.9 %collective-permute-start.6 = (bf16[24,5120]{1,0:T(8,128)(2,1)S(1)}, bf16[24,5120]{1,0:T(8,128)(2,1)S(1)}, u32[]{:S(2)}, u32[]{:S(2)}) collective-permute-start(bf16[24,5120]{1,0:T(8,128)(2,1)S(1)} %collective-permute-done.4.refs_12_), channel_id=1, source_target_pairs={{0,4},{4,8},{8,12},{12,14},{14,10},{10,6},{6,2},{2,0},{1,5},{5,9},... | collective-permute-start | bytes 737288 | tf_op jit(solution)/shard_map/ppermute | solution.py:238
  24.2 9.5 %collective-permute-start.5 = (bf16[24,4096]{1,0:T(8,128)(2,1)S(1)}, bf16[24,4096]{1,0:T(8,128)(2,1)S(1)}, u32[]{:S(2)}, u32[]{:S(2)}) collective-permute-start(bf16[24,4096]{1,0:T(8,128)(2,1)S(1)} %collective-permute-done.3.refs_4_.refs_6_), channel_id=1, source_target_pairs={{0,4},{4,8},{8,12},{12,14},{14,10},{10,6},{6,2},{2,0},{1,5},{5,9},... | collective-permute-start | bytes 589832 | tf_op jit(solution)/shard_map/ppermute | solution.py:238
  24.7 9.1 %collective-permute-start.10 = (bf16[24,4096]{1,0:T(8,128)(2,1)S(1)}, bf16[24,4096]{1,0:T(8,128)(2,1)S(1)}, u32[]{:S(2)}, u32[]{:S(2)}) collective-permute-start(bf16[24,4096]{1,0:T(8,128)(2,1)S(1)} %collective-permute-done.9.refs_5_.refs_7_), channel_id=1, source_target_pairs={{4,0},{8,4},{12,8},{14,12},{10,14},{6,10},{2,6},{0,2},{5,1},{9,5},... | collective-permute-start | bytes 589832 | tf_op jit(solution)/shard_map/ppermute | solution.py:241
  28.0 8.5 %collective-permute-start.15 = (bf16[24,5120]{1,0:T(8,128)(2,1)S(1)}, bf16[24,5120]{1,0:T(8,128)(2,1)S(1)}, u32[]{:S(2)}, u32[]{:S(2)}) collective-permute-start(bf16[24,5120]{1,0:T(8,128)(2,1)S(1)} %collective-permute-done.13.refs_15_), channel_id=1, source_target_pairs={{4,0},{8,4},{12,8},{14,12},{10,14},{6,10},{2,6},{0,2},{5,1},{9,5},... | collective-permute-start | bytes 737288 | tf_op jit(solution)/shard_map/ppermute | solution.py:241
  29.9 9.1 %collective-permute-start.14 = (bf16[24,5120]{1,0:T(8,128)(2,1)S(1)}, bf16[24,5120]{1,0:T(8,128)(2,1)S(1)}, u32[]{:S(2)}, u32[]{:S(2)}) collective-permute-start(bf16[24,5120]{1,0:T(8,128)(2,1)S(1)} %collective-permute-done.6.refs_14_), channel_id=1, source_target_pairs={{0,4},{4,8},{8,12},{12,14},{14,10},{10,6},{6,2},{2,0},{1,5},{5,9},... | collective-permute-start | bytes 737288 | tf_op jit(solution)/shard_map/ppermute | solution.py:238
  33.7 9.0 %collective-permute-start.7 = (bf16[24,4096]{1,0:T(8,128)(2,1)S(1)}, bf16[24,4096]{1,0:T(8,128)(2,1)S(1)}, u32[]{:S(2)}, u32[]{:S(2)}) collective-permute-start(bf16[24,4096]{1,0:T(8,128)(2,1)S(1)} %collective-permute-done.5.refs_6_.refs_8_), channel_id=1, source_target_pairs={{0,4},{4,8},{8,12},{12,14},{14,10},{10,6},{6,2},{2,0},{1,5},{5,9},... | collective-permute-start | bytes 589832 | tf_op jit(solution)/shard_map/ppermute | solution.py:238
  33.9 8.9 %collective-permute-start.11 = (bf16[168,1024]{1,0:T(8,128)(2,1)S(1)}, bf16[168,1024]{1,0:T(8,128)(2,1)S(1)}, u32[]{:S(2)}, u32[]{:S(2)}) collective-permute-start(bf16[168,1024]{1,0:T(8,128)(2,1)S(1)} %dynamic-slice_dynamic-update-slice_fusion), channel_id=1, source_target_pairs={{0,1},{1,0},{2,3},{3,2},{4,5},{5,4},{6,7},{7,6},{8,9},{9,8},{10,11... | collective-permute-start | bytes 1032200 | tf_op jit(solution)/shard_map/ppermute | solution.py:219
  36.5 14.2 %collective-permute-start.18 = (bf16[24,5120]{1,0:T(8,128)(2,1)S(1)}, bf16[24,5120]{1,0:T(8,128)(2,1)S(1)}, u32[]{:S(2)}, u32[]{:S(2)}) collective-permute-start(bf16[24,5120]{1,0:T(8,128)(2,1)S(1)} %collective-permute-done.15.refs_17_), channel_id=1, source_target_pairs={{4,0},{8,4},{12,8},{14,12},{10,14},{6,10},{2,6},{0,2},{5,1},{9,5},... | collective-permute-start | bytes 737288 | tf_op jit(solution)/shard_map/ppermute | solution.py:241
  39.1 3.7 %collective-permute-start.16 = (bf16[168,1280]{1,0:T(8,128)(2,1)S(1)}, bf16[168,1280]{1,0:T(8,128)(2,1)S(1)}, u32[]{:S(2)}, u32[]{:S(2)}) collective-permute-start(bf16[168,1280]{1,0:T(8,128)(2,1)S(1)} %maximum_dynamic-update-slice_fusion), channel_id=1, source_target_pairs={{0,1},{1,0},{2,3},{3,2},{4,5},{5,4},{6,7},{7,6},{8,9},{9,8},{10,11... | collective-permute-start | bytes 1290248 | tf_op jit(solution)/shard_map/ppermute | solution.py:219
  39.2 11.5 %collective-permute-start.19 = (bf16[24,1280]{1,0:T(8,128)(2,1)S(1)}, bf16[24,1280]{1,0:T(8,128)(2,1)S(1)}, u32[]{:S(2)}, u32[]{:S(2)}) collective-permute-start(bf16[24,1280]{1,0:T(8,128)(2,1)S(1)} %pad_maximum_fusion.2), channel_id=1, source_target_pairs={{4,1},{8,5},{13,8},{15,12},{11,14},{7,10},{2,7},{0,3},{20,17},{24,... | collective-permute-start | bytes 184328 | tf_op jit(solution)/shard_map/ppermute | solution.py:245
  42.8 1.3 %collective-permute-start.17 = (bf16[24,1024]{1,0:T(8,128)(2,1)S(1)}, bf16[24,1024]{1,0:T(8,128)(2,1)S(1)}, u32[]{:S(2)}, u32[]{:S(2)}) collective-permute-start(bf16[24,1024]{1,0:T(8,128)(2,1)S(1)} %constant_dynamic-slice_fusion.18), channel_id=1, source_target_pairs={{0,1},{1,0},{2,3},{3,2},{4,5},{5,4},{6,7},{7,6},{8,9},{9,8},{10,11... | collective-permute-start | bytes 147464 | tf_op jit(solution)/shard_map/ppermute | solution.py:225

commit v12 on v7

v12 whole, which is shorter than its diff:
```python
import functools

import jax
import jax.numpy as jnp
from jax import lax
from jax.experimental import pallas as pl
from jax.experimental.pallas import tpu as pltpu
from jax.sharding import PartitionSpec as P


SLOTS, PIECE = 4, 128


def chip_ring(rows):
    width = 2 if rows <= 8 else 4
    depth = rows // width
    order = [z * width for z in range(depth)]
    for step, z in enumerate(reversed(range(depth))):
        columns = range(1, width) if step % 2 == 0 else range(width - 1, 0, -1)
        order += [z * width + x for x in columns]
    return order


def gram_kernel(scale, left_ref, *refs):
    right_refs, out_ref, turned = refs[:-2], refs[-2], refs[-1]

    @pl.when(pl.program_id(0) == 0)
    def _():
        turned[...] = left_ref[...].T

    right = jnp.concatenate([ref[...] for ref in right_refs], axis=0)
    out_ref[...] = jnp.dot(turned[...], right, preferred_element_type=jnp.float32) * scale


def gram(left, rights, scale, steps, tile):
    tokens, height = left.shape
    return pl.pallas_call(
        functools.partial(gram_kernel, scale),
        grid=(steps,),
        in_specs=[pl.BlockSpec((tokens, height), lambda j: (0, 0))]
        + [pl.BlockSpec((part.shape[0], tile), lambda j: (0, j)) for part in rights],
        out_specs=pl.BlockSpec((height, tile), lambda j: (0, j)),
        out_shape=jax.ShapeDtypeStruct((height, steps * tile), jnp.float32),
        scratch_shapes=[pltpu.VMEM((height, tokens), jnp.bfloat16)],
        compiler_params=pltpu.CompilerParams(vmem_limit_bytes=32 * 1024 * 1024),
    )(left, *rights)


def tiles_kernel(scale, groups, ready, lists, outs, aliased, *refs):
    left_refs, refs = refs[: len(ready)], refs[len(ready) :]
    sources = []
    for shards in lists:
        sources.append(refs[:shards])
        refs = refs[shards:]
    refs = refs[aliased:]
    out_refs, turned = refs[:outs], list(refs[outs:-3])
    joined, buffer, sems = refs[-3:]
    turned = [left_ref if done else turned.pop(0) for left_ref, done in zip(left_refs, ready)]

    def shape_of(group):
        return group[1] // group[2], sum(part[3] for part in group[3])

    def copy(group, slot, j, m):
        (height, width), (which, row, column, stride) = shape_of(group), group[4:8]
        return pltpu.make_async_copy(
            buffer.at[slot, pl.ds(0, height), pl.ds(0, width)],
            out_refs[which].at[
                pl.ds(pl.multiple_of(row + m * height, 8), height),
                pl.ds(pl.multiple_of(column + j * stride, 128), width),
            ],
            sems.at[slot],
        )

    earlier, done = None, [index for index, is_ready in enumerate(ready) if is_ready]
    for group in groups:
        left = group[0]
        if left not in done:
            done.append(left)
            turned[left][...] = left_refs[left][...].T

        def step(n, carry, group=group, earlier=earlier):
            (height, width), pieces = shape_of(group), group[2]
            slot, j, m = lax.rem(n, SLOTS), lax.div(n, pieces), lax.rem(n, pieces)

            @pl.when(m == 0)
            def _():
                at = 0
                for source, first, apart, wide in group[3]:
                    here = pl.ds(pl.multiple_of(first + j * apart, 128), wide)
                    joined[:, at : at + wide] = jnp.concatenate([ref[:, here] for ref in sources[source]], axis=0)
                    at += wide

            @pl.when(n >= SLOTS)
            def _():
                copy(group, slot, 0, 0).wait()

            if earlier is not None:

                @pl.when(n < SLOTS)
                def _():
                    copy(earlier, slot, 0, 0).wait()

            for across in range(0, width, 256):
                right = joined[:, across : across + 256]
                for down in range(0, height, PIECE):
                    rows = turned[group[0]][pl.ds(pl.multiple_of(m * height + down, 128), PIECE), :]
                    product = jnp.dot(rows, right, preferred_element_type=jnp.float32)
                    buffer[slot, down : down + PIECE, across : across + 256] = product * scale
            copy(group, slot, j, m).start()
            return carry

        lax.fori_loop(0, group[2] * group[-1], step, 0)
        earlier = group
    for slot in range(SLOTS):
        copy(earlier, slot, 0, 0).wait()


def tiles(scale, groups, lefts, lists, out_shapes, out=None, ready=(), hand_on=False):
    ready = tuple(ready) or (False,) * len(lefts)
    tokens = lists[0][0].shape[0] * len(lists[0])
    whole, anywhere = pl.BlockSpec(memory_space=pltpu.VMEM), pl.BlockSpec(memory_space=pl.ANY)
    operands = [*lefts, *[part for parts in lists for part in parts]]
    specs, aliases = [whole] * len(operands), {}
    if out is not None:
        aliases = {len(operands): 0}
        operands.append(out)
        specs.append(anywhere)
    widths = [sum(part[3] for part in g[3]) for g in groups]
    area = sum(g[1] * width * g[8] for g, width in zip(groups, widths))
    turned = [(left.shape[1], tokens) for left, done in zip(lefts, ready) if not done]
    results = [jax.ShapeDtypeStruct(shape, jnp.float32) for shape in out_shapes]
    result_specs = [anywhere] * len(results)
    if hand_on:
        results.append(pltpu.VMEM(turned[0], jnp.bfloat16))
        result_specs.append(whole)
    return pl.pallas_call(
        functools.partial(
            tiles_kernel, scale, groups, ready, [len(parts) for parts in lists], len(out_shapes), len(aliases)
        ),
        in_specs=specs,
        out_specs=result_specs,
        out_shape=results,
        scratch_shapes=[pltpu.VMEM(shape, jnp.bfloat16) for shape in turned[int(hand_on) :]]
        + [
            pltpu.VMEM((tokens, max(widths)), jnp.bfloat16),
            pltpu.VMEM((SLOTS, max(g[1] // g[2] for g in groups), max(widths)), jnp.float32),
            pltpu.SemaphoreType.DMA((SLOTS,)),
        ],
        input_output_aliases=aliases,
        compiler_params=pltpu.CompilerParams(vmem_limit_bytes=32 * 1024 * 1024),
        cost_estimate=pl.CostEstimate(flops=2 * tokens * area, bytes_accessed=4 * area, transcendentals=0),
    )(*operands)


def split_kernel(halves, layout, half_ref, count_ref, *refs):
    sources, out_refs = refs[:-2], refs[-2:]
    slots = sources[0].shape[0]
    live = lax.broadcasted_iota(jnp.int32, (slots, 128), 0) < count_ref[0]
    for half in range(halves):
        for flip in (1, 0):

            @pl.when((half_ref[0] + flip) % halves == half)
            def _(half=half, flip=flip):
                own, target = (half + flip) % halves * slots, 0
                for source, start, width in layout:
                    first = half * (sources[source].shape[1] // halves) + start
                    values = sources[source][:, first : first + width]
                    mask = jnp.concatenate([live] * (width // 128), axis=1)
                    columns = slice(target, target + width)
                    out_refs[flip][own : own + slots, columns] = jnp.where(mask, values, jnp.zeros_like(values))
                    out_refs[flip][slots - own : 2 * slots - own, columns] = jnp.zeros_like(values)
                    target += width


def solution(mesh):
    rows, cols = mesh.shape["row"], mesh.shape["col"]
    order = chip_ring(rows)
    ahead = [(order[p], order[(p + 1) % rows]) for p in range(rows)]
    behind = [(target, source) for source, target in ahead]
    swap = [(0, 1), (1, 0)]
    half_rows = rows // cols
    scale = 1.0 / (9.0 * rows * cols)

    def local(activations, pseudo_grads, row_counts):
        row, col = lax.axis_index("row"), lax.axis_index("col")
        slots, act_width = activations.shape
        grad_width = pseudo_grads.shape[1]
        act_half, grad_half = act_width // cols, grad_width // cols
        act_block, grad_block = act_width // rows, grad_width // rows
        cut = act_block * 4 // 7 if act_block % 1792 == 0 else act_block
        rest = act_block - cut
        widths = [half_rows * cut, half_rows * rest + grad_half]
        if rest == 0:
            layouts = [[(1, 0, act_half)], [(0, 0, grad_half)]]
        else:
            layouts = [
                [(1, j * act_block, cut) for j in range(half_rows)],
                [(1, j * act_block + cut, rest) for j in range(half_rows)] + [(0, 0, grad_half)],
            ]
        chains = []
        for layout, width in zip(layouts, widths):
            used = sorted({source for source, _, _ in layout})
            frame = pltpu.VMEM((2 * slots, width), jnp.bfloat16)
            keep, send = pl.pallas_call(
                functools.partial(split_kernel, cols, [(used.index(n), start, wide) for n, start, wide in layout]),
                in_specs=[pl.BlockSpec(memory_space=pltpu.SMEM)] * 2
                + [pl.BlockSpec(memory_space=pltpu.VMEM)] * len(used),
                out_specs=[pl.BlockSpec(memory_space=pltpu.VMEM)] * 2,
                out_shape=[frame, frame],
            )(col[None], row_counts, *[(pseudo_grads, activations)[n] for n in used])
            chains.append([keep + lax.ppermute(send, "col", swap)])
        forward = [chain[0] for chain in chains]
        backward = list(forward)
        steps, halfway = [0] * len(chains), rows // 2
        sequence = [0, 1] * halfway
        mine = col == row // half_rows

        def block_of(part, pieces, block_row):
            cuts = [
                lax.dynamic_slice_in_dim(part, base + (block_row % half_rows) * size, size, 1) for base, size in pieces
            ]
            return cuts[0] if len(cuts) == 1 else jnp.concatenate(cuts, axis=1)

        def swapped(own):
            return own, lax.ppermute(own, "col", swap)

        def early_part(chain, pieces):
            return swapped(jnp.concatenate([block_of(part, pieces, row) for part in chain], axis=0))

        def left_part(early, late):
            return jnp.concatenate([jnp.where(mine, *early), jnp.where(mine, *late)], axis=0)

        first_pieces = [(0, cut)]
        second_pieces = [(0, rest), (half_rows * rest, grad_block)] if rest else [(0, grad_block)]
        previous, hold = (), []
        for k in sequence:
            chain, middle = chains[k], widths[k] // 2
            steps[k] += 1
            ahead_of, _ = lax.optimization_barrier((forward[k], previous))
            behind_of, _ = lax.optimization_barrier((backward[k], (previous, hold)))
            previous = forward[k]
            if steps[k] == halfway:
                ahead_of, behind_of = ahead_of[:, :middle], behind_of[:, middle:]
            forward[k] = lax.ppermute(ahead_of, "row", ahead)
            backward[k] = lax.ppermute(behind_of, "row", behind)
            if steps[k] < halfway:
                chain += [forward[k], backward[k]]
                latest = (forward[k], backward[k])
            elif k == 0:
                halves, _ = lax.optimization_barrier(((forward[k], backward[k]), latest))
                chain.append(jnp.concatenate(halves, axis=1))
                late = block_of(chain[-1], first_pieces, row)
                hold.append(late)
                left_first = left_part(early_part(chain[:-1], first_pieces), swapped(late))

        early_second = early_part(chains[1], second_pieces)
        if rest == 0:
            chains[1].append(jnp.concatenate((forward[1], backward[1]), axis=1))
            left_grad = left_part(early_second, swapped(block_of(chains[1][-1], second_pieces, row)))
            act_cov = gram(left_first, chains[0], scale, act_half // 256, 256)
            grad_cov = gram(left_grad, chains[1], scale, grad_half // 256, 256)
        else:
            first_part, second_part = (0, 0, cut, cut), (1, 0, rest, rest)
            grad_part = (1, half_rows * rest, grad_block, grad_block)
            act_shape, grad_shape = (act_block, act_half), (grad_block, grad_half)
            half_blocks = half_rows // 2

            def square(start, lefts, out, **more):
                parts = [(0, start * cut, cut, cut)]
                group = (0, cut, 2, parts, 0, 0, start * act_block, act_block, half_blocks)
                return tiles(scale, [group], lefts, [chains[0]], [act_shape], out, **more)

            act_cov, turned_first = square(0, [left_first], None, hand_on=True)
            halves, act_cov = lax.optimization_barrier(((forward[1], backward[1]), act_cov))
            chains[1].append(jnp.concatenate(halves, axis=1))
            left_second = left_part(early_second, swapped(block_of(chains[1][-1], second_pieces, row)))
            (act_cov,) = square(half_blocks, [turned_first], act_cov, ready=[True])
            act_cov, grad_cov = tiles(
                scale,
                [
                    (2, grad_block, 1, [grad_part], 1, 0, 0, grad_block, half_rows),
                    (1, rest, 2, [first_part, second_part], 0, cut, 0, act_block, half_rows),
                    (0, cut, 2, [second_part], 0, 0, cut, act_block, half_rows),
                ],
                [turned_first, left_second[:, :rest], left_second[:, rest:]],
                chains, [act_shape, grad_shape], act_cov, ready=[True, False, False],
            )
        return act_cov, grad_cov

    return jax.shard_map(
        local,
        mesh=mesh,
        in_specs=(
            P(("groups", "row", "col"), None),
            P(("groups", "row", "col"), None),
            P(("groups", "row", "col")),
        ),
        out_specs=(P(("groups", "row"), "col"), P(("groups", "row"), "col")),
        check_vma=False,
    )
```

time: 65.6 us -> 64.9 us (0.989)
  waiting for transfers between devices: 21.2 us -> 20.2 us
    pallas_call x1 -> x2, Pallas kernels: 1.15 us -> 2.23 us  [local(): pl.pallas_call(functools.partial(split_kernel, cols, [(used.index(n), sta...]
    ppermute x6, waiting for transfers between devices: 1 us -> 0.02 us  [the longest x4 0.01 us: swapped(): return (own, lax.ppermute(own, 'col', swap))]
    pallas_call x3, Pallas kernels: 22 us -> 21.1 us  [tiles(): pl.pallas_call(functools.partial(tiles_kernel, scale, groups, ready, [len...]
  transfers between devices with their start and end apart: 22 -> 22, of which waited for: 11 -> 10; matrix products, arithmetic and copies ran while one was open for 1% -> 1% of each run, Pallas kernels for 11% -> 14%
where the time goes in v12:
time: 64.9 us; the launch traced here: 64.7 us
  Pallas kernels  23.3 us (36%)
  waiting for transfers between devices  20.2 us (31%)
  starting transfers between devices  19 us (29%)
  between operations  1.64 us (3%)
    pallas_call x3, Pallas kernels, tiles(): pl.pallas_call(functools.partial(tiles_kernel, scale, groups, ready, [len...  21.1 us
    ppermute x8, starting transfers between devices, local(): backward[k] = lax.ppermute(behind_of, 'row', behind)  15.5 us
    ppermute x8, waiting for transfers between devices, local(): backward[k] = lax.ppermute(behind_of, 'row', behind)  11.4 us
    ppermute x8, waiting for transfers between devices, local(): forward[k] = lax.ppermute(ahead_of, 'row', ahead)  8.82 us
    pallas_call x2, Pallas kernels, local(): pl.pallas_call(functools.partial(split_kernel, cols, [(used.index(n), sta...  2.23 us
    ppermute x8, starting transfers between devices, local(): forward[k] = lax.ppermute(ahead_of, 'row', ahead)  2.06 us
  transfers between devices with their start and end apart: 22, of which 10 were waited for; matrix products, arithmetic and copies ran while one was open for 1% of the time, Pallas kernels for 14%

profile of v12, /device:TPU:0, one launch (start us, length us, event | category | flops | bytes accessed | tf_op | source)
XLA Modules:
  0.0 64.7 jit_solution(7726858950397536347)
XLA Ops:
  1.3 1.1 %shard_map.50 = (bf16[24,4096]{1,0:T(8,128)(2,1)S(1)}, bf16[24,4096]{1,0:T(8,128)(2,1)S(1)}) custom-call(s32[1]{0:T(128)} %bitcast.half_ref, s32[1]{0:T(128)S(6)} %copy.23.count_ref, bf16[12,14336]{1,0:T(8,128)(2,1)} %refs_1_.1), custom_call_target="tpu_custom_call" | custom-call | tf_op jit(solution)/shard_map/pallas_call | solution.py:204
  2.4 0.5 collective-permute-start
  2.9 1.2 %shard_map.51 = (bf16[24,5120]{1,0:T(8,128)(2,1)S(1)}, bf16[24,5120]{1,0:T(8,128)(2,1)S(1)}) custom-call(s32[1]{0:T(128)} %bitcast.half_ref, s32[1]{0:T(128)S(6)} %copy.23.count_ref, bf16[12,4096]{1,0:T(8,128)(2,1)} %refs_0_.3, bf16[12,14336]{1,0:T(8,128)(2,1)} %refs_1_.1), custom_call_target="tpu_custom_call" | custom-call | tf_op jit(solution)/shard_map/pallas_call | solution.py:204
  4.1 0.1 collective-permute-start.3
  4.2 0.0 collective-permute-done
  4.3 3.0 %collective-permute-start.2 = (bf16[24,4096]{1,0:T(8,128)(2,1)S(1)}, bf16[24,4096]{1,0:T(8,128)(2,1)S(1)}, u32[]{:S(2)}, u32[]{:S(2)}) collective-permute-start(bf16[24,4096]{1,0:T(8,128)(2,1)S(1)} %add.76.refs_1_.refs_3_), channel_id=1, source_target_pairs={{4,0},{8,4},{12,8},{14,12},{10,14},{6,10},{2,6},{0,2},{5,1},{9,5},... | collective-permute-start | bytes 589832 | tf_op jit(solution)/shard_map/ppermute | solution.py:245
  7.2 0.2 collective-permute-start.1
  7.4 0.0 collective-permute-done.3
  7.4 0.1 add.79.refs_11_
  7.5 1.9 %collective-permute-start.14 = (bf16[24,5120]{1,0:T(8,128)(2,1)S(1)}, bf16[24,5120]{1,0:T(8,128)(2,1)S(1)}, u32[]{:S(2)}, u32[]{:S(2)}) collective-permute-start(bf16[24,5120]{1,0:T(8,128)(2,1)S(1)} %add.79.refs_11_), channel_id=1, source_target_pairs={{4,0},{8,4},{12,8},{14,12},{10,14},{6,10},{2,6},{0,2},{5,1},{9,5},... | collective-permute-start | bytes 737288 | tf_op jit(solution)/shard_map/ppermute | solution.py:245
  9.4 0.2 collective-permute-start.6
  9.6 3.5 %collective-permute-done.2.refs_3_.refs_5_ = bf16[24,4096]{1,0:T(8,128)(2,1)S(1)} collective-permute-done((bf16[24,4096]{1,0:T(8,128)(2,1)S(1)}, bf16[24,4096]{1,0:T(8,128)(2,1)S(1)}, u32[]{:S(2)}, u32[]{:S(2)}) %collective-permute-start.2) | collective-permute-done | bytes 196640 | tf_op jit(solution)/shard_map/ppermute | solution.py:245
  13.0 2.0 %collective-permute-done.1.refs_2_.refs_4_ = bf16[24,4096]{1,0:T(8,128)(2,1)S(1)} collective-permute-done((bf16[24,4096]{1,0:T(8,128)(2,1)S(1)}, bf16[24,4096]{1,0:T(8,128)(2,1)S(1)}, u32[]{:S(2)}, u32[]{:S(2)}) %collective-permute-start.1) | collective-permute-done | bytes 196640 | tf_op jit(solution)/shard_map/ppermute | solution.py:244
  15.0 0.1 collective-permute-start.4
  15.2 1.9 %collective-permute-start.5 = (bf16[24,4096]{1,0:T(8,128)(2,1)S(1)}, bf16[24,4096]{1,0:T(8,128)(2,1)S(1)}, u32[]{:S(2)}, u32[]{:S(2)}) collective-permute-start(bf16[24,4096]{1,0:T(8,128)(2,1)S(1)} %collective-permute-done.2.refs_3_.refs_5_), channel_id=1, source_target_pairs={{4,0},{8,4},{12,8},{14,12},{10,14},{6,10},{2,6},{0,2},{5,1},{9,5},... | collective-permute-start | bytes 589832 | tf_op jit(solution)/shard_map/ppermute | solution.py:245
  17.1 1.2 %collective-permute-done.14.refs_13_ = bf16[24,5120]{1,0:T(8,128)(2,1)S(1)} collective-permute-done((bf16[24,5120]{1,0:T(8,128)(2,1)S(1)}, bf16[24,5120]{1,0:T(8,128)(2,1)S(1)}, u32[]{:S(2)}, u32[]{:S(2)}) %collective-permute-start.14) | collective-permute-done | bytes 245792 | tf_op jit(solution)/shard_map/ppermute | solution.py:245
  18.3 2.0 %collective-permute-start.15 = (bf16[24,5120]{1,0:T(8,128)(2,1)S(1)}, bf16[24,5120]{1,0:T(8,128)(2,1)S(1)}, u32[]{:S(2)}, u32[]{:S(2)}) collective-permute-start(bf16[24,5120]{1,0:T(8,128)(2,1)S(1)} %collective-permute-done.14.refs_13_), channel_id=1, source_target_pairs={{4,0},{8,4},{12,8},{14,12},{10,14},{6,10},{2,6},{0,2},{5,1},{9,5},... | collective-permute-start | bytes 737288 | tf_op jit(solution)/shard_map/ppermute | solution.py:245
  20.3 0.0 collective-permute-done.6.refs_12_
  20.3 0.1 collective-permute-start.10
  20.5 2.5 %collective-permute-done.5.refs_5_.refs_7_ = bf16[24,4096]{1,0:T(8,128)(2,1)S(1)} collective-permute-done((bf16[24,4096]{1,0:T(8,128)(2,1)S(1)}, bf16[24,4096]{1,0:T(8,128)(2,1)S(1)}, u32[]{:S(2)}, u32[]{:S(2)}) %collective-permute-start.5) | collective-permute-done | bytes 196640 | tf_op jit(solution)/shard_map/ppermute | solution.py:245
  23.0 1.5 %collective-permute-done.4.refs_4_.refs_6_ = bf16[24,4096]{1,0:T(8,128)(2,1)S(1)} collective-permute-done((bf16[24,4096]{1,0:T(8,128)(2,1)S(1)}, bf16[24,4096]{1,0:T(8,128)(2,1)S(1)}, u32[]{:S(2)}, u32[]{:S(2)}) %collective-permute-start.4) | collective-permute-done | bytes 196640 | tf_op jit(solution)/shard_map/ppermute | solution.py:244
  24.5 0.5 collective-permute-start.7
  25.0 1.5 %collective-permute-start.8 = (bf16[24,4096]{1,0:T(8,128)(2,1)S(1)}, bf16[24,4096]{1,0:T(8,128)(2,1)S(1)}, u32[]{:S(2)}, u32[]{:S(2)}) collective-permute-start(bf16[24,4096]{1,0:T(8,128)(2,1)S(1)} %collective-permute-done.5.refs_5_.refs_7_), channel_id=1, source_target_pairs={{4,0},{8,4},{12,8},{14,12},{10,14},{6,10},{2,6},{0,2},{5,1},{9,5},... | collective-permute-start | bytes 589832 | tf_op jit(solution)/shard_map/ppermute | solution.py:245
  26.6 1.7 %collective-permute-done.15.refs_15_ = bf16[24,5120]{1,0:T(8,128)(2,1)S(1)} collective-permute-done((bf16[24,5120]{1,0:T(8,128)(2,1)S(1)}, bf16[24,5120]{1,0:T(8,128)(2,1)S(1)}, u32[]{:S(2)}, u32[]{:S(2)}) %collective-permute-start.15) | collective-permute-done | bytes 245792 | tf_op jit(solution)/shard_map/ppermute | solution.py:245
  28.3 1.9 %collective-permute-start.16 = (bf16[24,5120]{1,0:T(8,128)(2,1)S(1)}, bf16[24,5120]{1,0:T(8,128)(2,1)S(1)}, u32[]{:S(2)}, u32[]{:S(2)}) collective-permute-start(bf16[24,5120]{1,0:T(8,128)(2,1)S(1)} %collective-permute-done.15.refs_15_), channel_id=1, source_target_pairs={{4,0},{8,4},{12,8},{14,12},{10,14},{6,10},{2,6},{0,2},{5,1},{9,5},... | collective-permute-start | bytes 737288 | tf_op jit(solution)/shard_map/ppermute | solution.py:245
  30.2 0.0 collective-permute-done.10.refs_14_
  30.2 0.1 collective-permute-start.13
  30.4 2.5 %collective-permute-done.8.refs_7_.refs_9_ = bf16[24,4096]{1,0:T(8,128)(2,1)S(1)} collective-permute-done((bf16[24,4096]{1,0:T(8,128)(2,1)S(1)}, bf16[24,4096]{1,0:T(8,128)(2,1)S(1)}, u32[]{:S(2)}, u32[]{:S(2)}) %collective-permute-start.8) | collective-permute-done | bytes 196640 | tf_op jit(solution)/shard_map/ppermute | solution.py:245
  32.8 1.2 %collective-permute-done.7.refs_6_.refs_8_ = bf16[24,4096]{1,0:T(8,128)(2,1)S(1)} collective-permute-done((bf16[24,4096]{1,0:T(8,128)(2,1)S(1)}, bf16[24,4096]{1,0:T(8,128)(2,1)S(1)}, u32[]{:S(2)}, u32[]{:S(2)}) %collective-permute-start.7) | collective-permute-done | bytes 196640 | tf_op jit(solution)/shard_map/ppermute | solution.py:244
  34.0 1.6 %collective-permute-start.12 = (bf16[24,2048]{1,0:T(8,128)(2,1)S(1)}, bf16[24,2048]{1,0:T(8,128)(2,1)S(1)}, u32[]{:S(2)}, u32[]{:S(2)}) collective-permute-start(bf16[24,2048]{1,0:T(8,128)(2,1)S(1)} %slice.19), channel_id=1, source_target_pairs={{4,0},{8,4},{12,8},{14,12},{10,14},{6,10},{2,6},{0,2},{5,1},{9,5},... | collective-permute-start | bytes 294920 | tf_op jit(solution)/shard_map/ppermute | solution.py:245
  35.7 0.4 collective-permute-start.11
  36.1 0.1 collective-permute-start.9
  36.2 2.9 %collective-permute-done.13.refs_16_ = bf16[24,5120]{1,0:T(8,128)(2,1)S(1)} collective-permute-done((bf16[24,5120]{1,0:T(8,128)(2,1)S(1)}, bf16[24,5120]{1,0:T(8,128)(2,1)S(1)}, u32[]{:S(2)}, u32[]{:S(2)}) %collective-permute-start.13) | collective-permute-done | bytes 245792 | tf_op jit(solution)/shard_map/ppermute | solution.py:244
  39.1 0.0 collective-permute-done.12
  39.1 1.2 %collective-permute-done.11 = bf16[24,2048]{1,0:T(8,128)(2,1)S(1)} collective-permute-done((bf16[24,2048]{1,0:T(8,128)(2,1)S(1)}, bf16[24,2048]{1,0:T(8,128)(2,1)S(1)}, u32[]{:S(2)}, u32[]{:S(2)}) %collective-permute-start.11) | collective-permute-done | bytes 98336 | tf_op jit(solution)/shard_map/ppermute | solution.py:244
  40.3 0.0 collective-permute-done.16.refs_17_
  40.3 0.1 collective-permute-start.17
  40.4 0.5 collective-permute-start.19
  40.9 1.6 %collective-permute-start.20 = (bf16[24,2560]{1,0:T(8,128)(2,1)S(1)}, bf16[24,2560]{1,0:T(8,128)(2,1)S(1)}, u32[]{:S(2)}, u32[]{:S(2)}) collective-permute-start(bf16[24,2560]{1,0:T(8,128)(2,1)S(1)} %slice.21), channel_id=1, source_target_pairs={{4,0},{8,4},{12,8},{14,12},{10,14},{6,10},{2,6},{0,2},{5,1},{9,5},... | collective-permute-start | bytes 368648 | tf_op jit(solution)/shard_map/ppermute | solution.py:245
  42.6 0.1 collective-permute-start.18
  42.7 0.0 collective-permute-done.17
  42.7 0.0 collective-permute-done.9
  42.7 0.1 broadcast_select_fusion.1
  42.8 4.0 %shard_map.52 = (f32[1792,7168]{1,0:T(8,128)}, bf16[1024,192]{1,0:T(8,128)(2,1)S(1)}) custom-call(bf16[192,1024]{1,0:T(8,128)(2,1)S(1)} %pad_maximum_fusion.refs_0_, bf16[24,4096]{1,0:T(8,128)(2,1)S(1)} %add.76.refs_1_.refs_3_, bf16[24,4096]{1,0:T(8,128)(2,1)S(1)} %collective-permute-done.1.refs_2_.refs_4_, ...), custom_call_target="tpu_custom_call" | custom-call | flops 805306368 | bytes 8388608 | tf_op jit(solution)/shard_map/pallas_call | solution.py:136
  46.8 0.0 collective-permute-done.19
  46.8 0.0 collective-permute-done.20
  46.9 0.5 collective-permute-start.21
  47.5 3.8 %shard_map.53.refs_19_ = f32[1792,7168]{1,0:T(8,128)} custom-call(bf16[1024,192]{1,0:T(8,128)(2,1)S(1)} %get-tuple-element.43.refs_0_, bf16[24,4096]{1,0:T(8,128)(2,1)S(1)} %add.76.refs_1_.refs_3_, bf16[24,4096]{1,0:T(8,128)(2,1)S(1)} %collective-permute-done.1.refs_2_.refs_4_, ...), custom_call_target="tpu_custom_call", output_to_operand_aliasing={{}: (9, {})} | custom-call | flops 805306368 | bytes 8388608 | tf_op jit(solution)/shard_map/pallas_call | solution.py:136
  51.3 0.0 collective-permute-done.21
  51.4 0.0 collective-permute-done.18
  51.5 13.2 %shard_map.54 = (f32[1792,7168]{1,0:T(8,128)}, f32[512,2048]{1,0:T(8,128)}) custom-call(bf16[1024,192]{1,0:T(8,128)(2,1)S(1)} %get-tuple-element.43.refs_0_, bf16[192,768]{1,0:T(8,128)(2,1)S(1)} %fusion.refs_1_, bf16[192,512]{1,0:T(8,128)(2,1)S(1)} %pad_maximum_fusion.1.refs_2_, ...), custom_call_target="tpu_custom_call", output_to_operand_aliasing={{0}: (19, {})} | custom-call | flops 3724541952 | bytes 38797312 | tf_op jit(solution)/shard_map/pallas_call | solution.py:136
  (47 shorter events, 0.5 us)
Async XLA Ops:
  2.4 1.8 %collective-permute-start = (bf16[24,4096]{1,0:T(8,128)(2,1)S(1)}, bf16[24,4096]{1,0:T(8,128)(2,1)S(1)}, u32[]{:S(2)}, u32[]{:S(2)}) collective-permute-start(bf16[24,4096]{1,0:T(8,128)(2,1)S(1)} %get-tuple-element.27), channel_id=1, source_target_pairs={{0,1},{1,0},{2,3},{3,2},{4,5},{5,4},{6,7},{7,6},{8,9},{9,8},{10,11... | collective-permute-start | bytes 589832 | tf_op jit(solution)/shard_map/ppermute | solution.py:211
  4.1 3.3 %collective-permute-start.3 = (bf16[24,5120]{1,0:T(8,128)(2,1)S(1)}, bf16[24,5120]{1,0:T(8,128)(2,1)S(1)}, u32[]{:S(2)}, u32[]{:S(2)}) collective-permute-start(bf16[24,5120]{1,0:T(8,128)(2,1)S(1)} %get-tuple-element.29), channel_id=1, source_target_pairs={{0,1},{1,0},{2,3},{3,2},{4,5},{5,4},{6,7},{7,6},{8,9},{9,8},{10,11... | collective-permute-start | bytes 737288 | tf_op jit(solution)/shard_map/ppermute | solution.py:211
  4.3 8.8 %collective-permute-start.2 = (bf16[24,4096]{1,0:T(8,128)(2,1)S(1)}, bf16[24,4096]{1,0:T(8,128)(2,1)S(1)}, u32[]{:S(2)}, u32[]{:S(2)}) collective-permute-start(bf16[24,4096]{1,0:T(8,128)(2,1)S(1)} %add.76.refs_1_.refs_3_), channel_id=1, source_target_pairs={{4,0},{8,4},{12,8},{14,12},{10,14},{6,10},{2,6},{0,2},{5,1},{9,5},... | collective-permute-start | bytes 589832 | tf_op jit(solution)/shard_map/ppermute | solution.py:245
  7.2 7.8 %collective-permute-start.1 = (bf16[24,4096]{1,0:T(8,128)(2,1)S(1)}, bf16[24,4096]{1,0:T(8,128)(2,1)S(1)}, u32[]{:S(2)}, u32[]{:S(2)}) collective-permute-start(bf16[24,4096]{1,0:T(8,128)(2,1)S(1)} %add.76.refs_1_.refs_3_), channel_id=1, source_target_pairs={{0,4},{4,8},{8,12},{12,14},{14,10},{10,6},{6,2},{2,0},{1,5},{5,9},... | collective-permute-start | bytes 589832 | tf_op jit(solution)/shard_map/ppermute | solution.py:244
  7.5 10.8 %collective-permute-start.14 = (bf16[24,5120]{1,0:T(8,128)(2,1)S(1)}, bf16[24,5120]{1,0:T(8,128)(2,1)S(1)}, u32[]{:S(2)}, u32[]{:S(2)}) collective-permute-start(bf16[24,5120]{1,0:T(8,128)(2,1)S(1)} %add.79.refs_11_), channel_id=1, source_target_pairs={{4,0},{8,4},{12,8},{14,12},{10,14},{6,10},{2,6},{0,2},{5,1},{9,5},... | collective-permute-start | bytes 737288 | tf_op jit(solution)/shard_map/ppermute | solution.py:245
  9.4 10.9 %collective-permute-start.6 = (bf16[24,5120]{1,0:T(8,128)(2,1)S(1)}, bf16[24,5120]{1,0:T(8,128)(2,1)S(1)}, u32[]{:S(2)}, u32[]{:S(2)}) collective-permute-start(bf16[24,5120]{1,0:T(8,128)(2,1)S(1)} %add.79.refs_11_), channel_id=1, source_target_pairs={{0,4},{4,8},{8,12},{12,14},{14,10},{10,6},{6,2},{2,0},{1,5},{5,9},... | collective-permute-start | bytes 737288 | tf_op jit(solution)/shard_map/ppermute | solution.py:244
  15.0 9.5 %collective-permute-start.4 = (bf16[24,4096]{1,0:T(8,128)(2,1)S(1)}, bf16[24,4096]{1,0:T(8,128)(2,1)S(1)}, u32[]{:S(2)}, u32[]{:S(2)}) collective-permute-start(bf16[24,4096]{1,0:T(8,128)(2,1)S(1)} %collective-permute-done.1.refs_2_.refs_4_), channel_id=1, source_target_pairs={{0,4},{4,8},{8,12},{12,14},{14,10},{10,6},{6,2},{2,0},{1,5},{5,9},... | collective-permute-start | bytes 589832 | tf_op jit(solution)/shard_map/ppermute | solution.py:244
  15.2 7.8 %collective-permute-start.5 = (bf16[24,4096]{1,0:T(8,128)(2,1)S(1)}, bf16[24,4096]{1,0:T(8,128)(2,1)S(1)}, u32[]{:S(2)}, u32[]{:S(2)}) collective-permute-start(bf16[24,4096]{1,0:T(8,128)(2,1)S(1)} %collective-permute-done.2.refs_3_.refs_5_), channel_id=1, source_target_pairs={{4,0},{8,4},{12,8},{14,12},{10,14},{6,10},{2,6},{0,2},{5,1},{9,5},... | collective-permute-start | bytes 589832 | tf_op jit(solution)/shard_map/ppermute | solution.py:245
  18.3 10.0 %collective-permute-start.15 = (bf16[24,5120]{1,0:T(8,128)(2,1)S(1)}, bf16[24,5120]{1,0:T(8,128)(2,1)S(1)}, u32[]{:S(2)}, u32[]{:S(2)}) collective-permute-start(bf16[24,5120]{1,0:T(8,128)(2,1)S(1)} %collective-permute-done.14.refs_13_), channel_id=1, source_target_pairs={{4,0},{8,4},{12,8},{14,12},{10,14},{6,10},{2,6},{0,2},{5,1},{9,5},... | collective-permute-start | bytes 737288 | tf_op jit(solution)/shard_map/ppermute | solution.py:245
  20.3 9.9 %collective-permute-start.10 = (bf16[24,5120]{1,0:T(8,128)(2,1)S(1)}, bf16[24,5120]{1,0:T(8,128)(2,1)S(1)}, u32[]{:S(2)}, u32[]{:S(2)}) collective-permute-start(bf16[24,5120]{1,0:T(8,128)(2,1)S(1)} %collective-permute-done.6.refs_12_), channel_id=1, source_target_pairs={{0,4},{4,8},{8,12},{12,14},{14,10},{10,6},{6,2},{2,0},{1,5},{5,9},... | collective-permute-start | bytes 737288 | tf_op jit(solution)/shard_map/ppermute | solution.py:244
  24.5 9.5 %collective-permute-start.7 = (bf16[24,4096]{1,0:T(8,128)(2,1)S(1)}, bf16[24,4096]{1,0:T(8,128)(2,1)S(1)}, u32[]{:S(2)}, u32[]{:S(2)}) collective-permute-start(bf16[24,4096]{1,0:T(8,128)(2,1)S(1)} %collective-permute-done.4.refs_4_.refs_6_), channel_id=1, source_target_pairs={{0,4},{4,8},{8,12},{12,14},{14,10},{10,6},{6,2},{2,0},{1,5},{5,9},... | collective-permute-start | bytes 589832 | tf_op jit(solution)/shard_map/ppermute | solution.py:244
  25.0 7.8 %collective-permute-start.8 = (bf16[24,4096]{1,0:T(8,128)(2,1)S(1)}, bf16[24,4096]{1,0:T(8,128)(2,1)S(1)}, u32[]{:S(2)}, u32[]{:S(2)}) collective-permute-start(bf16[24,4096]{1,0:T(8,128)(2,1)S(1)} %collective-permute-done.5.refs_5_.refs_7_), channel_id=1, source_target_pairs={{4,0},{8,4},{12,8},{14,12},{10,14},{6,10},{2,6},{0,2},{5,1},{9,5},... | collective-permute-start | bytes 589832 | tf_op jit(solution)/shard_map/ppermute | solution.py:245
  28.3 12.0 %collective-permute-start.16 = (bf16[24,5120]{1,0:T(8,128)(2,1)S(1)}, bf16[24,5120]{1,0:T(8,128)(2,1)S(1)}, u32[]{:S(2)}, u32[]{:S(2)}) collective-permute-start(bf16[24,5120]{1,0:T(8,128)(2,1)S(1)} %collective-permute-done.15.refs_15_), channel_id=1, source_target_pairs={{4,0},{8,4},{12,8},{14,12},{10,14},{6,10},{2,6},{0,2},{5,1},{9,5},... | collective-permute-start | bytes 737288 | tf_op jit(solution)/shard_map/ppermute | solution.py:245
  30.2 8.9 %collective-permute-start.13 = (bf16[24,5120]{1,0:T(8,128)(2,1)S(1)}, bf16[24,5120]{1,0:T(8,128)(2,1)S(1)}, u32[]{:S(2)}, u32[]{:S(2)}) collective-permute-start(bf16[24,5120]{1,0:T(8,128)(2,1)S(1)} %collective-permute-done.10.refs_14_), channel_id=1, source_target_pairs={{0,4},{4,8},{8,12},{12,14},{14,10},{10,6},{6,2},{2,0},{1,5},{5,9},... | collective-permute-start | bytes 737288 | tf_op jit(solution)/shard_map/ppermute | solution.py:244
  34.0 5.1 %collective-permute-start.12 = (bf16[24,2048]{1,0:T(8,128)(2,1)S(1)}, bf16[24,2048]{1,0:T(8,128)(2,1)S(1)}, u32[]{:S(2)}, u32[]{:S(2)}) collective-permute-start(bf16[24,2048]{1,0:T(8,128)(2,1)S(1)} %slice.19), channel_id=1, source_target_pairs={{4,0},{8,4},{12,8},{14,12},{10,14},{6,10},{2,6},{0,2},{5,1},{9,5},... | collective-permute-start | bytes 294920 | tf_op jit(solution)/shard_map/ppermute | solution.py:245
  35.7 4.6 %collective-permute-start.11 = (bf16[24,2048]{1,0:T(8,128)(2,1)S(1)}, bf16[24,2048]{1,0:T(8,128)(2,1)S(1)}, u32[]{:S(2)}, u32[]{:S(2)}) collective-permute-start(bf16[24,2048]{1,0:T(8,128)(2,1)S(1)} %slice.18), channel_id=1, source_target_pairs={{0,4},{4,8},{8,12},{12,14},{14,10},{10,6},{6,2},{2,0},{1,5},{5,9},... | collective-permute-start | bytes 294920 | tf_op jit(solution)/shard_map/ppermute | solution.py:244
  36.1 6.6 %collective-permute-start.9 = (bf16[168,1024]{1,0:T(8,128)(2,1)S(1)}, bf16[168,1024]{1,0:T(8,128)(2,1)S(1)}, u32[]{:S(2)}, u32[]{:S(2)}) collective-permute-start(bf16[168,1024]{1,0:T(8,128)(2,1)S(1)} %dynamic-slice_dynamic-update-slice_fusion), channel_id=1, source_target_pairs={{0,1},{1,0},{2,3},{3,2},{4,5},{5,4},{6,7},{7,6},{8,9},{9,8},{10,11... | collective-permute-start | bytes 1032200 | tf_op jit(solution)/shard_map/ppermute | solution.py:225
  40.3 2.3 %collective-permute-start.17 = (bf16[24,1024]{1,0:T(8,128)(2,1)S(1)}, bf16[24,1024]{1,0:T(8,128)(2,1)S(1)}, u32[]{:S(2)}, u32[]{:S(2)}) collective-permute-start(bf16[24,1024]{1,0:T(8,128)(2,1)S(1)} %constant_dynamic-slice_fusion.16), channel_id=1, source_target_pairs={{0,1},{1,0},{2,3},{3,2},{4,5},{5,4},{6,7},{7,6},{8,9},{9,8},{10,11... | collective-permute-start | bytes 147464 | tf_op jit(solution)/shard_map/ppermute | solution.py:225
  40.4 6.4 %collective-permute-start.19 = (bf16[24,2560]{1,0:T(8,128)(2,1)S(1)}, bf16[24,2560]{1,0:T(8,128)(2,1)S(1)}, u32[]{:S(2)}, u32[]{:S(2)}) collective-permute-start(bf16[24,2560]{1,0:T(8,128)(2,1)S(1)} %slice.20), channel_id=1, source_target_pairs={{0,4},{4,8},{8,12},{12,14},{14,10},{10,6},{6,2},{2,0},{1,5},{5,9},... | collective-permute-start | bytes 368648 | tf_op jit(solution)/shard_map/ppermute | solution.py:244
  40.9 5.9 %collective-permute-start.20 = (bf16[24,2560]{1,0:T(8,128)(2,1)S(1)}, bf16[24,2560]{1,0:T(8,128)(2,1)S(1)}, u32[]{:S(2)}, u32[]{:S(2)}) collective-permute-start(bf16[24,2560]{1,0:T(8,128)(2,1)S(1)} %slice.21), channel_id=1, source_target_pairs={{4,0},{8,4},{12,8},{14,12},{10,14},{6,10},{2,6},{0,2},{5,1},{9,5},... | collective-permute-start | bytes 368648 | tf_op jit(solution)/shard_map/ppermute | solution.py:245
  42.6 8.8 %collective-permute-start.18 = (bf16[168,1280]{1,0:T(8,128)(2,1)S(1)}, bf16[168,1280]{1,0:T(8,128)(2,1)S(1)}, u32[]{:S(2)}, u32[]{:S(2)}) collective-permute-start(bf16[168,1280]{1,0:T(8,128)(2,1)S(1)} %maximum_dynamic-update-slice_fusion), channel_id=1, source_target_pairs={{0,1},{1,0},{2,3},{3,2},{4,5},{5,4},{6,7},{7,6},{8,9},{9,8},{10,11... | collective-permute-start | bytes 1290248 | tf_op jit(solution)/shard_map/ppermute | solution.py:225
  46.9 4.4 %collective-permute-start.21 = (bf16[24,1280]{1,0:T(8,128)(2,1)S(1)}, bf16[24,1280]{1,0:T(8,128)(2,1)S(1)}, u32[]{:S(2)}, u32[]{:S(2)}) collective-permute-start(bf16[24,1280]{1,0:T(8,128)(2,1)S(1)} %pad_maximum_fusion.2), channel_id=1, source_target_pairs={{0,1},{1,0},{2,3},{3,2},{4,5},{5,4},{6,7},{7,6},{8,9},{9,8},{10,11... | collective-permute-start | bytes 184328 | tf_op jit(solution)/shard_map/ppermute | solution.py:225

commit v13 on v9

--- a/solution.py
+++ b/solution.py
@@ -46,33 +46,39 @@
     )(left, *rights)
 
 
-def tiles_kernel(scale, cut, rest, grad_tile, shards, *refs):
+def tiles_kernel(scale, cut, rest, grad_cut, grad_rest, shards, *refs):
     first_left, second_left = refs[:2]
     first, second = refs[2 : 2 + shards], refs[2 + shards : 2 + 2 * shards]
     act_out, grad_out, turned, turned_grad, joined, buffer, sems = refs[2 + 2 * shards :]
-    act_block, blocks = cut + rest, first[0].shape[1] // cut
-    groups = [(turned_grad, second, blocks * rest, grad_tile, grad_tile, grad_out, 0, grad_tile, blocks)]
-    groups.append((turned, second, 0, rest, rest, act_out, cut, act_block, blocks))
-    for start in range(0, cut, 256):
-        groups.append((turned, first, start, cut, 256, act_out, start, act_block, blocks))
+    act_block, grad_block, blocks = cut + rest, grad_cut + grad_rest, first[0].shape[1] // (cut + grad_cut)
+    grad_parts = [(first, blocks * cut, grad_cut, grad_cut), (second, blocks * rest, grad_rest, grad_rest)]
+    groups = [(turned_grad, grad_parts, grad_block, grad_out, 0, grad_block, blocks)]
+    groups.append((turned, [(second, 0, rest, rest)], rest, act_out, cut, act_block, blocks))
+    start = 0
+    for width in (cut // 2, cut // 4, cut // 4):
+        groups.append((turned, [(first, start, cut, width)], width, act_out, start, act_block, blocks))
+        start += width
 
     def copy(group, slot, j):
-        left, _, _, _, width, out, column, stride, _ = group
+        left, _, width, out, column, stride, _ = group
         return pltpu.make_async_copy(
             buffer.at[slot, pl.ds(0, left.shape[0]), pl.ds(0, width)],
             out.at[:, pl.ds(pl.multiple_of(column + j * stride, 128), width)],
             sems.at[slot],
         )
 
-    turned_grad[...] = second_left[:, rest:].T
+    turned_grad[:grad_cut, :] = first_left[:, cut:].T
+    turned_grad[grad_cut:, :] = second_left[:, rest:].T
     earlier = None
     for group in groups:
 
         def step(j, carry, group=group, earlier=earlier):
-            left, sources, start, apart, width, _, _, _, _ = group
-            height, slot = left.shape[0], lax.rem(j, SLOTS)
-            here = pl.ds(pl.multiple_of(start + j * apart, 128), width)
-            joined[:, :width] = jnp.concatenate([ref[:, here] for ref in sources], axis=0)
+            left, parts, width = group[:3]
+            height, slot, at = left.shape[0], lax.rem(j, SLOTS), 0
+            for sources, start, apart, wide in parts:
+                here = pl.ds(pl.multiple_of(start + j * apart, 128), wide)
+                joined[:, at : at + wide] = jnp.concatenate([ref[:, here] for ref in sources], axis=0)
+                at += wide
 
             @pl.when(j >= SLOTS)
             def _():
@@ -94,23 +100,23 @@
 
         lax.fori_loop(0, group[-1], step, 0)
         if earlier is None:
-            turned[:cut, :] = first_left[...].T
+            turned[:cut, :] = first_left[:, :cut].T
             turned[cut:, :] = second_left[:, :rest].T
         earlier = group
     for slot in range(SLOTS):
         copy(earlier, slot, 0).wait()
 
 
-def tiles(scale, cut, rest, first_left, second_left, chains):
+def tiles(scale, cut, rest, grad_cut, first_left, second_left, chains):
     shards = len(chains[0])
-    tokens, blocks = first_left.shape[0], chains[0][0].shape[1] // cut
-    act_block, grad_block = cut + rest, second_left.shape[1] - rest
-    grad_half = chains[1][0].shape[1] - blocks * rest
-    act_shape, grad_shape = (act_block, blocks * act_block), (grad_block, grad_half)
+    tokens, grad_rest = first_left.shape[0], second_left.shape[1] - rest
+    blocks = chains[0][0].shape[1] // (cut + grad_cut)
+    act_block, grad_block = cut + rest, grad_cut + grad_rest
+    act_shape, grad_shape = (act_block, blocks * act_block), (grad_block, blocks * grad_block)
     area = act_shape[0] * act_shape[1] + grad_shape[0] * grad_shape[1]
     whole = pl.BlockSpec(memory_space=pltpu.VMEM)
     return pl.pallas_call(
-        functools.partial(tiles_kernel, scale, cut, rest, grad_half // blocks, shards),
+        functools.partial(tiles_kernel, scale, cut, rest, grad_cut, grad_rest, shards),
         in_specs=[whole] * (2 + 2 * shards),
         out_specs=[pl.BlockSpec(memory_space=pl.ANY)] * 2,
         out_shape=[jax.ShapeDtypeStruct(shape, jnp.float32) for shape in (act_shape, grad_shape)],
@@ -167,13 +173,17 @@
         act_block, grad_block = act_width // rows, grad_width // rows
         cut = act_block * 4 // 7 if act_block % 1792 == 0 else act_block
         rest = act_block - cut
-        widths = [half_rows * cut, half_rows * rest + grad_half]
+        grad_cut = grad_block // 4 if rest else 0
+        grad_rest = grad_block - grad_cut
+        widths = [half_rows * (cut + grad_cut), half_rows * (rest + grad_rest)]
         if rest == 0:
             layouts = [[(1, 0, act_half)], [(0, 0, grad_half)]]
         else:
             layouts = [
-                [(1, j * act_block, cut) for j in range(half_rows)],
-                [(1, j * act_block + cut, rest) for j in range(half_rows)] + [(0, 0, grad_half)],
+                [(1, j * act_block, cut) for j in range(half_rows)]
+                + [(0, j * grad_block, grad_cut) for j in range(half_rows)],
+                [(1, j * act_block + cut, rest) for j in range(half_rows)]
+                + [(0, j * grad_block + grad_cut, grad_rest) for j in range(half_rows)],
             ]
         pieces = pl.pallas_call(
             functools.partial(split_kernel, cols, layouts),
@@ -211,14 +221,14 @@
                 backward[k] = lax.ppermute(behind_of, "row", behind)
                 chain.append(backward[k])
 
-        left_first = left_part(chains[0], [(0, cut)])
         if rest == 0:
-            left_grad = left_part(chains[1], [(0, grad_block)])
+            left_first, left_grad = left_part(chains[0], [(0, cut)]), left_part(chains[1], [(0, grad_block)])
             act_cov = gram(left_first, chains[0], scale, act_half // 256, 256)
             grad_cov = gram(left_grad, chains[1], scale, grad_half // 256, 256)
         else:
-            left_second = left_part(chains[1], [(0, rest), (half_rows * rest, grad_block)])
-            act_cov, grad_cov = tiles(scale, cut, rest, left_first, left_second, chains)
+            left_first = left_part(chains[0], [(0, cut), (half_rows * cut, grad_cut)])
+            left_second = left_part(chains[1], [(0, rest), (half_rows * rest, grad_rest)])
+            act_cov, grad_cov = tiles(scale, cut, rest, grad_cut, left_first, left_second, chains)
         return act_cov, grad_cov
 
     return jax.shard_map(

time: 64 us -> 65.2 us (1.019)
  waiting for transfers between devices: 25.2 us -> 26.5 us
    ppermute x7, waiting for transfers between devices: 11.4 us -> 13.6 us  [local(): backward[k] = lax.ppermute(behind_of, 'row', behind)]
  transfers between devices with their start and end apart: 20 -> 20, of which waited for: 12 -> 13; matrix products, arithmetic and copies ran while one was open for 1% -> 1% of each run, Pallas kernels for 0% -> 0%
where the time goes in v13:
time: 65.2 us; the launch traced here: 65.1 us
  waiting for transfers between devices  26.5 us (41%)
  Pallas kernels  20.1 us (31%)
  starting transfers between devices  16.2 us (25%)
  between operations  1.6 us (2%)
    pallas_call x1, Pallas kernels, tiles(): pl.pallas_call(functools.partial(tiles_kernel, scale, cut, rest, grad_cut...  18.9 us
    ppermute x7, waiting for transfers between devices, local(): backward[k] = lax.ppermute(behind_of, 'row', behind)  13.6 us
    ppermute x7, starting transfers between devices, local(): backward[k] = lax.ppermute(behind_of, 'row', behind)  13.6 us
    ppermute x7, waiting for transfers between devices, local(): forward[k] = lax.ppermute(ahead_of, 'row', ahead)  10.7 us
    ppermute x7, starting transfers between devices, local(): forward[k] = lax.ppermute(ahead_of, 'row', ahead)  1.71 us
  transfers between devices with their start and end apart: 20, of which 13 were waited for; matrix products, arithmetic and copies ran while one was open for 1% of the time, Pallas kernels for 0%

profile of v13, /device:TPU:0, one launch (start us, length us, event | category | flops | bytes accessed | tf_op | source)
XLA Modules:
  0.0 65.1 jit_solution(10980065905356380879)
XLA Ops:
  1.3 1.2 %shard_map.50 = (bf16[24,4608]{1,0:T(8,128)(2,1)S(1)}, bf16[24,4608]{1,0:T(8,128)(2,1)S(1)}, bf16[24,4608]{1,0:T(8,128)(2,1)S(1)}, bf16[24,4608]{1,0:T(8,128)(2,1)S(1)}) custom-call(s32[1]{0:T(128)} %bitcast.half_ref, s32[1]{0:T(128)S(6)} %copy.17.count_ref, bf16[12,14336]{1,0:T(8,128)(2,1)} %act_ref.1, bf16[12,4096]{1,0:T(8,128)(2,1)} %grad_ref.1), custom_call_target="tpu_custom_call" | custom-call | tf_op jit(solution)/shard_map/pallas_call | solution.py:188
  2.4 0.6 collective-permute-start
  3.0 0.1 collective-permute-start.3
  3.1 1.0 %collective-permute-done = bf16[24,4608]{1,0:T(8,128)(2,1)S(1)} collective-permute-done((bf16[24,4608]{1,0:T(8,128)(2,1)S(1)}, bf16[24,4608]{1,0:T(8,128)(2,1)S(1)}, u32[]{:S(2)}, u32[]{:S(2)}) %collective-permute-start) | collective-permute-done | bytes 221216 | tf_op jit(solution)/shard_map/ppermute | solution.py:194
  4.1 0.1 add.106.refs_2_
  4.2 2.9 %collective-permute-start.2 = (bf16[24,4608]{1,0:T(8,128)(2,1)S(1)}, bf16[24,4608]{1,0:T(8,128)(2,1)S(1)}, u32[]{:S(2)}, u32[]{:S(2)}) collective-permute-start(bf16[24,4608]{1,0:T(8,128)(2,1)S(1)} %add.106.refs_2_), channel_id=1, source_target_pairs={{4,0},{8,4},{12,8},{14,12},{10,14},{6,10},{2,6},{0,2},{5,1},{9,5},... | collective-permute-start | bytes 663560 | tf_op jit(solution)/shard_map/ppermute | solution.py:221
  7.0 0.2 collective-permute-start.1
  7.2 0.0 collective-permute-done.3
  7.2 0.1 add.111.refs_10_
  7.2 1.9 %collective-permute-start.13 = (bf16[24,4608]{1,0:T(8,128)(2,1)S(1)}, bf16[24,4608]{1,0:T(8,128)(2,1)S(1)}, u32[]{:S(2)}, u32[]{:S(2)}) collective-permute-start(bf16[24,4608]{1,0:T(8,128)(2,1)S(1)} %add.111.refs_10_), channel_id=1, source_target_pairs={{4,0},{8,4},{12,8},{14,12},{10,14},{6,10},{2,6},{0,2},{5,1},{9,5},... | collective-permute-start | bytes 663560 | tf_op jit(solution)/shard_map/ppermute | solution.py:221
  9.2 0.2 collective-permute-start.6
  9.4 3.9 %collective-permute-done.2.refs_4_ = bf16[24,4608]{1,0:T(8,128)(2,1)S(1)} collective-permute-done((bf16[24,4608]{1,0:T(8,128)(2,1)S(1)}, bf16[24,4608]{1,0:T(8,128)(2,1)S(1)}, u32[]{:S(2)}, u32[]{:S(2)}) %collective-permute-start.2) | collective-permute-done | bytes 221216 | tf_op jit(solution)/shard_map/ppermute | solution.py:221
  13.3 2.0 %collective-permute-done.1.refs_3_ = bf16[24,4608]{1,0:T(8,128)(2,1)S(1)} collective-permute-done((bf16[24,4608]{1,0:T(8,128)(2,1)S(1)}, bf16[24,4608]{1,0:T(8,128)(2,1)S(1)}, u32[]{:S(2)}, u32[]{:S(2)}) %collective-permute-start.1) | collective-permute-done | bytes 221216 | tf_op jit(solution)/shard_map/ppermute | solution.py:218
  15.4 0.1 collective-permute-start.4
  15.5 1.9 %collective-permute-start.5 = (bf16[24,4608]{1,0:T(8,128)(2,1)S(1)}, bf16[24,4608]{1,0:T(8,128)(2,1)S(1)}, u32[]{:S(2)}, u32[]{:S(2)}) collective-permute-start(bf16[24,4608]{1,0:T(8,128)(2,1)S(1)} %collective-permute-done.2.refs_4_), channel_id=1, source_target_pairs={{4,0},{8,4},{12,8},{14,12},{10,14},{6,10},{2,6},{0,2},{5,1},{9,5},... | collective-permute-start | bytes 663560 | tf_op jit(solution)/shard_map/ppermute | solution.py:221
  17.4 0.7 %collective-permute-done.13.refs_12_ = bf16[24,4608]{1,0:T(8,128)(2,1)S(1)} collective-permute-done((bf16[24,4608]{1,0:T(8,128)(2,1)S(1)}, bf16[24,4608]{1,0:T(8,128)(2,1)S(1)}, u32[]{:S(2)}, u32[]{:S(2)}) %collective-permute-start.13) | collective-permute-done | bytes 221216 | tf_op jit(solution)/shard_map/ppermute | solution.py:221
  18.1 2.0 %collective-permute-start.14 = (bf16[24,4608]{1,0:T(8,128)(2,1)S(1)}, bf16[24,4608]{1,0:T(8,128)(2,1)S(1)}, u32[]{:S(2)}, u32[]{:S(2)}) collective-permute-start(bf16[24,4608]{1,0:T(8,128)(2,1)S(1)} %collective-permute-done.13.refs_12_), channel_id=1, source_target_pairs={{4,0},{8,4},{12,8},{14,12},{10,14},{6,10},{2,6},{0,2},{5,1},{9,5},... | collective-permute-start | bytes 663560 | tf_op jit(solution)/shard_map/ppermute | solution.py:221
  20.0 0.0 collective-permute-done.6.refs_11_
  20.1 0.1 collective-permute-start.10
  20.4 4.4 %collective-permute-done.4.refs_5_ = bf16[24,4608]{1,0:T(8,128)(2,1)S(1)} collective-permute-done((bf16[24,4608]{1,0:T(8,128)(2,1)S(1)}, bf16[24,4608]{1,0:T(8,128)(2,1)S(1)}, u32[]{:S(2)}, u32[]{:S(2)}) %collective-permute-start.4) | collective-permute-done | bytes 221216 | tf_op jit(solution)/shard_map/ppermute | solution.py:218
  24.8 2.2 %collective-permute-done.14.refs_14_ = bf16[24,4608]{1,0:T(8,128)(2,1)S(1)} collective-permute-done((bf16[24,4608]{1,0:T(8,128)(2,1)S(1)}, bf16[24,4608]{1,0:T(8,128)(2,1)S(1)}, u32[]{:S(2)}, u32[]{:S(2)}) %collective-permute-start.14) | collective-permute-done | bytes 221216 | tf_op jit(solution)/shard_map/ppermute | solution.py:221
  27.1 1.7 %collective-permute-start.16 = (bf16[24,4608]{1,0:T(8,128)(2,1)S(1)}, bf16[24,4608]{1,0:T(8,128)(2,1)S(1)}, u32[]{:S(2)}, u32[]{:S(2)}) collective-permute-start(bf16[24,4608]{1,0:T(8,128)(2,1)S(1)} %collective-permute-done.14.refs_14_), channel_id=1, source_target_pairs={{4,0},{8,4},{12,8},{14,12},{10,14},{6,10},{2,6},{0,2},{5,1},{9,5},... | collective-permute-start | bytes 663560 | tf_op jit(solution)/shard_map/ppermute | solution.py:221
  28.7 0.0 collective-permute-done.5.refs_6_
  28.7 0.4 collective-permute-start.7
  29.1 1.7 %collective-permute-start.8 = (bf16[24,4608]{1,0:T(8,128)(2,1)S(1)}, bf16[24,4608]{1,0:T(8,128)(2,1)S(1)}, u32[]{:S(2)}, u32[]{:S(2)}) collective-permute-start(bf16[24,4608]{1,0:T(8,128)(2,1)S(1)} %collective-permute-done.5.refs_6_), channel_id=1, source_target_pairs={{4,0},{8,4},{12,8},{14,12},{10,14},{6,10},{2,6},{0,2},{5,1},{9,5},... | collective-permute-start | bytes 663560 | tf_op jit(solution)/shard_map/ppermute | solution.py:221
  30.8 0.0 collective-permute-done.10.refs_13_
  30.8 0.4 collective-permute-start.15
  31.3 4.1 %collective-permute-done.16.refs_16_ = bf16[24,4608]{1,0:T(8,128)(2,1)S(1)} collective-permute-done((bf16[24,4608]{1,0:T(8,128)(2,1)S(1)}, bf16[24,4608]{1,0:T(8,128)(2,1)S(1)}, u32[]{:S(2)}, u32[]{:S(2)}) %collective-permute-start.16) | collective-permute-done | bytes 221216 | tf_op jit(solution)/shard_map/ppermute | solution.py:221
  35.4 1.7 %collective-permute-done.7.refs_7_ = bf16[24,4608]{1,0:T(8,128)(2,1)S(1)} collective-permute-done((bf16[24,4608]{1,0:T(8,128)(2,1)S(1)}, bf16[24,4608]{1,0:T(8,128)(2,1)S(1)}, u32[]{:S(2)}, u32[]{:S(2)}) %collective-permute-start.7) | collective-permute-done | bytes 221216 | tf_op jit(solution)/shard_map/ppermute | solution.py:218
  37.1 1.6 %collective-permute-start.18 = (bf16[24,4608]{1,0:T(8,128)(2,1)S(1)}, bf16[24,4608]{1,0:T(8,128)(2,1)S(1)}, u32[]{:S(2)}, u32[]{:S(2)}) collective-permute-start(bf16[24,4608]{1,0:T(8,128)(2,1)S(1)} %collective-permute-done.16.refs_16_), channel_id=1, source_target_pairs={{4,0},{8,4},{12,8},{14,12},{10,14},{6,10},{2,6},{0,2},{5,1},{9,5},... | collective-permute-start | bytes 663560 | tf_op jit(solution)/shard_map/ppermute | solution.py:221
  38.7 0.4 collective-permute-start.11
  39.1 1.0 %collective-permute-done.8.refs_8_ = bf16[24,4608]{1,0:T(8,128)(2,1)S(1)} collective-permute-done((bf16[24,4608]{1,0:T(8,128)(2,1)S(1)}, bf16[24,4608]{1,0:T(8,128)(2,1)S(1)}, u32[]{:S(2)}, u32[]{:S(2)}) %collective-permute-start.8) | collective-permute-done | bytes 221216 | tf_op jit(solution)/shard_map/ppermute | solution.py:221
  40.2 0.1 collective-permute-start.9
  40.2 1.0 %collective-permute-done.15.refs_15_ = bf16[24,4608]{1,0:T(8,128)(2,1)S(1)} collective-permute-done((bf16[24,4608]{1,0:T(8,128)(2,1)S(1)}, bf16[24,4608]{1,0:T(8,128)(2,1)S(1)}, u32[]{:S(2)}, u32[]{:S(2)}) %collective-permute-start.15) | collective-permute-done | bytes 221216 | tf_op jit(solution)/shard_map/ppermute | solution.py:218
  41.3 0.1 collective-permute-start.17
  41.4 1.6 %collective-permute-done.18.refs_17_ = bf16[24,4608]{1,0:T(8,128)(2,1)S(1)} collective-permute-done((bf16[24,4608]{1,0:T(8,128)(2,1)S(1)}, bf16[24,4608]{1,0:T(8,128)(2,1)S(1)}, u32[]{:S(2)}, u32[]{:S(2)}) %collective-permute-start.18) | collective-permute-done | bytes 221216 | tf_op jit(solution)/shard_map/ppermute | solution.py:221
  43.0 0.1 collective-permute-start.19
  43.1 1.5 %collective-permute-done.11.refs_9_ = bf16[24,4608]{1,0:T(8,128)(2,1)S(1)} collective-permute-done((bf16[24,4608]{1,0:T(8,128)(2,1)S(1)}, bf16[24,4608]{1,0:T(8,128)(2,1)S(1)}, u32[]{:S(2)}, u32[]{:S(2)}) %collective-permute-start.11) | collective-permute-done | bytes 221216 | tf_op jit(solution)/shard_map/ppermute | solution.py:218
  44.6 0.1 collective-permute-start.12
  44.7 0.0 collective-permute-done.19
  44.7 1.2 %collective-permute-done.12 = bf16[24,1152]{1,0:T(8,128)(2,1)S(1)} collective-permute-done((bf16[24,1152]{1,0:T(8,128)(2,1)S(1)}, bf16[24,1152]{1,0:T(8,128)(2,1)S(1)}, u32[]{:S(2)}, u32[]{:S(2)}) %collective-permute-start.12) | collective-permute-done | bytes 55328 | tf_op jit(solution)/shard_map/ppermute | solution.py:208
  46.0 0.0 collective-permute-done.9
  46.1 0.0 collective-permute-done.17
  46.2 18.9 %shard_map.51 = (f32[1792,7168]{1,0:T(8,128)}, f32[512,2048]{1,0:T(8,128)}) custom-call(bf16[192,1152]{1,0:T(8,128)(2,1)S(1)} %pad_maximum_fusion.refs_0_, bf16[192,1152]{1,0:T(8,128)(2,1)S(1)} %pad_maximum_fusion.1.refs_1_, bf16[24,4608]{1,0:T(8,128)(2,1)S(1)} %add.106.refs_2_, bf16[24,4608]{1,0:T(8,128)(2,1)S(1)} %collective-permute-done.1.refs_3_, ...), custom_call_target="tpu_custom_call" | custom-call | flops 5335154688 | bytes 55574528 | tf_op jit(solution)/shard_map/pallas_call | solution.py:118
  (54 shorter events, 0.6 us)
Async XLA Ops:
  2.4 1.7 %collective-permute-start = (bf16[24,4608]{1,0:T(8,128)(2,1)S(1)}, bf16[24,4608]{1,0:T(8,128)(2,1)S(1)}, u32[]{:S(2)}, u32[]{:S(2)}) collective-permute-start(bf16[24,4608]{1,0:T(8,128)(2,1)S(1)} %get-tuple-element.18), channel_id=1, source_target_pairs={{0,1},{1,0},{2,3},{3,2},{4,5},{5,4},{6,7},{7,6},{8,9},{9,8},{10,11... | collective-permute-start | bytes 663560 | tf_op jit(solution)/shard_map/ppermute | solution.py:194
  3.0 4.2 %collective-permute-start.3 = (bf16[24,4608]{1,0:T(8,128)(2,1)S(1)}, bf16[24,4608]{1,0:T(8,128)(2,1)S(1)}, u32[]{:S(2)}, u32[]{:S(2)}) collective-permute-start(bf16[24,4608]{1,0:T(8,128)(2,1)S(1)} %get-tuple-element.20), channel_id=1, source_target_pairs={{0,1},{1,0},{2,3},{3,2},{4,5},{5,4},{6,7},{7,6},{8,9},{9,8},{10,11... | collective-permute-start | bytes 663560 | tf_op jit(solution)/shard_map/ppermute | solution.py:194
  4.2 9.2 %collective-permute-start.2 = (bf16[24,4608]{1,0:T(8,128)(2,1)S(1)}, bf16[24,4608]{1,0:T(8,128)(2,1)S(1)}, u32[]{:S(2)}, u32[]{:S(2)}) collective-permute-start(bf16[24,4608]{1,0:T(8,128)(2,1)S(1)} %add.106.refs_2_), channel_id=1, source_target_pairs={{4,0},{8,4},{12,8},{14,12},{10,14},{6,10},{2,6},{0,2},{5,1},{9,5},... | collective-permute-start | bytes 663560 | tf_op jit(solution)/shard_map/ppermute | solution.py:221
  7.0 8.3 %collective-permute-start.1 = (bf16[24,4608]{1,0:T(8,128)(2,1)S(1)}, bf16[24,4608]{1,0:T(8,128)(2,1)S(1)}, u32[]{:S(2)}, u32[]{:S(2)}) collective-permute-start(bf16[24,4608]{1,0:T(8,128)(2,1)S(1)} %add.106.refs_2_), channel_id=1, source_target_pairs={{0,4},{4,8},{8,12},{12,14},{14,10},{10,6},{6,2},{2,0},{1,5},{5,9},... | collective-permute-start | bytes 663560 | tf_op jit(solution)/shard_map/ppermute | solution.py:218
  7.2 10.8 %collective-permute-start.13 = (bf16[24,4608]{1,0:T(8,128)(2,1)S(1)}, bf16[24,4608]{1,0:T(8,128)(2,1)S(1)}, u32[]{:S(2)}, u32[]{:S(2)}) collective-permute-start(bf16[24,4608]{1,0:T(8,128)(2,1)S(1)} %add.111.refs_10_), channel_id=1, source_target_pairs={{4,0},{8,4},{12,8},{14,12},{10,14},{6,10},{2,6},{0,2},{5,1},{9,5},... | collective-permute-start | bytes 663560 | tf_op jit(solution)/shard_map/ppermute | solution.py:221
  9.2 10.9 %collective-permute-start.6 = (bf16[24,4608]{1,0:T(8,128)(2,1)S(1)}, bf16[24,4608]{1,0:T(8,128)(2,1)S(1)}, u32[]{:S(2)}, u32[]{:S(2)}) collective-permute-start(bf16[24,4608]{1,0:T(8,128)(2,1)S(1)} %add.111.refs_10_), channel_id=1, source_target_pairs={{0,4},{4,8},{8,12},{12,14},{14,10},{10,6},{6,2},{2,0},{1,5},{5,9},... | collective-permute-start | bytes 663560 | tf_op jit(solution)/shard_map/ppermute | solution.py:218
  15.4 9.5 %collective-permute-start.4 = (bf16[24,4608]{1,0:T(8,128)(2,1)S(1)}, bf16[24,4608]{1,0:T(8,128)(2,1)S(1)}, u32[]{:S(2)}, u32[]{:S(2)}) collective-permute-start(bf16[24,4608]{1,0:T(8,128)(2,1)S(1)} %collective-permute-done.1.refs_3_), channel_id=1, source_target_pairs={{0,4},{4,8},{8,12},{12,14},{14,10},{10,6},{6,2},{2,0},{1,5},{5,9},... | collective-permute-start | bytes 663560 | tf_op jit(solution)/shard_map/ppermute | solution.py:218
  15.5 13.3 %collective-permute-start.5 = (bf16[24,4608]{1,0:T(8,128)(2,1)S(1)}, bf16[24,4608]{1,0:T(8,128)(2,1)S(1)}, u32[]{:S(2)}, u32[]{:S(2)}) collective-permute-start(bf16[24,4608]{1,0:T(8,128)(2,1)S(1)} %collective-permute-done.2.refs_4_), channel_id=1, source_target_pairs={{4,0},{8,4},{12,8},{14,12},{10,14},{6,10},{2,6},{0,2},{5,1},{9,5},... | collective-permute-start | bytes 663560 | tf_op jit(solution)/shard_map/ppermute | solution.py:221
  18.1 9.0 %collective-permute-start.14 = (bf16[24,4608]{1,0:T(8,128)(2,1)S(1)}, bf16[24,4608]{1,0:T(8,128)(2,1)S(1)}, u32[]{:S(2)}, u32[]{:S(2)}) collective-permute-start(bf16[24,4608]{1,0:T(8,128)(2,1)S(1)} %collective-permute-done.13.refs_12_), channel_id=1, source_target_pairs={{4,0},{8,4},{12,8},{14,12},{10,14},{6,10},{2,6},{0,2},{5,1},{9,5},... | collective-permute-start | bytes 663560 | tf_op jit(solution)/shard_map/ppermute | solution.py:221
  20.1 10.7 %collective-permute-start.10 = (bf16[24,4608]{1,0:T(8,128)(2,1)S(1)}, bf16[24,4608]{1,0:T(8,128)(2,1)S(1)}, u32[]{:S(2)}, u32[]{:S(2)}) collective-permute-start(bf16[24,4608]{1,0:T(8,128)(2,1)S(1)} %collective-permute-done.6.refs_11_), channel_id=1, source_target_pairs={{0,4},{4,8},{8,12},{12,14},{14,10},{10,6},{6,2},{2,0},{1,5},{5,9},... | collective-permute-start | bytes 663560 | tf_op jit(solution)/shard_map/ppermute | solution.py:218
  27.1 8.4 %collective-permute-start.16 = (bf16[24,4608]{1,0:T(8,128)(2,1)S(1)}, bf16[24,4608]{1,0:T(8,128)(2,1)S(1)}, u32[]{:S(2)}, u32[]{:S(2)}) collective-permute-start(bf16[24,4608]{1,0:T(8,128)(2,1)S(1)} %collective-permute-done.14.refs_14_), channel_id=1, source_target_pairs={{4,0},{8,4},{12,8},{14,12},{10,14},{6,10},{2,6},{0,2},{5,1},{9,5},... | collective-permute-start | bytes 663560 | tf_op jit(solution)/shard_map/ppermute | solution.py:221
  28.7 8.4 %collective-permute-start.7 = (bf16[24,4608]{1,0:T(8,128)(2,1)S(1)}, bf16[24,4608]{1,0:T(8,128)(2,1)S(1)}, u32[]{:S(2)}, u32[]{:S(2)}) collective-permute-start(bf16[24,4608]{1,0:T(8,128)(2,1)S(1)} %collective-permute-done.4.refs_5_), channel_id=1, source_target_pairs={{0,4},{4,8},{8,12},{12,14},{14,10},{10,6},{6,2},{2,0},{1,5},{5,9},... | collective-permute-start | bytes 663560 | tf_op jit(solution)/shard_map/ppermute | solution.py:218
  29.1 11.0 %collective-permute-start.8 = (bf16[24,4608]{1,0:T(8,128)(2,1)S(1)}, bf16[24,4608]{1,0:T(8,128)(2,1)S(1)}, u32[]{:S(2)}, u32[]{:S(2)}) collective-permute-start(bf16[24,4608]{1,0:T(8,128)(2,1)S(1)} %collective-permute-done.5.refs_6_), channel_id=1, source_target_pairs={{4,0},{8,4},{12,8},{14,12},{10,14},{6,10},{2,6},{0,2},{5,1},{9,5},... | collective-permute-start | bytes 663560 | tf_op jit(solution)/shard_map/ppermute | solution.py:221
  30.8 10.5 %collective-permute-start.15 = (bf16[24,4608]{1,0:T(8,128)(2,1)S(1)}, bf16[24,4608]{1,0:T(8,128)(2,1)S(1)}, u32[]{:S(2)}, u32[]{:S(2)}) collective-permute-start(bf16[24,4608]{1,0:T(8,128)(2,1)S(1)} %collective-permute-done.10.refs_13_), channel_id=1, source_target_pairs={{0,4},{4,8},{8,12},{12,14},{14,10},{10,6},{6,2},{2,0},{1,5},{5,9},... | collective-permute-start | bytes 663560 | tf_op jit(solution)/shard_map/ppermute | solution.py:218
  37.1 5.9 %collective-permute-start.18 = (bf16[24,4608]{1,0:T(8,128)(2,1)S(1)}, bf16[24,4608]{1,0:T(8,128)(2,1)S(1)}, u32[]{:S(2)}, u32[]{:S(2)}) collective-permute-start(bf16[24,4608]{1,0:T(8,128)(2,1)S(1)} %collective-permute-done.16.refs_16_), channel_id=1, source_target_pairs={{4,0},{8,4},{12,8},{14,12},{10,14},{6,10},{2,6},{0,2},{5,1},{9,5},... | collective-permute-start | bytes 663560 | tf_op jit(solution)/shard_map/ppermute | solution.py:221
  38.7 5.9 %collective-permute-start.11 = (bf16[24,4608]{1,0:T(8,128)(2,1)S(1)}, bf16[24,4608]{1,0:T(8,128)(2,1)S(1)}, u32[]{:S(2)}, u32[]{:S(2)}) collective-permute-start(bf16[24,4608]{1,0:T(8,128)(2,1)S(1)} %collective-permute-done.7.refs_7_), channel_id=1, source_target_pairs={{0,4},{4,8},{8,12},{12,14},{14,10},{10,6},{6,2},{2,0},{1,5},{5,9},... | collective-permute-start | bytes 663560 | tf_op jit(solution)/shard_map/ppermute | solution.py:218
  40.2 5.8 %collective-permute-start.9 = (bf16[168,1152]{1,0:T(8,128)(2,1)S(1)}, bf16[168,1152]{1,0:T(8,128)(2,1)S(1)}, u32[]{:S(2)}, u32[]{:S(2)}) collective-permute-start(bf16[168,1152]{1,0:T(8,128)(2,1)S(1)} %maximum_dynamic-update-slice_fusion), channel_id=1, source_target_pairs={{0,1},{1,0},{2,3},{3,2},{4,5},{5,4},{6,7},{7,6},{8,9},{9,8},{10,11... | collective-permute-start | bytes 1161224 | tf_op jit(solution)/shard_map/ppermute | solution.py:208
  41.3 4.7 %collective-permute-start.17 = (bf16[168,1152]{1,0:T(8,128)(2,1)S(1)}, bf16[168,1152]{1,0:T(8,128)(2,1)S(1)}, u32[]{:S(2)}, u32[]{:S(2)}) collective-permute-start(bf16[168,1152]{1,0:T(8,128)(2,1)S(1)} %maximum_dynamic-update-slice_fusion.7), channel_id=1, source_target_pairs={{0,1},{1,0},{2,3},{3,2},{4,5},{5,4},{6,7},{7,6},{8,9},{9,8},{10,11... | collective-permute-start | bytes 1161224 | tf_op jit(solution)/shard_map/ppermute | solution.py:208
  43.0 1.7 %collective-permute-start.19 = (bf16[24,1152]{1,0:T(8,128)(2,1)S(1)}, bf16[24,1152]{1,0:T(8,128)(2,1)S(1)}, u32[]{:S(2)}, u32[]{:S(2)}) collective-permute-start(bf16[24,1152]{1,0:T(8,128)(2,1)S(1)} %pad_maximum_fusion.3), channel_id=1, source_target_pairs={{0,1},{1,0},{2,3},{3,2},{4,5},{5,4},{6,7},{7,6},{8,9},{9,8},{10,11... | collective-permute-start | bytes 165896 | tf_op jit(solution)/shard_map/ppermute | solution.py:208
  44.6 1.3 %collective-permute-start.12 = (bf16[24,1152]{1,0:T(8,128)(2,1)S(1)}, bf16[24,1152]{1,0:T(8,128)(2,1)S(1)}, u32[]{:S(2)}, u32[]{:S(2)}) collective-permute-start(bf16[24,1152]{1,0:T(8,128)(2,1)S(1)} %pad_maximum_fusion.2), channel_id=1, source_target_pairs={{0,1},{1,0},{2,3},{3,2},{4,5},{5,4},{6,7},{7,6},{8,9},{9,8},{10,11... | collective-permute-start | bytes 165896 | tf_op jit(solution)/shard_map/ppermute | solution.py:208

commit v14 on v8

--- a/solution.py
+++ b/solution.py
@@ -8,7 +8,7 @@
 from jax.sharding import PartitionSpec as P
 
 
-SLOTS, PIECE = 4, 128
+SLOTS, CHUNK, PIECE = 4, 256, 128
 
 
 def chip_ring(rows):
@@ -57,11 +57,12 @@
     joined, buffer, sems = refs[-3:]
     turned = [left_ref if done else turned.pop(0) for left_ref, done in zip(left_refs, ready)]
 
-    def copy(group, slot, j):
+    def copy(group, slot, j, down=0, rows=None):
         _, height, (_, _, _, width), which, row, column, stride, _ = group
+        rows = rows or height
         return pltpu.make_async_copy(
-            buffer.at[slot, pl.ds(0, height), pl.ds(0, width)],
-            out_refs[which].at[pl.ds(row, height), pl.ds(pl.multiple_of(column + j * stride, 128), width)],
+            buffer.at[slot, pl.ds(down, rows), pl.ds(0, width)],
+            out_refs[which].at[pl.ds(row + down, rows), pl.ds(pl.multiple_of(column + j * stride, 128), width)],
             sems.at[slot],
         )
 
@@ -88,13 +89,14 @@
                 def _():
                     copy(earlier, slot, 0).wait()
 
-            for across in range(0, width, 256):
-                right = joined[:, across : across + 256]
-                for down in range(0, height, PIECE):
-                    rows = turned[left][down : down + PIECE, :]
-                    product = jnp.dot(rows, right, preferred_element_type=jnp.float32)
-                    buffer[slot, down : down + PIECE, across : across + 256] = product * scale
-            copy(group, slot, j).start()
+            for down in range(0, height, CHUNK):
+                for across in range(0, width, 256):
+                    right = joined[:, across : across + 256]
+                    for at in range(down, down + CHUNK, PIECE):
+                        rows = turned[left][at : at + PIECE, :]
+                        product = jnp.dot(rows, right, preferred_element_type=jnp.float32)
+                        buffer[slot, at : at + PIECE, across : across + 256] = product * scale
+                copy(group, slot, j, down, CHUNK).start()
             return carry
 
         lax.fori_loop(0, group[-1], step, 0)

time: 64.1 us -> 63.5 us (level)
  transfers between devices with their start and end apart: 22 -> 22, of which waited for: 11 -> 11; matrix products, arithmetic and copies ran while one was open for 1% -> 1% of each run, Pallas kernels for 12% -> 11%
where the time goes in v14:
time: 63.5 us; the launch traced here: 63.4 us
  Pallas kernels  21.2 us (33%)
  waiting for transfers between devices  21.2 us (33%)
  starting transfers between devices  18.8 us (30%)
  between operations  1.62 us (3%)
    pallas_call x3, Pallas kernels, tiles(): pl.pallas_call(functools.partial(tiles_kernel, scale, groups, ready, [len...  20 us
    ppermute x8, starting transfers between devices, local(): backward[k] = lax.ppermute(behind_of, 'row', behind)  15.4 us
    ppermute x8, waiting for transfers between devices, local(): backward[k] = lax.ppermute(behind_of, 'row', behind)  11.4 us
    ppermute x8, waiting for transfers between devices, local(): forward[k] = lax.ppermute(ahead_of, 'row', ahead)  8.82 us
    ppermute x8, starting transfers between devices, local(): forward[k] = lax.ppermute(ahead_of, 'row', ahead)  2.06 us
  transfers between devices with their start and end apart: 22, of which 11 were waited for; matrix products, arithmetic and copies ran while one was open for 1% of the time, Pallas kernels for 11%

profile of v14, /device:TPU:0, one launch (start us, length us, event | category | flops | bytes accessed | tf_op | source)
XLA Modules:
  0.0 63.4 jit_solution(14952765659505868299)
XLA Ops:
  1.3 1.1 %shard_map.50 = (bf16[24,4096]{1,0:T(8,128)(2,1)S(1)}, bf16[24,4096]{1,0:T(8,128)(2,1)S(1)}, bf16[24,5120]{1,0:T(8,128)(2,1)S(1)}, bf16[24,5120]{1,0:T(8,128)(2,1)S(1)}) custom-call(s32[1]{0:T(128)} %bitcast.half_ref, s32[1]{0:T(128)S(6)} %copy.23.count_ref, bf16[12,14336]{1,0:T(8,128)(2,1)} %act_ref.1, bf16[12,4096]{1,0:T(8,128)(2,1)} %grad_ref.1), custom_call_target="tpu_custom_call" | custom-call | tf_op jit(solution)/shard_map/pallas_call | solution.py:193
  2.4 0.6 collective-permute-start
  3.0 0.1 collective-permute-start.3
  3.1 1.0 %collective-permute-done = bf16[24,4096]{1,0:T(8,128)(2,1)S(1)} collective-permute-done((bf16[24,4096]{1,0:T(8,128)(2,1)S(1)}, bf16[24,4096]{1,0:T(8,128)(2,1)S(1)}, u32[]{:S(2)}, u32[]{:S(2)}) %collective-permute-start) | collective-permute-done | bytes 196640 | tf_op jit(solution)/shard_map/ppermute | solution.py:199
  4.1 2.9 %collective-permute-start.2 = (bf16[24,4096]{1,0:T(8,128)(2,1)S(1)}, bf16[24,4096]{1,0:T(8,128)(2,1)S(1)}, u32[]{:S(2)}, u32[]{:S(2)}) collective-permute-start(bf16[24,4096]{1,0:T(8,128)(2,1)S(1)} %add.76.refs_1_.refs_3_), channel_id=1, source_target_pairs={{4,0},{8,4},{12,8},{14,12},{10,14},{6,10},{2,6},{0,2},{5,1},{9,5},... | collective-permute-start | bytes 589832 | tf_op jit(solution)/shard_map/ppermute | solution.py:228
  7.0 0.2 collective-permute-start.1
  7.1 0.0 collective-permute-done.3
  7.1 0.1 add.79.refs_11_
  7.2 1.9 %collective-permute-start.14 = (bf16[24,5120]{1,0:T(8,128)(2,1)S(1)}, bf16[24,5120]{1,0:T(8,128)(2,1)S(1)}, u32[]{:S(2)}, u32[]{:S(2)}) collective-permute-start(bf16[24,5120]{1,0:T(8,128)(2,1)S(1)} %add.79.refs_11_), channel_id=1, source_target_pairs={{4,0},{8,4},{12,8},{14,12},{10,14},{6,10},{2,6},{0,2},{5,1},{9,5},... | collective-permute-start | bytes 737288 | tf_op jit(solution)/shard_map/ppermute | solution.py:228
  9.1 0.2 collective-permute-start.6
  9.3 3.5 %collective-permute-done.2.refs_3_.refs_5_ = bf16[24,4096]{1,0:T(8,128)(2,1)S(1)} collective-permute-done((bf16[24,4096]{1,0:T(8,128)(2,1)S(1)}, bf16[24,4096]{1,0:T(8,128)(2,1)S(1)}, u32[]{:S(2)}, u32[]{:S(2)}) %collective-permute-start.2) | collective-permute-done | bytes 196640 | tf_op jit(solution)/shard_map/ppermute | solution.py:228
  12.8 2.0 %collective-permute-done.1.refs_2_.refs_4_ = bf16[24,4096]{1,0:T(8,128)(2,1)S(1)} collective-permute-done((bf16[24,4096]{1,0:T(8,128)(2,1)S(1)}, bf16[24,4096]{1,0:T(8,128)(2,1)S(1)}, u32[]{:S(2)}, u32[]{:S(2)}) %collective-permute-start.1) | collective-permute-done | bytes 196640 | tf_op jit(solution)/shard_map/ppermute | solution.py:227
  14.8 0.1 collective-permute-start.4
  14.9 1.9 %collective-permute-start.5 = (bf16[24,4096]{1,0:T(8,128)(2,1)S(1)}, bf16[24,4096]{1,0:T(8,128)(2,1)S(1)}, u32[]{:S(2)}, u32[]{:S(2)}) collective-permute-start(bf16[24,4096]{1,0:T(8,128)(2,1)S(1)} %collective-permute-done.2.refs_3_.refs_5_), channel_id=1, source_target_pairs={{4,0},{8,4},{12,8},{14,12},{10,14},{6,10},{2,6},{0,2},{5,1},{9,5},... | collective-permute-start | bytes 589832 | tf_op jit(solution)/shard_map/ppermute | solution.py:228
  16.8 1.2 %collective-permute-done.14.refs_13_ = bf16[24,5120]{1,0:T(8,128)(2,1)S(1)} collective-permute-done((bf16[24,5120]{1,0:T(8,128)(2,1)S(1)}, bf16[24,5120]{1,0:T(8,128)(2,1)S(1)}, u32[]{:S(2)}, u32[]{:S(2)}) %collective-permute-start.14) | collective-permute-done | bytes 245792 | tf_op jit(solution)/shard_map/ppermute | solution.py:228
  18.0 2.0 %collective-permute-start.15 = (bf16[24,5120]{1,0:T(8,128)(2,1)S(1)}, bf16[24,5120]{1,0:T(8,128)(2,1)S(1)}, u32[]{:S(2)}, u32[]{:S(2)}) collective-permute-start(bf16[24,5120]{1,0:T(8,128)(2,1)S(1)} %collective-permute-done.14.refs_13_), channel_id=1, source_target_pairs={{4,0},{8,4},{12,8},{14,12},{10,14},{6,10},{2,6},{0,2},{5,1},{9,5},... | collective-permute-start | bytes 737288 | tf_op jit(solution)/shard_map/ppermute | solution.py:228
  20.0 0.0 collective-permute-done.6.refs_12_
  20.0 0.1 collective-permute-start.10
  20.2 2.5 %collective-permute-done.5.refs_5_.refs_7_ = bf16[24,4096]{1,0:T(8,128)(2,1)S(1)} collective-permute-done((bf16[24,4096]{1,0:T(8,128)(2,1)S(1)}, bf16[24,4096]{1,0:T(8,128)(2,1)S(1)}, u32[]{:S(2)}, u32[]{:S(2)}) %collective-permute-start.5) | collective-permute-done | bytes 196640 | tf_op jit(solution)/shard_map/ppermute | solution.py:228
  22.7 1.5 %collective-permute-done.4.refs_4_.refs_6_ = bf16[24,4096]{1,0:T(8,128)(2,1)S(1)} collective-permute-done((bf16[24,4096]{1,0:T(8,128)(2,1)S(1)}, bf16[24,4096]{1,0:T(8,128)(2,1)S(1)}, u32[]{:S(2)}, u32[]{:S(2)}) %collective-permute-start.4) | collective-permute-done | bytes 196640 | tf_op jit(solution)/shard_map/ppermute | solution.py:227
  24.2 0.5 collective-permute-start.7
  24.7 1.5 %collective-permute-start.8 = (bf16[24,4096]{1,0:T(8,128)(2,1)S(1)}, bf16[24,4096]{1,0:T(8,128)(2,1)S(1)}, u32[]{:S(2)}, u32[]{:S(2)}) collective-permute-start(bf16[24,4096]{1,0:T(8,128)(2,1)S(1)} %collective-permute-done.5.refs_5_.refs_7_), channel_id=1, source_target_pairs={{4,0},{8,4},{12,8},{14,12},{10,14},{6,10},{2,6},{0,2},{5,1},{9,5},... | collective-permute-start | bytes 589832 | tf_op jit(solution)/shard_map/ppermute | solution.py:228
  26.3 1.7 %collective-permute-done.15.refs_15_ = bf16[24,5120]{1,0:T(8,128)(2,1)S(1)} collective-permute-done((bf16[24,5120]{1,0:T(8,128)(2,1)S(1)}, bf16[24,5120]{1,0:T(8,128)(2,1)S(1)}, u32[]{:S(2)}, u32[]{:S(2)}) %collective-permute-start.15) | collective-permute-done | bytes 245792 | tf_op jit(solution)/shard_map/ppermute | solution.py:228
  28.0 1.9 %collective-permute-start.16 = (bf16[24,5120]{1,0:T(8,128)(2,1)S(1)}, bf16[24,5120]{1,0:T(8,128)(2,1)S(1)}, u32[]{:S(2)}, u32[]{:S(2)}) collective-permute-start(bf16[24,5120]{1,0:T(8,128)(2,1)S(1)} %collective-permute-done.15.refs_15_), channel_id=1, source_target_pairs={{4,0},{8,4},{12,8},{14,12},{10,14},{6,10},{2,6},{0,2},{5,1},{9,5},... | collective-permute-start | bytes 737288 | tf_op jit(solution)/shard_map/ppermute | solution.py:228
  29.9 0.0 collective-permute-done.10.refs_14_
  29.9 0.1 collective-permute-start.13
  30.1 2.5 %collective-permute-done.8.refs_7_.refs_9_ = bf16[24,4096]{1,0:T(8,128)(2,1)S(1)} collective-permute-done((bf16[24,4096]{1,0:T(8,128)(2,1)S(1)}, bf16[24,4096]{1,0:T(8,128)(2,1)S(1)}, u32[]{:S(2)}, u32[]{:S(2)}) %collective-permute-start.8) | collective-permute-done | bytes 196640 | tf_op jit(solution)/shard_map/ppermute | solution.py:228
  32.6 1.2 %collective-permute-done.7.refs_6_.refs_8_ = bf16[24,4096]{1,0:T(8,128)(2,1)S(1)} collective-permute-done((bf16[24,4096]{1,0:T(8,128)(2,1)S(1)}, bf16[24,4096]{1,0:T(8,128)(2,1)S(1)}, u32[]{:S(2)}, u32[]{:S(2)}) %collective-permute-start.7) | collective-permute-done | bytes 196640 | tf_op jit(solution)/shard_map/ppermute | solution.py:227
  33.8 1.6 %collective-permute-start.12 = (bf16[24,2048]{1,0:T(8,128)(2,1)S(1)}, bf16[24,2048]{1,0:T(8,128)(2,1)S(1)}, u32[]{:S(2)}, u32[]{:S(2)}) collective-permute-start(bf16[24,2048]{1,0:T(8,128)(2,1)S(1)} %slice.19), channel_id=1, source_target_pairs={{4,0},{8,4},{12,8},{14,12},{10,14},{6,10},{2,6},{0,2},{5,1},{9,5},... | collective-permute-start | bytes 294920 | tf_op jit(solution)/shard_map/ppermute | solution.py:228
  35.4 0.4 collective-permute-start.11
  35.8 0.1 collective-permute-start.9
  35.9 3.0 %collective-permute-done.13.refs_16_ = bf16[24,5120]{1,0:T(8,128)(2,1)S(1)} collective-permute-done((bf16[24,5120]{1,0:T(8,128)(2,1)S(1)}, bf16[24,5120]{1,0:T(8,128)(2,1)S(1)}, u32[]{:S(2)}, u32[]{:S(2)}) %collective-permute-start.13) | collective-permute-done | bytes 245792 | tf_op jit(solution)/shard_map/ppermute | solution.py:227
  38.9 0.0 collective-permute-done.12
  38.9 1.1 %collective-permute-done.11 = bf16[24,2048]{1,0:T(8,128)(2,1)S(1)} collective-permute-done((bf16[24,2048]{1,0:T(8,128)(2,1)S(1)}, bf16[24,2048]{1,0:T(8,128)(2,1)S(1)}, u32[]{:S(2)}, u32[]{:S(2)}) %collective-permute-start.11) | collective-permute-done | bytes 98336 | tf_op jit(solution)/shard_map/ppermute | solution.py:227
  40.0 0.0 collective-permute-done.16.refs_17_
  40.1 0.1 collective-permute-start.17
  40.2 0.5 collective-permute-start.19
  40.7 1.6 %collective-permute-start.20 = (bf16[24,2560]{1,0:T(8,128)(2,1)S(1)}, bf16[24,2560]{1,0:T(8,128)(2,1)S(1)}, u32[]{:S(2)}, u32[]{:S(2)}) collective-permute-start(bf16[24,2560]{1,0:T(8,128)(2,1)S(1)} %slice.21), channel_id=1, source_target_pairs={{4,0},{8,4},{12,8},{14,12},{10,14},{6,10},{2,6},{0,2},{5,1},{9,5},... | collective-permute-start | bytes 368648 | tf_op jit(solution)/shard_map/ppermute | solution.py:228
  42.3 0.1 collective-permute-start.18
  42.4 0.0 collective-permute-done.17
  42.4 0.0 collective-permute-done.9
  42.4 0.1 broadcast_select_fusion.1
  42.5 3.7 %shard_map.51 = (f32[1792,7168]{1,0:T(8,128)}, bf16[1024,192]{1,0:T(8,128)(2,1)S(1)}) custom-call(bf16[192,1024]{1,0:T(8,128)(2,1)S(1)} %pad_maximum_fusion.refs_0_, bf16[24,4096]{1,0:T(8,128)(2,1)S(1)} %add.76.refs_1_.refs_3_, bf16[24,4096]{1,0:T(8,128)(2,1)S(1)} %collective-permute-done.1.refs_2_.refs_4_, ...), custom_call_target="tpu_custom_call" | custom-call | flops 805306368 | bytes 8388608 | tf_op jit(solution)/shard_map/pallas_call | solution.py:125
  46.2 0.0 collective-permute-done.19
  46.2 0.0 collective-permute-done.20
  46.3 0.5 collective-permute-start.21
  46.9 3.5 %shard_map.52.refs_19_ = f32[1792,7168]{1,0:T(8,128)} custom-call(bf16[1024,192]{1,0:T(8,128)(2,1)S(1)} %get-tuple-element.43.refs_0_, bf16[24,4096]{1,0:T(8,128)(2,1)S(1)} %add.76.refs_1_.refs_3_, bf16[24,4096]{1,0:T(8,128)(2,1)S(1)} %collective-permute-done.1.refs_2_.refs_4_, ...), custom_call_target="tpu_custom_call", output_to_operand_aliasing={{}: (9, {})} | custom-call | flops 805306368 | bytes 8388608 | tf_op jit(solution)/shard_map/pallas_call | solution.py:125
  50.4 0.0 collective-permute-done.21
  50.4 0.0 collective-permute-done.18
  50.6 12.8 %shard_map.53 = (f32[1792,7168]{1,0:T(8,128)}, f32[512,2048]{1,0:T(8,128)}) custom-call(bf16[1024,192]{1,0:T(8,128)(2,1)S(1)} %get-tuple-element.43.refs_0_, bf16[192,768]{1,0:T(8,128)(2,1)S(1)} %fusion.refs_1_, bf16[192,512]{1,0:T(8,128)(2,1)S(1)} %pad_maximum_fusion.1.refs_2_, ...), custom_call_target="tpu_custom_call", output_to_operand_aliasing={{0}: (19, {})} | custom-call | flops 3724541952 | bytes 38797312 | tf_op jit(solution)/shard_map/pallas_call | solution.py:125
  (47 shorter events, 0.5 us)
Async XLA Ops:
  2.4 1.6 %collective-permute-start = (bf16[24,4096]{1,0:T(8,128)(2,1)S(1)}, bf16[24,4096]{1,0:T(8,128)(2,1)S(1)}, u32[]{:S(2)}, u32[]{:S(2)}) collective-permute-start(bf16[24,4096]{1,0:T(8,128)(2,1)S(1)} %get-tuple-element.27), channel_id=1, source_target_pairs={{0,1},{1,0},{2,3},{3,2},{4,5},{5,4},{6,7},{7,6},{8,9},{9,8},{10,11... | collective-permute-start | bytes 589832 | tf_op jit(solution)/shard_map/ppermute | solution.py:199
  3.0 4.1 %collective-permute-start.3 = (bf16[24,5120]{1,0:T(8,128)(2,1)S(1)}, bf16[24,5120]{1,0:T(8,128)(2,1)S(1)}, u32[]{:S(2)}, u32[]{:S(2)}) collective-permute-start(bf16[24,5120]{1,0:T(8,128)(2,1)S(1)} %get-tuple-element.29), channel_id=1, source_target_pairs={{0,1},{1,0},{2,3},{3,2},{4,5},{5,4},{6,7},{7,6},{8,9},{9,8},{10,11... | collective-permute-start | bytes 737288 | tf_op jit(solution)/shard_map/ppermute | solution.py:199
  4.1 8.6 %collective-permute-start.2 = (bf16[24,4096]{1,0:T(8,128)(2,1)S(1)}, bf16[24,4096]{1,0:T(8,128)(2,1)S(1)}, u32[]{:S(2)}, u32[]{:S(2)}) collective-permute-start(bf16[24,4096]{1,0:T(8,128)(2,1)S(1)} %add.76.refs_1_.refs_3_), channel_id=1, source_target_pairs={{4,0},{8,4},{12,8},{14,12},{10,14},{6,10},{2,6},{0,2},{5,1},{9,5},... | collective-permute-start | bytes 589832 | tf_op jit(solution)/shard_map/ppermute | solution.py:228
  7.0 7.8 %collective-permute-start.1 = (bf16[24,4096]{1,0:T(8,128)(2,1)S(1)}, bf16[24,4096]{1,0:T(8,128)(2,1)S(1)}, u32[]{:S(2)}, u32[]{:S(2)}) collective-permute-start(bf16[24,4096]{1,0:T(8,128)(2,1)S(1)} %add.76.refs_1_.refs_3_), channel_id=1, source_target_pairs={{0,4},{4,8},{8,12},{12,14},{14,10},{10,6},{6,2},{2,0},{1,5},{5,9},... | collective-permute-start | bytes 589832 | tf_op jit(solution)/shard_map/ppermute | solution.py:227
  7.2 10.8 %collective-permute-start.14 = (bf16[24,5120]{1,0:T(8,128)(2,1)S(1)}, bf16[24,5120]{1,0:T(8,128)(2,1)S(1)}, u32[]{:S(2)}, u32[]{:S(2)}) collective-permute-start(bf16[24,5120]{1,0:T(8,128)(2,1)S(1)} %add.79.refs_11_), channel_id=1, source_target_pairs={{4,0},{8,4},{12,8},{14,12},{10,14},{6,10},{2,6},{0,2},{5,1},{9,5},... | collective-permute-start | bytes 737288 | tf_op jit(solution)/shard_map/ppermute | solution.py:228
  9.1 10.9 %collective-permute-start.6 = (bf16[24,5120]{1,0:T(8,128)(2,1)S(1)}, bf16[24,5120]{1,0:T(8,128)(2,1)S(1)}, u32[]{:S(2)}, u32[]{:S(2)}) collective-permute-start(bf16[24,5120]{1,0:T(8,128)(2,1)S(1)} %add.79.refs_11_), channel_id=1, source_target_pairs={{0,4},{4,8},{8,12},{12,14},{14,10},{10,6},{6,2},{2,0},{1,5},{5,9},... | collective-permute-start | bytes 737288 | tf_op jit(solution)/shard_map/ppermute | solution.py:227
  14.8 9.5 %collective-permute-start.4 = (bf16[24,4096]{1,0:T(8,128)(2,1)S(1)}, bf16[24,4096]{1,0:T(8,128)(2,1)S(1)}, u32[]{:S(2)}, u32[]{:S(2)}) collective-permute-start(bf16[24,4096]{1,0:T(8,128)(2,1)S(1)} %collective-permute-done.1.refs_2_.refs_4_), channel_id=1, source_target_pairs={{0,4},{4,8},{8,12},{12,14},{14,10},{10,6},{6,2},{2,0},{1,5},{5,9},... | collective-permute-start | bytes 589832 | tf_op jit(solution)/shard_map/ppermute | solution.py:227
  14.9 7.8 %collective-permute-start.5 = (bf16[24,4096]{1,0:T(8,128)(2,1)S(1)}, bf16[24,4096]{1,0:T(8,128)(2,1)S(1)}, u32[]{:S(2)}, u32[]{:S(2)}) collective-permute-start(bf16[24,4096]{1,0:T(8,128)(2,1)S(1)} %collective-permute-done.2.refs_3_.refs_5_), channel_id=1, source_target_pairs={{4,0},{8,4},{12,8},{14,12},{10,14},{6,10},{2,6},{0,2},{5,1},{9,5},... | collective-permute-start | bytes 589832 | tf_op jit(solution)/shard_map/ppermute | solution.py:228
  18.0 10.0 %collective-permute-start.15 = (bf16[24,5120]{1,0:T(8,128)(2,1)S(1)}, bf16[24,5120]{1,0:T(8,128)(2,1)S(1)}, u32[]{:S(2)}, u32[]{:S(2)}) collective-permute-start(bf16[24,5120]{1,0:T(8,128)(2,1)S(1)} %collective-permute-done.14.refs_13_), channel_id=1, source_target_pairs={{4,0},{8,4},{12,8},{14,12},{10,14},{6,10},{2,6},{0,2},{5,1},{9,5},... | collective-permute-start | bytes 737288 | tf_op jit(solution)/shard_map/ppermute | solution.py:228
  20.0 9.9 %collective-permute-start.10 = (bf16[24,5120]{1,0:T(8,128)(2,1)S(1)}, bf16[24,5120]{1,0:T(8,128)(2,1)S(1)}, u32[]{:S(2)}, u32[]{:S(2)}) collective-permute-start(bf16[24,5120]{1,0:T(8,128)(2,1)S(1)} %collective-permute-done.6.refs_12_), channel_id=1, source_target_pairs={{0,4},{4,8},{8,12},{12,14},{14,10},{10,6},{6,2},{2,0},{1,5},{5,9},... | collective-permute-start | bytes 737288 | tf_op jit(solution)/shard_map/ppermute | solution.py:227
  24.2 9.5 %collective-permute-start.7 = (bf16[24,4096]{1,0:T(8,128)(2,1)S(1)}, bf16[24,4096]{1,0:T(8,128)(2,1)S(1)}, u32[]{:S(2)}, u32[]{:S(2)}) collective-permute-start(bf16[24,4096]{1,0:T(8,128)(2,1)S(1)} %collective-permute-done.4.refs_4_.refs_6_), channel_id=1, source_target_pairs={{0,4},{4,8},{8,12},{12,14},{14,10},{10,6},{6,2},{2,0},{1,5},{5,9},... | collective-permute-start | bytes 589832 | tf_op jit(solution)/shard_map/ppermute | solution.py:227
  24.7 7.8 %collective-permute-start.8 = (bf16[24,4096]{1,0:T(8,128)(2,1)S(1)}, bf16[24,4096]{1,0:T(8,128)(2,1)S(1)}, u32[]{:S(2)}, u32[]{:S(2)}) collective-permute-start(bf16[24,4096]{1,0:T(8,128)(2,1)S(1)} %collective-permute-done.5.refs_5_.refs_7_), channel_id=1, source_target_pairs={{4,0},{8,4},{12,8},{14,12},{10,14},{6,10},{2,6},{0,2},{5,1},{9,5},... | collective-permute-start | bytes 589832 | tf_op jit(solution)/shard_map/ppermute | solution.py:228
  28.0 12.0 %collective-permute-start.16 = (bf16[24,5120]{1,0:T(8,128)(2,1)S(1)}, bf16[24,5120]{1,0:T(8,128)(2,1)S(1)}, u32[]{:S(2)}, u32[]{:S(2)}) collective-permute-start(bf16[24,5120]{1,0:T(8,128)(2,1)S(1)} %collective-permute-done.15.refs_15_), channel_id=1, source_target_pairs={{4,0},{8,4},{12,8},{14,12},{10,14},{6,10},{2,6},{0,2},{5,1},{9,5},... | collective-permute-start | bytes 737288 | tf_op jit(solution)/shard_map/ppermute | solution.py:228
  29.9 9.0 %collective-permute-start.13 = (bf16[24,5120]{1,0:T(8,128)(2,1)S(1)}, bf16[24,5120]{1,0:T(8,128)(2,1)S(1)}, u32[]{:S(2)}, u32[]{:S(2)}) collective-permute-start(bf16[24,5120]{1,0:T(8,128)(2,1)S(1)} %collective-permute-done.10.refs_14_), channel_id=1, source_target_pairs={{0,4},{4,8},{8,12},{12,14},{14,10},{10,6},{6,2},{2,0},{1,5},{5,9},... | collective-permute-start | bytes 737288 | tf_op jit(solution)/shard_map/ppermute | solution.py:227
  33.8 5.2 %collective-permute-start.12 = (bf16[24,2048]{1,0:T(8,128)(2,1)S(1)}, bf16[24,2048]{1,0:T(8,128)(2,1)S(1)}, u32[]{:S(2)}, u32[]{:S(2)}) collective-permute-start(bf16[24,2048]{1,0:T(8,128)(2,1)S(1)} %slice.19), channel_id=1, source_target_pairs={{4,0},{8,4},{12,8},{14,12},{10,14},{6,10},{2,6},{0,2},{5,1},{9,5},... | collective-permute-start | bytes 294920 | tf_op jit(solution)/shard_map/ppermute | solution.py:228
  35.4 4.6 %collective-permute-start.11 = (bf16[24,2048]{1,0:T(8,128)(2,1)S(1)}, bf16[24,2048]{1,0:T(8,128)(2,1)S(1)}, u32[]{:S(2)}, u32[]{:S(2)}) collective-permute-start(bf16[24,2048]{1,0:T(8,128)(2,1)S(1)} %slice.18), channel_id=1, source_target_pairs={{0,4},{4,8},{8,12},{12,14},{14,10},{10,6},{6,2},{2,0},{1,5},{5,9},... | collective-permute-start | bytes 294920 | tf_op jit(solution)/shard_map/ppermute | solution.py:227
  35.8 6.6 %collective-permute-start.9 = (bf16[168,1024]{1,0:T(8,128)(2,1)S(1)}, bf16[168,1024]{1,0:T(8,128)(2,1)S(1)}, u32[]{:S(2)}, u32[]{:S(2)}) collective-permute-start(bf16[168,1024]{1,0:T(8,128)(2,1)S(1)} %dynamic-slice_dynamic-update-slice_fusion), channel_id=1, source_target_pairs={{0,1},{1,0},{2,3},{3,2},{4,5},{5,4},{6,7},{7,6},{8,9},{9,8},{10,11... | collective-permute-start | bytes 1032200 | tf_op jit(solution)/shard_map/ppermute | solution.py:215
  40.1 2.3 %collective-permute-start.17 = (bf16[24,1024]{1,0:T(8,128)(2,1)S(1)}, bf16[24,1024]{1,0:T(8,128)(2,1)S(1)}, u32[]{:S(2)}, u32[]{:S(2)}) collective-permute-start(bf16[24,1024]{1,0:T(8,128)(2,1)S(1)} %constant_dynamic-slice_fusion.16), channel_id=1, source_target_pairs={{0,1},{1,0},{2,3},{3,2},{4,5},{5,4},{6,7},{7,6},{8,9},{9,8},{10,11... | collective-permute-start | bytes 147464 | tf_op jit(solution)/shard_map/ppermute | solution.py:215
  40.2 6.1 %collective-permute-start.19 = (bf16[24,2560]{1,0:T(8,128)(2,1)S(1)}, bf16[24,2560]{1,0:T(8,128)(2,1)S(1)}, u32[]{:S(2)}, u32[]{:S(2)}) collective-permute-start(bf16[24,2560]{1,0:T(8,128)(2,1)S(1)} %slice.20), channel_id=1, source_target_pairs={{0,4},{4,8},{8,12},{12,14},{14,10},{10,6},{6,2},{2,0},{1,5},{5,9},... | collective-permute-start | bytes 368648 | tf_op jit(solution)/shard_map/ppermute | solution.py:227
  40.7 5.6 %collective-permute-start.20 = (bf16[24,2560]{1,0:T(8,128)(2,1)S(1)}, bf16[24,2560]{1,0:T(8,128)(2,1)S(1)}, u32[]{:S(2)}, u32[]{:S(2)}) collective-permute-start(bf16[24,2560]{1,0:T(8,128)(2,1)S(1)} %slice.21), channel_id=1, source_target_pairs={{4,0},{8,4},{12,8},{14,12},{10,14},{6,10},{2,6},{0,2},{5,1},{9,5},... | collective-permute-start | bytes 368648 | tf_op jit(solution)/shard_map/ppermute | solution.py:228
  42.3 8.1 %collective-permute-start.18 = (bf16[168,1280]{1,0:T(8,128)(2,1)S(1)}, bf16[168,1280]{1,0:T(8,128)(2,1)S(1)}, u32[]{:S(2)}, u32[]{:S(2)}) collective-permute-start(bf16[168,1280]{1,0:T(8,128)(2,1)S(1)} %maximum_dynamic-update-slice_fusion), channel_id=1, source_target_pairs={{0,1},{1,0},{2,3},{3,2},{4,5},{5,4},{6,7},{7,6},{8,9},{9,8},{10,11... | collective-permute-start | bytes 1290248 | tf_op jit(solution)/shard_map/ppermute | solution.py:215
  46.3 4.1 %collective-permute-start.21 = (bf16[24,1280]{1,0:T(8,128)(2,1)S(1)}, bf16[24,1280]{1,0:T(8,128)(2,1)S(1)}, u32[]{:S(2)}, u32[]{:S(2)}) collective-permute-start(bf16[24,1280]{1,0:T(8,128)(2,1)S(1)} %pad_maximum_fusion.2), channel_id=1, source_target_pairs={{0,1},{1,0},{2,3},{3,2},{4,5},{5,4},{6,7},{7,6},{8,9},{9,8},{10,11... | collective-permute-start | bytes 184328 | tf_op jit(solution)/shard_map/ppermute | solution.py:215

commit v15 on v14

--- a/solution.py
+++ b/solution.py
@@ -66,29 +66,22 @@
             sems.at[slot],
         )
 
-    earlier, done = None, [index for index, is_ready in enumerate(ready) if is_ready]
-    for group in groups:
+    done = [index for index, is_ready in enumerate(ready) if is_ready]
+    banks = buffer.shape[0] // SLOTS
+    for number, group in enumerate(groups):
         left = group[0]
         if left not in done:
             done.append(left)
             turned[left][...] = left_refs[left][...].T
-
-        def step(j, carry, group=group, earlier=earlier):
+        earlier = groups[number - banks] if number >= banks else None
+
+        def step(j, carry, group=group, earlier=earlier, bank=number % banks):
             left, height, (source, first, apart, width), _, _, _, _, _ = group
-            slot = lax.rem(j, SLOTS)
+            slot = bank * SLOTS + j
             here = pl.ds(pl.multiple_of(first + j * apart, 128), width)
             joined[:, :width] = jnp.concatenate([ref[:, here] for ref in sources[source]], axis=0)
-
-            @pl.when(j >= SLOTS)
-            def _():
-                copy(group, slot, 0).wait()
-
             if earlier is not None:
-
-                @pl.when(j < SLOTS)
-                def _():
-                    copy(earlier, slot, 0).wait()
-
+                copy(earlier, slot, j).wait()
             for down in range(0, height, CHUNK):
                 for across in range(0, width, 256):
                     right = joined[:, across : across + 256]
@@ -99,13 +92,13 @@
                 copy(group, slot, j, down, CHUNK).start()
             return carry
 
-        lax.fori_loop(0, group[-1], step, 0)
-        earlier = group
-    for slot in range(SLOTS):
-        copy(earlier, slot, 0).wait()
-
-
-def tiles(scale, groups, lefts, lists, out_shapes, out=None, ready=(), hand_on=False):
+        lax.fori_loop(0, SLOTS, step, 0)
+    for number in range(max(0, len(groups) - banks), len(groups)):
+        for j in range(SLOTS):
+            copy(groups[number], number % banks * SLOTS + j, j).wait()
+
+
+def tiles(scale, groups, lefts, lists, out_shapes, out=None, ready=(), hand_on=False, banks=1):
     ready = tuple(ready) or (False,) * len(lefts)
     tokens = lists[0][0].shape[0] * len(lists[0])
     whole, anywhere = pl.BlockSpec(memory_space=pltpu.VMEM), pl.BlockSpec(memory_space=pl.ANY)
@@ -132,8 +125,8 @@
         scratch_shapes=[pltpu.VMEM(shape, jnp.bfloat16) for shape in turned[int(hand_on) :]]
         + [
             pltpu.VMEM((tokens, max(g[2][3] for g in groups)), jnp.bfloat16),
-            pltpu.VMEM((SLOTS, max(g[1] for g in groups), max(g[2][3] for g in groups)), jnp.float32),
-            pltpu.SemaphoreType.DMA((SLOTS,)),
+            pltpu.VMEM((banks * SLOTS, max(g[1] for g in groups), max(g[2][3] for g in groups)), jnp.float32),
+            pltpu.SemaphoreType.DMA((banks * SLOTS,)),
         ],
         input_output_aliases=aliases,
         compiler_params=pltpu.CompilerParams(vmem_limit_bytes=32 * 1024 * 1024),
@@ -180,7 +173,7 @@
         grad_width = pseudo_grads.shape[1]
         act_half, grad_half = act_width // cols, grad_width // cols
         act_block, grad_block = act_width // rows, grad_width // rows
-        cut = act_block * 4 // 7 if act_block % 1792 == 0 else act_block
+        cut = act_block * 4 // 7 if act_block % 1792 == 0 and half_rows == SLOTS else act_block
         rest = act_block - cut
         widths = [half_rows * cut, half_rows * rest + grad_half]
         if rest == 0:
@@ -248,7 +241,7 @@
             def square(part, lefts, out, **more):
                 starts = [part * cut // 2, part * cut // 2 + cut // 4]
                 groups = [(0, cut, (0, at, cut, cut // 4), 0, 0, at, act_block, half_rows) for at in starts]
-                return tiles(scale, groups, lefts, [chains[0]], [act_shape], out, **more)
+                return tiles(scale, groups, lefts, [chains[0]], [act_shape], out, banks=2, **more)
 
             act_cov, turned_first = square(0, [left_first], None, hand_on=True)
             last_second, act_cov = lax.optimization_barrier(((forward[1], backward[1]), act_cov))

time: 63.5 us -> 63.6 us (level)
  no operation moved by 1% of the time
where the time goes in v15:
time: 63.6 us; the launch traced here: 63.4 us
  Pallas kernels  21.2 us (33%)
  waiting for transfers between devices  21.2 us (33%)
  starting transfers between devices  18.8 us (30%)
  between operations  1.62 us (3%)
    pallas_call x3, Pallas kernels, tiles(): pl.pallas_call(functools.partial(tiles_kernel, scale, groups, ready, [len...  20.1 us
    ppermute x8, starting transfers between devices, local(): backward[k] = lax.ppermute(behind_of, 'row', behind)  15.4 us
    ppermute x8, waiting for transfers between devices, local(): backward[k] = lax.ppermute(behind_of, 'row', behind)  11.4 us
    ppermute x8, waiting for transfers between devices, local(): forward[k] = lax.ppermute(ahead_of, 'row', ahead)  8.82 us
    ppermute x8, starting transfers between devices, local(): forward[k] = lax.ppermute(ahead_of, 'row', ahead)  2.06 us
  transfers between devices with their start and end apart: 22, of which 11 were waited for; matrix products, arithmetic and copies ran while one was open for 1% of the time, Pallas kernels for 11%

profile of v15, /device:TPU:0, one launch (start us, length us, event | category | flops | bytes accessed | tf_op | source)
XLA Modules:
  0.0 63.4 jit_solution(3640656213222513268)
XLA Ops:
  1.3 1.1 %shard_map.50 = (bf16[24,4096]{1,0:T(8,128)(2,1)S(1)}, bf16[24,4096]{1,0:T(8,128)(2,1)S(1)}, bf16[24,5120]{1,0:T(8,128)(2,1)S(1)}, bf16[24,5120]{1,0:T(8,128)(2,1)S(1)}) custom-call(s32[1]{0:T(128)} %bitcast.half_ref, s32[1]{0:T(128)S(6)} %copy.23.count_ref, bf16[12,14336]{1,0:T(8,128)(2,1)} %act_ref.1, bf16[12,4096]{1,0:T(8,128)(2,1)} %grad_ref.1), custom_call_target="tpu_custom_call" | custom-call | tf_op jit(solution)/shard_map/pallas_call | solution.py:186
  2.4 0.6 collective-permute-start
  3.0 0.1 collective-permute-start.3
  3.1 1.0 %collective-permute-done = bf16[24,4096]{1,0:T(8,128)(2,1)S(1)} collective-permute-done((bf16[24,4096]{1,0:T(8,128)(2,1)S(1)}, bf16[24,4096]{1,0:T(8,128)(2,1)S(1)}, u32[]{:S(2)}, u32[]{:S(2)}) %collective-permute-start) | collective-permute-done | bytes 196640 | tf_op jit(solution)/shard_map/ppermute | solution.py:192
  4.1 2.9 %collective-permute-start.2 = (bf16[24,4096]{1,0:T(8,128)(2,1)S(1)}, bf16[24,4096]{1,0:T(8,128)(2,1)S(1)}, u32[]{:S(2)}, u32[]{:S(2)}) collective-permute-start(bf16[24,4096]{1,0:T(8,128)(2,1)S(1)} %add.76.refs_1_.refs_3_), channel_id=1, source_target_pairs={{4,0},{8,4},{12,8},{14,12},{10,14},{6,10},{2,6},{0,2},{5,1},{9,5},... | collective-permute-start | bytes 589832 | tf_op jit(solution)/shard_map/ppermute | solution.py:221
  7.0 0.2 collective-permute-start.1
  7.1 0.0 collective-permute-done.3
  7.1 0.1 add.79.refs_11_
  7.2 1.9 %collective-permute-start.14 = (bf16[24,5120]{1,0:T(8,128)(2,1)S(1)}, bf16[24,5120]{1,0:T(8,128)(2,1)S(1)}, u32[]{:S(2)}, u32[]{:S(2)}) collective-permute-start(bf16[24,5120]{1,0:T(8,128)(2,1)S(1)} %add.79.refs_11_), channel_id=1, source_target_pairs={{4,0},{8,4},{12,8},{14,12},{10,14},{6,10},{2,6},{0,2},{5,1},{9,5},... | collective-permute-start | bytes 737288 | tf_op jit(solution)/shard_map/ppermute | solution.py:221
  9.1 0.2 collective-permute-start.6
  9.3 3.5 %collective-permute-done.2.refs_3_.refs_5_ = bf16[24,4096]{1,0:T(8,128)(2,1)S(1)} collective-permute-done((bf16[24,4096]{1,0:T(8,128)(2,1)S(1)}, bf16[24,4096]{1,0:T(8,128)(2,1)S(1)}, u32[]{:S(2)}, u32[]{:S(2)}) %collective-permute-start.2) | collective-permute-done | bytes 196640 | tf_op jit(solution)/shard_map/ppermute | solution.py:221
  12.8 2.0 %collective-permute-done.1.refs_2_.refs_4_ = bf16[24,4096]{1,0:T(8,128)(2,1)S(1)} collective-permute-done((bf16[24,4096]{1,0:T(8,128)(2,1)S(1)}, bf16[24,4096]{1,0:T(8,128)(2,1)S(1)}, u32[]{:S(2)}, u32[]{:S(2)}) %collective-permute-start.1) | collective-permute-done | bytes 196640 | tf_op jit(solution)/shard_map/ppermute | solution.py:220
  14.8 0.1 collective-permute-start.4
  14.9 1.9 %collective-permute-start.5 = (bf16[24,4096]{1,0:T(8,128)(2,1)S(1)}, bf16[24,4096]{1,0:T(8,128)(2,1)S(1)}, u32[]{:S(2)}, u32[]{:S(2)}) collective-permute-start(bf16[24,4096]{1,0:T(8,128)(2,1)S(1)} %collective-permute-done.2.refs_3_.refs_5_), channel_id=1, source_target_pairs={{4,0},{8,4},{12,8},{14,12},{10,14},{6,10},{2,6},{0,2},{5,1},{9,5},... | collective-permute-start | bytes 589832 | tf_op jit(solution)/shard_map/ppermute | solution.py:221
  16.8 1.2 %collective-permute-done.14.refs_13_ = bf16[24,5120]{1,0:T(8,128)(2,1)S(1)} collective-permute-done((bf16[24,5120]{1,0:T(8,128)(2,1)S(1)}, bf16[24,5120]{1,0:T(8,128)(2,1)S(1)}, u32[]{:S(2)}, u32[]{:S(2)}) %collective-permute-start.14) | collective-permute-done | bytes 245792 | tf_op jit(solution)/shard_map/ppermute | solution.py:221
  18.0 2.0 %collective-permute-start.15 = (bf16[24,5120]{1,0:T(8,128)(2,1)S(1)}, bf16[24,5120]{1,0:T(8,128)(2,1)S(1)}, u32[]{:S(2)}, u32[]{:S(2)}) collective-permute-start(bf16[24,5120]{1,0:T(8,128)(2,1)S(1)} %collective-permute-done.14.refs_13_), channel_id=1, source_target_pairs={{4,0},{8,4},{12,8},{14,12},{10,14},{6,10},{2,6},{0,2},{5,1},{9,5},... | collective-permute-start | bytes 737288 | tf_op jit(solution)/shard_map/ppermute | solution.py:221
  20.0 0.0 collective-permute-done.6.refs_12_
  20.0 0.1 collective-permute-start.10
  20.2 2.5 %collective-permute-done.5.refs_5_.refs_7_ = bf16[24,4096]{1,0:T(8,128)(2,1)S(1)} collective-permute-done((bf16[24,4096]{1,0:T(8,128)(2,1)S(1)}, bf16[24,4096]{1,0:T(8,128)(2,1)S(1)}, u32[]{:S(2)}, u32[]{:S(2)}) %collective-permute-start.5) | collective-permute-done | bytes 196640 | tf_op jit(solution)/shard_map/ppermute | solution.py:221
  22.7 1.5 %collective-permute-done.4.refs_4_.refs_6_ = bf16[24,4096]{1,0:T(8,128)(2,1)S(1)} collective-permute-done((bf16[24,4096]{1,0:T(8,128)(2,1)S(1)}, bf16[24,4096]{1,0:T(8,128)(2,1)S(1)}, u32[]{:S(2)}, u32[]{:S(2)}) %collective-permute-start.4) | collective-permute-done | bytes 196640 | tf_op jit(solution)/shard_map/ppermute | solution.py:220
  24.2 0.5 collective-permute-start.7
  24.7 1.5 %collective-permute-start.8 = (bf16[24,4096]{1,0:T(8,128)(2,1)S(1)}, bf16[24,4096]{1,0:T(8,128)(2,1)S(1)}, u32[]{:S(2)}, u32[]{:S(2)}) collective-permute-start(bf16[24,4096]{1,0:T(8,128)(2,1)S(1)} %collective-permute-done.5.refs_5_.refs_7_), channel_id=1, source_target_pairs={{4,0},{8,4},{12,8},{14,12},{10,14},{6,10},{2,6},{0,2},{5,1},{9,5},... | collective-permute-start | bytes 589832 | tf_op jit(solution)/shard_map/ppermute | solution.py:221
  26.3 1.7 %collective-permute-done.15.refs_15_ = bf16[24,5120]{1,0:T(8,128)(2,1)S(1)} collective-permute-done((bf16[24,5120]{1,0:T(8,128)(2,1)S(1)}, bf16[24,5120]{1,0:T(8,128)(2,1)S(1)}, u32[]{:S(2)}, u32[]{:S(2)}) %collective-permute-start.15) | collective-permute-done | bytes 245792 | tf_op jit(solution)/shard_map/ppermute | solution.py:221
  28.0 1.9 %collective-permute-start.16 = (bf16[24,5120]{1,0:T(8,128)(2,1)S(1)}, bf16[24,5120]{1,0:T(8,128)(2,1)S(1)}, u32[]{:S(2)}, u32[]{:S(2)}) collective-permute-start(bf16[24,5120]{1,0:T(8,128)(2,1)S(1)} %collective-permute-done.15.refs_15_), channel_id=1, source_target_pairs={{4,0},{8,4},{12,8},{14,12},{10,14},{6,10},{2,6},{0,2},{5,1},{9,5},... | collective-permute-start | bytes 737288 | tf_op jit(solution)/shard_map/ppermute | solution.py:221
  29.9 0.0 collective-permute-done.10.refs_14_
  29.9 0.1 collective-permute-start.13
  30.1 2.5 %collective-permute-done.8.refs_7_.refs_9_ = bf16[24,4096]{1,0:T(8,128)(2,1)S(1)} collective-permute-done((bf16[24,4096]{1,0:T(8,128)(2,1)S(1)}, bf16[24,4096]{1,0:T(8,128)(2,1)S(1)}, u32[]{:S(2)}, u32[]{:S(2)}) %collective-permute-start.8) | collective-permute-done | bytes 196640 | tf_op jit(solution)/shard_map/ppermute | solution.py:221
  32.6 1.2 %collective-permute-done.7.refs_6_.refs_8_ = bf16[24,4096]{1,0:T(8,128)(2,1)S(1)} collective-permute-done((bf16[24,4096]{1,0:T(8,128)(2,1)S(1)}, bf16[24,4096]{1,0:T(8,128)(2,1)S(1)}, u32[]{:S(2)}, u32[]{:S(2)}) %collective-permute-start.7) | collective-permute-done | bytes 196640 | tf_op jit(solution)/shard_map/ppermute | solution.py:220
  33.8 1.6 %collective-permute-start.12 = (bf16[24,2048]{1,0:T(8,128)(2,1)S(1)}, bf16[24,2048]{1,0:T(8,128)(2,1)S(1)}, u32[]{:S(2)}, u32[]{:S(2)}) collective-permute-start(bf16[24,2048]{1,0:T(8,128)(2,1)S(1)} %slice.19), channel_id=1, source_target_pairs={{4,0},{8,4},{12,8},{14,12},{10,14},{6,10},{2,6},{0,2},{5,1},{9,5},... | collective-permute-start | bytes 294920 | tf_op jit(solution)/shard_map/ppermute | solution.py:221
  35.4 0.4 collective-permute-start.11
  35.8 0.1 collective-permute-start.9
  35.9 3.0 %collective-permute-done.13.refs_16_ = bf16[24,5120]{1,0:T(8,128)(2,1)S(1)} collective-permute-done((bf16[24,5120]{1,0:T(8,128)(2,1)S(1)}, bf16[24,5120]{1,0:T(8,128)(2,1)S(1)}, u32[]{:S(2)}, u32[]{:S(2)}) %collective-permute-start.13) | collective-permute-done | bytes 245792 | tf_op jit(solution)/shard_map/ppermute | solution.py:220
  38.9 0.0 collective-permute-done.12
  38.9 1.1 %collective-permute-done.11 = bf16[24,2048]{1,0:T(8,128)(2,1)S(1)} collective-permute-done((bf16[24,2048]{1,0:T(8,128)(2,1)S(1)}, bf16[24,2048]{1,0:T(8,128)(2,1)S(1)}, u32[]{:S(2)}, u32[]{:S(2)}) %collective-permute-start.11) | collective-permute-done | bytes 98336 | tf_op jit(solution)/shard_map/ppermute | solution.py:220
  40.0 0.0 collective-permute-done.16.refs_17_
  40.1 0.1 collective-permute-start.17
  40.2 0.5 collective-permute-start.19
  40.7 1.6 %collective-permute-start.20 = (bf16[24,2560]{1,0:T(8,128)(2,1)S(1)}, bf16[24,2560]{1,0:T(8,128)(2,1)S(1)}, u32[]{:S(2)}, u32[]{:S(2)}) collective-permute-start(bf16[24,2560]{1,0:T(8,128)(2,1)S(1)} %slice.21), channel_id=1, source_target_pairs={{4,0},{8,4},{12,8},{14,12},{10,14},{6,10},{2,6},{0,2},{5,1},{9,5},... | collective-permute-start | bytes 368648 | tf_op jit(solution)/shard_map/ppermute | solution.py:221
  42.3 0.1 collective-permute-start.18
  42.4 0.0 collective-permute-done.17
  42.4 0.0 collective-permute-done.9
  42.4 0.1 broadcast_select_fusion.1
  42.5 3.7 %shard_map.51 = (f32[1792,7168]{1,0:T(8,128)}, bf16[1024,192]{1,0:T(8,128)(2,1)S(1)}) custom-call(bf16[192,1024]{1,0:T(8,128)(2,1)S(1)} %pad_maximum_fusion.refs_0_, bf16[24,4096]{1,0:T(8,128)(2,1)S(1)} %add.76.refs_1_.refs_3_, bf16[24,4096]{1,0:T(8,128)(2,1)S(1)} %collective-permute-done.1.refs_2_.refs_4_, ...), custom_call_target="tpu_custom_call" | custom-call | flops 805306368 | bytes 8388608 | tf_op jit(solution)/shard_map/pallas_call | solution.py:118
  46.3 0.0 collective-permute-done.19
  46.3 0.0 collective-permute-done.20
  46.4 0.5 collective-permute-start.21
  46.9 3.5 %shard_map.52.refs_19_ = f32[1792,7168]{1,0:T(8,128)} custom-call(bf16[1024,192]{1,0:T(8,128)(2,1)S(1)} %get-tuple-element.43.refs_0_, bf16[24,4096]{1,0:T(8,128)(2,1)S(1)} %add.76.refs_1_.refs_3_, bf16[24,4096]{1,0:T(8,128)(2,1)S(1)} %collective-permute-done.1.refs_2_.refs_4_, ...), custom_call_target="tpu_custom_call", output_to_operand_aliasing={{}: (9, {})} | custom-call | flops 805306368 | bytes 8388608 | tf_op jit(solution)/shard_map/pallas_call | solution.py:118
  50.4 0.0 collective-permute-done.21
  50.5 0.0 collective-permute-done.18
  50.6 12.8 %shard_map.53 = (f32[1792,7168]{1,0:T(8,128)}, f32[512,2048]{1,0:T(8,128)}) custom-call(bf16[1024,192]{1,0:T(8,128)(2,1)S(1)} %get-tuple-element.43.refs_0_, bf16[192,768]{1,0:T(8,128)(2,1)S(1)} %fusion.refs_1_, bf16[192,512]{1,0:T(8,128)(2,1)S(1)} %pad_maximum_fusion.1.refs_2_, ...), custom_call_target="tpu_custom_call", output_to_operand_aliasing={{0}: (19, {})} | custom-call | flops 3724541952 | bytes 38797312 | tf_op jit(solution)/shard_map/pallas_call | solution.py:118
  (47 shorter events, 0.5 us)
Async XLA Ops:
  2.4 1.6 %collective-permute-start = (bf16[24,4096]{1,0:T(8,128)(2,1)S(1)}, bf16[24,4096]{1,0:T(8,128)(2,1)S(1)}, u32[]{:S(2)}, u32[]{:S(2)}) collective-permute-start(bf16[24,4096]{1,0:T(8,128)(2,1)S(1)} %get-tuple-element.27), channel_id=1, source_target_pairs={{0,1},{1,0},{2,3},{3,2},{4,5},{5,4},{6,7},{7,6},{8,9},{9,8},{10,11... | collective-permute-start | bytes 589832 | tf_op jit(solution)/shard_map/ppermute | solution.py:192
  3.0 4.1 %collective-permute-start.3 = (bf16[24,5120]{1,0:T(8,128)(2,1)S(1)}, bf16[24,5120]{1,0:T(8,128)(2,1)S(1)}, u32[]{:S(2)}, u32[]{:S(2)}) collective-permute-start(bf16[24,5120]{1,0:T(8,128)(2,1)S(1)} %get-tuple-element.29), channel_id=1, source_target_pairs={{0,1},{1,0},{2,3},{3,2},{4,5},{5,4},{6,7},{7,6},{8,9},{9,8},{10,11... | collective-permute-start | bytes 737288 | tf_op jit(solution)/shard_map/ppermute | solution.py:192
  4.1 8.6 %collective-permute-start.2 = (bf16[24,4096]{1,0:T(8,128)(2,1)S(1)}, bf16[24,4096]{1,0:T(8,128)(2,1)S(1)}, u32[]{:S(2)}, u32[]{:S(2)}) collective-permute-start(bf16[24,4096]{1,0:T(8,128)(2,1)S(1)} %add.76.refs_1_.refs_3_), channel_id=1, source_target_pairs={{4,0},{8,4},{12,8},{14,12},{10,14},{6,10},{2,6},{0,2},{5,1},{9,5},... | collective-permute-start | bytes 589832 | tf_op jit(solution)/shard_map/ppermute | solution.py:221
  7.0 7.8 %collective-permute-start.1 = (bf16[24,4096]{1,0:T(8,128)(2,1)S(1)}, bf16[24,4096]{1,0:T(8,128)(2,1)S(1)}, u32[]{:S(2)}, u32[]{:S(2)}) collective-permute-start(bf16[24,4096]{1,0:T(8,128)(2,1)S(1)} %add.76.refs_1_.refs_3_), channel_id=1, source_target_pairs={{0,4},{4,8},{8,12},{12,14},{14,10},{10,6},{6,2},{2,0},{1,5},{5,9},... | collective-permute-start | bytes 589832 | tf_op jit(solution)/shard_map/ppermute | solution.py:220
  7.2 10.8 %collective-permute-start.14 = (bf16[24,5120]{1,0:T(8,128)(2,1)S(1)}, bf16[24,5120]{1,0:T(8,128)(2,1)S(1)}, u32[]{:S(2)}, u32[]{:S(2)}) collective-permute-start(bf16[24,5120]{1,0:T(8,128)(2,1)S(1)} %add.79.refs_11_), channel_id=1, source_target_pairs={{4,0},{8,4},{12,8},{14,12},{10,14},{6,10},{2,6},{0,2},{5,1},{9,5},... | collective-permute-start | bytes 737288 | tf_op jit(solution)/shard_map/ppermute | solution.py:221
  9.1 10.9 %collective-permute-start.6 = (bf16[24,5120]{1,0:T(8,128)(2,1)S(1)}, bf16[24,5120]{1,0:T(8,128)(2,1)S(1)}, u32[]{:S(2)}, u32[]{:S(2)}) collective-permute-start(bf16[24,5120]{1,0:T(8,128)(2,1)S(1)} %add.79.refs_11_), channel_id=1, source_target_pairs={{0,4},{4,8},{8,12},{12,14},{14,10},{10,6},{6,2},{2,0},{1,5},{5,9},... | collective-permute-start | bytes 737288 | tf_op jit(solution)/shard_map/ppermute | solution.py:220
  14.8 9.5 %collective-permute-start.4 = (bf16[24,4096]{1,0:T(8,128)(2,1)S(1)}, bf16[24,4096]{1,0:T(8,128)(2,1)S(1)}, u32[]{:S(2)}, u32[]{:S(2)}) collective-permute-start(bf16[24,4096]{1,0:T(8,128)(2,1)S(1)} %collective-permute-done.1.refs_2_.refs_4_), channel_id=1, source_target_pairs={{0,4},{4,8},{8,12},{12,14},{14,10},{10,6},{6,2},{2,0},{1,5},{5,9},... | collective-permute-start | bytes 589832 | tf_op jit(solution)/shard_map/ppermute | solution.py:220
  14.9 7.8 %collective-permute-start.5 = (bf16[24,4096]{1,0:T(8,128)(2,1)S(1)}, bf16[24,4096]{1,0:T(8,128)(2,1)S(1)}, u32[]{:S(2)}, u32[]{:S(2)}) collective-permute-start(bf16[24,4096]{1,0:T(8,128)(2,1)S(1)} %collective-permute-done.2.refs_3_.refs_5_), channel_id=1, source_target_pairs={{4,0},{8,4},{12,8},{14,12},{10,14},{6,10},{2,6},{0,2},{5,1},{9,5},... | collective-permute-start | bytes 589832 | tf_op jit(solution)/shard_map/ppermute | solution.py:221
  18.0 10.0 %collective-permute-start.15 = (bf16[24,5120]{1,0:T(8,128)(2,1)S(1)}, bf16[24,5120]{1,0:T(8,128)(2,1)S(1)}, u32[]{:S(2)}, u32[]{:S(2)}) collective-permute-start(bf16[24,5120]{1,0:T(8,128)(2,1)S(1)} %collective-permute-done.14.refs_13_), channel_id=1, source_target_pairs={{4,0},{8,4},{12,8},{14,12},{10,14},{6,10},{2,6},{0,2},{5,1},{9,5},... | collective-permute-start | bytes 737288 | tf_op jit(solution)/shard_map/ppermute | solution.py:221
  20.0 9.9 %collective-permute-start.10 = (bf16[24,5120]{1,0:T(8,128)(2,1)S(1)}, bf16[24,5120]{1,0:T(8,128)(2,1)S(1)}, u32[]{:S(2)}, u32[]{:S(2)}) collective-permute-start(bf16[24,5120]{1,0:T(8,128)(2,1)S(1)} %collective-permute-done.6.refs_12_), channel_id=1, source_target_pairs={{0,4},{4,8},{8,12},{12,14},{14,10},{10,6},{6,2},{2,0},{1,5},{5,9},... | collective-permute-start | bytes 737288 | tf_op jit(solution)/shard_map/ppermute | solution.py:220
  24.2 9.5 %collective-permute-start.7 = (bf16[24,4096]{1,0:T(8,128)(2,1)S(1)}, bf16[24,4096]{1,0:T(8,128)(2,1)S(1)}, u32[]{:S(2)}, u32[]{:S(2)}) collective-permute-start(bf16[24,4096]{1,0:T(8,128)(2,1)S(1)} %collective-permute-done.4.refs_4_.refs_6_), channel_id=1, source_target_pairs={{0,4},{4,8},{8,12},{12,14},{14,10},{10,6},{6,2},{2,0},{1,5},{5,9},... | collective-permute-start | bytes 589832 | tf_op jit(solution)/shard_map/ppermute | solution.py:220
  24.7 7.8 %collective-permute-start.8 = (bf16[24,4096]{1,0:T(8,128)(2,1)S(1)}, bf16[24,4096]{1,0:T(8,128)(2,1)S(1)}, u32[]{:S(2)}, u32[]{:S(2)}) collective-permute-start(bf16[24,4096]{1,0:T(8,128)(2,1)S(1)} %collective-permute-done.5.refs_5_.refs_7_), channel_id=1, source_target_pairs={{4,0},{8,4},{12,8},{14,12},{10,14},{6,10},{2,6},{0,2},{5,1},{9,5},... | collective-permute-start | bytes 589832 | tf_op jit(solution)/shard_map/ppermute | solution.py:221
  28.0 12.0 %collective-permute-start.16 = (bf16[24,5120]{1,0:T(8,128)(2,1)S(1)}, bf16[24,5120]{1,0:T(8,128)(2,1)S(1)}, u32[]{:S(2)}, u32[]{:S(2)}) collective-permute-start(bf16[24,5120]{1,0:T(8,128)(2,1)S(1)} %collective-permute-done.15.refs_15_), channel_id=1, source_target_pairs={{4,0},{8,4},{12,8},{14,12},{10,14},{6,10},{2,6},{0,2},{5,1},{9,5},... | collective-permute-start | bytes 737288 | tf_op jit(solution)/shard_map/ppermute | solution.py:221
  29.9 9.0 %collective-permute-start.13 = (bf16[24,5120]{1,0:T(8,128)(2,1)S(1)}, bf16[24,5120]{1,0:T(8,128)(2,1)S(1)}, u32[]{:S(2)}, u32[]{:S(2)}) collective-permute-start(bf16[24,5120]{1,0:T(8,128)(2,1)S(1)} %collective-permute-done.10.refs_14_), channel_id=1, source_target_pairs={{0,4},{4,8},{8,12},{12,14},{14,10},{10,6},{6,2},{2,0},{1,5},{5,9},... | collective-permute-start | bytes 737288 | tf_op jit(solution)/shard_map/ppermute | solution.py:220
  33.8 5.2 %collective-permute-start.12 = (bf16[24,2048]{1,0:T(8,128)(2,1)S(1)}, bf16[24,2048]{1,0:T(8,128)(2,1)S(1)}, u32[]{:S(2)}, u32[]{:S(2)}) collective-permute-start(bf16[24,2048]{1,0:T(8,128)(2,1)S(1)} %slice.19), channel_id=1, source_target_pairs={{4,0},{8,4},{12,8},{14,12},{10,14},{6,10},{2,6},{0,2},{5,1},{9,5},... | collective-permute-start | bytes 294920 | tf_op jit(solution)/shard_map/ppermute | solution.py:221
  35.4 4.6 %collective-permute-start.11 = (bf16[24,2048]{1,0:T(8,128)(2,1)S(1)}, bf16[24,2048]{1,0:T(8,128)(2,1)S(1)}, u32[]{:S(2)}, u32[]{:S(2)}) collective-permute-start(bf16[24,2048]{1,0:T(8,128)(2,1)S(1)} %slice.18), channel_id=1, source_target_pairs={{0,4},{4,8},{8,12},{12,14},{14,10},{10,6},{6,2},{2,0},{1,5},{5,9},... | collective-permute-start | bytes 294920 | tf_op jit(solution)/shard_map/ppermute | solution.py:220
  35.8 6.6 %collective-permute-start.9 = (bf16[168,1024]{1,0:T(8,128)(2,1)S(1)}, bf16[168,1024]{1,0:T(8,128)(2,1)S(1)}, u32[]{:S(2)}, u32[]{:S(2)}) collective-permute-start(bf16[168,1024]{1,0:T(8,128)(2,1)S(1)} %dynamic-slice_dynamic-update-slice_fusion), channel_id=1, source_target_pairs={{0,1},{1,0},{2,3},{3,2},{4,5},{5,4},{6,7},{7,6},{8,9},{9,8},{10,11... | collective-permute-start | bytes 1032200 | tf_op jit(solution)/shard_map/ppermute | solution.py:208
  40.1 2.3 %collective-permute-start.17 = (bf16[24,1024]{1,0:T(8,128)(2,1)S(1)}, bf16[24,1024]{1,0:T(8,128)(2,1)S(1)}, u32[]{:S(2)}, u32[]{:S(2)}) collective-permute-start(bf16[24,1024]{1,0:T(8,128)(2,1)S(1)} %constant_dynamic-slice_fusion.16), channel_id=1, source_target_pairs={{0,1},{1,0},{2,3},{3,2},{4,5},{5,4},{6,7},{7,6},{8,9},{9,8},{10,11... | collective-permute-start | bytes 147464 | tf_op jit(solution)/shard_map/ppermute | solution.py:208
  40.2 6.1 %collective-permute-start.19 = (bf16[24,2560]{1,0:T(8,128)(2,1)S(1)}, bf16[24,2560]{1,0:T(8,128)(2,1)S(1)}, u32[]{:S(2)}, u32[]{:S(2)}) collective-permute-start(bf16[24,2560]{1,0:T(8,128)(2,1)S(1)} %slice.20), channel_id=1, source_target_pairs={{0,4},{4,8},{8,12},{12,14},{14,10},{10,6},{6,2},{2,0},{1,5},{5,9},... | collective-permute-start | bytes 368648 | tf_op jit(solution)/shard_map/ppermute | solution.py:220
  40.7 5.6 %collective-permute-start.20 = (bf16[24,2560]{1,0:T(8,128)(2,1)S(1)}, bf16[24,2560]{1,0:T(8,128)(2,1)S(1)}, u32[]{:S(2)}, u32[]{:S(2)}) collective-permute-start(bf16[24,2560]{1,0:T(8,128)(2,1)S(1)} %slice.21), channel_id=1, source_target_pairs={{4,0},{8,4},{12,8},{14,12},{10,14},{6,10},{2,6},{0,2},{5,1},{9,5},... | collective-permute-start | bytes 368648 | tf_op jit(solution)/shard_map/ppermute | solution.py:221
  42.3 8.2 %collective-permute-start.18 = (bf16[168,1280]{1,0:T(8,128)(2,1)S(1)}, bf16[168,1280]{1,0:T(8,128)(2,1)S(1)}, u32[]{:S(2)}, u32[]{:S(2)}) collective-permute-start(bf16[168,1280]{1,0:T(8,128)(2,1)S(1)} %maximum_dynamic-update-slice_fusion), channel_id=1, source_target_pairs={{0,1},{1,0},{2,3},{3,2},{4,5},{5,4},{6,7},{7,6},{8,9},{9,8},{10,11... | collective-permute-start | bytes 1290248 | tf_op jit(solution)/shard_map/ppermute | solution.py:208
  46.4 4.1 %collective-permute-start.21 = (bf16[24,1280]{1,0:T(8,128)(2,1)S(1)}, bf16[24,1280]{1,0:T(8,128)(2,1)S(1)}, u32[]{:S(2)}, u32[]{:S(2)}) collective-permute-start(bf16[24,1280]{1,0:T(8,128)(2,1)S(1)} %pad_maximum_fusion.2), channel_id=1, source_target_pairs={{0,1},{1,0},{2,3},{3,2},{4,5},{5,4},{6,7},{7,6},{8,9},{9,8},{10,11... | collective-permute-start | bytes 184328 | tf_op jit(solution)/shard_map/ppermute | solution.py:208

commit v16 on v15

--- a/solution.py
+++ b/solution.py
@@ -136,7 +136,9 @@
 
 def split_kernel(halves, layouts, half_ref, count_ref, act_ref, grad_ref, *out_refs):
     slots = act_ref.shape[0]
-    live = lax.broadcasted_iota(jnp.int32, (slots, 128), 0) < count_ref[0]
+    own = half_ref[0] * slots
+    position = lax.broadcasted_iota(jnp.int32, (halves * slots, 128), 0)
+    live = (position >= own) & (position < own + count_ref[0])
     for half in range(halves):
         for flip in (1, 0):
 
@@ -147,14 +149,11 @@
                     for source, start, width in layout:
                         ref = (grad_ref, act_ref)[source]
                         first = half * (ref.shape[1] // halves) + start
-                        values = ref[:, first : first + width]
+                        values = jnp.concatenate([ref[:, first : first + width]] * halves, axis=0)
                         mask = jnp.concatenate([live] * (width // 128), axis=1)
-                        masked = jnp.where(mask, values, jnp.zeros_like(values))
-                        own = (half + flip) % halves * slots
-                        out_ref, columns = out_refs[2 * chain + flip], slice(target, target + width)
-                        out_ref[own : own + slots, columns] = masked
-                        other = slots - own
-                        out_ref[other : other + slots, columns] = jnp.zeros_like(values)
+                        out_refs[2 * chain + flip][:, target : target + width] = jnp.where(
+                            mask, values, jnp.zeros_like(values)
+                        )
                         target += width
 
 

time: 63.6 us -> 63.6 us (level)
  no operation moved by 1% of the time
where the time goes in v16:
time: 63.6 us; the launch traced here: 63.5 us
  Pallas kernels  21.3 us (33%)
  waiting for transfers between devices  21.2 us (33%)
  starting transfers between devices  18.8 us (30%)
  between operations  1.62 us (3%)
    pallas_call x3, Pallas kernels, tiles(): pl.pallas_call(functools.partial(tiles_kernel, scale, groups, ready, [len...  20.1 us
    ppermute x8, starting transfers between devices, local(): backward[k] = lax.ppermute(behind_of, 'row', behind)  15.4 us
    ppermute x8, waiting for transfers between devices, local(): backward[k] = lax.ppermute(behind_of, 'row', behind)  11.4 us
    ppermute x8, waiting for transfers between devices, local(): forward[k] = lax.ppermute(ahead_of, 'row', ahead)  8.82 us
    ppermute x8, starting transfers between devices, local(): forward[k] = lax.ppermute(ahead_of, 'row', ahead)  2.06 us
  transfers between devices with their start and end apart: 22, of which 11 were waited for; matrix products, arithmetic and copies ran while one was open for 1% of the time, Pallas kernels for 11%

profile of v16, /device:TPU:0, one launch (start us, length us, event | category | flops | bytes accessed | tf_op | source)
XLA Modules:
  0.0 63.5 jit_solution(15864447300041466220)
XLA Ops:
  1.3 1.2 %shard_map.50 = (bf16[24,4096]{1,0:T(8,128)(2,1)S(1)}, bf16[24,4096]{1,0:T(8,128)(2,1)S(1)}, bf16[24,5120]{1,0:T(8,128)(2,1)S(1)}, bf16[24,5120]{1,0:T(8,128)(2,1)S(1)}) custom-call(s32[1]{0:T(128)} %bitcast.half_ref, s32[1]{0:T(128)S(6)} %copy.23.count_ref, bf16[12,14336]{1,0:T(8,128)(2,1)} %act_ref.1, bf16[12,4096]{1,0:T(8,128)(2,1)} %grad_ref.1), custom_call_target="tpu_custom_call" | custom-call | tf_op jit(solution)/shard_map/pallas_call | solution.py:185
  2.5 0.5 collective-permute-start
  3.0 0.1 collective-permute-start.3
  3.1 1.0 %collective-permute-done = bf16[24,4096]{1,0:T(8,128)(2,1)S(1)} collective-permute-done((bf16[24,4096]{1,0:T(8,128)(2,1)S(1)}, bf16[24,4096]{1,0:T(8,128)(2,1)S(1)}, u32[]{:S(2)}, u32[]{:S(2)}) %collective-permute-start) | collective-permute-done | bytes 196640 | tf_op jit(solution)/shard_map/ppermute | solution.py:191
  4.1 2.9 %collective-permute-start.2 = (bf16[24,4096]{1,0:T(8,128)(2,1)S(1)}, bf16[24,4096]{1,0:T(8,128)(2,1)S(1)}, u32[]{:S(2)}, u32[]{:S(2)}) collective-permute-start(bf16[24,4096]{1,0:T(8,128)(2,1)S(1)} %add.76.refs_1_.refs_3_), channel_id=1, source_target_pairs={{4,0},{8,4},{12,8},{14,12},{10,14},{6,10},{2,6},{0,2},{5,1},{9,5},... | collective-permute-start | bytes 589832 | tf_op jit(solution)/shard_map/ppermute | solution.py:220
  7.0 0.2 collective-permute-start.1
  7.2 0.0 collective-permute-done.3
  7.2 0.1 add.79.refs_11_
  7.3 1.9 %collective-permute-start.14 = (bf16[24,5120]{1,0:T(8,128)(2,1)S(1)}, bf16[24,5120]{1,0:T(8,128)(2,1)S(1)}, u32[]{:S(2)}, u32[]{:S(2)}) collective-permute-start(bf16[24,5120]{1,0:T(8,128)(2,1)S(1)} %add.79.refs_11_), channel_id=1, source_target_pairs={{4,0},{8,4},{12,8},{14,12},{10,14},{6,10},{2,6},{0,2},{5,1},{9,5},... | collective-permute-start | bytes 737288 | tf_op jit(solution)/shard_map/ppermute | solution.py:220
  9.2 0.2 collective-permute-start.6
  9.4 3.5 %collective-permute-done.2.refs_3_.refs_5_ = bf16[24,4096]{1,0:T(8,128)(2,1)S(1)} collective-permute-done((bf16[24,4096]{1,0:T(8,128)(2,1)S(1)}, bf16[24,4096]{1,0:T(8,128)(2,1)S(1)}, u32[]{:S(2)}, u32[]{:S(2)}) %collective-permute-start.2) | collective-permute-done | bytes 196640 | tf_op jit(solution)/shard_map/ppermute | solution.py:220
  12.8 2.0 %collective-permute-done.1.refs_2_.refs_4_ = bf16[24,4096]{1,0:T(8,128)(2,1)S(1)} collective-permute-done((bf16[24,4096]{1,0:T(8,128)(2,1)S(1)}, bf16[24,4096]{1,0:T(8,128)(2,1)S(1)}, u32[]{:S(2)}, u32[]{:S(2)}) %collective-permute-start.1) | collective-permute-done | bytes 196640 | tf_op jit(solution)/shard_map/ppermute | solution.py:219
  14.8 0.1 collective-permute-start.4
  14.9 1.9 %collective-permute-start.5 = (bf16[24,4096]{1,0:T(8,128)(2,1)S(1)}, bf16[24,4096]{1,0:T(8,128)(2,1)S(1)}, u32[]{:S(2)}, u32[]{:S(2)}) collective-permute-start(bf16[24,4096]{1,0:T(8,128)(2,1)S(1)} %collective-permute-done.2.refs_3_.refs_5_), channel_id=1, source_target_pairs={{4,0},{8,4},{12,8},{14,12},{10,14},{6,10},{2,6},{0,2},{5,1},{9,5},... | collective-permute-start | bytes 589832 | tf_op jit(solution)/shard_map/ppermute | solution.py:220
  16.9 1.2 %collective-permute-done.14.refs_13_ = bf16[24,5120]{1,0:T(8,128)(2,1)S(1)} collective-permute-done((bf16[24,5120]{1,0:T(8,128)(2,1)S(1)}, bf16[24,5120]{1,0:T(8,128)(2,1)S(1)}, u32[]{:S(2)}, u32[]{:S(2)}) %collective-permute-start.14) | collective-permute-done | bytes 245792 | tf_op jit(solution)/shard_map/ppermute | solution.py:220
  18.1 2.0 %collective-permute-start.15 = (bf16[24,5120]{1,0:T(8,128)(2,1)S(1)}, bf16[24,5120]{1,0:T(8,128)(2,1)S(1)}, u32[]{:S(2)}, u32[]{:S(2)}) collective-permute-start(bf16[24,5120]{1,0:T(8,128)(2,1)S(1)} %collective-permute-done.14.refs_13_), channel_id=1, source_target_pairs={{4,0},{8,4},{12,8},{14,12},{10,14},{6,10},{2,6},{0,2},{5,1},{9,5},... | collective-permute-start | bytes 737288 | tf_op jit(solution)/shard_map/ppermute | solution.py:220
  20.1 0.0 collective-permute-done.6.refs_12_
  20.1 0.1 collective-permute-start.10
  20.3 2.5 %collective-permute-done.5.refs_5_.refs_7_ = bf16[24,4096]{1,0:T(8,128)(2,1)S(1)} collective-permute-done((bf16[24,4096]{1,0:T(8,128)(2,1)S(1)}, bf16[24,4096]{1,0:T(8,128)(2,1)S(1)}, u32[]{:S(2)}, u32[]{:S(2)}) %collective-permute-start.5) | collective-permute-done | bytes 196640 | tf_op jit(solution)/shard_map/ppermute | solution.py:220
  22.8 1.5 %collective-permute-done.4.refs_4_.refs_6_ = bf16[24,4096]{1,0:T(8,128)(2,1)S(1)} collective-permute-done((bf16[24,4096]{1,0:T(8,128)(2,1)S(1)}, bf16[24,4096]{1,0:T(8,128)(2,1)S(1)}, u32[]{:S(2)}, u32[]{:S(2)}) %collective-permute-start.4) | collective-permute-done | bytes 196640 | tf_op jit(solution)/shard_map/ppermute | solution.py:219
  24.3 0.5 collective-permute-start.7
  24.8 1.5 %collective-permute-start.8 = (bf16[24,4096]{1,0:T(8,128)(2,1)S(1)}, bf16[24,4096]{1,0:T(8,128)(2,1)S(1)}, u32[]{:S(2)}, u32[]{:S(2)}) collective-permute-start(bf16[24,4096]{1,0:T(8,128)(2,1)S(1)} %collective-permute-done.5.refs_5_.refs_7_), channel_id=1, source_target_pairs={{4,0},{8,4},{12,8},{14,12},{10,14},{6,10},{2,6},{0,2},{5,1},{9,5},... | collective-permute-start | bytes 589832 | tf_op jit(solution)/shard_map/ppermute | solution.py:220
  26.3 1.7 %collective-permute-done.15.refs_15_ = bf16[24,5120]{1,0:T(8,128)(2,1)S(1)} collective-permute-done((bf16[24,5120]{1,0:T(8,128)(2,1)S(1)}, bf16[24,5120]{1,0:T(8,128)(2,1)S(1)}, u32[]{:S(2)}, u32[]{:S(2)}) %collective-permute-start.15) | collective-permute-done | bytes 245792 | tf_op jit(solution)/shard_map/ppermute | solution.py:220
  28.0 1.9 %collective-permute-start.16 = (bf16[24,5120]{1,0:T(8,128)(2,1)S(1)}, bf16[24,5120]{1,0:T(8,128)(2,1)S(1)}, u32[]{:S(2)}, u32[]{:S(2)}) collective-permute-start(bf16[24,5120]{1,0:T(8,128)(2,1)S(1)} %collective-permute-done.15.refs_15_), channel_id=1, source_target_pairs={{4,0},{8,4},{12,8},{14,12},{10,14},{6,10},{2,6},{0,2},{5,1},{9,5},... | collective-permute-start | bytes 737288 | tf_op jit(solution)/shard_map/ppermute | solution.py:220
  30.0 0.0 collective-permute-done.10.refs_14_
  30.0 0.1 collective-permute-start.13
  30.1 2.5 %collective-permute-done.8.refs_7_.refs_9_ = bf16[24,4096]{1,0:T(8,128)(2,1)S(1)} collective-permute-done((bf16[24,4096]{1,0:T(8,128)(2,1)S(1)}, bf16[24,4096]{1,0:T(8,128)(2,1)S(1)}, u32[]{:S(2)}, u32[]{:S(2)}) %collective-permute-start.8) | collective-permute-done | bytes 196640 | tf_op jit(solution)/shard_map/ppermute | solution.py:220
  32.6 1.2 %collective-permute-done.7.refs_6_.refs_8_ = bf16[24,4096]{1,0:T(8,128)(2,1)S(1)} collective-permute-done((bf16[24,4096]{1,0:T(8,128)(2,1)S(1)}, bf16[24,4096]{1,0:T(8,128)(2,1)S(1)}, u32[]{:S(2)}, u32[]{:S(2)}) %collective-permute-start.7) | collective-permute-done | bytes 196640 | tf_op jit(solution)/shard_map/ppermute | solution.py:219
  33.8 1.6 %collective-permute-start.12 = (bf16[24,2048]{1,0:T(8,128)(2,1)S(1)}, bf16[24,2048]{1,0:T(8,128)(2,1)S(1)}, u32[]{:S(2)}, u32[]{:S(2)}) collective-permute-start(bf16[24,2048]{1,0:T(8,128)(2,1)S(1)} %slice.19), channel_id=1, source_target_pairs={{4,0},{8,4},{12,8},{14,12},{10,14},{6,10},{2,6},{0,2},{5,1},{9,5},... | collective-permute-start | bytes 294920 | tf_op jit(solution)/shard_map/ppermute | solution.py:220
  35.4 0.4 collective-permute-start.11
  35.9 0.1 collective-permute-start.9
  36.0 3.0 %collective-permute-done.13.refs_16_ = bf16[24,5120]{1,0:T(8,128)(2,1)S(1)} collective-permute-done((bf16[24,5120]{1,0:T(8,128)(2,1)S(1)}, bf16[24,5120]{1,0:T(8,128)(2,1)S(1)}, u32[]{:S(2)}, u32[]{:S(2)}) %collective-permute-start.13) | collective-permute-done | bytes 245792 | tf_op jit(solution)/shard_map/ppermute | solution.py:219
  39.0 0.0 collective-permute-done.12
  39.0 1.1 %collective-permute-done.11 = bf16[24,2048]{1,0:T(8,128)(2,1)S(1)} collective-permute-done((bf16[24,2048]{1,0:T(8,128)(2,1)S(1)}, bf16[24,2048]{1,0:T(8,128)(2,1)S(1)}, u32[]{:S(2)}, u32[]{:S(2)}) %collective-permute-start.11) | collective-permute-done | bytes 98336 | tf_op jit(solution)/shard_map/ppermute | solution.py:219
  40.1 0.0 collective-permute-done.16.refs_17_
  40.1 0.1 collective-permute-start.17
  40.2 0.5 collective-permute-start.19
  40.7 1.6 %collective-permute-start.20 = (bf16[24,2560]{1,0:T(8,128)(2,1)S(1)}, bf16[24,2560]{1,0:T(8,128)(2,1)S(1)}, u32[]{:S(2)}, u32[]{:S(2)}) collective-permute-start(bf16[24,2560]{1,0:T(8,128)(2,1)S(1)} %slice.21), channel_id=1, source_target_pairs={{4,0},{8,4},{12,8},{14,12},{10,14},{6,10},{2,6},{0,2},{5,1},{9,5},... | collective-permute-start | bytes 368648 | tf_op jit(solution)/shard_map/ppermute | solution.py:220
  42.4 0.1 collective-permute-start.18
  42.5 0.0 collective-permute-done.17
  42.5 0.0 collective-permute-done.9
  42.5 0.1 broadcast_select_fusion.1
  42.6 3.7 %shard_map.51 = (f32[1792,7168]{1,0:T(8,128)}, bf16[1024,192]{1,0:T(8,128)(2,1)S(1)}) custom-call(bf16[192,1024]{1,0:T(8,128)(2,1)S(1)} %pad_maximum_fusion.refs_0_, bf16[24,4096]{1,0:T(8,128)(2,1)S(1)} %add.76.refs_1_.refs_3_, bf16[24,4096]{1,0:T(8,128)(2,1)S(1)} %collective-permute-done.1.refs_2_.refs_4_, ...), custom_call_target="tpu_custom_call" | custom-call | flops 805306368 | bytes 8388608 | tf_op jit(solution)/shard_map/pallas_call | solution.py:118
  46.3 0.0 collective-permute-done.19
  46.3 0.0 collective-permute-done.20
  46.4 0.5 collective-permute-start.21
  47.0 3.5 %shard_map.52.refs_19_ = f32[1792,7168]{1,0:T(8,128)} custom-call(bf16[1024,192]{1,0:T(8,128)(2,1)S(1)} %get-tuple-element.43.refs_0_, bf16[24,4096]{1,0:T(8,128)(2,1)S(1)} %add.76.refs_1_.refs_3_, bf16[24,4096]{1,0:T(8,128)(2,1)S(1)} %collective-permute-done.1.refs_2_.refs_4_, ...), custom_call_target="tpu_custom_call", output_to_operand_aliasing={{}: (9, {})} | custom-call | flops 805306368 | bytes 8388608 | tf_op jit(solution)/shard_map/pallas_call | solution.py:118
  50.5 0.0 collective-permute-done.21
  50.5 0.0 collective-permute-done.18
  50.7 12.8 %shard_map.53 = (f32[1792,7168]{1,0:T(8,128)}, f32[512,2048]{1,0:T(8,128)}) custom-call(bf16[1024,192]{1,0:T(8,128)(2,1)S(1)} %get-tuple-element.43.refs_0_, bf16[192,768]{1,0:T(8,128)(2,1)S(1)} %fusion.refs_1_, bf16[192,512]{1,0:T(8,128)(2,1)S(1)} %pad_maximum_fusion.1.refs_2_, ...), custom_call_target="tpu_custom_call", output_to_operand_aliasing={{0}: (19, {})} | custom-call | flops 3724541952 | bytes 38797312 | tf_op jit(solution)/shard_map/pallas_call | solution.py:118
  (47 shorter events, 0.5 us)
Async XLA Ops:
  2.5 1.6 %collective-permute-start = (bf16[24,4096]{1,0:T(8,128)(2,1)S(1)}, bf16[24,4096]{1,0:T(8,128)(2,1)S(1)}, u32[]{:S(2)}, u32[]{:S(2)}) collective-permute-start(bf16[24,4096]{1,0:T(8,128)(2,1)S(1)} %get-tuple-element.27), channel_id=1, source_target_pairs={{0,1},{1,0},{2,3},{3,2},{4,5},{5,4},{6,7},{7,6},{8,9},{9,8},{10,11... | collective-permute-start | bytes 589832 | tf_op jit(solution)/shard_map/ppermute | solution.py:191
  3.0 4.2 %collective-permute-start.3 = (bf16[24,5120]{1,0:T(8,128)(2,1)S(1)}, bf16[24,5120]{1,0:T(8,128)(2,1)S(1)}, u32[]{:S(2)}, u32[]{:S(2)}) collective-permute-start(bf16[24,5120]{1,0:T(8,128)(2,1)S(1)} %get-tuple-element.29), channel_id=1, source_target_pairs={{0,1},{1,0},{2,3},{3,2},{4,5},{5,4},{6,7},{7,6},{8,9},{9,8},{10,11... | collective-permute-start | bytes 737288 | tf_op jit(solution)/shard_map/ppermute | solution.py:191
  4.1 8.7 %collective-permute-start.2 = (bf16[24,4096]{1,0:T(8,128)(2,1)S(1)}, bf16[24,4096]{1,0:T(8,128)(2,1)S(1)}, u32[]{:S(2)}, u32[]{:S(2)}) collective-permute-start(bf16[24,4096]{1,0:T(8,128)(2,1)S(1)} %add.76.refs_1_.refs_3_), channel_id=1, source_target_pairs={{4,0},{8,4},{12,8},{14,12},{10,14},{6,10},{2,6},{0,2},{5,1},{9,5},... | collective-permute-start | bytes 589832 | tf_op jit(solution)/shard_map/ppermute | solution.py:220
  7.0 7.8 %collective-permute-start.1 = (bf16[24,4096]{1,0:T(8,128)(2,1)S(1)}, bf16[24,4096]{1,0:T(8,128)(2,1)S(1)}, u32[]{:S(2)}, u32[]{:S(2)}) collective-permute-start(bf16[24,4096]{1,0:T(8,128)(2,1)S(1)} %add.76.refs_1_.refs_3_), channel_id=1, source_target_pairs={{0,4},{4,8},{8,12},{12,14},{14,10},{10,6},{6,2},{2,0},{1,5},{5,9},... | collective-permute-start | bytes 589832 | tf_op jit(solution)/shard_map/ppermute | solution.py:219
  7.3 10.8 %collective-permute-start.14 = (bf16[24,5120]{1,0:T(8,128)(2,1)S(1)}, bf16[24,5120]{1,0:T(8,128)(2,1)S(1)}, u32[]{:S(2)}, u32[]{:S(2)}) collective-permute-start(bf16[24,5120]{1,0:T(8,128)(2,1)S(1)} %add.79.refs_11_), channel_id=1, source_target_pairs={{4,0},{8,4},{12,8},{14,12},{10,14},{6,10},{2,6},{0,2},{5,1},{9,5},... | collective-permute-start | bytes 737288 | tf_op jit(solution)/shard_map/ppermute | solution.py:220
  9.2 10.9 %collective-permute-start.6 = (bf16[24,5120]{1,0:T(8,128)(2,1)S(1)}, bf16[24,5120]{1,0:T(8,128)(2,1)S(1)}, u32[]{:S(2)}, u32[]{:S(2)}) collective-permute-start(bf16[24,5120]{1,0:T(8,128)(2,1)S(1)} %add.79.refs_11_), channel_id=1, source_target_pairs={{0,4},{4,8},{8,12},{12,14},{14,10},{10,6},{6,2},{2,0},{1,5},{5,9},... | collective-permute-start | bytes 737288 | tf_op jit(solution)/shard_map/ppermute | solution.py:219
  14.8 9.5 %collective-permute-start.4 = (bf16[24,4096]{1,0:T(8,128)(2,1)S(1)}, bf16[24,4096]{1,0:T(8,128)(2,1)S(1)}, u32[]{:S(2)}, u32[]{:S(2)}) collective-permute-start(bf16[24,4096]{1,0:T(8,128)(2,1)S(1)} %collective-permute-done.1.refs_2_.refs_4_), channel_id=1, source_target_pairs={{0,4},{4,8},{8,12},{12,14},{14,10},{10,6},{6,2},{2,0},{1,5},{5,9},... | collective-permute-start | bytes 589832 | tf_op jit(solution)/shard_map/ppermute | solution.py:219
  14.9 7.8 %collective-permute-start.5 = (bf16[24,4096]{1,0:T(8,128)(2,1)S(1)}, bf16[24,4096]{1,0:T(8,128)(2,1)S(1)}, u32[]{:S(2)}, u32[]{:S(2)}) collective-permute-start(bf16[24,4096]{1,0:T(8,128)(2,1)S(1)} %collective-permute-done.2.refs_3_.refs_5_), channel_id=1, source_target_pairs={{4,0},{8,4},{12,8},{14,12},{10,14},{6,10},{2,6},{0,2},{5,1},{9,5},... | collective-permute-start | bytes 589832 | tf_op jit(solution)/shard_map/ppermute | solution.py:220
  18.1 10.0 %collective-permute-start.15 = (bf16[24,5120]{1,0:T(8,128)(2,1)S(1)}, bf16[24,5120]{1,0:T(8,128)(2,1)S(1)}, u32[]{:S(2)}, u32[]{:S(2)}) collective-permute-start(bf16[24,5120]{1,0:T(8,128)(2,1)S(1)} %collective-permute-done.14.refs_13_), channel_id=1, source_target_pairs={{4,0},{8,4},{12,8},{14,12},{10,14},{6,10},{2,6},{0,2},{5,1},{9,5},... | collective-permute-start | bytes 737288 | tf_op jit(solution)/shard_map/ppermute | solution.py:220
  20.1 9.9 %collective-permute-start.10 = (bf16[24,5120]{1,0:T(8,128)(2,1)S(1)}, bf16[24,5120]{1,0:T(8,128)(2,1)S(1)}, u32[]{:S(2)}, u32[]{:S(2)}) collective-permute-start(bf16[24,5120]{1,0:T(8,128)(2,1)S(1)} %collective-permute-done.6.refs_12_), channel_id=1, source_target_pairs={{0,4},{4,8},{8,12},{12,14},{14,10},{10,6},{6,2},{2,0},{1,5},{5,9},... | collective-permute-start | bytes 737288 | tf_op jit(solution)/shard_map/ppermute | solution.py:219
  24.3 9.5 %collective-permute-start.7 = (bf16[24,4096]{1,0:T(8,128)(2,1)S(1)}, bf16[24,4096]{1,0:T(8,128)(2,1)S(1)}, u32[]{:S(2)}, u32[]{:S(2)}) collective-permute-start(bf16[24,4096]{1,0:T(8,128)(2,1)S(1)} %collective-permute-done.4.refs_4_.refs_6_), channel_id=1, source_target_pairs={{0,4},{4,8},{8,12},{12,14},{14,10},{10,6},{6,2},{2,0},{1,5},{5,9},... | collective-permute-start | bytes 589832 | tf_op jit(solution)/shard_map/ppermute | solution.py:219
  24.8 7.8 %collective-permute-start.8 = (bf16[24,4096]{1,0:T(8,128)(2,1)S(1)}, bf16[24,4096]{1,0:T(8,128)(2,1)S(1)}, u32[]{:S(2)}, u32[]{:S(2)}) collective-permute-start(bf16[24,4096]{1,0:T(8,128)(2,1)S(1)} %collective-permute-done.5.refs_5_.refs_7_), channel_id=1, source_target_pairs={{4,0},{8,4},{12,8},{14,12},{10,14},{6,10},{2,6},{0,2},{5,1},{9,5},... | collective-permute-start | bytes 589832 | tf_op jit(solution)/shard_map/ppermute | solution.py:220
  28.0 12.0 %collective-permute-start.16 = (bf16[24,5120]{1,0:T(8,128)(2,1)S(1)}, bf16[24,5120]{1,0:T(8,128)(2,1)S(1)}, u32[]{:S(2)}, u32[]{:S(2)}) collective-permute-start(bf16[24,5120]{1,0:T(8,128)(2,1)S(1)} %collective-permute-done.15.refs_15_), channel_id=1, source_target_pairs={{4,0},{8,4},{12,8},{14,12},{10,14},{6,10},{2,6},{0,2},{5,1},{9,5},... | collective-permute-start | bytes 737288 | tf_op jit(solution)/shard_map/ppermute | solution.py:220
  30.0 9.0 %collective-permute-start.13 = (bf16[24,5120]{1,0:T(8,128)(2,1)S(1)}, bf16[24,5120]{1,0:T(8,128)(2,1)S(1)}, u32[]{:S(2)}, u32[]{:S(2)}) collective-permute-start(bf16[24,5120]{1,0:T(8,128)(2,1)S(1)} %collective-permute-done.10.refs_14_), channel_id=1, source_target_pairs={{0,4},{4,8},{8,12},{12,14},{14,10},{10,6},{6,2},{2,0},{1,5},{5,9},... | collective-permute-start | bytes 737288 | tf_op jit(solution)/shard_map/ppermute | solution.py:219
  33.8 5.2 %collective-permute-start.12 = (bf16[24,2048]{1,0:T(8,128)(2,1)S(1)}, bf16[24,2048]{1,0:T(8,128)(2,1)S(1)}, u32[]{:S(2)}, u32[]{:S(2)}) collective-permute-start(bf16[24,2048]{1,0:T(8,128)(2,1)S(1)} %slice.19), channel_id=1, source_target_pairs={{4,0},{8,4},{12,8},{14,12},{10,14},{6,10},{2,6},{0,2},{5,1},{9,5},... | collective-permute-start | bytes 294920 | tf_op jit(solution)/shard_map/ppermute | solution.py:220
  35.4 4.6 %collective-permute-start.11 = (bf16[24,2048]{1,0:T(8,128)(2,1)S(1)}, bf16[24,2048]{1,0:T(8,128)(2,1)S(1)}, u32[]{:S(2)}, u32[]{:S(2)}) collective-permute-start(bf16[24,2048]{1,0:T(8,128)(2,1)S(1)} %slice.18), channel_id=1, source_target_pairs={{0,4},{4,8},{8,12},{12,14},{14,10},{10,6},{6,2},{2,0},{1,5},{5,9},... | collective-permute-start | bytes 294920 | tf_op jit(solution)/shard_map/ppermute | solution.py:219
  35.9 6.6 %collective-permute-start.9 = (bf16[168,1024]{1,0:T(8,128)(2,1)S(1)}, bf16[168,1024]{1,0:T(8,128)(2,1)S(1)}, u32[]{:S(2)}, u32[]{:S(2)}) collective-permute-start(bf16[168,1024]{1,0:T(8,128)(2,1)S(1)} %dynamic-slice_dynamic-update-slice_fusion), channel_id=1, source_target_pairs={{0,1},{1,0},{2,3},{3,2},{4,5},{5,4},{6,7},{7,6},{8,9},{9,8},{10,11... | collective-permute-start | bytes 1032200 | tf_op jit(solution)/shard_map/ppermute | solution.py:207
  40.1 2.3 %collective-permute-start.17 = (bf16[24,1024]{1,0:T(8,128)(2,1)S(1)}, bf16[24,1024]{1,0:T(8,128)(2,1)S(1)}, u32[]{:S(2)}, u32[]{:S(2)}) collective-permute-start(bf16[24,1024]{1,0:T(8,128)(2,1)S(1)} %constant_dynamic-slice_fusion.16), channel_id=1, source_target_pairs={{0,1},{1,0},{2,3},{3,2},{4,5},{5,4},{6,7},{7,6},{8,9},{9,8},{10,11... | collective-permute-start | bytes 147464 | tf_op jit(solution)/shard_map/ppermute | solution.py:207
  40.2 6.1 %collective-permute-start.19 = (bf16[24,2560]{1,0:T(8,128)(2,1)S(1)}, bf16[24,2560]{1,0:T(8,128)(2,1)S(1)}, u32[]{:S(2)}, u32[]{:S(2)}) collective-permute-start(bf16[24,2560]{1,0:T(8,128)(2,1)S(1)} %slice.20), channel_id=1, source_target_pairs={{0,4},{4,8},{8,12},{12,14},{14,10},{10,6},{6,2},{2,0},{1,5},{5,9},... | collective-permute-start | bytes 368648 | tf_op jit(solution)/shard_map/ppermute | solution.py:219
  40.7 5.6 %collective-permute-start.20 = (bf16[24,2560]{1,0:T(8,128)(2,1)S(1)}, bf16[24,2560]{1,0:T(8,128)(2,1)S(1)}, u32[]{:S(2)}, u32[]{:S(2)}) collective-permute-start(bf16[24,2560]{1,0:T(8,128)(2,1)S(1)} %slice.21), channel_id=1, source_target_pairs={{4,0},{8,4},{12,8},{14,12},{10,14},{6,10},{2,6},{0,2},{5,1},{9,5},... | collective-permute-start | bytes 368648 | tf_op jit(solution)/shard_map/ppermute | solution.py:220
  42.4 8.2 %collective-permute-start.18 = (bf16[168,1280]{1,0:T(8,128)(2,1)S(1)}, bf16[168,1280]{1,0:T(8,128)(2,1)S(1)}, u32[]{:S(2)}, u32[]{:S(2)}) collective-permute-start(bf16[168,1280]{1,0:T(8,128)(2,1)S(1)} %maximum_dynamic-update-slice_fusion), channel_id=1, source_target_pairs={{0,1},{1,0},{2,3},{3,2},{4,5},{5,4},{6,7},{7,6},{8,9},{9,8},{10,11... | collective-permute-start | bytes 1290248 | tf_op jit(solution)/shard_map/ppermute | solution.py:207
  46.4 4.1 %collective-permute-start.21 = (bf16[24,1280]{1,0:T(8,128)(2,1)S(1)}, bf16[24,1280]{1,0:T(8,128)(2,1)S(1)}, u32[]{:S(2)}, u32[]{:S(2)}) collective-permute-start(bf16[24,1280]{1,0:T(8,128)(2,1)S(1)} %pad_maximum_fusion.2), channel_id=1, source_target_pairs={{0,1},{1,0},{2,3},{3,2},{4,5},{5,4},{6,7},{7,6},{8,9},{9,8},{10,11... | collective-permute-start | bytes 184328 | tf_op jit(solution)/shard_map/ppermute | solution.py:207

commit v17 on v15

--- a/solution.py
+++ b/solution.py
@@ -239,9 +239,9 @@
             grad_part = (1, grad_first, grad_block, grad_block)
 
             def square(part, lefts, out, **more):
-                starts = [part * cut // 2, part * cut // 2 + cut // 4]
-                groups = [(0, cut, (0, at, cut, cut // 4), 0, 0, at, act_block, half_rows) for at in starts]
-                return tiles(scale, groups, lefts, [chains[0]], [act_shape], out, banks=2, **more)
+                at = part * cut // 2
+                group = (0, cut, (0, at, cut, cut // 2), 0, 0, at, act_block, half_rows)
+                return tiles(scale, [group], lefts, [chains[0]], [act_shape], out, **more)
 
             act_cov, turned_first = square(0, [left_first], None, hand_on=True)
             last_second, act_cov = lax.optimization_barrier(((forward[1], backward[1]), act_cov))

time: 63.6 us -> 63.6 us (level)
  no operation moved by 1% of the time
where the time goes in v17:
time: 63.6 us; the launch traced here: 63.5 us
  Pallas kernels  21.2 us (33%)
  waiting for transfers between devices  21.2 us (33%)
  starting transfers between devices  18.8 us (30%)
  between operations  1.62 us (3%)
    pallas_call x3, Pallas kernels, tiles(): pl.pallas_call(functools.partial(tiles_kernel, scale, groups, ready, [len...  20.1 us
    ppermute x8, starting transfers between devices, local(): backward[k] = lax.ppermute(behind_of, 'row', behind)  15.4 us
    ppermute x8, waiting for transfers between devices, local(): backward[k] = lax.ppermute(behind_of, 'row', behind)  11.4 us
    ppermute x8, waiting for transfers between devices, local(): forward[k] = lax.ppermute(ahead_of, 'row', ahead)  8.82 us
    ppermute x8, starting transfers between devices, local(): forward[k] = lax.ppermute(ahead_of, 'row', ahead)  2.06 us
  transfers between devices with their start and end apart: 22, of which 11 were waited for; matrix products, arithmetic and copies ran while one was open for 1% of the time, Pallas kernels for 11%

profile of v17, /device:TPU:0, one launch (start us, length us, event | category | flops | bytes accessed | tf_op | source)
XLA Modules:
  0.0 63.5 jit_solution(4968645880188809059)
XLA Ops:
  1.3 1.1 %shard_map.50 = (bf16[24,4096]{1,0:T(8,128)(2,1)S(1)}, bf16[24,4096]{1,0:T(8,128)(2,1)S(1)}, bf16[24,5120]{1,0:T(8,128)(2,1)S(1)}, bf16[24,5120]{1,0:T(8,128)(2,1)S(1)}) custom-call(s32[1]{0:T(128)} %bitcast.half_ref, s32[1]{0:T(128)S(6)} %copy.23.count_ref, bf16[12,14336]{1,0:T(8,128)(2,1)} %act_ref.1, bf16[12,4096]{1,0:T(8,128)(2,1)} %grad_ref.1), custom_call_target="tpu_custom_call" | custom-call | tf_op jit(solution)/shard_map/pallas_call | solution.py:186
  2.4 0.6 collective-permute-start
  3.0 0.1 collective-permute-start.3
  3.1 1.0 %collective-permute-done = bf16[24,4096]{1,0:T(8,128)(2,1)S(1)} collective-permute-done((bf16[24,4096]{1,0:T(8,128)(2,1)S(1)}, bf16[24,4096]{1,0:T(8,128)(2,1)S(1)}, u32[]{:S(2)}, u32[]{:S(2)}) %collective-permute-start) | collective-permute-done | bytes 196640 | tf_op jit(solution)/shard_map/ppermute | solution.py:192
  4.1 2.9 %collective-permute-start.2 = (bf16[24,4096]{1,0:T(8,128)(2,1)S(1)}, bf16[24,4096]{1,0:T(8,128)(2,1)S(1)}, u32[]{:S(2)}, u32[]{:S(2)}) collective-permute-start(bf16[24,4096]{1,0:T(8,128)(2,1)S(1)} %add.76.refs_1_.refs_3_), channel_id=1, source_target_pairs={{4,0},{8,4},{12,8},{14,12},{10,14},{6,10},{2,6},{0,2},{5,1},{9,5},... | collective-permute-start | bytes 589832 | tf_op jit(solution)/shard_map/ppermute | solution.py:221
  7.0 0.2 collective-permute-start.1
  7.1 0.0 collective-permute-done.3
  7.1 0.1 add.79.refs_11_
  7.2 1.9 %collective-permute-start.14 = (bf16[24,5120]{1,0:T(8,128)(2,1)S(1)}, bf16[24,5120]{1,0:T(8,128)(2,1)S(1)}, u32[]{:S(2)}, u32[]{:S(2)}) collective-permute-start(bf16[24,5120]{1,0:T(8,128)(2,1)S(1)} %add.79.refs_11_), channel_id=1, source_target_pairs={{4,0},{8,4},{12,8},{14,12},{10,14},{6,10},{2,6},{0,2},{5,1},{9,5},... | collective-permute-start | bytes 737288 | tf_op jit(solution)/shard_map/ppermute | solution.py:221
  9.1 0.2 collective-permute-start.6
  9.3 3.5 %collective-permute-done.2.refs_3_.refs_5_ = bf16[24,4096]{1,0:T(8,128)(2,1)S(1)} collective-permute-done((bf16[24,4096]{1,0:T(8,128)(2,1)S(1)}, bf16[24,4096]{1,0:T(8,128)(2,1)S(1)}, u32[]{:S(2)}, u32[]{:S(2)}) %collective-permute-start.2) | collective-permute-done | bytes 196640 | tf_op jit(solution)/shard_map/ppermute | solution.py:221
  12.8 2.0 %collective-permute-done.1.refs_2_.refs_4_ = bf16[24,4096]{1,0:T(8,128)(2,1)S(1)} collective-permute-done((bf16[24,4096]{1,0:T(8,128)(2,1)S(1)}, bf16[24,4096]{1,0:T(8,128)(2,1)S(1)}, u32[]{:S(2)}, u32[]{:S(2)}) %collective-permute-start.1) | collective-permute-done | bytes 196640 | tf_op jit(solution)/shard_map/ppermute | solution.py:220
  14.8 0.1 collective-permute-start.4
  14.9 1.9 %collective-permute-start.5 = (bf16[24,4096]{1,0:T(8,128)(2,1)S(1)}, bf16[24,4096]{1,0:T(8,128)(2,1)S(1)}, u32[]{:S(2)}, u32[]{:S(2)}) collective-permute-start(bf16[24,4096]{1,0:T(8,128)(2,1)S(1)} %collective-permute-done.2.refs_3_.refs_5_), channel_id=1, source_target_pairs={{4,0},{8,4},{12,8},{14,12},{10,14},{6,10},{2,6},{0,2},{5,1},{9,5},... | collective-permute-start | bytes 589832 | tf_op jit(solution)/shard_map/ppermute | solution.py:221
  16.8 1.2 %collective-permute-done.14.refs_13_ = bf16[24,5120]{1,0:T(8,128)(2,1)S(1)} collective-permute-done((bf16[24,5120]{1,0:T(8,128)(2,1)S(1)}, bf16[24,5120]{1,0:T(8,128)(2,1)S(1)}, u32[]{:S(2)}, u32[]{:S(2)}) %collective-permute-start.14) | collective-permute-done | bytes 245792 | tf_op jit(solution)/shard_map/ppermute | solution.py:221
  18.0 2.0 %collective-permute-start.15 = (bf16[24,5120]{1,0:T(8,128)(2,1)S(1)}, bf16[24,5120]{1,0:T(8,128)(2,1)S(1)}, u32[]{:S(2)}, u32[]{:S(2)}) collective-permute-start(bf16[24,5120]{1,0:T(8,128)(2,1)S(1)} %collective-permute-done.14.refs_13_), channel_id=1, source_target_pairs={{4,0},{8,4},{12,8},{14,12},{10,14},{6,10},{2,6},{0,2},{5,1},{9,5},... | collective-permute-start | bytes 737288 | tf_op jit(solution)/shard_map/ppermute | solution.py:221
  20.0 0.0 collective-permute-done.6.refs_12_
  20.0 0.1 collective-permute-start.10
  20.2 2.5 %collective-permute-done.5.refs_5_.refs_7_ = bf16[24,4096]{1,0:T(8,128)(2,1)S(1)} collective-permute-done((bf16[24,4096]{1,0:T(8,128)(2,1)S(1)}, bf16[24,4096]{1,0:T(8,128)(2,1)S(1)}, u32[]{:S(2)}, u32[]{:S(2)}) %collective-permute-start.5) | collective-permute-done | bytes 196640 | tf_op jit(solution)/shard_map/ppermute | solution.py:221
  22.7 1.5 %collective-permute-done.4.refs_4_.refs_6_ = bf16[24,4096]{1,0:T(8,128)(2,1)S(1)} collective-permute-done((bf16[24,4096]{1,0:T(8,128)(2,1)S(1)}, bf16[24,4096]{1,0:T(8,128)(2,1)S(1)}, u32[]{:S(2)}, u32[]{:S(2)}) %collective-permute-start.4) | collective-permute-done | bytes 196640 | tf_op jit(solution)/shard_map/ppermute | solution.py:220
  24.2 0.5 collective-permute-start.7
  24.7 1.5 %collective-permute-start.8 = (bf16[24,4096]{1,0:T(8,128)(2,1)S(1)}, bf16[24,4096]{1,0:T(8,128)(2,1)S(1)}, u32[]{:S(2)}, u32[]{:S(2)}) collective-permute-start(bf16[24,4096]{1,0:T(8,128)(2,1)S(1)} %collective-permute-done.5.refs_5_.refs_7_), channel_id=1, source_target_pairs={{4,0},{8,4},{12,8},{14,12},{10,14},{6,10},{2,6},{0,2},{5,1},{9,5},... | collective-permute-start | bytes 589832 | tf_op jit(solution)/shard_map/ppermute | solution.py:221
  26.3 1.7 %collective-permute-done.15.refs_15_ = bf16[24,5120]{1,0:T(8,128)(2,1)S(1)} collective-permute-done((bf16[24,5120]{1,0:T(8,128)(2,1)S(1)}, bf16[24,5120]{1,0:T(8,128)(2,1)S(1)}, u32[]{:S(2)}, u32[]{:S(2)}) %collective-permute-start.15) | collective-permute-done | bytes 245792 | tf_op jit(solution)/shard_map/ppermute | solution.py:221
  28.0 1.9 %collective-permute-start.16 = (bf16[24,5120]{1,0:T(8,128)(2,1)S(1)}, bf16[24,5120]{1,0:T(8,128)(2,1)S(1)}, u32[]{:S(2)}, u32[]{:S(2)}) collective-permute-start(bf16[24,5120]{1,0:T(8,128)(2,1)S(1)} %collective-permute-done.15.refs_15_), channel_id=1, source_target_pairs={{4,0},{8,4},{12,8},{14,12},{10,14},{6,10},{2,6},{0,2},{5,1},{9,5},... | collective-permute-start | bytes 737288 | tf_op jit(solution)/shard_map/ppermute | solution.py:221
  29.9 0.0 collective-permute-done.10.refs_14_
  29.9 0.1 collective-permute-start.13
  30.1 2.5 %collective-permute-done.8.refs_7_.refs_9_ = bf16[24,4096]{1,0:T(8,128)(2,1)S(1)} collective-permute-done((bf16[24,4096]{1,0:T(8,128)(2,1)S(1)}, bf16[24,4096]{1,0:T(8,128)(2,1)S(1)}, u32[]{:S(2)}, u32[]{:S(2)}) %collective-permute-start.8) | collective-permute-done | bytes 196640 | tf_op jit(solution)/shard_map/ppermute | solution.py:221
  32.6 1.2 %collective-permute-done.7.refs_6_.refs_8_ = bf16[24,4096]{1,0:T(8,128)(2,1)S(1)} collective-permute-done((bf16[24,4096]{1,0:T(8,128)(2,1)S(1)}, bf16[24,4096]{1,0:T(8,128)(2,1)S(1)}, u32[]{:S(2)}, u32[]{:S(2)}) %collective-permute-start.7) | collective-permute-done | bytes 196640 | tf_op jit(solution)/shard_map/ppermute | solution.py:220
  33.8 1.6 %collective-permute-start.12 = (bf16[24,2048]{1,0:T(8,128)(2,1)S(1)}, bf16[24,2048]{1,0:T(8,128)(2,1)S(1)}, u32[]{:S(2)}, u32[]{:S(2)}) collective-permute-start(bf16[24,2048]{1,0:T(8,128)(2,1)S(1)} %slice.19), channel_id=1, source_target_pairs={{4,0},{8,4},{12,8},{14,12},{10,14},{6,10},{2,6},{0,2},{5,1},{9,5},... | collective-permute-start | bytes 294920 | tf_op jit(solution)/shard_map/ppermute | solution.py:221
  35.4 0.4 collective-permute-start.11
  35.8 0.1 collective-permute-start.9
  35.9 3.0 %collective-permute-done.13.refs_16_ = bf16[24,5120]{1,0:T(8,128)(2,1)S(1)} collective-permute-done((bf16[24,5120]{1,0:T(8,128)(2,1)S(1)}, bf16[24,5120]{1,0:T(8,128)(2,1)S(1)}, u32[]{:S(2)}, u32[]{:S(2)}) %collective-permute-start.13) | collective-permute-done | bytes 245792 | tf_op jit(solution)/shard_map/ppermute | solution.py:220
  38.9 0.0 collective-permute-done.12
  38.9 1.1 %collective-permute-done.11 = bf16[24,2048]{1,0:T(8,128)(2,1)S(1)} collective-permute-done((bf16[24,2048]{1,0:T(8,128)(2,1)S(1)}, bf16[24,2048]{1,0:T(8,128)(2,1)S(1)}, u32[]{:S(2)}, u32[]{:S(2)}) %collective-permute-start.11) | collective-permute-done | bytes 98336 | tf_op jit(solution)/shard_map/ppermute | solution.py:220
  40.0 0.0 collective-permute-done.16.refs_17_
  40.1 0.1 collective-permute-start.17
  40.2 0.5 collective-permute-start.19
  40.7 1.6 %collective-permute-start.20 = (bf16[24,2560]{1,0:T(8,128)(2,1)S(1)}, bf16[24,2560]{1,0:T(8,128)(2,1)S(1)}, u32[]{:S(2)}, u32[]{:S(2)}) collective-permute-start(bf16[24,2560]{1,0:T(8,128)(2,1)S(1)} %slice.21), channel_id=1, source_target_pairs={{4,0},{8,4},{12,8},{14,12},{10,14},{6,10},{2,6},{0,2},{5,1},{9,5},... | collective-permute-start | bytes 368648 | tf_op jit(solution)/shard_map/ppermute | solution.py:221
  42.3 0.1 collective-permute-start.18
  42.4 0.0 collective-permute-done.17
  42.4 0.0 collective-permute-done.9
  42.4 0.1 broadcast_select_fusion.1
  42.5 3.7 %shard_map.51 = (f32[1792,7168]{1,0:T(8,128)}, bf16[1024,192]{1,0:T(8,128)(2,1)S(1)}) custom-call(bf16[192,1024]{1,0:T(8,128)(2,1)S(1)} %pad_maximum_fusion.refs_0_, bf16[24,4096]{1,0:T(8,128)(2,1)S(1)} %add.76.refs_1_.refs_3_, bf16[24,4096]{1,0:T(8,128)(2,1)S(1)} %collective-permute-done.1.refs_2_.refs_4_, ...), custom_call_target="tpu_custom_call" | custom-call | flops 805306368 | bytes 8388608 | tf_op jit(solution)/shard_map/pallas_call | solution.py:118
  46.3 0.0 collective-permute-done.19
  46.3 0.0 collective-permute-done.20
  46.4 0.5 collective-permute-start.21
  46.9 3.5 %shard_map.52.refs_19_ = f32[1792,7168]{1,0:T(8,128)} custom-call(bf16[1024,192]{1,0:T(8,128)(2,1)S(1)} %get-tuple-element.43.refs_0_, bf16[24,4096]{1,0:T(8,128)(2,1)S(1)} %add.76.refs_1_.refs_3_, bf16[24,4096]{1,0:T(8,128)(2,1)S(1)} %collective-permute-done.1.refs_2_.refs_4_, ...), custom_call_target="tpu_custom_call", output_to_operand_aliasing={{}: (9, {})} | custom-call | flops 805306368 | bytes 8388608 | tf_op jit(solution)/shard_map/pallas_call | solution.py:118
  50.5 0.0 collective-permute-done.21
  50.5 0.0 collective-permute-done.18
  50.6 12.8 %shard_map.53 = (f32[1792,7168]{1,0:T(8,128)}, f32[512,2048]{1,0:T(8,128)}) custom-call(bf16[1024,192]{1,0:T(8,128)(2,1)S(1)} %get-tuple-element.43.refs_0_, bf16[192,768]{1,0:T(8,128)(2,1)S(1)} %fusion.refs_1_, bf16[192,512]{1,0:T(8,128)(2,1)S(1)} %pad_maximum_fusion.1.refs_2_, ...), custom_call_target="tpu_custom_call", output_to_operand_aliasing={{0}: (19, {})} | custom-call | flops 3724541952 | bytes 38797312 | tf_op jit(solution)/shard_map/pallas_call | solution.py:118
  (47 shorter events, 0.5 us)
Async XLA Ops:
  2.4 1.6 %collective-permute-start = (bf16[24,4096]{1,0:T(8,128)(2,1)S(1)}, bf16[24,4096]{1,0:T(8,128)(2,1)S(1)}, u32[]{:S(2)}, u32[]{:S(2)}) collective-permute-start(bf16[24,4096]{1,0:T(8,128)(2,1)S(1)} %get-tuple-element.27), channel_id=1, source_target_pairs={{0,1},{1,0},{2,3},{3,2},{4,5},{5,4},{6,7},{7,6},{8,9},{9,8},{10,11... | collective-permute-start | bytes 589832 | tf_op jit(solution)/shard_map/ppermute | solution.py:192
  3.0 4.1 %collective-permute-start.3 = (bf16[24,5120]{1,0:T(8,128)(2,1)S(1)}, bf16[24,5120]{1,0:T(8,128)(2,1)S(1)}, u32[]{:S(2)}, u32[]{:S(2)}) collective-permute-start(bf16[24,5120]{1,0:T(8,128)(2,1)S(1)} %get-tuple-element.29), channel_id=1, source_target_pairs={{0,1},{1,0},{2,3},{3,2},{4,5},{5,4},{6,7},{7,6},{8,9},{9,8},{10,11... | collective-permute-start | bytes 737288 | tf_op jit(solution)/shard_map/ppermute | solution.py:192
  4.1 8.6 %collective-permute-start.2 = (bf16[24,4096]{1,0:T(8,128)(2,1)S(1)}, bf16[24,4096]{1,0:T(8,128)(2,1)S(1)}, u32[]{:S(2)}, u32[]{:S(2)}) collective-permute-start(bf16[24,4096]{1,0:T(8,128)(2,1)S(1)} %add.76.refs_1_.refs_3_), channel_id=1, source_target_pairs={{4,0},{8,4},{12,8},{14,12},{10,14},{6,10},{2,6},{0,2},{5,1},{9,5},... | collective-permute-start | bytes 589832 | tf_op jit(solution)/shard_map/ppermute | solution.py:221
  7.0 7.8 %collective-permute-start.1 = (bf16[24,4096]{1,0:T(8,128)(2,1)S(1)}, bf16[24,4096]{1,0:T(8,128)(2,1)S(1)}, u32[]{:S(2)}, u32[]{:S(2)}) collective-permute-start(bf16[24,4096]{1,0:T(8,128)(2,1)S(1)} %add.76.refs_1_.refs_3_), channel_id=1, source_target_pairs={{0,4},{4,8},{8,12},{12,14},{14,10},{10,6},{6,2},{2,0},{1,5},{5,9},... | collective-permute-start | bytes 589832 | tf_op jit(solution)/shard_map/ppermute | solution.py:220
  7.2 10.8 %collective-permute-start.14 = (bf16[24,5120]{1,0:T(8,128)(2,1)S(1)}, bf16[24,5120]{1,0:T(8,128)(2,1)S(1)}, u32[]{:S(2)}, u32[]{:S(2)}) collective-permute-start(bf16[24,5120]{1,0:T(8,128)(2,1)S(1)} %add.79.refs_11_), channel_id=1, source_target_pairs={{4,0},{8,4},{12,8},{14,12},{10,14},{6,10},{2,6},{0,2},{5,1},{9,5},... | collective-permute-start | bytes 737288 | tf_op jit(solution)/shard_map/ppermute | solution.py:221
  9.1 10.9 %collective-permute-start.6 = (bf16[24,5120]{1,0:T(8,128)(2,1)S(1)}, bf16[24,5120]{1,0:T(8,128)(2,1)S(1)}, u32[]{:S(2)}, u32[]{:S(2)}) collective-permute-start(bf16[24,5120]{1,0:T(8,128)(2,1)S(1)} %add.79.refs_11_), channel_id=1, source_target_pairs={{0,4},{4,8},{8,12},{12,14},{14,10},{10,6},{6,2},{2,0},{1,5},{5,9},... | collective-permute-start | bytes 737288 | tf_op jit(solution)/shard_map/ppermute | solution.py:220
  14.8 9.5 %collective-permute-start.4 = (bf16[24,4096]{1,0:T(8,128)(2,1)S(1)}, bf16[24,4096]{1,0:T(8,128)(2,1)S(1)}, u32[]{:S(2)}, u32[]{:S(2)}) collective-permute-start(bf16[24,4096]{1,0:T(8,128)(2,1)S(1)} %collective-permute-done.1.refs_2_.refs_4_), channel_id=1, source_target_pairs={{0,4},{4,8},{8,12},{12,14},{14,10},{10,6},{6,2},{2,0},{1,5},{5,9},... | collective-permute-start | bytes 589832 | tf_op jit(solution)/shard_map/ppermute | solution.py:220
  14.9 7.8 %collective-permute-start.5 = (bf16[24,4096]{1,0:T(8,128)(2,1)S(1)}, bf16[24,4096]{1,0:T(8,128)(2,1)S(1)}, u32[]{:S(2)}, u32[]{:S(2)}) collective-permute-start(bf16[24,4096]{1,0:T(8,128)(2,1)S(1)} %collective-permute-done.2.refs_3_.refs_5_), channel_id=1, source_target_pairs={{4,0},{8,4},{12,8},{14,12},{10,14},{6,10},{2,6},{0,2},{5,1},{9,5},... | collective-permute-start | bytes 589832 | tf_op jit(solution)/shard_map/ppermute | solution.py:221
  18.0 10.0 %collective-permute-start.15 = (bf16[24,5120]{1,0:T(8,128)(2,1)S(1)}, bf16[24,5120]{1,0:T(8,128)(2,1)S(1)}, u32[]{:S(2)}, u32[]{:S(2)}) collective-permute-start(bf16[24,5120]{1,0:T(8,128)(2,1)S(1)} %collective-permute-done.14.refs_13_), channel_id=1, source_target_pairs={{4,0},{8,4},{12,8},{14,12},{10,14},{6,10},{2,6},{0,2},{5,1},{9,5},... | collective-permute-start | bytes 737288 | tf_op jit(solution)/shard_map/ppermute | solution.py:221
  20.0 9.9 %collective-permute-start.10 = (bf16[24,5120]{1,0:T(8,128)(2,1)S(1)}, bf16[24,5120]{1,0:T(8,128)(2,1)S(1)}, u32[]{:S(2)}, u32[]{:S(2)}) collective-permute-start(bf16[24,5120]{1,0:T(8,128)(2,1)S(1)} %collective-permute-done.6.refs_12_), channel_id=1, source_target_pairs={{0,4},{4,8},{8,12},{12,14},{14,10},{10,6},{6,2},{2,0},{1,5},{5,9},... | collective-permute-start | bytes 737288 | tf_op jit(solution)/shard_map/ppermute | solution.py:220
  24.2 9.5 %collective-permute-start.7 = (bf16[24,4096]{1,0:T(8,128)(2,1)S(1)}, bf16[24,4096]{1,0:T(8,128)(2,1)S(1)}, u32[]{:S(2)}, u32[]{:S(2)}) collective-permute-start(bf16[24,4096]{1,0:T(8,128)(2,1)S(1)} %collective-permute-done.4.refs_4_.refs_6_), channel_id=1, source_target_pairs={{0,4},{4,8},{8,12},{12,14},{14,10},{10,6},{6,2},{2,0},{1,5},{5,9},... | collective-permute-start | bytes 589832 | tf_op jit(solution)/shard_map/ppermute | solution.py:220
  24.7 7.8 %collective-permute-start.8 = (bf16[24,4096]{1,0:T(8,128)(2,1)S(1)}, bf16[24,4096]{1,0:T(8,128)(2,1)S(1)}, u32[]{:S(2)}, u32[]{:S(2)}) collective-permute-start(bf16[24,4096]{1,0:T(8,128)(2,1)S(1)} %collective-permute-done.5.refs_5_.refs_7_), channel_id=1, source_target_pairs={{4,0},{8,4},{12,8},{14,12},{10,14},{6,10},{2,6},{0,2},{5,1},{9,5},... | collective-permute-start | bytes 589832 | tf_op jit(solution)/shard_map/ppermute | solution.py:221
  28.0 12.0 %collective-permute-start.16 = (bf16[24,5120]{1,0:T(8,128)(2,1)S(1)}, bf16[24,5120]{1,0:T(8,128)(2,1)S(1)}, u32[]{:S(2)}, u32[]{:S(2)}) collective-permute-start(bf16[24,5120]{1,0:T(8,128)(2,1)S(1)} %collective-permute-done.15.refs_15_), channel_id=1, source_target_pairs={{4,0},{8,4},{12,8},{14,12},{10,14},{6,10},{2,6},{0,2},{5,1},{9,5},... | collective-permute-start | bytes 737288 | tf_op jit(solution)/shard_map/ppermute | solution.py:221
  29.9 9.0 %collective-permute-start.13 = (bf16[24,5120]{1,0:T(8,128)(2,1)S(1)}, bf16[24,5120]{1,0:T(8,128)(2,1)S(1)}, u32[]{:S(2)}, u32[]{:S(2)}) collective-permute-start(bf16[24,5120]{1,0:T(8,128)(2,1)S(1)} %collective-permute-done.10.refs_14_), channel_id=1, source_target_pairs={{0,4},{4,8},{8,12},{12,14},{14,10},{10,6},{6,2},{2,0},{1,5},{5,9},... | collective-permute-start | bytes 737288 | tf_op jit(solution)/shard_map/ppermute | solution.py:220
  33.8 5.2 %collective-permute-start.12 = (bf16[24,2048]{1,0:T(8,128)(2,1)S(1)}, bf16[24,2048]{1,0:T(8,128)(2,1)S(1)}, u32[]{:S(2)}, u32[]{:S(2)}) collective-permute-start(bf16[24,2048]{1,0:T(8,128)(2,1)S(1)} %slice.19), channel_id=1, source_target_pairs={{4,0},{8,4},{12,8},{14,12},{10,14},{6,10},{2,6},{0,2},{5,1},{9,5},... | collective-permute-start | bytes 294920 | tf_op jit(solution)/shard_map/ppermute | solution.py:221
  35.4 4.6 %collective-permute-start.11 = (bf16[24,2048]{1,0:T(8,128)(2,1)S(1)}, bf16[24,2048]{1,0:T(8,128)(2,1)S(1)}, u32[]{:S(2)}, u32[]{:S(2)}) collective-permute-start(bf16[24,2048]{1,0:T(8,128)(2,1)S(1)} %slice.18), channel_id=1, source_target_pairs={{0,4},{4,8},{8,12},{12,14},{14,10},{10,6},{6,2},{2,0},{1,5},{5,9},... | collective-permute-start | bytes 294920 | tf_op jit(solution)/shard_map/ppermute | solution.py:220
  35.8 6.6 %collective-permute-start.9 = (bf16[168,1024]{1,0:T(8,128)(2,1)S(1)}, bf16[168,1024]{1,0:T(8,128)(2,1)S(1)}, u32[]{:S(2)}, u32[]{:S(2)}) collective-permute-start(bf16[168,1024]{1,0:T(8,128)(2,1)S(1)} %dynamic-slice_dynamic-update-slice_fusion), channel_id=1, source_target_pairs={{0,1},{1,0},{2,3},{3,2},{4,5},{5,4},{6,7},{7,6},{8,9},{9,8},{10,11... | collective-permute-start | bytes 1032200 | tf_op jit(solution)/shard_map/ppermute | solution.py:208
  40.1 2.3 %collective-permute-start.17 = (bf16[24,1024]{1,0:T(8,128)(2,1)S(1)}, bf16[24,1024]{1,0:T(8,128)(2,1)S(1)}, u32[]{:S(2)}, u32[]{:S(2)}) collective-permute-start(bf16[24,1024]{1,0:T(8,128)(2,1)S(1)} %constant_dynamic-slice_fusion.16), channel_id=1, source_target_pairs={{0,1},{1,0},{2,3},{3,2},{4,5},{5,4},{6,7},{7,6},{8,9},{9,8},{10,11... | collective-permute-start | bytes 147464 | tf_op jit(solution)/shard_map/ppermute | solution.py:208
  40.2 6.1 %collective-permute-start.19 = (bf16[24,2560]{1,0:T(8,128)(2,1)S(1)}, bf16[24,2560]{1,0:T(8,128)(2,1)S(1)}, u32[]{:S(2)}, u32[]{:S(2)}) collective-permute-start(bf16[24,2560]{1,0:T(8,128)(2,1)S(1)} %slice.20), channel_id=1, source_target_pairs={{0,4},{4,8},{8,12},{12,14},{14,10},{10,6},{6,2},{2,0},{1,5},{5,9},... | collective-permute-start | bytes 368648 | tf_op jit(solution)/shard_map/ppermute | solution.py:220
  40.7 5.6 %collective-permute-start.20 = (bf16[24,2560]{1,0:T(8,128)(2,1)S(1)}, bf16[24,2560]{1,0:T(8,128)(2,1)S(1)}, u32[]{:S(2)}, u32[]{:S(2)}) collective-permute-start(bf16[24,2560]{1,0:T(8,128)(2,1)S(1)} %slice.21), channel_id=1, source_target_pairs={{4,0},{8,4},{12,8},{14,12},{10,14},{6,10},{2,6},{0,2},{5,1},{9,5},... | collective-permute-start | bytes 368648 | tf_op jit(solution)/shard_map/ppermute | solution.py:221
  42.3 8.2 %collective-permute-start.18 = (bf16[168,1280]{1,0:T(8,128)(2,1)S(1)}, bf16[168,1280]{1,0:T(8,128)(2,1)S(1)}, u32[]{:S(2)}, u32[]{:S(2)}) collective-permute-start(bf16[168,1280]{1,0:T(8,128)(2,1)S(1)} %maximum_dynamic-update-slice_fusion), channel_id=1, source_target_pairs={{0,1},{1,0},{2,3},{3,2},{4,5},{5,4},{6,7},{7,6},{8,9},{9,8},{10,11... | collective-permute-start | bytes 1290248 | tf_op jit(solution)/shard_map/ppermute | solution.py:208
  46.4 4.1 %collective-permute-start.21 = (bf16[24,1280]{1,0:T(8,128)(2,1)S(1)}, bf16[24,1280]{1,0:T(8,128)(2,1)S(1)}, u32[]{:S(2)}, u32[]{:S(2)}) collective-permute-start(bf16[24,1280]{1,0:T(8,128)(2,1)S(1)} %pad_maximum_fusion.2), channel_id=1, source_target_pairs={{0,1},{1,0},{2,3},{3,2},{4,5},{5,4},{6,7},{7,6},{8,9},{9,8},{10,11... | collective-permute-start | bytes 184328 | tf_op jit(solution)/shard_map/ppermute | solution.py:208
